TPU v7x, 32 devices: a whole 2x2x4 slice. The times are simulated.
32 devices in a mesh: case: 2 (over y), strip: 8 (over z, x), clus: 2 (over core).
Axes of the slice: x: 2, y: 2, z: 4, core: 2. Of those that a mesh axis runs over, the one named last changes fastest.
Arguments:
- loads: float32 [4, 32768], P(None, ('case', 'strip', 'clus')), parts along dimension 1, may hold values from -60 to 60, as said below
- self_term: float32 [32768], P(('case', 'strip', 'clus')), parts along dimension 0, may hold values from 1 to 4
- near_tiles: bfloat16 [2560, 128, 128], P(('case', 'strip', 'clus')), parts along dimension 0, may hold values from -0.083496094 to 0.083496094
- near_list: int32 [2560, 2], P(('case', 'strip', 'clus')), parts along dimension 0, may hold values from 0 to 47, as said below
- far_rows: float32 [32, 32768], P(None, ('case', 'strip', 'clus')), parts along dimension 1, may hold values from -1 to 1
- far_cols: float32 [32, 32768], P(None, ('case', 'strip', 'clus')), parts along dimension 1, may hold values from -0.1875 to 0.1875
- coupling: float32 [16, 16, 32, 32], P(None, ('strip', 'clus')), may hold values from -0.375 to 0.375
- ranks: int32 [16, 16], P(None, ('strip', 'clus')), may hold values from 0 to 32, as said below
Outputs:
- solution: float32 [4, 32768], P(None, ('case', 'strip', 'clus')), parts along dimension 1
There are 2 independent parts, one for each index of `case`. A program takes and returns all parts, laid end to end along the dimension named above; an argument that names none is the same for every part. Nothing has to cross between parts.
Inputs may be any that keep to these rules, and one draw needn't show every extreme that they name: `loads`: rises about threefold in scale from the first panel to the last. `near_list`: column 0 is a target block row of the group, 0 to 7, each of which has at least one block; column 1 is a source block of the window, 0 to 47; the same pair may repeat. `ranks`: zero exactly where the two groups' strips are less than two apart, otherwise 32 // 4 to 32.
All inputs are finite; a program needn't handle non-finite values.
Results may differ from a plain program's by a relative error of at most 0.00044.
Values may be sent and summed in bfloat16 or wider, within the bound.
No kernel may reach another device: no remote copies, remote signals or barrier semaphores. Data moves between devices by JAX's collectives and lax.ppermute only.
A program may use at most 64 MiB of HBM per device.

v0:
```python
import jax
import jax.numpy as jnp
from jax import lax
from jax.sharding import PartitionSpec as P

ITERS = 2


HIGH = lax.Precision.HIGHEST


def padded(array, sides, width):
    for axis, dim in sides:
        devices, length = (lax.axis_size(axis), array.shape[dim])
        up = [(i, (i + 1) % devices) for i in range(devices - 1)]
        down = [(j, i) for i, j in up]
        last = lax.slice_in_dim(array, length - width, length, axis=dim)
        leading = lax.slice_in_dim(array, 0, width, axis=dim)
        before = lax.ppermute(last, axis, up)
        after = lax.ppermute(leading, axis, down)
        array = jnp.concatenate([before, array, after], axis=dim)
    return array


def near_field(field, near_tiles, near_list):
    nrhs = field.shape[0]
    tile = near_tiles.shape[1]
    rounded = field.astype(jnp.bfloat16)
    paired = lax.all_gather(rounded, "clus", axis=1, tiled=True)
    window = padded(paired, (("strip", 1),), paired.shape[1])
    blocks = window.reshape(nrhs, -1, tile)
    sources = jnp.take(blocks, near_list[:, 1], axis=1)
    product = jnp.einsum("rnk,nkt->rnt", sources, near_tiles, preferred_element_type=jnp.float32)
    block_rows = field.shape[1] // tile
    onehot = (near_list[:, 0][:, None] == jnp.arange(block_rows, dtype=jnp.int32)[None, :]).astype(
        jnp.float32
    )
    summed = jnp.einsum("rnt,nb->rbt", product, onehot, precision=HIGH)
    return summed.reshape(nrhs, -1)


def far_field(field, far_rows, far_cols, coupling, ranks):
    rank = far_cols.shape[0]
    proj = jnp.einsum("rp,ap->ra", field, far_cols, precision=HIGH)
    masks = (jnp.arange(rank, dtype=jnp.int32)[None, :] < ranks[:, 0][:, None]).astype(jnp.float32)
    masked = masks[:, None, :] * proj[None]
    couple = coupling[:, 0]
    local = lax.psum_scatter(
        jnp.einsum("ira,iab->irb", masked, couple, precision=HIGH),
        ("strip", "clus"),
        scatter_dimension=0,
        tiled=True,
    )[0]
    return jnp.einsum("rb,bp->rp", local, far_rows, precision=HIGH)


def apply_operator(field, self_term, near_tiles, near_list, far_rows, far_cols, coupling, ranks):
    near = near_field(field, near_tiles, near_list)
    far = far_field(field, far_rows, far_cols, coupling, ranks)
    return self_term[None, :] * field + near + far


def small_solve(hess, beta):
    gram = [
        [sum((hess[j][k] * hess[j][l] for j in range(ITERS + 1))) for l in range(ITERS)]
        for k in range(ITERS)
    ]
    target = [beta * hess[0][k] for k in range(ITERS)]
    lower = [[None] * ITERS for k in range(ITERS)]
    for i in range(ITERS):
        for j in range(i + 1):
            total = gram[i][j]
            for m in range(j):
                total = total - lower[i][m] * lower[j][m]
            if i == j:
                lower[i][j] = jnp.sqrt(total)
            else:
                lower[i][j] = total / lower[j][j]
    middle = []
    for i in range(ITERS):
        total = target[i]
        for m in range(i):
            total = total - lower[i][m] * middle[m]
        middle.append(total / lower[i][i])
    coeffs = [None] * ITERS
    for i in reversed(range(ITERS)):
        total = middle[i]
        for m in range(i + 1, ITERS):
            total = total - lower[m][i] * coeffs[m]
        coeffs[i] = total / lower[i][i]
    return coeffs


def body(loads, self_term, near_tiles, near_list, far_rows, far_cols, coupling, ranks):
    nrhs = loads.shape[0]
    beta = jnp.sqrt(lax.psum(jnp.sum(loads * loads, axis=1), ("strip", "clus")))
    basis = [loads / beta[:, None]]
    zeros = jnp.zeros((nrhs,), jnp.float32)
    hess = [[zeros for k in range(ITERS)] for j in range(ITERS + 1)]
    for k in range(ITERS):
        image = apply_operator(
            basis[k], self_term, near_tiles, near_list, far_rows, far_cols, coupling, ranks
        )
        inner_list = []
        for j in range(k + 1):
            value = lax.psum(jnp.sum(basis[j] * image, axis=1), ("strip", "clus"))
            image = image - value[:, None] * basis[j]
            inner_list.append(value)
        height = jnp.sqrt(lax.psum(jnp.sum(image * image, axis=1), ("strip", "clus")))
        for j in range(k + 1):
            hess[j][k] = inner_list[j]
        hess[k + 1][k] = height
        basis.append(image / height[:, None])
    coeffs = small_solve(hess, beta)
    solution = coeffs[0][:, None] * basis[0]
    k = 1
    solution = solution + coeffs[k][:, None] * basis[k]
    return solution


def solution(mesh):
    in_specs = (
        P(None, ("case", "strip", "clus")),
        P(("case", "strip", "clus")),
        P(("case", "strip", "clus"), None, None),
        P(("case", "strip", "clus"), None),
        P(None, ("case", "strip", "clus")),
        P(None, ("case", "strip", "clus")),
        P(None, ("strip", "clus"), None, None),
        P(None, ("strip", "clus")),
    )
    out_specs = P(None, ("case", "strip", "clus"))
    return jax.shard_map(body, mesh=mesh, in_specs=in_specs, out_specs=out_specs, check_vma=False)
```

profile of v0, /device:TPU:0, one launch (start us, length us, event | category | flops | bytes accessed | tf_op | source)
XLA Modules:
  0.0 325.4 jit_solution(4118117123540527726)
XLA Ops:
  0.0 1.0 multiply_reduce_fusion.5
  1.0 34.9 %psum.42 = f32[4]{0:T(128)S(1)} all-reduce(f32[4]{0:T(128)S(1)} %multiply_reduce_fusion.5), channel_id=1, replica_groups=mesh['case'=2,'strip'=8,'clus'=2] {'strip','clus'}, use_global_device_ids=true, to_apply=%region_1.0 | all-reduce | flops 4 | bytes 32 | tf_op jit(solution)/shard_map/psum | solution.py:96
  35.9 0.8 fusion.31
  36.7 1.8 all_gather.6
  38.5 1.3 collective-permute-start
  39.8 1.3 collective-permute-start.1
  42.5 0.7 fusion.20
  43.2 1.1 fusion.32
  44.3 1.3 fusion.2
  45.6 1.2 dynamic-slice
  46.9 59.7 %all-reduce = f32[16,4,32]{2,1,0:T(4,128)S(1)} all-reduce(f32[16,4,32]{2,1,0:T(4,128)S(1)} %fusion.2), channel_id=2, replica_groups=mesh['case'=2,'strip'=8,'clus'=2] {'strip','clus'}, use_global_device_ids=true, to_apply=%region_2.0.clone | all-reduce | flops 2048 | bytes 16384
  107.3 0.8 convolution_bitcast_fusion.1
  108.3 0.9 multiply_reduce_fusion.4
  109.2 29.5 %psum.43 = f32[4]{0:T(128)S(1)} all-reduce(f32[4]{0:T(128)S(1)} %get-tuple-element.16), channel_id=1, replica_groups=mesh['case'=2,'strip'=8,'clus'=2] {'strip','clus'}, use_global_device_ids=true, to_apply=%region_4.6 | all-reduce | flops 4 | bytes 32 | tf_op jit(solution)/shard_map/psum | solution.py:106
  138.9 29.5 %psum.44 = f32[4]{0:T(128)S(1)} all-reduce(f32[4]{0:T(128)S(1)} %multiply_reduce_fusion.3), channel_id=1, replica_groups=mesh['case'=2,'strip'=8,'clus'=2] {'strip','clus'}, use_global_device_ids=true, to_apply=%region_6.8 | all-reduce | flops 4 | bytes 32 | tf_op jit(solution)/shard_map/psum | solution.py:109
  168.5 1.8 all_gather.7
  170.3 1.3 collective-permute-start.2
  171.6 1.3 collective-permute-start.3
  173.5 59.7 %all-reduce.1 = f32[16,4,32]{2,1,0:T(4,128)S(1)} all-reduce(f32[16,4,32]{2,1,0:T(4,128)S(1)} %fusion), channel_id=3, replica_groups=mesh['case'=2,'strip'=8,'clus'=2] {'strip','clus'}, use_global_device_ids=true, to_apply=%region_7.9.clone | all-reduce | flops 2048 | bytes 16384
  233.9 0.8 convolution_bitcast_fusion
  234.9 0.9 multiply_reduce_fusion.2
  235.8 29.5 %psum.45 = f32[4]{0:T(128)S(1)} all-reduce(f32[4]{0:T(128)S(1)} %get-tuple-element.18), channel_id=1, replica_groups=mesh['case'=2,'strip'=8,'clus'=2] {'strip','clus'}, use_global_device_ids=true, to_apply=%region_9.11 | all-reduce | flops 4 | bytes 32 | tf_op jit(solution)/shard_map/psum | solution.py:106
  265.5 29.5 %psum.46 = f32[4]{0:T(128)S(1)} all-reduce(f32[4]{0:T(128)S(1)} %multiply_reduce_fusion.1), channel_id=1, replica_groups=mesh['case'=2,'strip'=8,'clus'=2] {'strip','clus'}, use_global_device_ids=true, to_apply=%region_11.13 | all-reduce | flops 4 | bytes 32 | tf_op jit(solution)/shard_map/psum | solution.py:106
  295.2 29.5 %psum.47 = f32[4]{0:T(128)S(1)} all-reduce(f32[4]{0:T(128)S(1)} %multiply_reduce_fusion), channel_id=1, replica_groups=mesh['case'=2,'strip'=8,'clus'=2] {'strip','clus'}, use_global_device_ids=true, to_apply=%region_13.15 | all-reduce | flops 4 | bytes 32 | tf_op jit(solution)/shard_map/psum | solution.py:109
  (34 shorter events, 5.1 us)
Async XLA Ops:
  0.0 107.3 %copy-start = (bf16[80,128,128]{2,1,0:T(8,128)(2,1)S(1)}, bf16[80,128,128]{2,1,0:T(8,128)(2,1)}, u32[]{:S(2)}) copy-start(bf16[80,128,128]{2,1,0:T(8,128)(2,1)} %param.12) | copy-start | bytes 7864324
  0.0 172.9 %copy-start.2 = (f32[32,1024]{1,0:T(8,128)S(1)}, f32[32,1024]{1,0:T(8,128)}, u32[]{:S(2)}) copy-start(f32[32,1024]{1,0:T(8,128)} %param.15) | copy-start | bytes 393220
  0.0 173.1 %copy-start.1 = (f32[16,1,32,32]{3,2,1,0:T(8,128)S(1)}, f32[16,1,32,32]{3,2,1,0:T(8,128)}, u32[]{:S(2)}) copy-start(f32[16,1,32,32]{3,2,1,0:T(8,128)} %param.16) | copy-start | bytes 196612
  0.0 108.3 %copy-start.4 = (f32[1024]{0:T(1024)S(1)}, f32[1024]{0:T(1024)}, u32[]{:S(2)}) copy-start(f32[1024]{0:T(1024)} %param.11) | copy-start | bytes 12292
  0.0 108.3 %copy-start.3 = (f32[32,1024]{1,0:T(8,128)S(1)}, f32[32,1024]{1,0:T(8,128)}, u32[]{:S(2)}) copy-start(f32[32,1024]{1,0:T(8,128)} %param.14) | copy-start | bytes 393220
  38.5 68.0 %collective-permute-start = (bf16[4,2048]{1,0:T(4,128)(2,1)S(1)}, bf16[4,2048]{1,0:T(4,128)(2,1)S(1)}, u32[]{:S(2)}, u32[]{:S(2)}) collective-permute-start(bf16[4,2048]{1,0:T(4,128)(2,1)S(1)} %all_gather.6), channel_id=1, source_target_pairs={{0,2},{2,4},{4,6},{6,8},{8,10},{10,12},{12,14},{1,3},{3,5},{5,7},{... | collective-permute-start | bytes 49160 | tf_op jit(solution)/shard_map/ppermute | solution.py:19
  39.8 66.7 %collective-permute-start.1 = (bf16[4,2048]{1,0:T(4,128)(2,1)S(1)}, bf16[4,2048]{1,0:T(4,128)(2,1)S(1)}, u32[]{:S(2)}, u32[]{:S(2)}) collective-permute-start(bf16[4,2048]{1,0:T(4,128)(2,1)S(1)} %all_gather.6), channel_id=1, source_target_pairs={{2,0},{4,2},{6,4},{8,6},{10,8},{12,10},{14,12},{3,1},{5,3},{7,5},{... | collective-permute-start | bytes 49160 | tf_op jit(solution)/shard_map/ppermute | solution.py:20
  170.3 62.8 %collective-permute-start.2 = (bf16[4,2048]{1,0:T(4,128)(2,1)S(1)}, bf16[4,2048]{1,0:T(4,128)(2,1)S(1)}, u32[]{:S(2)}, u32[]{:S(2)}) collective-permute-start(bf16[4,2048]{1,0:T(4,128)(2,1)S(1)} %all_gather.7), channel_id=1, source_target_pairs={{0,2},{2,4},{4,6},{6,8},{8,10},{10,12},{12,14},{1,3},{3,5},{5,7},{... | collective-permute-start | bytes 49160 | tf_op jit(solution)/shard_map/ppermute | solution.py:19
  171.6 61.6 %collective-permute-start.3 = (bf16[4,2048]{1,0:T(4,128)(2,1)S(1)}, bf16[4,2048]{1,0:T(4,128)(2,1)S(1)}, u32[]{:S(2)}, u32[]{:S(2)}) collective-permute-start(bf16[4,2048]{1,0:T(4,128)(2,1)S(1)} %all_gather.7), channel_id=1, source_target_pairs={{2,0},{4,2},{6,4},{8,6},{10,8},{12,10},{14,12},{3,1},{5,3},{7,5},{... | collective-permute-start | bytes 49160 | tf_op jit(solution)/shard_map/ppermute | solution.py:20
where the time goes:
time: 326 us; the launch traced here: 325 us
  blocking collectives  305 us (94%)
  matrix products  6.87 us (2%)
  starting transfers between devices  5.14 us (2%)
  other arithmetic  4.66 us (1%)
  local copies, waits for them, and re-layouts  3.31 us (1%)
    unnamed x2, blocking collectives  119 us
    psum x3, blocking collectives, body(): value = lax.psum(jnp.sum(basis[j] * image, axis=1), ('strip', 'clus'))  88.5 us
    psum x2, blocking collectives, body(): lax.psum(jnp.sum(image * image, axis=1), ('strip', 'clus'))  59 us
    psum x1, blocking collectives, body(): beta = jnp.sqrt(lax.psum(jnp.sum(loads * loads, axis=1), ('strip', 'clus')))  34.9 us
  transfers between devices with their start and end apart: 4, of which 0 were waited for; matrix products, arithmetic and copies ran while one was open for 2% of the time, Pallas kernels for 0%

commit v1 on v0

v1 whole, which is shorter than its diff:
```python
import jax
import jax.numpy as jnp
from jax import lax
from jax.sharding import PartitionSpec as P

HIGH = lax.Precision.HIGHEST
GROUP = ("strip", "clus")


def window_of(field):
    paired = lax.all_gather(field, "clus", axis=1, tiled=True)
    devices = lax.axis_size("strip")
    up = [(i, i + 1) for i in range(devices - 1)]
    down = [(j, i) for i, j in up]
    before = lax.ppermute(paired, "strip", up)
    after = lax.ppermute(paired, "strip", down)
    return jnp.concatenate([before, paired, after], axis=1)


def near_field(window, near_tiles, near_list, block_rows):
    nrhs = window.shape[0]
    tile = near_tiles.shape[1]
    blocks = window.astype(jnp.bfloat16).reshape(nrhs, -1, tile)
    sources = jnp.take(blocks, near_list[:, 1], axis=1)
    product = jnp.einsum("rnk,nkt->rnt", sources, near_tiles, preferred_element_type=jnp.float32)
    onehot = (near_list[:, 0][:, None] == jnp.arange(block_rows, dtype=jnp.int32)[None, :]).astype(
        jnp.float32
    )
    summed = jnp.einsum("rnt,nb->rbt", product, onehot, precision=HIGH)
    return summed.reshape(nrhs, -1)


def far_terms(field, far_cols, couple, masks):
    proj = jnp.einsum("rp,ap->ra", field, far_cols, precision=HIGH)
    return jnp.einsum("ira,iab->irb", masks[:, None, :] * proj[None], couple, precision=HIGH)


def exchange(terms, stats):
    groups, nrhs, rank = terms.shape
    kinds = stats.shape[0]
    flat = terms.reshape(groups, nrhs * rank)
    every = jnp.broadcast_to(stats.reshape(1, kinds * nrhs), (groups, kinds * nrhs))
    sent = jnp.concatenate([flat, every], axis=1)
    got = lax.all_to_all(sent, GROUP, 0, 0, tiled=True)
    far_sum = jnp.sum(got[:, : nrhs * rank], axis=0).reshape(nrhs, rank)
    return far_sum, got[:, nrhs * rank :].reshape(groups, kinds, nrhs)


def exchange_stats(stats):
    kinds, nrhs = stats.shape
    groups = lax.axis_size("strip") * lax.axis_size("clus")
    every = jnp.broadcast_to(stats.reshape(1, kinds * nrhs), (groups, kinds * nrhs))
    got = lax.all_to_all(every, GROUP, 0, 0, tiled=True)
    return got.reshape(groups, kinds, nrhs)


def body(loads, self_term, near_tiles, near_list, far_rows, far_cols, coupling, ranks):
    nrhs, panels = loads.shape
    rank = far_cols.shape[0]
    block_rows = panels // near_tiles.shape[1]
    masks = (jnp.arange(rank, dtype=jnp.int32)[None, :] < ranks[:, 0][:, None]).astype(jnp.float32)
    couple = coupling[:, 0]

    def image_of(field, window, far_sum):
        near = near_field(window, near_tiles, near_list, block_rows)
        far = jnp.einsum("rb,bp->rp", far_sum, far_rows, precision=HIGH)
        return self_term[None, :] * field + near + far

    loads_window = window_of(loads)
    far_loads, got = exchange(
        far_terms(loads, far_cols, couple, masks), jnp.sum(loads * loads, axis=1)[None]
    )
    beta = jnp.sqrt(jnp.sum(got[:, 0], axis=0))
    basis0 = loads / beta[:, None]
    window0 = loads_window / beta[:, None]
    far0 = far_loads / beta[:, None]
    image0 = image_of(basis0, window0, far0)

    norm = jnp.sum(basis0 * basis0, axis=1)
    dot = jnp.sum(basis0 * image0, axis=1)
    share = jnp.where(norm > 0, dot / jnp.where(norm > 0, norm, 1.0), 0.0)
    rest = image0 - share[:, None] * basis0
    stats = jnp.stack([norm, dot, share, jnp.sum(rest * rest, axis=1)])
    image_window = window_of(image0)
    far_image, got = exchange(far_terms(image0, far_cols, couple, masks), stats)
    h00 = jnp.sum(got[:, 1], axis=0)
    h10 = jnp.sqrt(jnp.sum(got[:, 3] + got[:, 0] * (got[:, 2] - h00[None]) ** 2, axis=0))
    basis1 = (image0 - h00[:, None] * basis0) / h10[:, None]
    window1 = (image_window - h00[:, None] * window0) / h10[:, None]
    far1 = (far_image - h00[:, None] * far0) / h10[:, None]
    image1 = image_of(basis1, window1, far1)

    stats = jnp.stack(
        [
            jnp.sum(basis0 * image1, axis=1),
            jnp.sum(basis1 * image1, axis=1),
            jnp.sum(image1 * image1, axis=1),
        ]
    )
    h01, h11, gram11 = jnp.sum(exchange_stats(stats), axis=0)
    gram00 = h00 * h00 + h10 * h10
    gram01 = h00 * h01 + h10 * h11
    lower00 = jnp.sqrt(gram00)
    lower10 = gram01 / lower00
    lower11 = jnp.sqrt(gram11 - lower10 * lower10)
    middle0 = beta * h00 / lower00
    middle1 = (beta * h01 - lower10 * middle0) / lower11
    y1 = middle1 / lower11
    y0 = (middle0 - lower10 * y1) / lower00
    return y0[:, None] * basis0 + y1[:, None] * basis1


def solution(mesh):
    in_specs = (
        P(None, ("case", "strip", "clus")),
        P(("case", "strip", "clus")),
        P(("case", "strip", "clus"), None, None),
        P(("case", "strip", "clus"), None),
        P(None, ("case", "strip", "clus")),
        P(None, ("case", "strip", "clus")),
        P(None, ("strip", "clus"), None, None),
        P(None, ("strip", "clus")),
    )
    out_specs = P(None, ("case", "strip", "clus"))
    return jax.shard_map(body, mesh=mesh, in_specs=in_specs, out_specs=out_specs, check_vma=False)
```

time: 326 us -> 60.9 us (0.19)
  blocking collectives: 305 us -> 18 us
  starting transfers between devices: 5.14 us -> 22.3 us
  waiting for transfers between devices: 0.01 us -> 5.99 us
    psum x6 -> x0, blocking collectives: 182 us -> none  [the longest x3 88.5 us: body(): value = lax.psum(jnp.sum(basis[j] * image, axis=1), ('strip', 'clus'))]
    unnamed x2 -> x0, blocking collectives: 119 us -> none
    all_to_all x0 -> x1, blocking collectives: none -> 13.9 us  [exchange_stats(): got = lax.all_to_all(every, GROUP, 0, 0, tiled=True)]
    all_to_all x0 -> x2, starting transfers between devices: none -> 9.82 us  [exchange(): got = lax.all_to_all(sent, GROUP, 0, 0, tiled=True)]
    ppermute x4, starting transfers between devices: 5.14 us -> 12.5 us  [the longest x2 9.91 us: window_of(): before = lax.ppermute(paired, 'strip', up)]
    all_to_all x0 -> x2, waiting for transfers between devices: none -> 5.12 us  [exchange(): got = lax.all_to_all(sent, GROUP, 0, 0, tiled=True)]
  transfers between devices with their start and end apart: 4 -> 6, of which waited for: 0 -> 2; matrix products, arithmetic and copies ran while one was open for 2% -> 10% of each run, Pallas kernels for 0% -> 0%
where the time goes in v1:
time: 60.9 us; the launch traced here: 60.4 us
  starting transfers between devices  22.3 us (37%)
  blocking collectives  18 us (30%)
  waiting for transfers between devices  5.99 us (10%)
  matrix products  5.74 us (9%)
  other arithmetic  4.19 us (7%)
  local copies, waits for them, and re-layouts  3.94 us (6%)
    all_to_all x1, blocking collectives, exchange_stats(): got = lax.all_to_all(every, GROUP, 0, 0, tiled=True)  13.9 us
    ppermute x2, starting transfers between devices, window_of(): before = lax.ppermute(paired, 'strip', up)  9.91 us
    all_to_all x2, starting transfers between devices, exchange(): got = lax.all_to_all(sent, GROUP, 0, 0, tiled=True)  9.82 us
    all_to_all x2, waiting for transfers between devices, exchange(): got = lax.all_to_all(sent, GROUP, 0, 0, tiled=True)  5.12 us
    all_gather x2, blocking collectives, window_of(): paired = lax.all_gather(field, 'clus', axis=1, tiled=True)  4.13 us
    ppermute x2, starting transfers between devices, window_of(): after = lax.ppermute(paired, 'strip', down)  2.56 us
    dot_general x2, matrix products, near_field(): jnp.einsum('rnk,nkt->rnt', sources, near_tiles, preferred_element_type=jn...  1.66 us
    dot_general x2, matrix products, far_terms(): jnp.einsum('ira,iab->irb', masks[:, None, :] * proj[None], couple, precis...  1.65 us
  transfers between devices with their start and end apart: 6, of which 2 were waited for; matrix products, arithmetic and copies ran while one was open for 10% of the time, Pallas kernels for 0%

profile of v1, /device:TPU:0, one launch (start us, length us, event | category | flops | bytes accessed | tf_op | source)
XLA Modules:
  0.0 60.4 jit_solution(3143509716686801129)
XLA Ops:
  0.0 2.3 %all_gather.6 = f32[4,2048]{1,0:T(4,128)S(1)} all-gather(f32[4,1024]{1,0:T(4,128)} %param.10), channel_id=1, replica_groups=mesh['case'=2,'strip'=8,'clus'=2] {'clus'}, dimensions={1}, use_global_device_ids=true | all-gather | bytes 49152 | tf_op jit(solution)/shard_map/all_gather | solution.py:11
  2.3 1.3 %collective-permute-start.1 = (f32[4,2048]{1,0:T(4,128)S(1)}, f32[4,2048]{1,0:T(4,128)S(1)}, u32[]{:S(2)}, u32[]{:S(2)}) collective-permute-start(f32[4,2048]{1,0:T(4,128)S(1)} %all_gather.6), channel_id=1, source_target_pairs={{2,0},{4,2},{6,4},{8,6},{10,8},{12,10},{14,12},{3,1},{5,3},{7,5},{... | collective-permute-start | bytes 98312 | tf_op jit(solution)/shard_map/ppermute | solution.py:16
  3.6 5.4 %collective-permute-start = (f32[4,2048]{1,0:T(4,128)S(1)}, f32[4,2048]{1,0:T(4,128)S(1)}, u32[]{:S(2)}, u32[]{:S(2)}) collective-permute-start(f32[4,2048]{1,0:T(4,128)S(1)} %all_gather.6), channel_id=1, source_target_pairs={{0,2},{2,4},{4,6},{6,8},{8,10},{10,12},{12,14},{1,3},{3,5},{5,7},{... | collective-permute-start | bytes 98312 | tf_op jit(solution)/shard_map/ppermute | solution.py:15
  9.0 0.8 %multiply_reduce_fusion.6 = f32[4]{0:T(128)S(1)} fusion(f32[4,1024]{1,0:T(4,128)} %param.10), kind=kLoop, calls=%fused_computation.43 | loop fusion | flops 8188 | bytes 16400 | tf_op jit(solution)/shard_map/reduce_sum | solution.py:71
  9.8 1.1 %fusion.43 = f32[4,32]{1,0:T(4,128)S(1)} fusion(f32[4,1024]{1,0:T(4,128)} %param.10, f32[32,1024]{1,0:T(8,128)} %param.15), kind=kOutput, calls=%fused_computation.91 | convolution fusion | flops 1572864 | bytes 147968 | tf_op jit(solution)/shard_map/rp,ap->ra/dot_general | solution.py:34
  10.9 0.8 %fusion.22 = f32[16,32]{1,0:T(8,128)S(1)} fusion(s32[16]{0:T(128)} %bitcast.99), kind=kLoop, calls=%fused_computation.51 | loop fusion | flops 1024 | bytes 2112 | tf_op jit(solution)/shard_map/convert_element_type | solution.py:61
  11.7 1.3 %fusion.2 = f32[16,4,32]{2,1,0:T(4,128)S(1)} fusion(f32[16,1,32,32]{3,2,1,0:T(8,128)} %param.16, f32[4,32]{1,0:T(4,128)S(1)} %fusion.43, f32[16,32]{1,0:T(8,128)S(1)} %fusion.22), kind=kOutput, calls=%fused_computation.10 | convolution fusion | flops 788480 | bytes 76288 | tf_op jit(solution)/shard_map/ira,iab->irb/dot_general | solution.py:35
  13.1 0.6 %all_to_all.20 = f32[16,1,132]{2,1,0:T(1,128)} reshape(f32[16,132]{1,0:T(8,128)S(1)} %pad_maximum_fusion) | data formatting | bytes 16896 | tf_op jit(solution)/shard_map/all_to_all | solution.py:44
  13.7 6.3 %all-to-all-start = ((f32[16,1,132]{2,1,0:T(1,128)}), f32[16,1,132]{2,1,0:T(1,128)S(1)}, u32[]{:S(2)}, u32[]{:S(2)}) async-start(f32[16,1,132]{2,1,0:T(1,128)} %all_to_all.20), calls=%async_computation | async-start | bytes 32768 | tf_op jit(solution)/shard_map/all_to_all | solution.py:44
  20.0 0.7 %compare_and_fusion = (pred[80]{0:T(512)(128)(4,1)S(1)}, s32[80]{0:T(128)S(1)}) fusion(s32[80,2]{0,1:T(2,128)} %param.13), kind=kLoop, calls=%fused_computation.76 | loop fusion | flops 480 | bytes 720 | tf_op jit(solution)/shard_map/jit(_take)/and | solution.py:24
  20.7 0.7 %slice_bitcast_fusion.3 = s32[80]{0:T(128)S(1)} fusion(s32[80,2]{0,1:T(2,128)} %param.13), kind=kLoop, calls=%fused_computation.87 | loop fusion | bytes 640 | tf_op jit(solution)/shard_map/eq | solution.py:26
  21.4 5.1 %all-to-all-done = f32[16,1,132]{2,1,0:T(1,128)S(1)} async-done(((f32[16,1,132]{2,1,0:T(1,128)}), f32[16,1,132]{2,1,0:T(1,128)S(1)}, u32[]{:S(2)}, u32[]{:S(2)}) %all-to-all-start) | async-done | bytes 8480 | tf_op jit(solution)/shard_map/all_to_all | solution.py:44
  26.8 0.7 %gather_fusion = bf16[80,4,128]{2,1,0:T(4,128)(2,1)S(1)} fusion(bf16[4,48,128]{2,0,1:T(4,128)(2,1)S(1)} %get-tuple-element.15, s32[1024]{0:T(1024)S(1)} %pad_clamp_fusion), kind=kCustom, calls=%fused_computation.clone | custom fusion | bytes 164160 | tf_op jit(solution)/shard_map/jit(_take)/gather | solution.py:24
  27.5 0.8 %convolution_bitcast_fusion.1 = f32[4,80,128]{2,0,1:T(4,128)S(1)} fusion(bf16[80,128,128]{2,1,0:T(8,128)(2,1)S(1)} %copy-done, bf16[80,4,128]{2,1,0:T(4,128)(2,1)S(1)} %gather_fusion, pred[80]{0:T(512)(128)(4,1)S(1)} %get-tuple-element.13), kind=kOutput, calls=%fused_computation.3 | convolution fusion | flops 10526720 | bytes 2867280 | tf_op jit(solution)/shard_map/rnk,nkt->rnt/dot_general | solution.py:25
  29.9 0.6 %all_to_all.23 = f32[16,1,144]{2,1,0:T(1,128)} reshape(f32[16,144]{1,0:T(8,128)S(1)} %pad_maximum_fusion.1) | data formatting | bytes 18432 | tf_op jit(solution)/shard_map/all_to_all | solution.py:44
  30.5 3.5 %all-to-all-start.1 = ((f32[16,1,144]{2,1,0:T(1,128)}), f32[16,1,144]{2,1,0:T(1,128)S(1)}, u32[]{:S(2)}, u32[]{:S(2)}) async-start(f32[16,1,144]{2,1,0:T(1,128)} %all_to_all.23), calls=%async_computation.1 | async-start | bytes 32768 | tf_op jit(solution)/shard_map/all_to_all | solution.py:44
  34.0 1.8 %all_gather.7 = f32[4,2048]{1,0:T(4,128)S(1)} all-gather(f32[4,1024]{1,0:T(4,128)S(1)} %get-tuple-element.19), channel_id=1, replica_groups=mesh['case'=2,'strip'=8,'clus'=2] {'clus'}, dimensions={1}, use_global_device_ids=true | all-gather | bytes 49152 | tf_op jit(solution)/shard_map/all_gather | solution.py:11
  35.8 1.3 %collective-permute-start.3 = (f32[4,2048]{1,0:T(4,128)S(1)}, f32[4,2048]{1,0:T(4,128)S(1)}, u32[]{:S(2)}, u32[]{:S(2)}) collective-permute-start(f32[4,2048]{1,0:T(4,128)S(1)} %all_gather.7), channel_id=1, source_target_pairs={{2,0},{4,2},{6,4},{8,6},{10,8},{12,10},{14,12},{3,1},{5,3},{7,5},{... | collective-permute-start | bytes 98312 | tf_op jit(solution)/shard_map/ppermute | solution.py:16
  37.1 4.5 %collective-permute-start.2 = (f32[4,2048]{1,0:T(4,128)S(1)}, f32[4,2048]{1,0:T(4,128)S(1)}, u32[]{:S(2)}, u32[]{:S(2)}) collective-permute-start(f32[4,2048]{1,0:T(4,128)S(1)} %all_gather.7), channel_id=1, source_target_pairs={{0,2},{2,4},{4,6},{6,8},{8,10},{10,12},{12,14},{1,3},{3,5},{5,7},{... | collective-permute-start | bytes 98312 | tf_op jit(solution)/shard_map/ppermute | solution.py:15
  42.4 0.9 %collective-permute-done.2 = f32[4,2048]{1,0:T(4,128)S(1)} collective-permute-done((f32[4,2048]{1,0:T(4,128)S(1)}, f32[4,2048]{1,0:T(4,128)S(1)}, u32[]{:S(2)}, u32[]{:S(2)}) %collective-permute-start.2) | collective-permute-done | bytes 32800 | tf_op jit(solution)/shard_map/ppermute | solution.py:15
  43.4 0.7 %gather_fusion.1 = bf16[80,4,128]{2,1,0:T(4,128)(2,1)S(1)} fusion(bf16[4,48,128]{2,0,1:T(4,128)(2,1)S(1)} %fusion.7, s32[1024]{0:T(1024)S(1)} %pad_clamp_fusion), kind=kCustom, calls=%fused_computation.1.clone | custom fusion | bytes 164160 | tf_op jit(solution)/shard_map/jit(_take)/gather | solution.py:24
  44.0 0.8 %convolution_bitcast_fusion = f32[4,80,128]{2,0,1:T(4,128)S(1)} fusion(bf16[80,128,128]{2,1,0:T(8,128)(2,1)S(1)} %copy-done, bf16[80,4,128]{2,1,0:T(4,128)(2,1)S(1)} %gather_fusion.1, pred[80]{0:T(512)(128)(4,1)S(1)} %get-tuple-element.13), kind=kOutput, calls=%fused_computation.2 | convolution fusion | flops 10526720 | bytes 2867280 | tf_op jit(solution)/shard_map/rnk,nkt->rnt/dot_general | solution.py:25
  45.6 13.9 %all_to_all.30 = f32[16,1,12]{2,1,0:T(1,128)S(1)} all-to-all(f32[16,1,12]{2,1,0:T(1,128)S(1)} %broadcast_in_dim.32), channel_id=1, replica_groups=mesh['case'=2,'strip'=8,'clus'=2] {'strip','clus'}, dimensions={0} | all-to-all | bytes 1536 | tf_op jit(solution)/shard_map/all_to_all | solution.py:53
  59.6 0.7 %multiply_add_fusion = f32[4,1024]{1,0:T(4,128)} fusion(f32[4,1024]{1,0:T(4,128)S(1)} %subtract_divide_fusion, f32[4]{0:T(128)S(1)} %get-tuple-element.12, f32[4]{0:T(128)S(1)} %get-tuple-element.11, f32[4,1024]{1,0:T(4,128)S(1)} %copy-done.2, f32[4]{0:T(128)S(1)} %sqrt.30), kind=kLoop, calls=%fused_computation.34 | loop fusion | flops 16384 | bytes 49200 | tf_op jit(solution)/shard_map/add | solution.py:110
  (55 shorter events, 3.6 us)
Async XLA Ops:
  0.0 27.5 %copy-start = (bf16[80,128,128]{2,1,0:T(8,128)(2,1)S(1)}, bf16[80,128,128]{2,1,0:T(8,128)(2,1)}, u32[]{:S(2)}) copy-start(bf16[80,128,128]{2,1,0:T(8,128)(2,1)} %param.12) | copy-start | bytes 7864324
  0.0 28.5 %copy-start.2 = (f32[4,1024]{1,0:T(4,128)S(1)}, f32[4,1024]{1,0:T(4,128)}, u32[]{:S(2)}) copy-start(f32[4,1024]{1,0:T(4,128)} %param.10) | copy-start | bytes 49156
  0.0 28.9 %copy-start.3 = (f32[32,1024]{1,0:T(8,128)S(1)}, f32[32,1024]{1,0:T(8,128)}, u32[]{:S(2)}) copy-start(f32[32,1024]{1,0:T(8,128)} %param.15) | copy-start | bytes 393220
  0.0 29.1 %copy-start.1 = (f32[16,1,32,32]{3,2,1,0:T(8,128)S(1)}, f32[16,1,32,32]{3,2,1,0:T(8,128)}, u32[]{:S(2)}) copy-start(f32[16,1,32,32]{3,2,1,0:T(8,128)} %param.16) | copy-start | bytes 196612
  0.0 28.5 %copy-start.4 = (f32[32,1024]{1,0:T(8,128)S(1)}, f32[32,1024]{1,0:T(8,128)}, u32[]{:S(2)}) copy-start(f32[32,1024]{1,0:T(8,128)} %param.14) | copy-start | bytes 393220
  0.0 28.5 %copy-start.5 = (f32[1024]{0:T(1024)S(1)}, f32[1024]{0:T(1024)}, u32[]{:S(2)}) copy-start(f32[1024]{0:T(1024)} %param.11) | copy-start | bytes 12292
  2.3 24.3 %collective-permute-start.1 = (f32[4,2048]{1,0:T(4,128)S(1)}, f32[4,2048]{1,0:T(4,128)S(1)}, u32[]{:S(2)}, u32[]{:S(2)}) collective-permute-start(f32[4,2048]{1,0:T(4,128)S(1)} %all_gather.6), channel_id=1, source_target_pairs={{2,0},{4,2},{6,4},{8,6},{10,8},{12,10},{14,12},{3,1},{5,3},{7,5},{... | collective-permute-start | bytes 98312 | tf_op jit(solution)/shard_map/ppermute | solution.py:16
  3.6 23.0 %collective-permute-start = (f32[4,2048]{1,0:T(4,128)S(1)}, f32[4,2048]{1,0:T(4,128)S(1)}, u32[]{:S(2)}, u32[]{:S(2)}) collective-permute-start(f32[4,2048]{1,0:T(4,128)S(1)} %all_gather.6), channel_id=1, source_target_pairs={{0,2},{2,4},{4,6},{6,8},{8,10},{10,12},{12,14},{1,3},{3,5},{5,7},{... | collective-permute-start | bytes 98312 | tf_op jit(solution)/shard_map/ppermute | solution.py:15
  13.7 12.8 %all-to-all-start = ((f32[16,1,132]{2,1,0:T(1,128)}), f32[16,1,132]{2,1,0:T(1,128)S(1)}, u32[]{:S(2)}, u32[]{:S(2)}) async-start(f32[16,1,132]{2,1,0:T(1,128)} %all_to_all.20), calls=%async_computation | async-start | bytes 32768 | tf_op jit(solution)/shard_map/all_to_all | solution.py:44
  30.5 11.2 %all-to-all-start.1 = ((f32[16,1,144]{2,1,0:T(1,128)}), f32[16,1,144]{2,1,0:T(1,128)S(1)}, u32[]{:S(2)}, u32[]{:S(2)}) async-start(f32[16,1,144]{2,1,0:T(1,128)} %all_to_all.23), calls=%async_computation.1 | async-start | bytes 32768 | tf_op jit(solution)/shard_map/all_to_all | solution.py:44
  35.8 6.6 %collective-permute-start.3 = (f32[4,2048]{1,0:T(4,128)S(1)}, f32[4,2048]{1,0:T(4,128)S(1)}, u32[]{:S(2)}, u32[]{:S(2)}) collective-permute-start(f32[4,2048]{1,0:T(4,128)S(1)} %all_gather.7), channel_id=1, source_target_pairs={{2,0},{4,2},{6,4},{8,6},{10,8},{12,10},{14,12},{3,1},{5,3},{7,5},{... | collective-permute-start | bytes 98312 | tf_op jit(solution)/shard_map/ppermute | solution.py:16
  37.1 6.1 %collective-permute-start.2 = (f32[4,2048]{1,0:T(4,128)S(1)}, f32[4,2048]{1,0:T(4,128)S(1)}, u32[]{:S(2)}, u32[]{:S(2)}) collective-permute-start(f32[4,2048]{1,0:T(4,128)S(1)} %all_gather.7), channel_id=1, source_target_pairs={{0,2},{2,4},{4,6},{6,8},{8,10},{10,12},{12,14},{1,3},{3,5},{5,7},{... | collective-permute-start | bytes 98312 | tf_op jit(solution)/shard_map/ppermute | solution.py:15

commit v2 on v1

v2 whole, which is shorter than its diff:
```python
import jax
import jax.numpy as jnp
from jax import lax
from jax.sharding import Mesh
from jax.sharding import PartitionSpec as P

HIGH = lax.Precision.HIGHEST
LAYER = ("lo", "clus")
GROUP = ("hi", "lo", "clus")


def near_field(blocks, near_tiles, target, source, block_rows):
    sources = jnp.take(blocks, source, axis=0)
    product = jnp.einsum("nrk,nkt->nrt", sources, near_tiles, preferred_element_type=jnp.float32)
    onehot = (target[:, None] == jnp.arange(block_rows, dtype=jnp.int32)[None, :]).astype(jnp.float32)
    summed = jnp.einsum("nrt,nb->rbt", product, onehot, precision=HIGH)
    return summed.reshape(summed.shape[0], -1)


def far_terms(field, far_cols, couple, masks):
    proj = jnp.einsum("rp,ap->ra", field, far_cols, precision=HIGH)
    return jnp.einsum("ira,iab->irb", masks[:, None, :] * proj[None], couple, precision=HIGH)


def packed(field, terms, stats):
    width = field.shape[1]
    rows = -(-terms.size // width)
    flat = jnp.pad(terms.reshape(-1), (0, rows * width - terms.size)).reshape(rows, width)
    last = jnp.pad(stats.reshape(-1), (0, width - stats.size)).reshape(1, width)
    return jnp.concatenate([field, flat, last], axis=0)


def combine(stats):
    norm = jnp.sum(stats[:, 0], axis=0)
    dot = jnp.sum(stats[:, 1], axis=0)
    share = jnp.where(norm > 0, dot / jnp.where(norm > 0, norm, 1.0), 0.0)
    rest = jnp.sum(stats[:, 3] + stats[:, 0] * (stats[:, 2] - share[None]) ** 2, axis=0)
    return jnp.stack([norm, dot, share, rest])


def body(loads, self_term, near_tiles, near_list, far_rows, far_cols, coupling, ranks):
    nrhs, panels = loads.shape
    rank = far_cols.shape[0]
    tile = near_tiles.shape[1]
    block_rows = panels // tile
    layers, lows, cores = (lax.axis_size(axis) for axis in GROUP)
    groups = layers * lows * cores
    layer, low, core = (lax.axis_index(axis) for axis in GROUP)
    me = (layer * lows + low) * cores + core
    masks = (jnp.arange(rank, dtype=jnp.int32)[None, :] < ranks[:, 0][:, None]).astype(jnp.float32)
    couple = coupling[:, 0]
    target = near_list[:, 0]
    source = near_list[:, 1] + low * (cores * block_rows)
    term_size = groups * nrhs * rank

    def split(gathered):
        count = gathered.shape[0]
        field = gathered[:, :nrhs]
        terms = gathered[:, nrhs:-1].reshape(count, -1)[:, :term_size].reshape(count, groups, nrhs, rank)
        stats = gathered[:, -1]
        return field, terms, stats

    def first_round(field, terms, stats):
        kinds = stats.shape[0]
        got = lax.all_gather(packed(field, terms, stats), "hi", axis=0)
        fields, terms, stats = split(got)
        stats = stats[:, : kinds * nrhs].reshape(layers, kinds, nrhs)
        wanted = layer + 1 - 2 * low
        beside = lax.dynamic_index_in_dim(fields, jnp.clip(wanted, 0, layers - 1), 0, keepdims=False)
        beside = jnp.where((wanted >= 0) & (wanted < layers), beside, 0.0)
        both = jnp.concatenate([field, beside], axis=0)
        stats = combine(stats) if kinds == 4 else jnp.sum(stats, axis=0)
        got = lax.all_gather(packed(both, jnp.sum(terms, axis=0), stats), LAYER, axis=0)
        own = got[:, :nrhs].reshape(lows, cores, nrhs, panels)
        beside = got[:, nrhs : 2 * nrhs].reshape(lows, cores, nrhs, panels)
        window = jnp.concatenate([beside[1], own[0], own[1], beside[0]], axis=0)
        _, terms, stats = split(got[:, nrhs:])
        far = jnp.sum(lax.dynamic_index_in_dim(terms, me, 1, keepdims=False), axis=0)
        return window, far, stats[:, : kinds * nrhs].reshape(-1, kinds, nrhs)

    def second_round(field, terms, stats):
        if groups > 64:
            return first_round(field, terms, stats)
        kinds = stats.shape[0]
        got = lax.all_gather(packed(field, terms, stats), GROUP, axis=0)
        fields, terms, stats = split(got)
        far = jnp.sum(lax.dynamic_index_in_dim(terms, me, 1, keepdims=False), axis=0)
        edge = jnp.zeros((cores,) + fields.shape[1:], fields.dtype)
        fields = jnp.concatenate([edge, fields, edge], axis=0)
        window = lax.dynamic_slice_in_dim(fields, layer * lows * cores, (lows + 2) * cores, 0)
        return window, far, stats[:, : kinds * nrhs].reshape(-1, kinds, nrhs)

    def image_of(field, window, far_sum):
        blocks = window.astype(jnp.bfloat16).reshape(-1, nrhs, block_rows, tile)
        blocks = blocks.transpose(0, 2, 1, 3).reshape(-1, nrhs, tile)
        near = near_field(blocks, near_tiles, target, source, block_rows)
        far = jnp.einsum("rb,bp->rp", far_sum, far_rows, precision=HIGH)
        return self_term[None, :] * field + near + far

    square = jnp.sum(loads * loads, axis=1)[None]
    window, far, stats = first_round(loads, far_terms(loads, far_cols, couple, masks), square)
    beta = jnp.sqrt(jnp.sum(stats[:, 0], axis=0))
    basis0 = loads / beta[:, None]
    window0 = window / beta[None, :, None]
    far0 = far / beta[:, None]
    image0 = image_of(basis0, window0, far0)

    norm = jnp.sum(basis0 * basis0, axis=1)
    dot = jnp.sum(basis0 * image0, axis=1)
    share = jnp.where(norm > 0, dot / jnp.where(norm > 0, norm, 1.0), 0.0)
    rest = image0 - share[:, None] * basis0
    stats = jnp.stack([norm, dot, share, jnp.sum(rest * rest, axis=1)])
    window, far, stats = second_round(image0, far_terms(image0, far_cols, couple, masks), stats)
    _, h00, _, square = combine(stats)
    h10 = jnp.sqrt(square)
    basis1 = (image0 - h00[:, None] * basis0) / h10[:, None]
    window1 = (window - h00[None, :, None] * window0) / h10[None, :, None]
    far1 = (far - h00[:, None] * far0) / h10[:, None]
    image1 = image_of(basis1, window1, far1)

    stats = jnp.stack(
        [
            jnp.sum(basis0 * image1, axis=1),
            jnp.sum(basis1 * image1, axis=1),
            jnp.sum(image1 * image1, axis=1),
        ]
    )
    stats = lax.all_gather(lax.all_gather(stats, LAYER, axis=0), "hi", axis=0)
    h01, h11, gram11 = jnp.sum(stats, axis=(0, 1))
    gram00 = h00 * h00 + h10 * h10
    gram01 = h00 * h01 + h10 * h11
    lower00 = jnp.sqrt(gram00)
    lower10 = gram01 / lower00
    lower11 = jnp.sqrt(gram11 - lower10 * lower10)
    middle0 = beta * h00 / lower00
    middle1 = (beta * h01 - lower10 * middle0) / lower11
    y1 = middle1 / lower11
    y0 = (middle0 - lower10 * y1) / lower00
    return y0[:, None] * basis0 + y1[:, None] * basis1


def solution(mesh):
    cases, strips, cores = (mesh.shape[axis] for axis in ("case", "strip", "clus"))
    fine = Mesh(mesh.devices.reshape(cases, strips // 2, 2, cores), ("case",) + GROUP)
    every = ("case",) + GROUP
    in_specs = (
        P(None, every),
        P(every),
        P(every, None, None),
        P(every, None),
        P(None, every),
        P(None, every),
        P(None, GROUP, None, None),
        P(None, GROUP),
    )
    return jax.shard_map(body, mesh=fine, in_specs=in_specs, out_specs=P(None, every), check_vma=False)
```

time: 60.9 us -> 84.8 us (1.39)
  blocking collectives: 18 us -> 62.5 us
  starting transfers between devices: 22.3 us -> 0 us
  waiting for transfers between devices: 5.99 us -> 0 us
  other arithmetic: 4.19 us -> 7.77 us
  local copies, waits for them, and re-layouts: 3.94 us -> 7.06 us
    all_gather x2 -> x5, blocking collectives: 4.13 us -> 62.5 us  [the longest x1 23.2 us: second_round(): got = lax.all_gather(packed(field, terms, stats), GROUP, axis=0)]
    all_to_all x1 -> x0, blocking collectives: 13.9 us -> none  [exchange_stats(): got = lax.all_to_all(every, GROUP, 0, 0, tiled=True)]
    ppermute x4 -> x0, starting transfers between devices: 12.5 us -> none  [the longest x2 9.91 us: window_of(): before = lax.ppermute(paired, 'strip', up)]
    all_to_all x2 -> x0, starting transfers between devices: 9.82 us -> none  [exchange(): got = lax.all_to_all(sent, GROUP, 0, 0, tiled=True)]
    all_to_all x2 -> x0, waiting for transfers between devices: 5.12 us -> none  [exchange(): got = lax.all_to_all(sent, GROUP, 0, 0, tiled=True)]
    unnamed x13 -> x51, local copies, waits for them, and re-layouts: 0.03 us -> 2.9 us
    unnamed x0 -> x4, other arithmetic: none -> 1.54 us
    all_to_all x3 -> x0, local copies, waits for them, and re-layouts: 1.35 us -> none  [exchange(): got = lax.all_to_all(sent, GROUP, 0, 0, tiled=True)]
  transfers between devices with their start and end apart: 6 -> 0, of which waited for: 2 -> 0; matrix products, arithmetic and copies ran while one was open for 10% -> 0% of each run, Pallas kernels for 0% -> 0%
where the time goes in v2:
time: 84.8 us; the launch traced here: 84.2 us
  blocking collectives  62.5 us (74%)
  other arithmetic  7.77 us (9%)
  local copies, waits for them, and re-layouts  7.06 us (8%)
  matrix products  6.3 us (7%)
    all_gather x1, blocking collectives, second_round(): got = lax.all_gather(packed(field, terms, stats), GROUP, axis=0)  23.2 us
    all_gather x2, blocking collectives, body(): stats = lax.all_gather(lax.all_gather(stats, LAYER, axis=0), 'hi', axis=0)  18.3 us
    all_gather x1, blocking collectives, first_round(): got = lax.all_gather(packed(field, terms, stats), 'hi', axis=0)  15.1 us
    all_gather x1, blocking collectives, first_round(): lax.all_gather(packed(both, jnp.sum(terms, axis=0), stats), LAYER, axis=0)  5.92 us
    unnamed x51, local copies, waits for them, and re-layouts  2.9 us
    dot_general x2, matrix products, near_field(): jnp.einsum('nrk,nkt->nrt', sources, near_tiles, preferred_element_type=jn...  2.28 us

profile of v2, /device:TPU:0, one launch (start us, length us, event | category | flops | bytes accessed | tf_op | source)
XLA Modules:
  0.0 84.2 jit_solution(406134668751312902)
XLA Ops:
  0.0 0.8 slice_bitcast_fusion.2
  0.8 0.8 multiply_reduce_fusion.6
  1.7 0.7 compare_and_fusion
  2.4 1.1 %fusion.58 = f32[4,32]{1,0:T(4,128)S(1)} fusion(f32[4,1024]{1,0:T(4,128)} %param.10, f32[32,1024]{1,0:T(8,128)} %param.15), kind=kOutput, calls=%fused_computation.116 | convolution fusion | flops 1572864 | bytes 147968 | tf_op jit(solution)/shard_map/rp,ap->ra/dot_general | solution.py:21
  3.5 0.7 fusion.29
  4.3 1.3 %fusion.2 = f32[16,4,32]{2,1,0:T(4,128)S(1)} fusion(f32[16,1,32,32]{3,2,1,0:T(8,128)} %param.16, f32[4,32]{1,0:T(4,128)S(1)} %fusion.58, f32[16,32]{1,0:T(8,128)S(1)} %fusion.29), kind=kOutput, calls=%fused_computation.11 | convolution fusion | flops 788480 | bytes 76288 | tf_op jit(solution)/shard_map/ira,iab->irb/dot_general | solution.py:22
  5.6 0.7 maximum_bitcast_fusion.1
  6.4 15.1 %all-gather.5 = f32[4,7,1024]{2,1,0:T(8,128)S(1)} all-gather(f32[1,7,1024]{2,1,0:T(8,128)S(1)} %maximum_bitcast_fusion.1), channel_id=2, replica_groups=mesh['case'=2,'hi'=4,'lo'=2,'clus'=2] {'hi'}, dimensions={0}, use_global_device_ids=true | all-gather | bytes 143360 | tf_op jit(solution)/shard_map/all_gather | solution.py:65
  21.6 0.8 maximum_bitcast_fusion
  22.4 5.9 %all-gather.6 = f32[4,11,1024]{2,1,0:T(8,128)S(1)} all-gather(f32[1,11,1024]{2,1,0:T(8,128)S(1)} %maximum_bitcast_fusion), channel_id=3, replica_groups=mesh['case'=2,'hi'=4,'lo'=2,'clus'=2] {'lo','clus'}, dimensions={0}, use_global_device_ids=true | all-gather | bytes 225280 | tf_op jit(solution)/shard_map/all_gather | solution.py:73
  29.0 0.7 copy.58
  30.3 0.7 gather_fusion
  31.0 0.8 fusion.15
  33.7 23.2 %all-gather.7 = f32[16,7,1024]{2,1,0:T(8,128)S(1)} all-gather(f32[1,7,1024]{2,1,0:T(8,128)S(1)} %maximum_bitcast_fusion.2), channel_id=4, replica_groups=mesh['case'=2,'hi'=4,'lo'=2,'clus'=2] {'hi','lo','clus'}, dimensions={0}, use_global_device_ids=true | all-gather | bytes 487424 | tf_op jit(solution)/shard_map/all_gather | solution.py:85
  56.9 0.7 slice.117
  58.2 0.6 dynamic-slice_reduce_fusion
  58.8 1.0 %copy.56 = f32[16,1,1024]{0,2,1:T(8,128)S(1)} copy(f32[16,1,1024]{2,1,0:T(1,128)} %slice.117) | data formatting | bytes 131072
  60.3 1.0 %fusion.20 = bf16[8,4,8,128]{3,0,2,1:T(8,128)(2,1)S(1)} fusion(f32[4]{0:T(128)S(1)} %sqrt.55, f32[4]{0:T(128)} %copy-done.7, f32[2,4,1024]{2,0,1:T(2,128)} %copy-done.5, f32[4,4,1024]{2,0,1:T(4,128)} %copy.58, f32[2,4,1024]{2,0,1:T(2,128)} %copy-done.4, f32[4]{0:T(128)S(1)} %get-tuple-element.11, s32[]{:T(128)S(6)} %select_n.86, ...), kind=kLoop, calls=%fused_computation.33 | loop fusion | flops 294912 | bytes 491572 | tf_op jit(solution)/shard_map/reshape | solution.py:94
  61.3 0.8 subtract_divide_fusion
  62.2 0.8 gather_fusion.1
  63.0 1.4 %fusion.13 = f32[80,4,128]{2,1,0:T(4,128)S(1)} fusion(bf16[80,128,128]{2,1,0:T(8,128)(2,1)S(1)} %copy-done, bf16[80,4,128]{2,1,0:T(4,128)(2,1)S(1)} %gather_fusion.1, pred[80]{0:T(512)(128)(4,1)} %copy-done.10), kind=kOutput, calls=%fused_computation.24 | convolution fusion | flops 10526720 | bytes 2867280 | tf_op jit(solution)/shard_map/nrk,nkt->nrt/dot_general | solution.py:14
  65.1 5.2 %all-gather.8 = f32[4,3,4]{2,1,0:T(4,128)S(1)} all-gather(f32[1,3,4]{2,1,0:T(4,128)S(1)} %maximum_bitcast_fusion.3), channel_id=5, replica_groups=mesh['case'=2,'hi'=4,'lo'=2,'clus'=2] {'lo','clus'}, dimensions={0}, use_global_device_ids=true | all-gather | bytes 240 | tf_op jit(solution)/shard_map/all_gather | solution.py:128
  70.3 13.1 %all-gather.4 = f32[16,3,4]{2,1,0:T(4,128)S(1)} all-gather(f32[4,3,4]{2,1,0:T(4,128)S(1)} %all-gather.8), channel_id=6, replica_groups=mesh['case'=2,'hi'=4,'lo'=2,'clus'=2] {'hi'}, dimensions={0}, use_global_device_ids=true | all-gather | bytes 960 | tf_op jit(solution)/shard_map/all_gather | solution.py:128
  83.5 0.7 multiply_add_fusion
  (101 shorter events, 4.9 us)
Async XLA Ops:
  0.0 31.0 %copy-start = (bf16[80,128,128]{2,1,0:T(8,128)(2,1)S(1)}, bf16[80,128,128]{2,1,0:T(8,128)(2,1)}, u32[]{:S(2)}) copy-start(bf16[80,128,128]{2,1,0:T(8,128)(2,1)} %param.12) | copy-start | bytes 7864324
  0.8 31.0 %copy-start.13 = (s32[80]{0:T(128)}, s32[80]{0:T(128)S(1)}, u32[]{:S(2)}) copy-start(s32[80]{0:T(128)S(1)} %slice_bitcast_fusion.2) | copy-start | bytes 964
  2.4 29.5 %copy-start.10 = (pred[80]{0:T(512)(128)(4,1)}, pred[80]{0:T(512)(128)(4,1)S(1)}, u32[]{:S(2)}) copy-start(pred[80]{0:T(512)(128)(4,1)S(1)} %get-tuple-element.15) | copy-start | bytes 244
  3.5 28.3 %copy-start.9 = (s32[1024]{0:T(1024)}, s32[1024]{0:T(1024)S(1)}, u32[]{:S(2)}) copy-start(s32[1024]{0:T(1024)S(1)} %pad_clamp_fusion) | copy-start | bytes 12292
  21.6 10.6 %copy-start.2 = (f32[4,1024]{1,0:T(4,128)S(1)}, f32[4,1024]{1,0:T(4,128)}, u32[]{:S(2)}) copy-start(f32[4,1024]{1,0:T(4,128)} %param.10) | copy-start | bytes 49156
  21.6 10.6 %copy-start.18 = (f32[32,1024]{1,0:T(8,128)S(1)}, f32[32,1024]{1,0:T(8,128)}, u32[]{:S(2)}) copy-start(f32[32,1024]{1,0:T(8,128)} %param.14) | copy-start | bytes 393220
  21.6 10.6 %copy-start.20 = (f32[1024]{0:T(1024)S(1)}, f32[1024]{0:T(1024)}, u32[]{:S(2)}) copy-start(f32[1024]{0:T(1024)} %param.11) | copy-start | bytes 12292
  22.4 10.6 %copy-start.3 = (f32[32,1024]{1,0:T(8,128)S(1)}, f32[32,1024]{1,0:T(8,128)}, u32[]{:S(2)}) copy-start(f32[32,1024]{1,0:T(8,128)} %param.15) | copy-start | bytes 393220
  28.3 4.9 %copy-start.1 = (f32[16,1,32,32]{3,2,1,0:T(8,128)S(1)}, f32[16,1,32,32]{3,2,1,0:T(8,128)}, u32[]{:S(2)}) copy-start(f32[16,1,32,32]{3,2,1,0:T(8,128)} %param.16) | copy-start | bytes 196612
  28.4 0.5 copy-start.11
  28.4 5.1 %copy-start.7 = (f32[4]{0:T(128)}, f32[4]{0:T(128)S(1)}, u32[]{:S(2)}) copy-start(f32[4]{0:T(128)S(1)} %sqrt.54) | copy-start | bytes 52
  29.0 0.9 %copy-start.4 = (f32[2,4,1024]{2,0,1:T(2,128)}, f32[2,4,1024]{2,0,1:T(2,128)S(1)}, u32[]{:S(2)}) copy-start(f32[2,4,1024]{2,0,1:T(2,128)S(1)} %copy.54) | copy-start | bytes 98308
  29.7 0.6 copy-start.5
  32.2 25.5 %copy-start.16 = (f32[4,32]{1,0:T(4,128)}, f32[4,32]{1,0:T(4,128)S(1)}, u32[]{:S(2)}) copy-start(f32[4,32]{1,0:T(4,128)S(1)} %dynamic-slice_reduce_fusion.1) | copy-start | bytes 1540
  32.6 25.1 %copy-start.6 = (f32[4,1024]{1,0:T(4,128)}, f32[4,1024]{1,0:T(4,128)S(1)}, u32[]{:S(2)}) copy-start(f32[4,1024]{1,0:T(4,128)S(1)} %get-tuple-element.23) | copy-start | bytes 49156
  58.8 5.6 %copy-start.14 = (s32[80]{0:T(128)S(1)}, s32[80]{0:T(128)}, u32[]{:S(2)}) copy-start(s32[80]{0:T(128)} %copy-done.13) | copy-start | bytes 964
  58.8 5.8 %copy-start.8 = (f32[4]{0:T(128)S(1)}, f32[4]{0:T(128)}, u32[]{:S(2)}) copy-start(f32[4]{0:T(128)} %copy-done.7) | copy-start | bytes 52
  58.8 5.8 %copy-start.15 = (f32[4,32]{1,0:T(4,128)S(1)}, f32[4,32]{1,0:T(4,128)}, u32[]{:S(2)}) copy-start(f32[4,32]{1,0:T(4,128)} %dynamic-slice_reduce_fusion) | copy-start | bytes 1540
  58.8 5.8 %copy-start.17 = (f32[4,32]{1,0:T(4,128)S(1)}, f32[4,32]{1,0:T(4,128)}, u32[]{:S(2)}) copy-start(f32[4,32]{1,0:T(4,128)} %copy-done.16) | copy-start | bytes 1540
  58.8 5.8 %copy-start.21 = (f32[1024]{0:T(1024)S(1)}, f32[1024]{0:T(1024)}, u32[]{:S(2)}) copy-start(f32[1024]{0:T(1024)} %param.11) | copy-start | bytes 12292
  58.8 24.6 %copy-start.12 = (f32[4]{0:T(128)S(1)}, f32[4]{0:T(128)}, u32[]{:S(2)}) copy-start(f32[4]{0:T(128)} %copy-done.11) | copy-start | bytes 52
  59.9 4.8 %copy-start.19 = (f32[32,1024]{1,0:T(8,128)S(1)}, f32[32,1024]{1,0:T(8,128)}, u32[]{:S(2)}) copy-start(f32[32,1024]{1,0:T(8,128)} %param.14) | copy-start | bytes 393220

commit v3 on v1

v3 whole, which is shorter than its diff:
```python
import functools

import jax
import jax.numpy as jnp
from jax import lax
from jax.experimental import pallas as pl
from jax.experimental.pallas import tpu as pltpu
from jax.sharding import PartitionSpec as P

HIGH = lax.Precision.HIGHEST
GROUP = ("strip", "clus")
LANES = 128
CHUNK = 16
F32 = jnp.float32


def lanes_of(shape):
    return lax.broadcasted_iota(jnp.int32, shape, 1)


def rows_of(shape):
    return lax.broadcasted_iota(jnp.int32, shape, 0)


def stats_row(columns, rank):
    shape = (columns[0].shape[0], LANES)
    first = lanes_of(shape) - rank * rows_of(shape)
    spread = sum(jnp.where(first == k, column, 0.0) for k, column in enumerate(columns))
    return jnp.sum(spread, axis=0, keepdims=True)


def stat_column(row, k, nrhs, rank):
    shape = (nrhs, LANES)
    first = lanes_of(shape) - rank * rows_of(shape)
    return jnp.sum(jnp.where(first == k, row, 0.0), axis=1, keepdims=True)


def shifted(value, k):
    return pltpu.roll(value, LANES - k, 1)


def far_sum_of(got_ref, nrhs, rank):
    row = jnp.sum(got_ref[:, 0, :LANES], axis=0, keepdims=True)
    shape = (nrhs, LANES)
    first = lanes_of(shape) - rank * rows_of(shape)
    own = jnp.where((first >= 0) & (first < rank), row, 0.0)
    return sum((pltpu.roll(own, k * rank, 1) for k in range(1, LANES // rank)), own)


def put_message(field, columns, far_cols_ref, couple_ref, ranks_ref, sent_ref):
    nrhs, rank = field.shape[0], far_cols_ref.shape[0]
    groups = sent_ref.shape[0]
    proj = lax.dot_general(
        field, far_cols_ref[...], (((1,), (1,)), ((), ())), precision=HIGH, preferred_element_type=F32
    )
    wide = jnp.concatenate([proj] * CHUNK, axis=1)
    shape = (CHUNK, CHUNK * rank)
    owner = lax.div(lanes_of(shape), rank)
    inner = lax.rem(lanes_of(shape), rank)
    row = stats_row(columns, rank)
    for start in range(0, groups, CHUNK):
        limit = jnp.zeros(shape, jnp.int32)
        for i in range(CHUNK):
            limit = jnp.where(owner == i, ranks_ref[0, start + i], limit)
        keep = (owner == rows_of(shape)) & (inner < limit)
        spread = jnp.concatenate([jnp.where(keep, wide[r : r + 1], 0.0) for r in range(nrhs)], axis=0)
        couple = couple_ref[pl.ds(start * rank, CHUNK * rank), :]
        terms = jnp.dot(spread, couple, precision=HIGH, preferred_element_type=F32)
        terms = jnp.concatenate([terms[r * CHUNK : (r + 1) * CHUNK] for r in range(nrhs)], axis=1)
        sent_ref[pl.ds(start, CHUNK), 0, :LANES] = terms
        sent_ref[pl.ds(start, CHUNK), 0, LANES:] = jnp.broadcast_to(row, (CHUNK, LANES))


def put_blocks(part, first, window):
    part = part.astype(jnp.bfloat16).astype(F32)
    part = jnp.concatenate([part, jnp.zeros_like(part)], axis=0)
    for c in range(part.shape[1] // LANES):
        window[first + c] = part[:, c * LANES : (c + 1) * LANES]


def near_field(window, tiles_ref, list_ref, sums):
    for total in sums:
        total[...] = jnp.zeros_like(total)
    for n in range(tiles_ref.shape[0]):
        total = sums[n % len(sums)]
        source = window[list_ref[1, n]].astype(jnp.bfloat16)
        product = jnp.dot(source, tiles_ref[n], preferred_element_type=F32)
        total[list_ref[0, n]] += product
    whole = sum((total[...] for total in sums[1:]), sums[0][...])
    return jnp.concatenate([whole[b] for b in range(whole.shape[0])], axis=1)


def start_kernel(loads_ref, far_cols_ref, couple_ref, ranks_ref, sent_ref, field_ref):
    loads = loads_ref[...]
    field_ref[...] = loads
    square = jnp.sum(loads * loads, axis=1, keepdims=True)
    put_message(loads, [square], far_cols_ref, couple_ref, ranks_ref, sent_ref)


def image_of(field, far, self_ref, far_rows_ref, near):
    rank = far_rows_ref.shape[0]
    far = jnp.dot(far[:, :rank], far_rows_ref[...], precision=HIGH, preferred_element_type=F32)
    return self_ref[...] * field + near[: field.shape[0]] + far


def step0_kernel(
    loads_ref, before_ref, pair_ref, after_ref, got_ref, self_ref, tiles_ref, list_ref, far_rows_ref,
    far_cols_ref, couple_ref, ranks_ref, sent_ref, image_ref, state_ref, window, *sums,
):
    nrhs, rank = loads_ref.shape[0], far_rows_ref.shape[0]
    row = jnp.sum(got_ref[:, 0, LANES:], axis=0, keepdims=True)
    beta = jnp.sqrt(stat_column(row, 0, nrhs, rank))
    basis = loads_ref[...] / beta
    first = 0
    for part in (before_ref, pair_ref, after_ref):
        put_blocks(part[...] / beta, first, window)
        first += part.shape[1] // LANES
    far = far_sum_of(got_ref, nrhs, rank) / beta
    near = near_field(window, tiles_ref, list_ref, sums)
    image = image_of(basis, far, self_ref, far_rows_ref, near)
    image_ref[...] = image
    state_ref[...] = jnp.concatenate([far, jnp.broadcast_to(beta, far.shape)], axis=0)
    norm = jnp.sum(basis * basis, axis=1, keepdims=True)
    dot = jnp.sum(basis * image, axis=1, keepdims=True)
    share = jnp.where(norm > 0, dot / jnp.where(norm > 0, norm, 1.0), 0.0)
    rest = image - share * basis
    rest = jnp.sum(rest * rest, axis=1, keepdims=True)
    put_message(image, [norm, dot, share, rest], far_cols_ref, couple_ref, ranks_ref, sent_ref)


def step1_kernel(
    loads_ref, before_ref, pair_ref, after_ref, image_ref, image_before_ref, image_pair_ref, image_after_ref,
    got_ref, state_ref, self_ref, tiles_ref, list_ref, far_rows_ref, sent_ref, basis_ref, coeff_ref, window, *sums,
):
    nrhs, rank = loads_ref.shape[0], far_rows_ref.shape[0]
    beta = state_ref[nrhs:, :1]
    far0 = state_ref[:nrhs, :]
    stats = got_ref[:, 0, LANES:]
    row = jnp.sum(stats, axis=0, keepdims=True)
    h00 = stat_column(row, 1, nrhs, rank)
    away = shifted(stats, 2) - shifted(row, 1)
    rest = jnp.sum(shifted(stats, 3) + stats * away * away, axis=0, keepdims=True)
    h10 = jnp.sqrt(stat_column(rest, 0, nrhs, rank))
    basis0 = loads_ref[...] / beta
    basis1 = (image_ref[...] - h00 * basis0) / h10
    first = 0
    for part, image_part in (
        (before_ref, image_before_ref), (pair_ref, image_pair_ref), (after_ref, image_after_ref)
    ):
        put_blocks((image_part[...] - h00 * (part[...] / beta)) / h10, first, window)
        first += part.shape[1] // LANES
    far = (far_sum_of(got_ref, nrhs, rank) - h00 * far0) / h10
    near = near_field(window, tiles_ref, list_ref, sums)
    image = image_of(basis1, far, self_ref, far_rows_ref, near)
    columns = [jnp.sum(a * image, axis=1, keepdims=True) for a in (basis0, basis1, image)]
    row = stats_row(columns, rank)
    sent_ref[:, 0, :] = jnp.broadcast_to(row, (sent_ref.shape[0], LANES))
    basis_ref[...] = jnp.concatenate([basis0, basis1], axis=0)
    coeff_ref[...] = jnp.concatenate([jnp.broadcast_to(v, (nrhs, LANES)) for v in (beta, h00, h10)], axis=0)


def finish_kernel(rank, got_ref, basis_ref, coeff_ref, out_ref):
    nrhs = out_ref.shape[0]
    row = jnp.sum(got_ref[:, 0, :], axis=0, keepdims=True)
    h01, h11, gram11 = (stat_column(row, k, nrhs, rank) for k in range(3))
    beta, h00, h10 = (coeff_ref[k * nrhs : (k + 1) * nrhs, :1] for k in range(3))
    gram00 = h00 * h00 + h10 * h10
    gram01 = h00 * h01 + h10 * h11
    lower00 = jnp.sqrt(gram00)
    lower10 = gram01 / lower00
    lower11 = jnp.sqrt(gram11 - lower10 * lower10)
    middle0 = beta * h00 / lower00
    middle1 = (beta * h01 - lower10 * middle0) / lower11
    y1 = middle1 / lower11
    y0 = (middle0 - lower10 * y1) / lower00
    out_ref[...] = y0 * basis_ref[:nrhs, :] + y1 * basis_ref[nrhs:, :]


def call(kernel, args, outs, scratch=(), smem=()):
    in_specs = [
        pl.BlockSpec(memory_space=pltpu.SMEM if i in smem else pltpu.VMEM) for i in range(len(args))
    ]
    return pl.pallas_call(
        kernel,
        out_shape=[jax.ShapeDtypeStruct(shape, F32) for shape in outs],
        in_specs=in_specs,
        out_specs=[pl.BlockSpec(memory_space=pltpu.VMEM)] * len(outs),
        scratch_shapes=list(scratch),
        compiler_params=pltpu.CompilerParams(vmem_limit_bytes=32 * 2**20),
    )(*args)


def window_of(field):
    pair = lax.all_gather(field, "clus", axis=1, tiled=True)
    devices = lax.axis_size("strip")
    up = [(i, i + 1) for i in range(devices - 1)]
    down = [(j, i) for i, j in up]
    return lax.ppermute(pair, "strip", up), pair, lax.ppermute(pair, "strip", down)


def exchanged(message):
    return lax.all_to_all(message, GROUP, 0, 0, tiled=True)


def body(loads, self_term, near_tiles, near_list, far_rows, far_cols, coupling, ranks):
    nrhs, panels = loads.shape
    rank = far_cols.shape[0]
    tile = near_tiles.shape[1]
    rows = panels // tile
    cores = lax.axis_size("clus")
    groups = lax.axis_size("strip") * cores
    couple = coupling.reshape(groups * rank, rank)
    near_list = near_list.T
    ranks = ranks.reshape(1, groups)
    self_term = self_term.reshape(1, panels)
    message = (groups, 1, 2 * LANES)
    scratch = [pltpu.VMEM((3 * cores * rows, 2 * nrhs, tile), F32)]
    scratch += [pltpu.VMEM((rows, 2 * nrhs, tile), F32)] * 4

    sent, field = call(start_kernel, (loads, far_cols, couple, ranks), [message, loads.shape], smem=(3,))
    got = exchanged(sent)
    before, pair, after = window_of(field)
    sent, image, state = call(
        step0_kernel,
        (loads, before, pair, after, got, self_term, near_tiles, near_list, far_rows, far_cols, couple, ranks),
        [message, loads.shape, (2 * nrhs, LANES)],
        scratch,
        smem=(7, 11),
    )
    got = exchanged(sent)
    image_before, image_pair, image_after = window_of(image)
    sent, basis, coeff = call(
        step1_kernel,
        (
            loads, before, pair, after, image, image_before, image_pair, image_after, got, state, self_term,
            near_tiles, near_list, far_rows,
        ),
        [(groups, 1, LANES), (2 * nrhs, panels), (3 * nrhs, LANES)],
        scratch,
        smem=(12,),
    )
    got = exchanged(sent)
    return call(functools.partial(finish_kernel, rank), (got, basis, coeff), [loads.shape])[0]


def solution(mesh):
    every = ("case",) + GROUP
    in_specs = (
        P(None, every),
        P(every),
        P(every, None, None),
        P(every, None),
        P(None, every),
        P(None, every),
        P(None, GROUP, None, None),
        P(None, GROUP),
    )
    return jax.shard_map(body, mesh=mesh, in_specs=in_specs, out_specs=P(None, every), check_vma=False)
```

time: 60.9 us -> 60.9 us (level)
  blocking collectives: 18 us -> 34.4 us
  starting transfers between devices: 22.3 us -> 12.5 us
  Pallas kernels: 0 us -> 6.15 us
  waiting for transfers between devices: 5.99 us -> 0.01 us
  matrix products: 5.74 us -> 0 us
  other arithmetic: 4.19 us -> 0 us
  local copies, waits for them, and re-layouts: 3.94 us -> 7.24 us
    all_to_all x1 -> x3, blocking collectives: 13.9 us -> 30.7 us  [exchanged(): return lax.all_to_all(message, GROUP, 0, 0, tiled=True)]
    all_to_all x2 -> x0, starting transfers between devices: 9.82 us -> none  [exchange(): got = lax.all_to_all(sent, GROUP, 0, 0, tiled=True)]
    unnamed x13 -> x20, local copies, waits for them, and re-layouts: 0.03 us -> 7.24 us
    pallas_call x0 -> x4, Pallas kernels: none -> 6.15 us  [call(): pl.pallas_call(kernel, out_shape=[jax.ShapeDtypeStruct(shape, F32) for sh...]
    dot_general x10 -> x0, matrix products: 5.74 us -> none  [the longest x2 1.66 us: near_field(): jnp.einsum('rnk,nkt->rnt', sources, near_tiles, preferred_element_type=jn...]
    all_to_all x2 -> x0, waiting for transfers between devices: 5.12 us -> none  [exchange(): got = lax.all_to_all(sent, GROUP, 0, 0, tiled=True)]
    reduce_sum x8 -> x0, other arithmetic: 1.53 us -> none  [the longest x1 0.84 us: body(): jnp.sum(loads * loads, axis=1)[None]]
    all_to_all x3 -> x0, local copies, waits for them, and re-layouts: 1.35 us -> none  [exchange(): got = lax.all_to_all(sent, GROUP, 0, 0, tiled=True)]
  transfers between devices with their start and end apart: 6 -> 4, of which waited for: 2 -> 0; matrix products, arithmetic and copies ran while one was open for 10% -> 0% of each run, Pallas kernels for 0% -> 0%
where the time goes in v3:
time: 60.9 us; the launch traced here: 60.4 us
  blocking collectives  34.4 us (56%)
  starting transfers between devices  12.5 us (21%)
  local copies, waits for them, and re-layouts  7.24 us (12%)
  Pallas kernels  6.15 us (10%)
    all_to_all x3, blocking collectives, exchanged(): return lax.all_to_all(message, GROUP, 0, 0, tiled=True)  30.7 us
    ppermute x2, starting transfers between devices, window_of(): lax.ppermute(pair, 'strip', up)  9.91 us
    unnamed x20, local copies, waits for them, and re-layouts  7.24 us
    pallas_call x4, Pallas kernels, call(): pl.pallas_call(kernel, out_shape=[jax.ShapeDtypeStruct(shape, F32) for sh...  6.15 us
    all_gather x2, blocking collectives, window_of(): pair = lax.all_gather(field, 'clus', axis=1, tiled=True)  3.78 us
    ppermute x2, starting transfers between devices, window_of(): lax.ppermute(pair, 'strip', down)  2.56 us
  transfers between devices with their start and end apart: 4, of which 0 were waited for; matrix products, arithmetic and copies ran while one was open for 0% of the time, Pallas kernels for 0%

profile of v3, /device:TPU:0, one launch (start us, length us, event | category | flops | bytes accessed | tf_op | source)
XLA Modules:
  0.0 60.4 jit_solution(16912581837044655806)
XLA Ops:
  0.0 0.9 %copy-done.2 = f32[16,1,32,32]{3,2,1,0:T(8,128)S(1)} copy-done((f32[16,1,32,32]{3,2,1,0:T(8,128)S(1)}, f32[16,1,32,32]{3,2,1,0:T(8,128)}, u32[]{:S(2)}) %copy-start.2) | copy-done | bytes 65560
  1.0 0.9 %copy-done.4 = f32[32,1024]{1,0:T(8,128)S(1)} copy-done((f32[32,1024]{1,0:T(8,128)S(1)}, f32[32,1024]{1,0:T(8,128)}, u32[]{:S(2)}) %copy-start.4) | copy-done | bytes 131096
  1.9 0.7 %copy-done.5 = f32[4,1024]{1,0:T(4,128)S(1)} copy-done((f32[4,1024]{1,0:T(4,128)S(1)}, f32[4,1024]{1,0:T(4,128)}, u32[]{:S(2)}) %copy-start.5) | copy-done | bytes 16408
  2.6 0.7 %copy-done.9 = s32[16,1]{0,1:T(1,128)S(1)} copy-done((s32[16,1]{0,1:T(1,128)S(1)}, s32[16,1]{0,1:T(1,128)}, u32[]{:S(2)}) %copy-start.9) | copy-done | bytes 88
  3.2 1.3 %shard_map.82 = (f32[16,1,256]{2,1,0:T(1,128)S(1)}, f32[4,1024]{1,0:T(4,128)S(1)}) custom-call(f32[4,1024]{1,0:T(4,128)S(1)} %copy-done.5, f32[32,1024]{1,0:T(8,128)S(1)} %copy-done.4, f32[512,32]{1,0:T(8,128)S(1)} %bitcast.4, s32[1,16]{1,0:T(1,128)S(1)} %bitcast.10), custom_call_target="tpu_custom_call" | custom-call | tf_op jit(solution)/shard_map/pallas_call | solution.py:183
  4.6 1.9 %all_gather.6.pair_ref = f32[4,2048]{1,0:T(4,128)S(1)} all-gather(f32[4,1024]{1,0:T(4,128)S(1)} %get-tuple-element.13), channel_id=1, replica_groups=mesh['case'=2,'strip'=8,'clus'=2] {'clus'}, dimensions={1}, use_global_device_ids=true | all-gather | bytes 49152 | tf_op jit(solution)/shard_map/all_gather | solution.py:194
  6.5 1.3 %collective-permute-start.1 = (f32[4,2048]{1,0:T(4,128)S(1)}, f32[4,2048]{1,0:T(4,128)S(1)}, u32[]{:S(2)}, u32[]{:S(2)}) collective-permute-start(f32[4,2048]{1,0:T(4,128)S(1)} %all_gather.6.pair_ref), channel_id=1, source_target_pairs={{2,0},{4,2},{6,4},{8,6},{10,8},{12,10},{14,12},{3,1},{5,3},{7,5},{... | collective-permute-start | bytes 98312 | tf_op jit(solution)/shard_map/ppermute | solution.py:198
  7.8 5.4 %collective-permute-start = (f32[4,2048]{1,0:T(4,128)S(1)}, f32[4,2048]{1,0:T(4,128)S(1)}, u32[]{:S(2)}, u32[]{:S(2)}) collective-permute-start(f32[4,2048]{1,0:T(4,128)S(1)} %all_gather.6.pair_ref), channel_id=1, source_target_pairs={{0,2},{2,4},{4,6},{6,8},{8,10},{10,12},{12,14},{1,3},{3,5},{5,7},{... | collective-permute-start | bytes 98312 | tf_op jit(solution)/shard_map/ppermute | solution.py:198
  13.2 12.6 %all_to_all.15.got_ref = f32[16,1,256]{2,1,0:T(1,128)S(1)} all-to-all(f32[16,1,256]{2,1,0:T(1,128)S(1)} %get-tuple-element.14), channel_id=1, replica_groups=mesh['case'=2,'strip'=8,'clus'=2] {'strip','clus'}, dimensions={0} | all-to-all | bytes 32768 | tf_op jit(solution)/shard_map/all_to_all | solution.py:202
  25.8 0.0 collective-permute-done.1.after_ref
  25.8 1.7 %copy-done = bf16[80,128,128]{2,1,0:T(8,128)(2,1)S(1)} copy-done((bf16[80,128,128]{2,1,0:T(8,128)(2,1)S(1)}, bf16[80,128,128]{2,1,0:T(8,128)(2,1)}, u32[]{:S(2)}) %copy-start) | copy-done | bytes 2621464
  27.5 0.9 %copy-done.3 = f32[32,1024]{1,0:T(8,128)S(1)} copy-done((f32[32,1024]{1,0:T(8,128)S(1)}, f32[32,1024]{1,0:T(8,128)}, u32[]{:S(2)}) %copy-start.3) | copy-done | bytes 131096
  28.4 0.7 %copy-done.6 = f32[1024]{0:T(1024)S(1)} copy-done((f32[1024]{0:T(1024)S(1)}, f32[1024]{0:T(1024)}, u32[]{:S(2)}) %copy-start.6) | copy-done | bytes 4120
  29.1 0.7 %copy-done.8 = s32[80,2]{0,1:T(2,128)S(1)} copy-done((s32[80,2]{0,1:T(2,128)S(1)}, s32[80,2]{0,1:T(2,128)}, u32[]{:S(2)}) %copy-start.8) | copy-done | bytes 664
  29.8 2.3 %shard_map.83 = (f32[16,1,256]{2,1,0:T(1,128)S(1)}, f32[4,1024]{1,0:T(4,128)S(1)}, f32[8,128]{1,0:T(8,128)S(1)}) custom-call(f32[4,1024]{1,0:T(4,128)S(1)} %copy-done.5, f32[4,2048]{1,0:T(4,128)S(1)} %collective-permute-done.before_ref, f32[4,2048]{1,0:T(4,128)S(1)} %all_gather.6.pair_ref, f32[4,2048]{1,0:T(4,128)S(1)} %collective-permute-done.1.after_ref, ...), custom_call_target="tpu_custom_call" | custom-call | tf_op jit(solution)/shard_map/pallas_call | solution.py:183
  32.1 1.8 %all_gather.7.image_pair_ref = f32[4,2048]{1,0:T(4,128)S(1)} all-gather(f32[4,1024]{1,0:T(4,128)S(1)} %get-tuple-element.15.image_ref), channel_id=1, replica_groups=mesh['case'=2,'strip'=8,'clus'=2] {'clus'}, dimensions={1}, use_global_device_ids=true | all-gather | bytes 49152 | tf_op jit(solution)/shard_map/all_gather | solution.py:194
  33.9 1.3 %collective-permute-start.3 = (f32[4,2048]{1,0:T(4,128)S(1)}, f32[4,2048]{1,0:T(4,128)S(1)}, u32[]{:S(2)}, u32[]{:S(2)}) collective-permute-start(f32[4,2048]{1,0:T(4,128)S(1)} %all_gather.7.image_pair_ref), channel_id=1, source_target_pairs={{2,0},{4,2},{6,4},{8,6},{10,8},{12,10},{14,12},{3,1},{5,3},{7,5},{... | collective-permute-start | bytes 98312 | tf_op jit(solution)/shard_map/ppermute | solution.py:198
  35.2 4.5 %collective-permute-start.2 = (f32[4,2048]{1,0:T(4,128)S(1)}, f32[4,2048]{1,0:T(4,128)S(1)}, u32[]{:S(2)}, u32[]{:S(2)}) collective-permute-start(f32[4,2048]{1,0:T(4,128)S(1)} %all_gather.7.image_pair_ref), channel_id=1, source_target_pairs={{0,2},{2,4},{4,6},{6,8},{8,10},{10,12},{12,14},{1,3},{3,5},{5,7},{... | collective-permute-start | bytes 98312 | tf_op jit(solution)/shard_map/ppermute | solution.py:198
  39.8 9.1 %all_to_all.16.got_ref = f32[16,1,256]{2,1,0:T(1,128)S(1)} all-to-all(f32[16,1,256]{2,1,0:T(1,128)S(1)} %get-tuple-element.16), channel_id=1, replica_groups=mesh['case'=2,'strip'=8,'clus'=2] {'strip','clus'}, dimensions={0} | all-to-all | bytes 32768 | tf_op jit(solution)/shard_map/all_to_all | solution.py:202
  48.9 0.0 collective-permute-done.3.image_after_ref
  48.9 0.0 collective-permute-done.2.image_before_ref
  48.9 1.7 %shard_map.84 = (f32[16,1,128]{2,1,0:T(1,128)S(1)}, f32[8,1024]{1,0:T(8,128)S(1)}, f32[12,128]{1,0:T(8,128)S(1)}) custom-call(f32[4,1024]{1,0:T(4,128)S(1)} %copy-done.5, f32[4,2048]{1,0:T(4,128)S(1)} %collective-permute-done.before_ref, f32[4,2048]{1,0:T(4,128)S(1)} %all_gather.6.pair_ref, f32[4,2048]{1,0:T(4,128)S(1)} %collective-permute-done.1.after_ref, ...), custom_call_target="tpu_custom_call" | custom-call | tf_op jit(solution)/shard_map/pallas_call | solution.py:183
  50.6 9.0 %all_to_all.17.got_ref = f32[16,1,128]{2,1,0:T(1,128)S(1)} all-to-all(f32[16,1,128]{2,1,0:T(1,128)S(1)} %get-tuple-element.18), channel_id=1, replica_groups=mesh['case'=2,'strip'=8,'clus'=2] {'strip','clus'}, dimensions={0} | all-to-all | bytes 16384 | tf_op jit(solution)/shard_map/all_to_all | solution.py:202
  59.6 0.8 %shard_map.85 = f32[4,1024]{1,0:T(4,128)} custom-call(f32[16,1,128]{2,1,0:T(1,128)S(1)} %all_to_all.17.got_ref, f32[8,1024]{1,0:T(8,128)S(1)} %get-tuple-element.19.basis_ref, f32[12,128]{1,0:T(8,128)S(1)} %get-tuple-element.20.coeff_ref), custom_call_target="tpu_custom_call" | custom-call | tf_op jit(solution)/shard_map/pallas_call | solution.py:183
  (13 shorter events, 0.0 us)
Async XLA Ops:
  0.0 0.9 %copy-start.2 = (f32[16,1,32,32]{3,2,1,0:T(8,128)S(1)}, f32[16,1,32,32]{3,2,1,0:T(8,128)}, u32[]{:S(2)}) copy-start(f32[16,1,32,32]{3,2,1,0:T(8,128)} %param.14) | copy-start | bytes 196612
  1.0 0.9 %copy-start.4 = (f32[32,1024]{1,0:T(8,128)S(1)}, f32[32,1024]{1,0:T(8,128)}, u32[]{:S(2)}) copy-start(f32[32,1024]{1,0:T(8,128)} %far_cols_ref.3) | copy-start | bytes 393220
  1.9 0.7 %copy-start.5 = (f32[4,1024]{1,0:T(4,128)S(1)}, f32[4,1024]{1,0:T(4,128)}, u32[]{:S(2)}) copy-start(f32[4,1024]{1,0:T(4,128)} %loads_ref.5) | copy-start | bytes 49156
  2.6 0.7 %copy-start.9 = (s32[16,1]{0,1:T(1,128)S(1)}, s32[16,1]{0,1:T(1,128)}, u32[]{:S(2)}) copy-start(s32[16,1]{0,1:T(1,128)} %param.15) | copy-start | bytes 196
  3.2 45.6 %copy-start.7 = (f32[1024]{0:T(1024)S(1)}, f32[1024]{0:T(1024)}, u32[]{:S(2)}) copy-start(f32[1024]{0:T(1024)} %param.9) | copy-start | bytes 12292
  6.5 19.3 %collective-permute-start.1 = (f32[4,2048]{1,0:T(4,128)S(1)}, f32[4,2048]{1,0:T(4,128)S(1)}, u32[]{:S(2)}, u32[]{:S(2)}) collective-permute-start(f32[4,2048]{1,0:T(4,128)S(1)} %all_gather.6.pair_ref), channel_id=1, source_target_pairs={{2,0},{4,2},{6,4},{8,6},{10,8},{12,10},{14,12},{3,1},{5,3},{7,5},{... | collective-permute-start | bytes 98312 | tf_op jit(solution)/shard_map/ppermute | solution.py:198
  7.8 18.0 %collective-permute-start = (f32[4,2048]{1,0:T(4,128)S(1)}, f32[4,2048]{1,0:T(4,128)S(1)}, u32[]{:S(2)}, u32[]{:S(2)}) collective-permute-start(f32[4,2048]{1,0:T(4,128)S(1)} %all_gather.6.pair_ref), channel_id=1, source_target_pairs={{0,2},{2,4},{4,6},{6,8},{8,10},{10,12},{12,14},{1,3},{3,5},{5,7},{... | collective-permute-start | bytes 98312 | tf_op jit(solution)/shard_map/ppermute | solution.py:198
  25.8 1.7 %copy-start = (bf16[80,128,128]{2,1,0:T(8,128)(2,1)S(1)}, bf16[80,128,128]{2,1,0:T(8,128)(2,1)}, u32[]{:S(2)}) copy-start(bf16[80,128,128]{2,1,0:T(8,128)(2,1)} %tiles_ref.3) | copy-start | bytes 7864324
  27.5 0.9 %copy-start.3 = (f32[32,1024]{1,0:T(8,128)S(1)}, f32[32,1024]{1,0:T(8,128)}, u32[]{:S(2)}) copy-start(f32[32,1024]{1,0:T(8,128)} %far_rows_ref.3) | copy-start | bytes 393220
  28.4 0.7 %copy-start.6 = (f32[1024]{0:T(1024)S(1)}, f32[1024]{0:T(1024)}, u32[]{:S(2)}) copy-start(f32[1024]{0:T(1024)} %param.9) | copy-start | bytes 12292
  29.1 0.7 %copy-start.8 = (s32[80,2]{0,1:T(2,128)S(1)}, s32[80,2]{0,1:T(2,128)}, u32[]{:S(2)}) copy-start(s32[80,2]{0,1:T(2,128)} %param.11) | copy-start | bytes 1924
  29.8 19.1 %copy-start.1 = (bf16[80,128,128]{2,1,0:T(8,128)(2,1)S(1)}, bf16[80,128,128]{2,1,0:T(8,128)(2,1)}, u32[]{:S(2)}) copy-start(bf16[80,128,128]{2,1,0:T(8,128)(2,1)} %tiles_ref.3) | copy-start | bytes 7864324
  33.9 14.9 %collective-permute-start.3 = (f32[4,2048]{1,0:T(4,128)S(1)}, f32[4,2048]{1,0:T(4,128)S(1)}, u32[]{:S(2)}, u32[]{:S(2)}) collective-permute-start(f32[4,2048]{1,0:T(4,128)S(1)} %all_gather.7.image_pair_ref), channel_id=1, source_target_pairs={{2,0},{4,2},{6,4},{8,6},{10,8},{12,10},{14,12},{3,1},{5,3},{7,5},{... | collective-permute-start | bytes 98312 | tf_op jit(solution)/shard_map/ppermute | solution.py:198
  35.2 13.6 %collective-permute-start.2 = (f32[4,2048]{1,0:T(4,128)S(1)}, f32[4,2048]{1,0:T(4,128)S(1)}, u32[]{:S(2)}, u32[]{:S(2)}) collective-permute-start(f32[4,2048]{1,0:T(4,128)S(1)} %all_gather.7.image_pair_ref), channel_id=1, source_target_pairs={{0,2},{2,4},{4,6},{6,8},{8,10},{10,12},{12,14},{1,3},{3,5},{5,7},{... | collective-permute-start | bytes 98312 | tf_op jit(solution)/shard_map/ppermute | solution.py:198

commit v4 on v3

v4 whole, which is shorter than its diff:
```python
import functools

import jax
import jax.numpy as jnp
from jax import lax
from jax.experimental import pallas as pl
from jax.experimental.pallas import tpu as pltpu
from jax.sharding import Mesh
from jax.sharding import PartitionSpec as P

HIGH = lax.Precision.HIGHEST
GROUP = ("hi", "lo", "clus")
LANES = 128
CHUNK = 16
F32 = jnp.float32


def lanes_of(shape):
    return lax.broadcasted_iota(jnp.int32, shape, 1)


def rows_of(shape):
    return lax.broadcasted_iota(jnp.int32, shape, 0)


def stats_row(columns, rank):
    shape = (columns[0].shape[0], LANES)
    first = lanes_of(shape) - rank * rows_of(shape)
    spread = sum(jnp.where(first == k, column, 0.0) for k, column in enumerate(columns))
    return jnp.sum(spread, axis=0, keepdims=True)


def stat_column(row, k, nrhs, rank):
    shape = (nrhs, LANES)
    first = lanes_of(shape) - rank * rows_of(shape)
    return jnp.sum(jnp.where(first == k, row, 0.0), axis=1, keepdims=True)


def shifted(value, k):
    return pltpu.roll(value, LANES - k, 1)


def far_sum_of(row, nrhs, rank):
    shape = (nrhs, LANES)
    first = lanes_of(shape) - rank * rows_of(shape)
    own = jnp.where((first >= 0) & (first < rank), row, 0.0)
    return sum((pltpu.roll(own, k * rank, 1) for k in range(1, LANES // rank)), own)


def total(rows):
    return jnp.sum(rows, axis=0, keepdims=True)


def put_message(field, columns, far_cols, couple_ref, ranks_ref, groups, put):
    nrhs, rank = field.shape[0], far_cols.shape[0]
    proj = lax.dot_general(
        field, far_cols, (((1,), (1,)), ((), ())), precision=HIGH, preferred_element_type=F32
    )
    wide = jnp.concatenate([proj] * CHUNK, axis=1)
    shape = (CHUNK, CHUNK * rank)
    owner = lax.div(lanes_of(shape), rank)
    inner = lax.rem(lanes_of(shape), rank)
    row = stats_row(columns, rank)
    for start in range(0, groups, CHUNK):
        limit = jnp.zeros(shape, jnp.int32)
        for i in range(CHUNK):
            limit = jnp.where(owner == i, ranks_ref[0, start + i], limit)
        keep = (owner == rows_of(shape)) & (inner < limit)
        spread = jnp.concatenate([jnp.where(keep, wide[r : r + 1], 0.0) for r in range(nrhs)], axis=0)
        couple = couple_ref[pl.ds(start * rank, CHUNK * rank), :]
        terms = jnp.dot(spread, couple, precision=HIGH, preferred_element_type=F32)
        terms = jnp.concatenate([terms[r * CHUNK : (r + 1) * CHUNK] for r in range(nrhs)], axis=1)
        put(start, terms, row)


def put_blocks(part, first, window):
    part = part.astype(jnp.bfloat16).astype(F32)
    part = jnp.concatenate([part, jnp.zeros_like(part)], axis=0)
    for c in range(part.shape[1] // LANES):
        window[first + c] = part[:, c * LANES : (c + 1) * LANES]


def near_field(window, tiles_ref, list_ref, sums):
    for held in sums:
        held[...] = jnp.zeros_like(held)
    for n in range(tiles_ref.shape[0]):
        held = sums[n % len(sums)]
        source = window[list_ref[1, n]].astype(jnp.bfloat16)
        product = jnp.dot(source, tiles_ref[n], preferred_element_type=F32)
        held[list_ref[0, n]] += product
    whole = sum((held[...] for held in sums[1:]), sums[0][...])
    return jnp.concatenate([whole[b] for b in range(whole.shape[0])], axis=1)


def start_kernel(loads_ref, ranks_ref, *refs):
    count = 5
    sources, (sent_ref, field_ref), held, sems = refs[:count], refs[count : count + 2], refs[count + 2 : -1], refs[-1]
    copies = [pltpu.make_async_copy(a, b, sems.at[i]) for i, (a, b) in enumerate(zip(sources, held))]
    for copy in copies:
        copy.start()
    loads = loads_ref[...]
    field_ref[...] = loads
    square = jnp.sum(loads * loads, axis=1, keepdims=True)
    copies[0].wait()
    copies[1].wait()

    def put(start, terms, row):
        sent_ref[pl.ds(start, CHUNK), 0, :LANES] = terms
        sent_ref[pl.ds(start, CHUNK), 0, LANES:] = jnp.broadcast_to(row, terms.shape)

    put_message(loads, [square], held[0][...], held[1], ranks_ref, sent_ref.shape[0], put)
    for copy in copies[2:]:
        copy.wait()


def image_of(field, far, self_ref, far_rows_ref, near):
    rank = far_rows_ref.shape[0]
    far = jnp.dot(far[:, :rank], far_rows_ref[...], precision=HIGH, preferred_element_type=F32)
    return self_ref[...] * field + near[: field.shape[0]] + far


def step0_kernel(
    loads_ref, pair_ref, even_ref, odd_ref, got_ref, far_cols_ref, couple_ref, tiles_ref, far_rows_ref, self_ref,
    list_ref, ranks_ref, sent_ref, window0_ref, state_ref, window, *sums,
):
    nrhs, rank = loads_ref.shape[0], far_rows_ref.shape[0]
    span = pair_ref.shape[1] // LANES
    low, core = lax.axis_index("lo"), lax.axis_index("clus")
    mine = lax.rem(rows_of((got_ref.shape[1], LANES)), 2) == core
    got = [jnp.where(mine, got_ref[0, :, 0, k : k + LANES], 0.0) + jnp.where(mine, got_ref[1, :, 0, k : k + LANES], 0.0) for k in (0, LANES)]
    beta = jnp.sqrt(stat_column(total(got[1]), 0, nrhs, rank))
    basis = loads_ref[...] / beta
    for part_ref, place in ((pair_ref, 1), (even_ref, 2 * (1 - low)), (odd_ref, 2 * low)):
        part = part_ref[...] / beta
        window0_ref[place] = part
        put_blocks(part, place * span, window)
    far = far_sum_of(total(got[0]), nrhs, rank) / beta
    near = near_field(window, tiles_ref, list_ref, sums)
    image = image_of(basis, far, self_ref, far_rows_ref, near)
    state_ref[...] = jnp.concatenate([far, jnp.broadcast_to(beta, far.shape)], axis=0)
    norm = jnp.sum(basis * basis, axis=1, keepdims=True)
    dot = jnp.sum(basis * image, axis=1, keepdims=True)
    share = jnp.where(norm > 0, dot / jnp.where(norm > 0, norm, 1.0), 0.0)
    rest = image - share * basis
    rest = jnp.sum(rest * rest, axis=1, keepdims=True)

    def put(start, terms, row):
        blank = jnp.zeros((nrhs - 2, LANES), F32)
        for i in range(CHUNK):
            tail = jnp.concatenate([terms[i : i + 1], row, blank], axis=0)
            sent_ref[start + i] = jnp.concatenate([image, tail], axis=1)

    put_message(image, [norm, dot, share, rest], far_cols_ref[...], couple_ref, ranks_ref, sent_ref.shape[0], put)


def step1_kernel(
    loads_ref, window0_ref, got_ref, state_ref, tiles_ref, far_rows_ref, self_ref, list_ref,
    sent_ref, basis_ref, coeff_ref, window, *sums,
):
    nrhs, rank = loads_ref.shape[0], far_rows_ref.shape[0]
    panels = loads_ref.shape[1]
    groups = got_ref.shape[0]
    beta = state_ref[nrhs:, :1]
    far0 = state_ref[:nrhs, :]
    tail = got_ref[:, :, panels:]
    summed = jnp.sum(tail, axis=0)
    h00 = stat_column(summed[1:2], 1, nrhs, rank)
    stats = tail[:, 1]
    away = shifted(stats, 2) - shifted(summed[1:2], 1)
    rest = total(shifted(stats, 3) + stats * away * away)
    h10 = jnp.sqrt(stat_column(rest, 0, nrhs, rank))
    basis0 = loads_ref[...] / beta
    strip = lax.axis_index("hi") * 2 + lax.axis_index("lo")
    core = lax.axis_index("clus")
    cores = lax.axis_size("clus")
    image0 = got_ref[strip * cores + core, :, :panels]
    basis1 = (image0 - h00 * basis0) / h10
    span = panels // LANES
    for i in range(3 * cores):
        owner = (strip - 1) * cores + i
        inside = (owner >= 0) & (owner < groups)
        owner = jnp.clip(owner, 0, groups - 1)
        field = jnp.where(inside, got_ref[owner, :, :panels], 0.0)
        field0 = window0_ref[i // cores, :, (i % cores) * panels : (i % cores + 1) * panels]
        put_blocks((field - h00 * field0) / h10, i * span, window)
    far = (far_sum_of(summed[0:1], nrhs, rank) - h00 * far0) / h10
    near = near_field(window, tiles_ref, list_ref, sums)
    image = image_of(basis1, far, self_ref, far_rows_ref, near)
    columns = [jnp.sum(a * image, axis=1, keepdims=True) for a in (basis0, basis1, image)]
    row = stats_row(columns, rank)
    sent_ref[:, 0, :] = jnp.broadcast_to(row, (sent_ref.shape[0], LANES))
    basis_ref[...] = jnp.concatenate([basis0, basis1], axis=0)
    coeff_ref[...] = jnp.concatenate([jnp.broadcast_to(v, (nrhs, LANES)) for v in (beta, h00, h10)], axis=0)


def relay_kernel(got_ref, sent_ref):
    row = total(got_ref[:, 0, :])
    sent_ref[:, 0, :] = jnp.broadcast_to(row, (sent_ref.shape[0], LANES))


def finish_kernel(rank, got_ref, basis_ref, coeff_ref, out_ref):
    nrhs = out_ref.shape[0]
    row = total(got_ref[:, 0, :])
    h01, h11, gram11 = (stat_column(row, k, nrhs, rank) for k in range(3))
    beta, h00, h10 = (coeff_ref[k * nrhs : (k + 1) * nrhs, :1] for k in range(3))
    gram00 = h00 * h00 + h10 * h10
    gram01 = h00 * h01 + h10 * h11
    lower00 = jnp.sqrt(gram00)
    lower10 = gram01 / lower00
    lower11 = jnp.sqrt(gram11 - lower10 * lower10)
    middle0 = beta * h00 / lower00
    middle1 = (beta * h01 - lower10 * middle0) / lower11
    y1 = middle1 / lower11
    y0 = (middle0 - lower10 * y1) / lower00
    out_ref[...] = y0 * basis_ref[:nrhs, :] + y1 * basis_ref[nrhs:, :]


def call(kernel, args, outs, scratch=(), smem=(), held=()):
    space = {i: pltpu.SMEM for i in smem} | {i: pl.ANY for i in held}
    args = [pltpu.with_memory_space_constraint(a, pltpu.HBM) if i in held else a for i, a in enumerate(args)]
    return pl.pallas_call(
        kernel,
        out_shape=[
            in_vmem_like(out) if hasattr(out, "dtype") else jax.ShapeDtypeStruct(out, F32) for out in outs
        ],
        in_specs=[pl.BlockSpec(memory_space=space.get(i, pltpu.VMEM)) for i in range(len(args))],
        out_specs=[pl.BlockSpec(memory_space=pltpu.VMEM)] * len(outs),
        scratch_shapes=list(scratch),
        compiler_params=pltpu.CompilerParams(vmem_limit_bytes=24 * 2**20),
    )(*args)


def in_vmem_like(array):
    return pltpu.VMEM(array.shape, array.dtype)


def in_vmem(arrays):
    return [pltpu.with_memory_space_constraint(a, pltpu.VMEM) for a in arrays]


def body(loads, self_term, near_tiles, near_list, far_rows, far_cols, coupling, ranks):
    nrhs, panels = loads.shape
    rank = far_cols.shape[0]
    tile = near_tiles.shape[1]
    rows = panels // tile
    layers, lows, cores = (lax.axis_size(axis) for axis in GROUP)
    strips = layers * lows
    groups = strips * cores
    couple = coupling.reshape(groups * rank, rank)
    near_list = near_list.T
    ranks = ranks.reshape(1, groups)
    self_term = self_term.reshape(1, panels)
    scratch = [pltpu.VMEM((3 * cores * rows, 2 * nrhs, tile), F32)]
    scratch += [pltpu.VMEM((rows, 2 * nrhs, tile), F32)] * 4

    constants = (far_cols, couple, near_tiles, far_rows, self_term)
    sent, field, *constants = call(
        start_kernel,
        (loads, ranks) + constants,
        [(groups, 1, 2 * LANES), loads.shape] + list(constants),
        [pltpu.SemaphoreType.DMA((5,))],
        smem=(1,),
        held=range(2, 7),
    )
    far_cols, couple, near_tiles, far_rows, self_term = constants = in_vmem(constants)
    even = [(i, i ^ 1) for i in range(strips)]
    odd = [(i, j) for i in range(1, strips - 1, 2) for i, j in ((i, i + 1), (i + 1, i))]
    even, odd = (lax.ppermute(field, ("hi", "lo"), pairs) for pairs in (even, odd))
    got = lax.all_to_all(sent, ("hi", "lo"), 0, 0, tiled=True)
    pair, even, odd = (lax.all_gather(a, "clus", axis=1, tiled=True) for a in (field, even, odd))
    got = lax.all_gather(got, "clus", axis=0)
    sent, window0, state = call(
        step0_kernel,
        (loads, pair, even, odd, got, *constants, near_list, ranks),
        [(groups, nrhs, panels + LANES), (3, nrhs, cores * panels), (2 * nrhs, LANES)],
        scratch,
        smem=(10, 11),
    )
    got = lax.all_to_all(sent, GROUP, 0, 0, tiled=True)
    sent, basis, coeff = call(
        step1_kernel,
        (loads, window0, got, state, near_tiles, far_rows, self_term, near_list),
        [(layers, 1, LANES), (2 * nrhs, panels), (3 * nrhs, LANES)],
        scratch,
        smem=(7,),
    )
    got = lax.all_to_all(sent, "hi", 0, 0, tiled=True)
    (sent,) = call(relay_kernel, (got,), [(lows * cores, 1, LANES)])
    got = lax.all_to_all(sent, ("lo", "clus"), 0, 0, tiled=True)
    return call(functools.partial(finish_kernel, rank), (got, basis, coeff), [loads.shape])[0]


def solution(mesh):
    cases, strips, cores = (mesh.shape[axis] for axis in ("case", "strip", "clus"))
    fine = Mesh(mesh.devices.reshape(cases, strips // 2, 2, cores), ("case",) + GROUP)
    every = ("case",) + GROUP
    in_specs = (
        P(None, every),
        P(every),
        P(every, None, None),
        P(every, None),
        P(None, every),
        P(None, every),
        P(None, GROUP, None, None),
        P(None, GROUP),
    )
    return jax.shard_map(body, mesh=fine, in_specs=in_specs, out_specs=P(None, every), check_vma=False)
```

time: 60.9 us -> 57.8 us (0.949)
  local copies, waits for them, and re-layouts: 7.24 us -> 1.41 us
  blocking collectives: 34.4 us -> 36.3 us
  Pallas kernels: 6.15 us -> 7.92 us
  starting transfers between devices: 12.5 us -> 11.7 us
    ppermute x4 -> x2, starting transfers between devices: 12.5 us -> 2.68 us  [body(): lax.ppermute(field, ('hi', 'lo'), pairs)]
    all_to_all x0 -> x1, starting transfers between devices: none -> 9.05 us  [body(): got = lax.all_to_all(sent, ('hi', 'lo'), 0, 0, tiled=True)]
    unnamed x20 -> x10, local copies, waits for them, and re-layouts: 7.24 us -> 1.41 us
    all_gather x2 -> x4, blocking collectives: 3.78 us -> 7.28 us  [the longest x3 5.46 us: body(): lax.all_gather(a, 'clus', axis=1, tiled=True)]
    pallas_call x4 -> x5, Pallas kernels: 6.15 us -> 7.92 us  [call(): pl.pallas_call(kernel, out_shape=[in_vmem_like(out) if hasattr(out, 'dtyp...]
    all_to_all x3, blocking collectives: 30.7 us -> 29 us  [the longest x1 15 us: body(): got = lax.all_to_all(sent, GROUP, 0, 0, tiled=True)]
  transfers between devices with their start and end apart: 4 -> 3, of which waited for: 0 -> 0; matrix products, arithmetic and copies ran while one was open for 0% -> 0% of each run, Pallas kernels for 0% -> 0%
where the time goes in v4:
time: 57.8 us; the launch traced here: 57.4 us
  blocking collectives  36.3 us (63%)
  starting transfers between devices  11.7 us (20%)
  Pallas kernels  7.92 us (14%)
  local copies, waits for them, and re-layouts  1.41 us (2%)
    all_to_all x1, blocking collectives, body(): got = lax.all_to_all(sent, GROUP, 0, 0, tiled=True)  15 us
    all_to_all x1, starting transfers between devices, body(): got = lax.all_to_all(sent, ('hi', 'lo'), 0, 0, tiled=True)  9.05 us
    pallas_call x5, Pallas kernels, call(): pl.pallas_call(kernel, out_shape=[in_vmem_like(out) if hasattr(out, 'dtyp...  7.92 us
    all_to_all x1, blocking collectives, body(): got = lax.all_to_all(sent, 'hi', 0, 0, tiled=True)  7.88 us
    all_to_all x1, blocking collectives, body(): got = lax.all_to_all(sent, ('lo', 'clus'), 0, 0, tiled=True)  6.09 us
    all_gather x3, blocking collectives, body(): lax.all_gather(a, 'clus', axis=1, tiled=True)  5.46 us
    ppermute x2, starting transfers between devices, body(): lax.ppermute(field, ('hi', 'lo'), pairs)  2.68 us
    all_gather x1, blocking collectives, body(): got = lax.all_gather(got, 'clus', axis=0)  1.82 us
  transfers between devices with their start and end apart: 3, of which 0 were waited for; matrix products, arithmetic and copies ran while one was open for 0% of the time, Pallas kernels for 0%

profile of v4, /device:TPU:0, one launch (start us, length us, event | category | flops | bytes accessed | tf_op | source)
XLA Modules:
  0.0 57.4 jit_solution(16925989407703763011)
XLA Ops:
  0.0 0.0 copy-start.4
  0.0 0.0 copy-start.2
  0.0 0.7 %copy-done = f32[4,1024]{1,0:T(4,128)S(1)} copy-done((f32[4,1024]{1,0:T(4,128)S(1)}, f32[4,1024]{1,0:T(4,128)}, u32[]{:S(2)}) %copy-start) | copy-done | bytes 16408
  0.8 0.7 %copy-done.3 = s32[16,1]{0,1:T(1,128)S(1)} copy-done((s32[16,1]{0,1:T(1,128)S(1)}, s32[16,1]{0,1:T(1,128)}, u32[]{:S(2)}) %copy-start.3) | copy-done | bytes 88
  1.4 3.1 %shard_map.82 = (f32[16,1,256]{2,1,0:T(1,128)}, f32[4,1024]{1,0:T(4,128)S(1)}, f32[32,1024]{1,0:T(8,128)S(1)}, f32[512,32]{1,0:T(8,128)S(1)}, bf16[80,128,128]{2...) custom-call(f32[4,1024]{1,0:T(4,128)S(1)} %copy-done, s32[1,16]{1,0:T(1,128)S(1)} %bitcast.8, ...), custom_call_target="tpu_custom_call" | custom-call | tf_op jit(solution)/shard_map/pallas_call | solution.py:221
  4.5 0.7 %collective-permute-start.1 = (f32[4,1024]{1,0:T(4,128)S(1)}, f32[4,1024]{1,0:T(4,128)S(1)}, u32[]{:S(2)}, u32[]{:S(2)}) collective-permute-start(f32[4,1024]{1,0:T(4,128)S(1)} %get-tuple-element.18), channel_id=1, source_target_pairs={{2,4},{4,2},{6,8},{8,6},{10,12},{12,10},{3,5},{5,3},{7,9},{9,7},{1... | collective-permute-start | bytes 49160 | tf_op jit(solution)/shard_map/ppermute | solution.py:268
  5.2 9.0 %all-to-all-start = ((f32[16,1,256]{2,1,0:T(1,128)}), f32[16,1,256]{2,1,0:T(1,128)S(1)}, u32[]{:S(2)}, u32[]{:S(2)}) async-start(f32[16,1,256]{2,1,0:T(1,128)} %get-tuple-element.19), calls=%async_computation | async-start | bytes 32768 | tf_op jit(solution)/shard_map/all_to_all | solution.py:269
  14.2 2.0 %collective-permute-start = (f32[4,1024]{1,0:T(4,128)S(1)}, f32[4,1024]{1,0:T(4,128)S(1)}, u32[]{:S(2)}, u32[]{:S(2)}) collective-permute-start(f32[4,1024]{1,0:T(4,128)S(1)} %get-tuple-element.18), channel_id=1, source_target_pairs={{0,2},{2,0},{4,6},{6,4},{8,10},{10,8},{12,14},{14,12},{1,3},{3,1},... | collective-permute-start | bytes 49160 | tf_op jit(solution)/shard_map/ppermute | solution.py:268
  16.2 1.8 %all_gather.15.pair_ref = f32[4,2048]{1,0:T(4,128)S(1)} all-gather(f32[4,1024]{1,0:T(4,128)S(1)} %get-tuple-element.18), channel_id=1, replica_groups=mesh['case'=2,'hi'=4,'lo'=2,'clus'=2] {'clus'}, dimensions={1}, use_global_device_ids=true | all-gather | bytes 49152 | tf_op jit(solution)/shard_map/all_gather | solution.py:270
  18.1 0.0 collective-permute-done.1
  18.1 1.8 %all_gather.17.odd_ref = f32[4,2048]{1,0:T(4,128)S(1)} all-gather(f32[4,1024]{1,0:T(4,128)S(1)} %collective-permute-done.1), channel_id=1, replica_groups=mesh['case'=2,'hi'=4,'lo'=2,'clus'=2] {'clus'}, dimensions={1}, use_global_device_ids=true | all-gather | bytes 49152 | tf_op jit(solution)/shard_map/all_gather | solution.py:270
  19.9 0.0 collective-permute-done
  19.9 1.8 %all_gather.16.even_ref = f32[4,2048]{1,0:T(4,128)S(1)} all-gather(f32[4,1024]{1,0:T(4,128)S(1)} %collective-permute-done), channel_id=1, replica_groups=mesh['case'=2,'hi'=4,'lo'=2,'clus'=2] {'clus'}, dimensions={1}, use_global_device_ids=true | all-gather | bytes 49152 | tf_op jit(solution)/shard_map/all_gather | solution.py:270
  21.7 0.0 all-to-all-done
  21.7 1.8 %all-gather = f32[32,1,256]{2,1,0:T(1,128)S(1)} all-gather(f32[16,1,256]{2,1,0:T(1,128)S(1)} %all-to-all-done), channel_id=2, replica_groups=mesh['case'=2,'hi'=4,'lo'=2,'clus'=2] {'clus'}, dimensions={0}, use_global_device_ids=true | all-gather | bytes 49152 | tf_op jit(solution)/shard_map/all_gather | solution.py:271
  23.5 0.0 copy-done.4
  23.5 0.0 copy-done.2
  23.5 0.0 copy-done.1
  23.5 2.3 %shard_map.83 = (f32[16,4,1152]{2,1,0:T(4,128)S(1)}, f32[3,4,2048]{2,1,0:T(4,128)S(1)}, f32[8,128]{1,0:T(8,128)S(1)}) custom-call(f32[4,1024]{1,0:T(4,128)S(1)} %copy-done.1, f32[4,2048]{1,0:T(4,128)S(1)} %all_gather.15.pair_ref, f32[4,2048]{1,0:T(4,128)S(1)} %all_gather.16.even_ref, f32[4,2048]{1,0:T(4,128)S(1)} %all_gather.17.odd_ref, ...), custom_call_target="tpu_custom_call" | custom-call | tf_op jit(solution)/shard_map/pallas_call | solution.py:221
  25.9 15.0 %all_to_all.20.got_ref = f32[16,4,1152]{2,1,0:T(4,128)S(1)} all-to-all(f32[16,4,1152]{2,1,0:T(4,128)S(1)} %get-tuple-element.26), channel_id=1, replica_groups=mesh['case'=2,'hi'=4,'lo'=2,'clus'=2] {'hi','lo','clus'}, dimensions={0} | all-to-all | bytes 589824 | tf_op jit(solution)/shard_map/all_to_all | solution.py:279
  40.9 1.7 %shard_map.84 = (f32[4,1,128]{2,1,0:T(1,128)S(1)}, f32[8,1024]{1,0:T(8,128)S(1)}, f32[12,128]{1,0:T(8,128)S(1)}) custom-call(f32[4,1024]{1,0:T(4,128)S(1)} %copy-done.1, f32[3,4,2048]{2,1,0:T(4,128)S(1)} %get-tuple-element.25.window0_ref, f32[16,4,1152]{2,1,0:T(4,128)S(1)} %all_to_all.20.got_ref, f32[8,128]{1,0:T(8,128)S(1)} %get-tuple-element.27.state_ref, ...), custom_call_target="tpu_custom_call" | custom-call | tf_op jit(solution)/shard_map/pallas_call | solution.py:221
  42.6 7.9 %all_to_all.21.got_ref = f32[4,1,128]{2,1,0:T(1,128)S(1)} all-to-all(f32[4,1,128]{2,1,0:T(1,128)S(1)} %get-tuple-element.28), channel_id=1, replica_groups=mesh['case'=2,'hi'=4,'lo'=2,'clus'=2] {'hi'}, dimensions={0} | all-to-all | bytes 4096 | tf_op jit(solution)/shard_map/all_to_all | solution.py:287
  50.5 6.1 %all_to_all.22.got_ref = f32[4,1,128]{2,1,0:T(1,128)S(1)} all-to-all(f32[4,1,128]{2,1,0:T(1,128)S(1)} %shard_map.85), channel_id=1, replica_groups=mesh['case'=2,'hi'=4,'lo'=2,'clus'=2] {'lo','clus'}, dimensions={0} | all-to-all | bytes 4096 | tf_op jit(solution)/shard_map/all_to_all | solution.py:289
  56.6 0.8 %shard_map.86 = f32[4,1024]{1,0:T(4,128)} custom-call(f32[4,1,128]{2,1,0:T(1,128)S(1)} %all_to_all.22.got_ref, f32[8,1024]{1,0:T(8,128)S(1)} %get-tuple-element.29.basis_ref, f32[12,128]{1,0:T(8,128)S(1)} %get-tuple-element.30.coeff_ref), custom_call_target="tpu_custom_call" | custom-call | tf_op jit(solution)/shard_map/pallas_call | solution.py:221
  (4 shorter events, 0.0 us)
Async XLA Ops:
  0.0 23.5 %copy-start.4 = (s32[16,1]{0,1:T(1,128)S(1)}, s32[16,1]{0,1:T(1,128)}, u32[]{:S(2)}) copy-start(s32[16,1]{0,1:T(1,128)} %param.15) | copy-start | bytes 196
  0.0 23.5 %copy-start.2 = (s32[80,2]{0,1:T(2,128)S(1)}, s32[80,2]{0,1:T(2,128)}, u32[]{:S(2)}) copy-start(s32[80,2]{0,1:T(2,128)} %param.11) | copy-start | bytes 1924
  0.0 0.7 %copy-start = (f32[4,1024]{1,0:T(4,128)S(1)}, f32[4,1024]{1,0:T(4,128)}, u32[]{:S(2)}) copy-start(f32[4,1024]{1,0:T(4,128)} %loads_ref.5) | copy-start | bytes 49156
  0.8 0.7 %copy-start.3 = (s32[16,1]{0,1:T(1,128)S(1)}, s32[16,1]{0,1:T(1,128)}, u32[]{:S(2)}) copy-start(s32[16,1]{0,1:T(1,128)} %param.15) | copy-start | bytes 196
  1.4 22.1 %copy-start.1 = (f32[4,1024]{1,0:T(4,128)S(1)}, f32[4,1024]{1,0:T(4,128)}, u32[]{:S(2)}) copy-start(f32[4,1024]{1,0:T(4,128)} %loads_ref.5) | copy-start | bytes 49156
  4.5 13.6 %collective-permute-start.1 = (f32[4,1024]{1,0:T(4,128)S(1)}, f32[4,1024]{1,0:T(4,128)S(1)}, u32[]{:S(2)}, u32[]{:S(2)}) collective-permute-start(f32[4,1024]{1,0:T(4,128)S(1)} %get-tuple-element.18), channel_id=1, source_target_pairs={{2,4},{4,2},{6,8},{8,6},{10,12},{12,10},{3,5},{5,3},{7,9},{9,7},{1... | collective-permute-start | bytes 49160 | tf_op jit(solution)/shard_map/ppermute | solution.py:268
  5.2 16.5 %all-to-all-start = ((f32[16,1,256]{2,1,0:T(1,128)}), f32[16,1,256]{2,1,0:T(1,128)S(1)}, u32[]{:S(2)}, u32[]{:S(2)}) async-start(f32[16,1,256]{2,1,0:T(1,128)} %get-tuple-element.19), calls=%async_computation | async-start | bytes 32768 | tf_op jit(solution)/shard_map/all_to_all | solution.py:269
  14.2 5.7 %collective-permute-start = (f32[4,1024]{1,0:T(4,128)S(1)}, f32[4,1024]{1,0:T(4,128)S(1)}, u32[]{:S(2)}, u32[]{:S(2)}) collective-permute-start(f32[4,1024]{1,0:T(4,128)S(1)} %get-tuple-element.18), channel_id=1, source_target_pairs={{0,2},{2,0},{4,6},{6,4},{8,10},{10,8},{12,14},{14,12},{1,3},{3,1},... | collective-permute-start | bytes 49160 | tf_op jit(solution)/shard_map/ppermute | solution.py:268

commit v5 on v4

v5 whole, which is shorter than its diff:
```python
import functools

import jax
import jax.numpy as jnp
from jax import lax
from jax.experimental import pallas as pl
from jax.experimental.pallas import tpu as pltpu
from jax.sharding import Mesh
from jax.sharding import PartitionSpec as P

HIGH = lax.Precision.HIGHEST
STRIP = ("high", "mid", "low")
GROUP = STRIP + ("clus",)
LANES = 128
CHUNK = 16
PIECES = 8
F32 = jnp.float32


def fold_of(strips, field):
    return max(LANES, field.size // strips)


def lanes_of(shape):
    return lax.broadcasted_iota(jnp.int32, shape, 1)


def rows_of(shape):
    return lax.broadcasted_iota(jnp.int32, shape, 0)


def stats_row(columns, rank):
    shape = (columns[0].shape[0], LANES)
    first = lanes_of(shape) - rank * rows_of(shape)
    spread = sum(jnp.where(first == k, column, 0.0) for k, column in enumerate(columns))
    return jnp.sum(spread, axis=0, keepdims=True)


def stat_column(row, k, nrhs, rank):
    shape = (nrhs, LANES)
    first = lanes_of(shape) - rank * rows_of(shape)
    return jnp.sum(jnp.where(first == k, row, 0.0), axis=1, keepdims=True)


def shifted(value, k):
    return pltpu.roll(value, LANES - k, 1)


def far_sum_of(row, nrhs, rank):
    shape = (nrhs, LANES)
    first = lanes_of(shape) - rank * rows_of(shape)
    own = jnp.where((first >= 0) & (first < rank), row, 0.0)
    return sum((pltpu.roll(own, k * rank, 1) for k in range(1, LANES // rank)), own)


def total(rows):
    return jnp.sum(rows, axis=0, keepdims=True)


def put_message(field, columns, far_cols, couple_ref, ranks_ref, sent_ref):
    nrhs, rank = field.shape[0], far_cols.shape[0]
    strips, fold = sent_ref.shape[0], fold_of(sent_ref.shape[0], field)
    for part in range(field.shape[1] // fold):
        sent_ref[pl.ds(part * nrhs, nrhs), 0, :fold] = field[:, part * fold : (part + 1) * fold]
    proj = lax.dot_general(
        field, far_cols, (((1,), (1,)), ((), ())), precision=HIGH, preferred_element_type=F32
    )
    wide = jnp.concatenate([proj] * CHUNK, axis=1)
    shape = (CHUNK, CHUNK * rank)
    owner = lax.div(lanes_of(shape), rank)
    inner = lax.rem(lanes_of(shape), rank)
    row = stats_row(columns, rank)
    half = CHUNK // 2
    number = rows_of(shape)
    number = jnp.where(number < half, 2 * number, 2 * (number - half) + 1)
    for start in range(0, strips, half):
        limit = jnp.zeros(shape, jnp.int32)
        for i in range(CHUNK):
            limit = jnp.where(owner == i, ranks_ref[0, 2 * start + i], limit)
        keep = (owner == number) & (inner < limit)
        spread = jnp.concatenate([jnp.where(keep, wide[r : r + 1], 0.0) for r in range(nrhs)], axis=0)
        couple = couple_ref[pl.ds(2 * start * rank, CHUNK * rank), :]
        terms = jnp.dot(spread, couple, precision=HIGH, preferred_element_type=F32)
        terms = jnp.concatenate([terms[r * CHUNK : (r + 1) * CHUNK] for r in range(nrhs)], axis=1)
        here = pl.ds(start, half)
        sent_ref[here, 0, fold : fold + LANES] = terms[:half]
        sent_ref[here, 0, fold + LANES : fold + 2 * LANES] = terms[half:]
        sent_ref[here, 0, fold + 2 * LANES :] = jnp.broadcast_to(row, (half, LANES))


def message_parts(got_ref, core, fold):
    whole = got_ref.shape[2] // 2
    near = [k * whole + fold for k in (0, 1)]
    terms = [
        jnp.where(core == 0, got_ref[:, 0, k : k + LANES], got_ref[:, 0, k + LANES : k + 2 * LANES]) for k in near
    ]
    stats = [got_ref[:, 0, k + 2 * LANES : k + 3 * LANES] for k in near]
    return jnp.concatenate(terms, axis=0), jnp.concatenate(stats, axis=0)


def field_of(pair_ref, core, nrhs, panels, fold):
    base = core * (pair_ref.shape[2] // 2)
    return jnp.concatenate(
        [pair_ref[pl.ds(part * nrhs, nrhs), 0, base : base + fold] for part in range(panels // fold)], axis=1
    )


def put_blocks(part, first, window):
    part = part.astype(jnp.bfloat16).astype(F32)
    part = jnp.concatenate([part, jnp.zeros_like(part)], axis=0)
    for c in range(part.shape[1] // LANES):
        window[first + c] = part[:, c * LANES : (c + 1) * LANES]


def near_field(window, tiles_ref, list_ref, sums, copies=()):
    every = tiles_ref.shape[0] // max(len(copies), 1)
    for held in sums:
        held[...] = jnp.zeros_like(held)
    for n in range(tiles_ref.shape[0]):
        if copies and n % every == 0:
            copies[n // every].wait()
        held = sums[n % len(sums)]
        source = window[list_ref[1, n]].astype(jnp.bfloat16)
        product = jnp.dot(source, tiles_ref[n], preferred_element_type=F32)
        held[list_ref[0, n]] += product
    whole = sum((held[...] for held in sums[1:]), sums[0][...])
    return jnp.concatenate([whole[b] for b in range(whole.shape[0])], axis=1)


def start_kernel(*refs):
    count = 5
    ranks_hbm, sources = refs[0], refs[1 : 1 + count]
    sent_ref, held = refs[1 + count], refs[2 + count : 2 + 2 * count]
    ranks_ref, sems = refs[2 + 2 * count :]
    pairs = [(ranks_hbm, ranks_ref)] + list(zip(sources, held))
    copies = [pltpu.make_async_copy(a, b, sems.at[i]) for i, (a, b) in enumerate(pairs)]
    for copy in copies:
        copy.start()
    for copy in copies:
        copy.wait()
    loads_ref, far_cols_ref, couple_ref = held[:3]
    loads = loads_ref[...]
    square = jnp.sum(loads * loads, axis=1, keepdims=True)
    put_message(loads, [square], far_cols_ref[...], couple_ref, ranks_ref, sent_ref)


def image_of(field, far, self_ref, far_rows_ref, near):
    rank = far_rows_ref.shape[0]
    far = jnp.dot(far[:, :rank], far_rows_ref[...], precision=HIGH, preferred_element_type=F32)
    return self_ref[...] * field + near[: field.shape[0]] + far


def places():
    low = lax.axis_index("low")
    return 1, 2 * (1 - low), 2 * low


def step0_kernel(
    loads_ref, pair_ref, even_ref, odd_ref, got_ref, far_cols_ref, couple_ref, far_rows_ref, self_ref, tiles_hbm,
    list_ref, ranks_ref, sent_ref, state_ref, tiles_ref, sems, window, *sums,
):
    (nrhs, panels), rank = loads_ref.shape, far_rows_ref.shape[0]
    every = tiles_ref.shape[0] // PIECES
    pieces = [pl.ds(i * every, every) for i in range(PIECES)]
    copies = [pltpu.make_async_copy(tiles_hbm.at[p], tiles_ref.at[p], sems.at[i]) for i, p in enumerate(pieces)]
    for copy in copies:
        copy.start()
    span = panels // LANES
    fold = fold_of(sent_ref.shape[0], loads_ref)
    terms, stats = message_parts(got_ref, lax.axis_index("clus"), fold)
    beta = jnp.sqrt(stat_column(total(stats), 0, nrhs, rank))
    basis = loads_ref[...] / beta
    for part_ref, place in zip((pair_ref, even_ref, odd_ref), places()):
        for core in range(2):
            put_blocks(field_of(part_ref, core, nrhs, panels, fold) / beta, (2 * place + core) * span, window)
    far = far_sum_of(total(terms), nrhs, rank) / beta
    near = near_field(window, tiles_ref, list_ref, sums, copies)
    image = image_of(basis, far, self_ref, far_rows_ref, near)
    state_ref[...] = jnp.concatenate([far, jnp.broadcast_to(beta, far.shape)], axis=0)
    norm = jnp.sum(basis * basis, axis=1, keepdims=True)
    dot = jnp.sum(basis * image, axis=1, keepdims=True)
    share = jnp.where(norm > 0, dot / jnp.where(norm > 0, norm, 1.0), 0.0)
    rest = image - share * basis
    rest = jnp.sum(rest * rest, axis=1, keepdims=True)
    put_message(image, [norm, dot, share, rest], far_cols_ref[...], couple_ref, ranks_ref, sent_ref)


def step1_kernel(
    loads_ref, pair_ref, even_ref, odd_ref, sent_image_ref, image_pair_ref, image_even_ref, image_odd_ref, got_ref,
    state_ref, far_rows_ref, self_ref, tiles_ref, list_ref, sent_ref, basis_ref, coeff_ref, window, *sums,
):
    (nrhs, panels), rank = loads_ref.shape, far_rows_ref.shape[0]
    span = panels // LANES
    fold = fold_of(got_ref.shape[0], loads_ref)
    beta = state_ref[nrhs:, :1]
    far0 = state_ref[:nrhs, :]
    terms, stats = message_parts(got_ref, lax.axis_index("clus"), fold)
    summed = total(stats)
    h00 = stat_column(summed, 1, nrhs, rank)
    away = shifted(stats, 2) - shifted(summed, 1)
    rest = total(shifted(stats, 3) + stats * away * away)
    h10 = jnp.sqrt(stat_column(rest, 0, nrhs, rank))
    basis0 = loads_ref[...] / beta
    basis1 = (field_of(sent_image_ref, 0, nrhs, panels, fold) - h00 * basis0) / h10
    refs = zip((pair_ref, even_ref, odd_ref), (image_pair_ref, image_even_ref, image_odd_ref), places())
    for part_ref, image_ref, place in refs:
        for core in range(2):
            part = field_of(part_ref, core, nrhs, panels, fold) / beta
            part = (field_of(image_ref, core, nrhs, panels, fold) - h00 * part) / h10
            put_blocks(part, (2 * place + core) * span, window)
    far = (far_sum_of(total(terms), nrhs, rank) - h00 * far0) / h10
    near = near_field(window, tiles_ref, list_ref, sums)
    image = image_of(basis1, far, self_ref, far_rows_ref, near)
    columns = [jnp.sum(a * image, axis=1, keepdims=True) for a in (basis0, basis1, image)]
    sent_ref[0] = stats_row(columns, rank)
    basis_ref[...] = jnp.concatenate([basis0, basis1], axis=0)
    coeff_ref[...] = jnp.concatenate([jnp.broadcast_to(v, (nrhs, LANES)) for v in (beta, h00, h10)], axis=0)


def finish_kernel(rank, got_ref, basis_ref, coeff_ref, out_ref):
    nrhs = out_ref.shape[0]
    row = total(got_ref[:, 0, :])
    h01, h11, gram11 = (stat_column(row, k, nrhs, rank) for k in range(3))
    beta, h00, h10 = (coeff_ref[k * nrhs : (k + 1) * nrhs, :1] for k in range(3))
    gram00 = h00 * h00 + h10 * h10
    gram01 = h00 * h01 + h10 * h11
    lower00 = jnp.sqrt(gram00)
    lower10 = gram01 / lower00
    lower11 = jnp.sqrt(gram11 - lower10 * lower10)
    middle0 = beta * h00 / lower00
    middle1 = (beta * h01 - lower10 * middle0) / lower11
    y1 = middle1 / lower11
    y0 = (middle0 - lower10 * y1) / lower00
    out_ref[...] = y0 * basis_ref[:nrhs, :] + y1 * basis_ref[nrhs:, :]


def call(kernel, args, outs, scratch=(), smem=(), held=()):
    space = {i: pltpu.SMEM for i in smem} | {i: pl.ANY for i in held}
    args = [pltpu.with_memory_space_constraint(a, pltpu.HBM) if i in held else a for i, a in enumerate(args)]
    return pl.pallas_call(
        kernel,
        out_shape=[
            in_vmem_like(out) if hasattr(out, "dtype") else jax.ShapeDtypeStruct(out, F32) for out in outs
        ],
        in_specs=[pl.BlockSpec(memory_space=space.get(i, pltpu.VMEM)) for i in range(len(args))],
        out_specs=[pl.BlockSpec(memory_space=pltpu.VMEM)] * len(outs),
        scratch_shapes=list(scratch),
        compiler_params=pltpu.CompilerParams(vmem_limit_bytes=24 * 2**20),
    )(*args)


def in_vmem_like(array):
    return pltpu.VMEM(array.shape, array.dtype)


def in_vmem(arrays):
    return [pltpu.with_memory_space_constraint(a, pltpu.VMEM) for a in arrays]


def exchanged(sent):
    strips = sent.shape[0]
    even = [(i, i ^ 1) for i in range(strips)]
    odd = [(i, j) for i in range(1, strips - 1, 2) for i, j in ((i, i + 1), (i + 1, i))]
    pair = lax.all_gather(sent, "clus", axis=2, tiled=True)
    even, odd = (lax.ppermute(pair, STRIP, pairs) for pairs in (even, odd))
    return pair, even, odd, lax.all_to_all(pair, STRIP, 0, 0, tiled=True)


def body(loads, self_term, near_tiles, near_list, far_rows, far_cols, coupling, ranks):
    nrhs, panels = loads.shape
    rank = far_cols.shape[0]
    tile = near_tiles.shape[1]
    rows = panels // tile
    strips = coupling.shape[0] // 2
    couple = coupling.reshape(2 * strips * rank, rank)
    near_list = near_list.T
    ranks = ranks.reshape(1, 2 * strips)
    self_term = self_term.reshape(1, panels)
    scratch = [pltpu.VMEM((6 * rows, 2 * nrhs, tile), F32)]
    scratch += [pltpu.VMEM((rows, 2 * nrhs, tile), F32)] * 4
    message = (strips, 1, fold_of(strips, loads) + 3 * LANES)

    held = (loads, far_cols, couple, far_rows, self_term)
    sent, *held = call(
        start_kernel,
        (ranks,) + held,
        [message] + list(held),
        [pltpu.SMEM(ranks.shape, jnp.int32), pltpu.SemaphoreType.DMA((6,))],
        held=range(6),
    )
    loads, far_cols, couple, far_rows, self_term = in_vmem(held)
    first = exchanged(sent)
    sent, state, near_tiles = call(
        step0_kernel,
        (loads, *first, far_cols, couple, far_rows, self_term, near_tiles, near_list, ranks),
        [message, (2 * nrhs, LANES), near_tiles],
        [pltpu.SemaphoreType.DMA((PIECES,))] + scratch,
        smem=(10, 11),
        held=(9,),
    )
    (near_tiles,) = in_vmem([near_tiles])
    second = exchanged(sent)
    sent, basis, coeff = call(
        step1_kernel,
        (loads, *first[:3], sent, *second, state, far_rows, self_term, near_tiles, near_list),
        [(1, 1, LANES), (2 * nrhs, panels), (3 * nrhs, LANES)],
        scratch,
        smem=(13,),
    )
    for axis in reversed(GROUP):
        sent = lax.all_gather(sent, axis, axis=0, tiled=True)
    return call(functools.partial(finish_kernel, rank), (sent, basis, coeff), [loads.shape])[0]


def solution(mesh):
    cases, strips, cores = (mesh.shape[axis] for axis in ("case", "strip", "clus"))
    fine = Mesh(mesh.devices.reshape(cases, strips // 4, 2, 2, cores), ("case",) + GROUP)
    every = ("case",) + GROUP
    in_specs = (
        P(None, every),
        P(every),
        P(every, None, None),
        P(every, None),
        P(None, every),
        P(None, every),
        P(None, GROUP, None, None),
        P(None, GROUP),
    )
    return jax.shard_map(body, mesh=fine, in_specs=in_specs, out_specs=P(None, every), check_vma=False)
```

time: 57.8 us -> 58.5 us (1.012)
  blocking collectives: 36.3 us -> 19.6 us
  starting transfers between devices: 11.7 us -> 23.1 us
  waiting for transfers between devices: 0.01 us -> 4.74 us
  Pallas kernels: 7.92 us -> 9.07 us
    all_to_all x3 -> x0, blocking collectives: 29 us -> none  [the longest x1 15 us: body(): got = lax.all_to_all(sent, GROUP, 0, 0, tiled=True)]
    all_gather x4 -> x6, blocking collectives: 7.28 us -> 19.6 us  [the longest x4 15.6 us: body(): sent = lax.all_gather(sent, axis, axis=0, tiled=True)]
    ppermute x2 -> x4, starting transfers between devices: 2.68 us -> 10.9 us  [exchanged(): even, odd = (lax.ppermute(pair, STRIP, pairs) for pairs in (even, odd))]
    ppermute x2 -> x4, waiting for transfers between devices: 0.01 us -> 4.73 us  [exchanged(): even, odd = (lax.ppermute(pair, STRIP, pairs) for pairs in (even, odd))]
    all_to_all x1 -> x2, starting transfers between devices: 9.05 us -> 12.2 us  [exchanged(): return (pair, even, odd, lax.all_to_all(pair, STRIP, 0, 0, tiled=True))]
    pallas_call x5 -> x4, Pallas kernels: 7.92 us -> 9.07 us  [call(): pl.pallas_call(kernel, out_shape=[in_vmem_like(out) if hasattr(out, 'dtyp...]
    unnamed x10 -> x6, local copies, waits for them, and re-layouts: 1.41 us -> 1.34 us
  transfers between devices with their start and end apart: 3 -> 6, of which waited for: 0 -> 2; matrix products, arithmetic and copies ran while one was open for 0% -> 0% of each run, Pallas kernels for 0% -> 0%
where the time goes in v5:
time: 58.5 us; the launch traced here: 58 us
  starting transfers between devices  23.1 us (39%)
  blocking collectives  19.6 us (34%)
  Pallas kernels  9.07 us (16%)
  waiting for transfers between devices  4.74 us (8%)
  local copies, waits for them, and re-layouts  1.34 us (2%)
    all_gather x4, blocking collectives, body(): sent = lax.all_gather(sent, axis, axis=0, tiled=True)  15.6 us
    all_to_all x2, starting transfers between devices, exchanged(): return (pair, even, odd, lax.all_to_all(pair, STRIP, 0, 0, tiled=True))  12.2 us
    ppermute x4, starting transfers between devices, exchanged(): even, odd = (lax.ppermute(pair, STRIP, pairs) for pairs in (even, odd))  10.9 us
    pallas_call x4, Pallas kernels, call(): pl.pallas_call(kernel, out_shape=[in_vmem_like(out) if hasattr(out, 'dtyp...  9.07 us
    ppermute x4, waiting for transfers between devices, exchanged(): even, odd = (lax.ppermute(pair, STRIP, pairs) for pairs in (even, odd))  4.73 us
    all_gather x2, blocking collectives, exchanged(): pair = lax.all_gather(sent, 'clus', axis=2, tiled=True)  4.07 us
    unnamed x6, local copies, waits for them, and re-layouts  1.34 us
  transfers between devices with their start and end apart: 6, of which 2 were waited for; matrix products, arithmetic and copies ran while one was open for 0% of the time, Pallas kernels for 0%

profile of v5, /device:TPU:0, one launch (start us, length us, event | category | flops | bytes accessed | tf_op | source)
XLA Modules:
  0.0 58.0 jit_solution(11192584719534856889)
XLA Ops:
  0.0 1.9 %shard_map.82 = (f32[8,1,896]{2,1,0:T(1,128)S(1)}, f32[4,1024]{1,0:T(4,128)S(1)}, f32[32,1024]{1,0:T(8,128)S(1)}, f32[512,32]{1,0:T(8,128)S(1)}, f32[32,1024]{1,0:T(8,128)S(1)}, /*index=5*/f32[1,1024]{1,0:T(1,128)S(1)}) custom-call(s32[1,16]{1,0:T(1,128)} %bitcast.6, f32[4,1024]{1,0:T(4,128)} %refs_1_.1, f32[32,1024]{1,0:T(8,128)} %refs_2_.1, ...), custom_call_target="tpu_custom_call" | custom-call | tf_op jit(solution)/shard_map/pallas_call | solution.py:240
  1.9 2.1 %all_gather.18.pair_ref = f32[8,1,1792]{2,1,0:T(1,128)} all-gather(f32[8,1,896]{2,1,0:T(1,128)S(1)} %get-tuple-element.18), channel_id=1, replica_groups=mesh['case'=2,'high'=2,'mid'=2,'low'=2,'clus'=2] {'clus'}, dimensions={2}, use_global_device_ids=true | all-gather | bytes 86016 | tf_op jit(solution)/shard_map/all_gather | solution.py:264
  4.0 7.1 %all-to-all-start = ((f32[8,1,1792]{2,1,0:T(1,128)}), f32[8,1,1792]{2,1,0:T(1,128)S(1)}, u32[]{:S(2)}, u32[]{:S(2)}) async-start(f32[8,1,1792]{2,1,0:T(1,128)} %all_gather.18.pair_ref), calls=%async_computation | async-start | bytes 114688 | tf_op jit(solution)/shard_map/all_to_all | solution.py:266
  11.2 0.7 %collective-permute-start.1 = (f32[8,1,1792]{2,1,0:T(1,128)}, f32[8,1,1792]{2,1,0:T(1,128)S(1)}, u32[]{:S(2)}, u32[]{:S(2)}) collective-permute-start(f32[8,1,1792]{2,1,0:T(1,128)} %all_gather.18.pair_ref), channel_id=1, source_target_pairs={{2,4},{4,2},{6,8},{8,6},{10,12},{12,10},{3,5},{5,3},{7,9},{9,7},{1... | collective-permute-start | bytes 172040 | tf_op jit(solution)/shard_map/ppermute | solution.py:265
  11.8 4.8 %collective-permute-start = (f32[8,1,1792]{2,1,0:T(1,128)}, f32[8,1,1792]{2,1,0:T(1,128)S(1)}, u32[]{:S(2)}, u32[]{:S(2)}) collective-permute-start(f32[8,1,1792]{2,1,0:T(1,128)} %all_gather.18.pair_ref), channel_id=1, source_target_pairs={{0,2},{2,0},{4,6},{6,4},{8,10},{10,8},{12,14},{14,12},{1,3},{3,1},... | collective-permute-start | bytes 172040 | tf_op jit(solution)/shard_map/ppermute | solution.py:265
  16.6 0.0 collective-permute-done.1.odd_ref
  16.6 2.4 %collective-permute-done.even_ref = f32[8,1,1792]{2,1,0:T(1,128)S(1)} collective-permute-done((f32[8,1,1792]{2,1,0:T(1,128)}, f32[8,1,1792]{2,1,0:T(1,128)S(1)}, u32[]{:S(2)}, u32[]{:S(2)}) %collective-permute-start) | collective-permute-done | bytes 57376 | tf_op jit(solution)/shard_map/ppermute | solution.py:265
  19.0 0.0 all-to-all-done.got_ref
  19.0 0.7 %copy-done = s32[80,2]{0,1:T(2,128)S(1)} copy-done((s32[80,2]{0,1:T(2,128)S(1)}, s32[80,2]{0,1:T(2,128)}, u32[]{:S(2)}) %copy-start) | copy-done | bytes 664
  19.7 0.7 %copy-done.2 = s32[16,1]{0,1:T(1,128)S(1)} copy-done((s32[16,1]{0,1:T(1,128)S(1)}, s32[16,1]{0,1:T(1,128)}, u32[]{:S(2)}) %copy-start.2) | copy-done | bytes 88
  20.3 4.3 %shard_map.83 = (f32[8,1,896]{2,1,0:T(1,128)S(1)}, f32[8,128]{1,0:T(8,128)S(1)}, bf16[80,128,128]{2,1,0:T(8,128)(2,1)S(1)}) custom-call(f32[4,1024]{1,0:T(4,128)S(1)} %get-tuple-element.17.loads_ref, f32[8,1,1792]{2,1,0:T(1,128)} %all_gather.18.pair_ref, f32[8,1,1792]{2,1,0:T(1,128)S(1)} %collective-permute-done.even_ref, ...), custom_call_target="tpu_custom_call" | custom-call | tf_op jit(solution)/shard_map/pallas_call | solution.py:240
  24.7 2.0 %all_gather.19.image_pair_ref = f32[8,1,1792]{2,1,0:T(1,128)} all-gather(f32[8,1,896]{2,1,0:T(1,128)S(1)} %get-tuple-element.23.sent_image_ref), channel_id=1, replica_groups=mesh['case'=2,'high'=2,'mid'=2,'low'=2,'clus'=2] {'clus'}, dimensions={2}, use_global_device_ids=true | all-gather | bytes 86016 | tf_op jit(solution)/shard_map/all_gather | solution.py:264
  26.6 5.1 %all-to-all-start.1 = ((f32[8,1,1792]{2,1,0:T(1,128)}), f32[8,1,1792]{2,1,0:T(1,128)S(1)}, u32[]{:S(2)}, u32[]{:S(2)}) async-start(f32[8,1,1792]{2,1,0:T(1,128)} %all_gather.19.image_pair_ref), calls=%async_computation.1 | async-start | bytes 114688 | tf_op jit(solution)/shard_map/all_to_all | solution.py:266
  31.7 0.7 %collective-permute-start.3 = (f32[8,1,1792]{2,1,0:T(1,128)}, f32[8,1,1792]{2,1,0:T(1,128)S(1)}, u32[]{:S(2)}, u32[]{:S(2)}) collective-permute-start(f32[8,1,1792]{2,1,0:T(1,128)} %all_gather.19.image_pair_ref), channel_id=1, source_target_pairs={{2,4},{4,2},{6,8},{8,6},{10,12},{12,10},{3,5},{5,3},{7,9},{9,7},{1... | collective-permute-start | bytes 172040 | tf_op jit(solution)/shard_map/ppermute | solution.py:265
  32.4 4.8 %collective-permute-start.2 = (f32[8,1,1792]{2,1,0:T(1,128)}, f32[8,1,1792]{2,1,0:T(1,128)S(1)}, u32[]{:S(2)}, u32[]{:S(2)}) collective-permute-start(f32[8,1,1792]{2,1,0:T(1,128)} %all_gather.19.image_pair_ref), channel_id=1, source_target_pairs={{0,2},{2,0},{4,6},{6,4},{8,10},{10,8},{12,14},{14,12},{1,3},{3,1},... | collective-permute-start | bytes 172040 | tf_op jit(solution)/shard_map/ppermute | solution.py:265
  37.2 0.0 collective-permute-done.3.image_odd_ref
  37.2 2.4 %collective-permute-done.2.image_even_ref = f32[8,1,1792]{2,1,0:T(1,128)S(1)} collective-permute-done((f32[8,1,1792]{2,1,0:T(1,128)}, f32[8,1,1792]{2,1,0:T(1,128)S(1)}, u32[]{:S(2)}, u32[]{:S(2)}) %collective-permute-start.2) | collective-permute-done | bytes 57376 | tf_op jit(solution)/shard_map/ppermute | solution.py:265
  39.6 0.0 all-to-all-done.1.got_ref
  39.6 2.0 %shard_map.84 = (f32[1,1,128]{2,1,0:T(1,128)S(1)}, f32[8,1024]{1,0:T(8,128)S(1)}, f32[12,128]{1,0:T(8,128)S(1)}) custom-call(f32[4,1024]{1,0:T(4,128)S(1)} %get-tuple-element.17.loads_ref, f32[8,1,1792]{2,1,0:T(1,128)} %all_gather.18.pair_ref, f32[8,1,1792]{2,1,0:T(1,128)S(1)} %collective-permute-done.even_ref, ...), custom_call_target="tpu_custom_call" | custom-call | tf_op jit(solution)/shard_map/pallas_call | solution.py:240
  41.6 1.8 %all_gather.20 = f32[2,1,128]{2,1,0:T(1,128)S(1)} all-gather(f32[1,1,128]{2,1,0:T(1,128)S(1)} %get-tuple-element.26), channel_id=1, replica_groups=mesh['case'=2,'high'=2,'mid'=2,'low'=2,'clus'=2] {'clus'}, dimensions={0}, use_global_device_ids=true | all-gather | bytes 1536 | tf_op jit(solution)/shard_map/all_gather | solution.py:311
  43.4 4.2 %all_gather.21 = f32[4,1,128]{2,1,0:T(1,128)S(1)} all-gather(f32[2,1,128]{2,1,0:T(1,128)S(1)} %all_gather.20), channel_id=1, replica_groups=mesh['case'=2,'high'=2,'mid'=2,'low'=2,'clus'=2] {'low'}, dimensions={0}, use_global_device_ids=true | all-gather | bytes 3072 | tf_op jit(solution)/shard_map/all_gather | solution.py:311
  47.6 4.3 %all_gather.22 = f32[8,1,128]{2,1,0:T(1,128)S(1)} all-gather(f32[4,1,128]{2,1,0:T(1,128)S(1)} %all_gather.21), channel_id=1, replica_groups=mesh['case'=2,'high'=2,'mid'=2,'low'=2,'clus'=2] {'mid'}, dimensions={0}, use_global_device_ids=true | all-gather | bytes 6144 | tf_op jit(solution)/shard_map/all_gather | solution.py:311
  51.9 5.2 %all_gather.23.got_ref = f32[16,1,128]{2,1,0:T(1,128)S(1)} all-gather(f32[8,1,128]{2,1,0:T(1,128)S(1)} %all_gather.22), channel_id=1, replica_groups=mesh['case'=2,'high'=2,'mid'=2,'low'=2,'clus'=2] {'high'}, dimensions={0}, use_global_device_ids=true | all-gather | bytes 12288 | tf_op jit(solution)/shard_map/all_gather | solution.py:311
  57.2 0.8 %shard_map.85 = f32[4,1024]{1,0:T(4,128)} custom-call(f32[16,1,128]{2,1,0:T(1,128)S(1)} %all_gather.23.got_ref, f32[8,1024]{1,0:T(8,128)S(1)} %get-tuple-element.27.basis_ref, f32[12,128]{1,0:T(8,128)S(1)} %get-tuple-element.28.coeff_ref), custom_call_target="tpu_custom_call" | custom-call | tf_op jit(solution)/shard_map/pallas_call | solution.py:240
  (4 shorter events, 0.0 us)
Async XLA Ops:
  0.0 39.6 %copy-start.1 = (s32[80,2]{0,1:T(2,128)S(1)}, s32[80,2]{0,1:T(2,128)}, u32[]{:S(2)}) copy-start(s32[80,2]{0,1:T(2,128)} %param.11) | copy-start | bytes 1924
  4.0 15.0 %all-to-all-start = ((f32[8,1,1792]{2,1,0:T(1,128)}), f32[8,1,1792]{2,1,0:T(1,128)S(1)}, u32[]{:S(2)}, u32[]{:S(2)}) async-start(f32[8,1,1792]{2,1,0:T(1,128)} %all_gather.18.pair_ref), calls=%async_computation | async-start | bytes 114688 | tf_op jit(solution)/shard_map/all_to_all | solution.py:266
  11.2 5.5 %collective-permute-start.1 = (f32[8,1,1792]{2,1,0:T(1,128)}, f32[8,1,1792]{2,1,0:T(1,128)S(1)}, u32[]{:S(2)}, u32[]{:S(2)}) collective-permute-start(f32[8,1,1792]{2,1,0:T(1,128)} %all_gather.18.pair_ref), channel_id=1, source_target_pairs={{2,4},{4,2},{6,8},{8,6},{10,12},{12,10},{3,5},{5,3},{7,9},{9,7},{1... | collective-permute-start | bytes 172040 | tf_op jit(solution)/shard_map/ppermute | solution.py:265
  11.8 7.2 %collective-permute-start = (f32[8,1,1792]{2,1,0:T(1,128)}, f32[8,1,1792]{2,1,0:T(1,128)S(1)}, u32[]{:S(2)}, u32[]{:S(2)}) collective-permute-start(f32[8,1,1792]{2,1,0:T(1,128)} %all_gather.18.pair_ref), channel_id=1, source_target_pairs={{0,2},{2,0},{4,6},{6,4},{8,10},{10,8},{12,14},{14,12},{1,3},{3,1},... | collective-permute-start | bytes 172040 | tf_op jit(solution)/shard_map/ppermute | solution.py:265
  19.0 0.7 %copy-start = (s32[80,2]{0,1:T(2,128)S(1)}, s32[80,2]{0,1:T(2,128)}, u32[]{:S(2)}) copy-start(s32[80,2]{0,1:T(2,128)} %param.11) | copy-start | bytes 1924
  19.7 0.7 %copy-start.2 = (s32[16,1]{0,1:T(1,128)S(1)}, s32[16,1]{0,1:T(1,128)}, u32[]{:S(2)}) copy-start(s32[16,1]{0,1:T(1,128)} %param.15) | copy-start | bytes 196
  26.6 12.9 %all-to-all-start.1 = ((f32[8,1,1792]{2,1,0:T(1,128)}), f32[8,1,1792]{2,1,0:T(1,128)S(1)}, u32[]{:S(2)}, u32[]{:S(2)}) async-start(f32[8,1,1792]{2,1,0:T(1,128)} %all_gather.19.image_pair_ref), calls=%async_computation.1 | async-start | bytes 114688 | tf_op jit(solution)/shard_map/all_to_all | solution.py:266
  31.7 5.5 %collective-permute-start.3 = (f32[8,1,1792]{2,1,0:T(1,128)}, f32[8,1,1792]{2,1,0:T(1,128)S(1)}, u32[]{:S(2)}, u32[]{:S(2)}) collective-permute-start(f32[8,1,1792]{2,1,0:T(1,128)} %all_gather.19.image_pair_ref), channel_id=1, source_target_pairs={{2,4},{4,2},{6,8},{8,6},{10,12},{12,10},{3,5},{5,3},{7,9},{9,7},{1... | collective-permute-start | bytes 172040 | tf_op jit(solution)/shard_map/ppermute | solution.py:265
  32.4 7.2 %collective-permute-start.2 = (f32[8,1,1792]{2,1,0:T(1,128)}, f32[8,1,1792]{2,1,0:T(1,128)S(1)}, u32[]{:S(2)}, u32[]{:S(2)}) collective-permute-start(f32[8,1,1792]{2,1,0:T(1,128)} %all_gather.19.image_pair_ref), channel_id=1, source_target_pairs={{0,2},{2,0},{4,6},{6,4},{8,10},{10,8},{12,14},{14,12},{1,3},{3,1},... | collective-permute-start | bytes 172040 | tf_op jit(solution)/shard_map/ppermute | solution.py:265

commit v6 on v5

v6 whole, which is shorter than its diff:
```python
import functools

import jax
import jax.numpy as jnp
from jax import lax
from jax.experimental import pallas as pl
from jax.experimental.pallas import tpu as pltpu
from jax.sharding import PartitionSpec as P

HIGH = lax.Precision.HIGHEST
GROUP = ("strip", "clus")
LANES = 128
CHUNK = 16
PIECES = 8
F32 = jnp.float32


CORES = 2


def lanes_of(shape):
    return lax.broadcasted_iota(jnp.int32, shape, 1)


def rows_of(shape):
    return lax.broadcasted_iota(jnp.int32, shape, 0)


def stats_row(columns, rank):
    shape = (columns[0].shape[0], LANES)
    first = lanes_of(shape) - rank * rows_of(shape)
    spread = sum(jnp.where(first == k, column, 0.0) for k, column in enumerate(columns))
    return jnp.sum(spread, axis=0, keepdims=True)


def stat_column(row, k, nrhs, rank):
    shape = (nrhs, LANES)
    first = lanes_of(shape) - rank * rows_of(shape)
    return jnp.sum(jnp.where(first == k, row, 0.0), axis=1, keepdims=True)


def shifted(value, k):
    return pltpu.roll(value, LANES - k, 1)


def far_sum_of(row, nrhs, rank):
    shape = (nrhs, LANES)
    first = lanes_of(shape) - rank * rows_of(shape)
    own = jnp.where((first >= 0) & (first < rank), row, 0.0)
    return sum((pltpu.roll(own, k * rank, 1) for k in range(1, LANES // rank)), own)


def total(rows):
    return jnp.sum(rows, axis=0, keepdims=True)


def put_message(field, columns, far_cols, couple_ref, ranks_ref, sent_ref):
    (nrhs, panels), rank = field.shape, far_cols.shape[0]
    strips = sent_ref.shape[0]
    proj = lax.dot_general(
        field, far_cols, (((1,), (1,)), ((), ())), precision=HIGH, preferred_element_type=F32
    )
    wide = jnp.concatenate([proj] * CHUNK, axis=1)
    shape = (CHUNK, CHUNK * rank)
    owner = lax.div(lanes_of(shape), rank)
    inner = lax.rem(lanes_of(shape), rank)
    row = stats_row(columns, rank)
    half = CHUNK // 2
    number = rows_of(shape)
    number = jnp.where(number < half, 2 * number, 2 * (number - half) + 1)
    for start in range(0, strips, half):
        limit = jnp.zeros(shape, jnp.int32)
        for i in range(CHUNK):
            limit = jnp.where(owner == i, ranks_ref[0, 2 * start + i], limit)
        keep = (owner == number) & (inner < limit)
        spread = jnp.concatenate([jnp.where(keep, wide[r : r + 1], 0.0) for r in range(nrhs)], axis=0)
        couple = couple_ref[pl.ds(2 * start * rank, CHUNK * rank), :]
        terms = jnp.dot(spread, couple, precision=HIGH, preferred_element_type=F32)
        terms = jnp.concatenate([terms[r * CHUNK : (r + 1) * CHUNK] for r in range(nrhs)], axis=1)
        blank = jnp.zeros((nrhs - 3, LANES), F32)
        for i in range(half):
            tail = [terms[i : i + 1], terms[half + i : half + i + 1], row, blank]
            sent_ref[start + i, :, :panels] = field
            sent_ref[start + i, :, panels:] = jnp.concatenate(tail, axis=0)


def message_parts(got_ref, panels):
    terms = jnp.sum(got_ref[:, :, panels:], axis=0)
    terms = jnp.where(lax.axis_index("clus") == 0, terms[0:1], terms[1:2])
    return terms, got_ref[:, 2, panels:]


def window_fields(strips):
    strip = lax.axis_index("strip")
    for place in range(3):
        owner = strip + (place - 1)
        inside = (owner >= 0) & (owner < strips)
        for core in range(CORES):
            yield inside, core * strips + jnp.clip(owner, 0, strips - 1)


def own_place(strips):
    return lax.axis_index("clus") * strips + lax.axis_index("strip")


def fetch(pairs, sems):
    copies = [pltpu.make_async_copy(a, b, sems.at[i]) for i, (a, b) in enumerate(pairs)]
    for copy in copies:
        copy.start()
    return copies


def put_blocks(part, first, window):
    part = part.astype(jnp.bfloat16).astype(F32)
    part = jnp.concatenate([part, jnp.zeros_like(part)], axis=0)
    for c in range(part.shape[1] // LANES):
        window[first + c] = part[:, c * LANES : (c + 1) * LANES]


def near_field(window, tiles_ref, list_ref, sums):
    for held in sums:
        held[...] = jnp.zeros_like(held)
    for n in range(tiles_ref.shape[0]):
        held = sums[n % len(sums)]
        source = window[list_ref[1, n]].astype(jnp.bfloat16)
        product = jnp.dot(source, tiles_ref[n], preferred_element_type=F32)
        held[list_ref[0, n]] += product
    whole = sum((held[...] for held in sums[1:]), sums[0][...])
    return jnp.concatenate([whole[b] for b in range(whole.shape[0])], axis=1)


def start_kernel(
    loads_hbm, cols_hbm, couple_hbm, ranks_hbm, sent_ref, cols_ref, couple_ref, done_ref, loads_ref, ranks_ref, sems
):
    pairs = ((loads_hbm, loads_ref), (cols_hbm, cols_ref), (couple_hbm, couple_ref), (ranks_hbm, ranks_ref))
    for copy in fetch(pairs, sems):
        copy.wait()
    loads = loads_ref[...]
    square = jnp.sum(loads * loads, axis=1, keepdims=True)
    put_message(loads, [square], cols_ref[...], couple_ref, ranks_ref, sent_ref)
    done_ref[...] = jnp.zeros_like(done_ref)


def fetch_kernel(done_ref, tiles_hbm, rows_hbm, self_hbm, tiles_ref, rows_ref, self_ref, sems):
    del done_ref
    every = tiles_hbm.shape[0] // PIECES
    pieces = [pl.ds(i * every, every) for i in range(PIECES)]
    pairs = [(tiles_hbm.at[p], tiles_ref.at[p]) for p in pieces]
    for copy in fetch(pairs + [(rows_hbm, rows_ref), (self_hbm, self_ref)], sems):
        copy.wait()


def image_of(field, far, self_ref, far_rows_ref, near):
    rank = far_rows_ref.shape[0]
    far = jnp.dot(far[:, :rank], far_rows_ref[...], precision=HIGH, preferred_element_type=F32)
    return self_ref[...] * field + near[: field.shape[0]] + far


def step0_kernel(
    got_ref, cols_ref, couple_ref, rows_ref, self_ref, tiles_ref, list_hbm, ranks_hbm,
    sent_ref, state_ref, list_ref, ranks_ref, sems, window, *sums,
):
    panels, rank = cols_ref.shape[1], cols_ref.shape[0]
    nrhs, strips = got_ref.shape[1], got_ref.shape[0] // CORES
    span = panels // LANES
    copies = fetch(((list_hbm, list_ref), (ranks_hbm, ranks_ref)), sems)
    terms, stats = message_parts(got_ref, panels)
    beta = jnp.sqrt(stat_column(total(stats), 0, nrhs, rank))
    basis = got_ref[own_place(strips), :, :panels] / beta
    for i, (inside, place) in enumerate(window_fields(strips)):
        field = jnp.where(inside, got_ref[place, :, :panels], 0.0)
        put_blocks(field / beta, i * span, window)
    far = far_sum_of(terms, nrhs, rank) / beta
    for copy in copies:
        copy.wait()
    near = near_field(window, tiles_ref, list_ref, sums)
    image = image_of(basis, far, self_ref, rows_ref, near)
    state_ref[...] = jnp.concatenate([far, jnp.broadcast_to(beta, far.shape)], axis=0)
    norm = jnp.sum(basis * basis, axis=1, keepdims=True)
    dot = jnp.sum(basis * image, axis=1, keepdims=True)
    share = jnp.where(norm > 0, dot / jnp.where(norm > 0, norm, 1.0), 0.0)
    rest = image - share * basis
    rest = jnp.sum(rest * rest, axis=1, keepdims=True)
    put_message(image, [norm, dot, share, rest], cols_ref[...], couple_ref, ranks_ref, sent_ref)


def step1_kernel(
    got0_ref, got_ref, state_ref, rows_ref, self_ref, tiles_ref, list_hbm,
    sent_ref, basis_ref, coeff_ref, list_ref, sems, window, *sums,
):
    panels, rank = rows_ref.shape[1], rows_ref.shape[0]
    nrhs, strips = got_ref.shape[1], got_ref.shape[0] // CORES
    span = panels // LANES
    (copy,) = fetch(((list_hbm, list_ref),), sems)
    beta = state_ref[nrhs:, :1]
    far0 = state_ref[:nrhs, :]
    terms, stats = message_parts(got_ref, panels)
    summed = total(stats)
    h00 = stat_column(summed, 1, nrhs, rank)
    away = shifted(stats, 2) - shifted(summed, 1)
    rest = total(shifted(stats, 3) + stats * away * away)
    h10 = jnp.sqrt(stat_column(rest, 0, nrhs, rank))
    mine = own_place(strips)
    basis0 = got0_ref[mine, :, :panels] / beta
    basis1 = (got_ref[mine, :, :panels] - h00 * basis0) / h10
    for i, (inside, place) in enumerate(window_fields(strips)):
        field = (got_ref[place, :, :panels] - h00 * (got0_ref[place, :, :panels] / beta)) / h10
        put_blocks(jnp.where(inside, field, 0.0), i * span, window)
    far = (far_sum_of(terms, nrhs, rank) - h00 * far0) / h10
    copy.wait()
    near = near_field(window, tiles_ref, list_ref, sums)
    image = image_of(basis1, far, self_ref, rows_ref, near)
    columns = [jnp.sum(a * image, axis=1, keepdims=True) for a in (basis0, basis1, image)]
    sent_ref[:, 0, :] = jnp.broadcast_to(stats_row(columns, rank), (strips, LANES))
    basis_ref[...] = jnp.concatenate([basis0, basis1], axis=0)
    coeff_ref[...] = jnp.concatenate([jnp.broadcast_to(v, (nrhs, LANES)) for v in (beta, h00, h10)], axis=0)


def finish_kernel(rank, got_ref, basis_ref, coeff_ref, out_ref):
    nrhs = out_ref.shape[0]
    row = total(got_ref[:, 0, :])
    h01, h11, gram11 = (stat_column(row, k, nrhs, rank) for k in range(3))
    beta, h00, h10 = (coeff_ref[k * nrhs : (k + 1) * nrhs, :1] for k in range(3))
    gram00 = h00 * h00 + h10 * h10
    gram01 = h00 * h01 + h10 * h11
    lower00 = jnp.sqrt(gram00)
    lower10 = gram01 / lower00
    lower11 = jnp.sqrt(gram11 - lower10 * lower10)
    middle0 = beta * h00 / lower00
    middle1 = (beta * h01 - lower10 * middle0) / lower11
    y1 = middle1 / lower11
    y0 = (middle0 - lower10 * y1) / lower00
    out_ref[...] = y0 * basis_ref[:nrhs, :] + y1 * basis_ref[nrhs:, :]


def call(kernel, args, outs, scratch=(), held=()):
    args = [pltpu.with_memory_space_constraint(a, pltpu.HBM) if i in held else a for i, a in enumerate(args)]
    return pl.pallas_call(
        kernel,
        out_shape=[
            in_vmem_like(out) if hasattr(out, "dtype") else jax.ShapeDtypeStruct(out, F32) for out in outs
        ],
        in_specs=[pl.BlockSpec(memory_space=pl.ANY if i in held else pltpu.VMEM) for i in range(len(args))],
        out_specs=[pl.BlockSpec(memory_space=pltpu.VMEM)] * len(outs),
        scratch_shapes=list(scratch),
        compiler_params=pltpu.CompilerParams(vmem_limit_bytes=24 * 2**20),
    )(*args)


def in_vmem_like(array):
    return pltpu.VMEM(array.shape, array.dtype)


def in_vmem(arrays):
    return [pltpu.with_memory_space_constraint(a, pltpu.VMEM) for a in arrays]


def exchanged(sent):
    return lax.all_gather(lax.all_to_all(sent, "strip", 0, 0, tiled=True), "clus", axis=0, tiled=True)


def body(loads, self_term, near_tiles, near_list, far_rows, far_cols, coupling, ranks):
    nrhs, panels = loads.shape
    rank = far_cols.shape[0]
    tile = near_tiles.shape[1]
    rows = panels // tile
    strips = coupling.shape[0] // CORES
    couple = coupling.reshape(CORES * strips * rank, rank)
    near_list = near_list.T
    ranks = ranks.reshape(1, CORES * strips)
    self_term = self_term.reshape(1, panels)
    indices = [pltpu.SMEM(near_list.shape, jnp.int32), pltpu.SMEM(ranks.shape, jnp.int32)]
    scratch = [pltpu.VMEM((3 * CORES * rows, 2 * nrhs, tile), F32)]
    scratch += [pltpu.VMEM((rows, 2 * nrhs, tile), F32)] * 4
    message = (strips, nrhs, panels + LANES)

    sent, far_cols, couple, done = call(
        start_kernel,
        (loads, far_cols, couple, ranks),
        [message, far_cols, couple, (8, LANES)],
        [pltpu.VMEM(loads.shape, F32), indices[1], pltpu.SemaphoreType.DMA((4,))],
        held=range(4),
    )
    near_tiles, far_rows, self_term = call(
        fetch_kernel,
        (done, near_tiles, far_rows, self_term),
        [near_tiles, far_rows, self_term],
        [pltpu.SemaphoreType.DMA((PIECES + 2,))],
        held=range(1, 4),
    )
    far_cols, couple, near_tiles, far_rows, self_term = in_vmem((far_cols, couple, near_tiles, far_rows, self_term))
    got0 = exchanged(sent)
    sent, state = call(
        step0_kernel,
        (got0, far_cols, couple, far_rows, self_term, near_tiles, near_list, ranks),
        [message, (2 * nrhs, LANES)],
        indices + [pltpu.SemaphoreType.DMA((2,))] + scratch,
        held=(6, 7),
    )
    got1 = exchanged(sent)
    sent, basis, coeff = call(
        step1_kernel,
        (got0, got1, state, far_rows, self_term, near_tiles, near_list),
        [(strips, 1, LANES), (2 * nrhs, panels), (3 * nrhs, LANES)],
        indices[:1] + [pltpu.SemaphoreType.DMA((1,))] + scratch,
        held=(6,),
    )
    return call(functools.partial(finish_kernel, rank), (exchanged(sent), basis, coeff), [loads.shape])[0]


def solution(mesh):
    every = ("case",) + GROUP
    in_specs = (
        P(None, every),
        P(every),
        P(every, None, None),
        P(every, None),
        P(None, every),
        P(None, every),
        P(None, GROUP, None, None),
        P(None, GROUP),
    )
    return jax.shard_map(body, mesh=mesh, in_specs=in_specs, out_specs=P(None, every), check_vma=False)
```

time: 58.5 us -> 47.6 us (0.81)
  starting transfers between devices: 23.1 us -> 7.26 us
  blocking collectives: 19.6 us -> 25.1 us
  local copies, waits for them, and re-layouts: 1.34 us -> 0 us
  waiting for transfers between devices: 4.74 us -> 5.66 us
    all_to_all x0 -> x2, blocking collectives: none -> 19.3 us  [exchanged(): lax.all_to_all(sent, 'strip', 0, 0, tiled=True)]
    all_gather x6 -> x3, blocking collectives: 19.6 us -> 5.79 us  [exchanged(): lax.all_gather(lax.all_to_all(sent, 'strip', 0, 0, tiled=True), 'clus', a...]
    ppermute x4 -> x0, starting transfers between devices: 10.9 us -> none  [exchanged(): even, odd = (lax.ppermute(pair, STRIP, pairs) for pairs in (even, odd))]
    all_to_all x2 -> x1, waiting for transfers between devices: 0.01 us -> 5.66 us  [exchanged(): lax.all_to_all(sent, 'strip', 0, 0, tiled=True)]
    all_to_all x2 -> x1, starting transfers between devices: 12.2 us -> 7.26 us  [exchanged(): lax.all_to_all(sent, 'strip', 0, 0, tiled=True)]
    ppermute x4 -> x0, waiting for transfers between devices: 4.73 us -> none  [exchanged(): even, odd = (lax.ppermute(pair, STRIP, pairs) for pairs in (even, odd))]
    unnamed x6 -> x0, local copies, waits for them, and re-layouts: 1.34 us -> none
    pallas_call x4 -> x5, Pallas kernels: 9.07 us -> 9.2 us  [call(): pl.pallas_call(kernel, out_shape=[in_vmem_like(out) if hasattr(out, 'dtyp...]
  transfers between devices with their start and end apart: 6 -> 1, of which waited for: 2 -> 1; matrix products, arithmetic and copies ran while one was open for 0% -> 0% of each run, Pallas kernels for 0% -> 4%
where the time goes in v6:
time: 47.6 us; the launch traced here: 47.2 us
  blocking collectives  25.1 us (53%)
  Pallas kernels  9.2 us (19%)
  starting transfers between devices  7.26 us (15%)
  waiting for transfers between devices  5.66 us (12%)
    all_to_all x2, blocking collectives, exchanged(): lax.all_to_all(sent, 'strip', 0, 0, tiled=True)  19.3 us
    pallas_call x5, Pallas kernels, call(): pl.pallas_call(kernel, out_shape=[in_vmem_like(out) if hasattr(out, 'dtyp...  9.2 us
    all_to_all x1, starting transfers between devices, exchanged(): lax.all_to_all(sent, 'strip', 0, 0, tiled=True)  7.26 us
    all_gather x3, blocking collectives, exchanged(): lax.all_gather(lax.all_to_all(sent, 'strip', 0, 0, tiled=True), 'clus', a...  5.79 us
    all_to_all x1, waiting for transfers between devices, exchanged(): lax.all_to_all(sent, 'strip', 0, 0, tiled=True)  5.66 us
  transfers between devices with their start and end apart: 1, of which 1 were waited for; matrix products, arithmetic and copies ran while one was open for 0% of the time, Pallas kernels for 4%

profile of v6, /device:TPU:0, one launch (start us, length us, event | category | flops | bytes accessed | tf_op | source)
XLA Modules:
  0.0 47.2 jit_solution(12032655033893382543)
XLA Ops:
  0.0 2.5 %shard_map.82 = (f32[8,4,1152]{2,1,0:T(4,128)}, f32[32,1024]{1,0:T(8,128)S(1)}, f32[512,32]{1,0:T(8,128)S(1)}, f32[8,128]{1,0:T(8,128)S(1)}) custom-call(f32[4,1024]{1,0:T(4,128)} %loads_hbm.1, f32[32,1024]{1,0:T(8,128)} %cols_hbm.1, f32[512,32]{1,0:T(8,128)} %bitcast.4, s32[1,16]{1,0:T(1,128)} %bitcast.8), custom_call_target="tpu_custom_call" | custom-call | tf_op jit(solution)/shard_map/pallas_call | solution.py:238
  2.5 7.3 %all-to-all-start = ((f32[8,4,1152]{2,1,0:T(4,128)}), f32[8,4,1152]{2,1,0:T(4,128)S(1)}, u32[]{:S(2)}, u32[]{:S(2)}) async-start(f32[8,4,1152]{2,1,0:T(4,128)} %get-tuple-element.17), calls=%async_computation | async-start | bytes 294912 | tf_op jit(solution)/shard_map/all_to_all | solution.py:259
  9.8 1.8 %shard_map.83 = (bf16[80,128,128]{2,1,0:T(8,128)(2,1)S(1)}, f32[32,1024]{1,0:T(8,128)S(1)}, f32[1,1024]{1,0:T(1,128)S(1)}) custom-call(f32[8,128]{1,0:T(8,128)S(1)} %get-tuple-element.20.done_ref, bf16[80,128,128]{2,1,0:T(8,128)(2,1)} %tiles_hbm.1, f32[32,1024]{1,0:T(8,128)} %rows_hbm.1, f32[1,1024]{1,0:T(1,128)} %bitcast.5), custom_call_target="tpu_custom_call" | custom-call | tf_op jit(solution)/shard_map/pallas_call | solution.py:238
  11.6 5.7 %all-to-all-done = f32[8,4,1152]{2,1,0:T(4,128)S(1)} async-done(((f32[8,4,1152]{2,1,0:T(4,128)}), f32[8,4,1152]{2,1,0:T(4,128)S(1)}, u32[]{:S(2)}, u32[]{:S(2)}) %all-to-all-start) | async-done | bytes 147488 | tf_op jit(solution)/shard_map/all_to_all | solution.py:259
  17.2 2.0 %all_gather.9.got_ref.got0_ref = f32[16,4,1152]{2,1,0:T(4,128)S(1)} all-gather(f32[8,4,1152]{2,1,0:T(4,128)S(1)} %all-to-all-done), channel_id=1, replica_groups=mesh['case'=2,'strip'=8,'clus'=2] {'clus'}, dimensions={0}, use_global_device_ids=true | all-gather | bytes 442368 | tf_op jit(solution)/shard_map/all_gather | solution.py:259
  19.2 2.4 %shard_map.84 = (f32[8,4,1152]{2,1,0:T(4,128)S(1)}, f32[8,128]{1,0:T(8,128)S(1)}) custom-call(f32[16,4,1152]{2,1,0:T(4,128)S(1)} %all_gather.9.got_ref.got0_ref, f32[32,1024]{1,0:T(8,128)S(1)} %get-tuple-element.18.cols_ref, f32[512,32]{1,0:T(8,128)S(1)} %get-tuple-element.19.couple_ref, f32[32,1024]{1,0:T(8,128)S(1)} %get-tuple-element.21.rows_ref, ...), custom_call_target="tpu_custom_call" | custom-call | tf_op jit(solution)/shard_map/pallas_call | solution.py:238
  21.6 10.2 %all_to_all.15 = f32[8,4,1152]{2,1,0:T(4,128)S(1)} all-to-all(f32[8,4,1152]{2,1,0:T(4,128)S(1)} %get-tuple-element.24), channel_id=1, replica_groups=mesh['case'=2,'strip'=8,'clus'=2] {'strip'}, dimensions={0} | all-to-all | bytes 294912 | tf_op jit(solution)/shard_map/all_to_all | solution.py:259
  31.8 2.0 %all_gather.10.got_ref = f32[16,4,1152]{2,1,0:T(4,128)S(1)} all-gather(f32[8,4,1152]{2,1,0:T(4,128)S(1)} %all_to_all.15), channel_id=1, replica_groups=mesh['case'=2,'strip'=8,'clus'=2] {'clus'}, dimensions={0}, use_global_device_ids=true | all-gather | bytes 442368 | tf_op jit(solution)/shard_map/all_gather | solution.py:259
  33.8 1.7 %shard_map.85 = (f32[8,1,128]{2,1,0:T(1,128)S(1)}, f32[8,1024]{1,0:T(8,128)S(1)}, f32[12,128]{1,0:T(8,128)S(1)}) custom-call(f32[16,4,1152]{2,1,0:T(4,128)S(1)} %all_gather.9.got_ref.got0_ref, f32[16,4,1152]{2,1,0:T(4,128)S(1)} %all_gather.10.got_ref, f32[8,128]{1,0:T(8,128)S(1)} %get-tuple-element.25.state_ref, f32[32,1024]{1,0:T(8,128)S(1)} %get-tuple-element.21.rows_ref, ...), custom_call_target="tpu_custom_call" | custom-call | tf_op jit(solution)/shard_map/pallas_call | solution.py:238
  35.6 9.1 %all_to_all.16 = f32[8,1,128]{2,1,0:T(1,128)S(1)} all-to-all(f32[8,1,128]{2,1,0:T(1,128)S(1)} %get-tuple-element.26), channel_id=1, replica_groups=mesh['case'=2,'strip'=8,'clus'=2] {'strip'}, dimensions={0} | all-to-all | bytes 8192 | tf_op jit(solution)/shard_map/all_to_all | solution.py:259
  44.7 1.8 %all_gather.11.got_ref = f32[16,1,128]{2,1,0:T(1,128)S(1)} all-gather(f32[8,1,128]{2,1,0:T(1,128)S(1)} %all_to_all.16), channel_id=1, replica_groups=mesh['case'=2,'strip'=8,'clus'=2] {'clus'}, dimensions={0}, use_global_device_ids=true | all-gather | bytes 12288 | tf_op jit(solution)/shard_map/all_gather | solution.py:259
  46.4 0.8 %shard_map.86 = f32[4,1024]{1,0:T(4,128)} custom-call(f32[16,1,128]{2,1,0:T(1,128)S(1)} %all_gather.11.got_ref, f32[8,1024]{1,0:T(8,128)S(1)} %get-tuple-element.27.basis_ref, f32[12,128]{1,0:T(8,128)S(1)} %get-tuple-element.28.coeff_ref), custom_call_target="tpu_custom_call" | custom-call | tf_op jit(solution)/shard_map/pallas_call | solution.py:238
Async XLA Ops:
  2.5 14.7 %all-to-all-start = ((f32[8,4,1152]{2,1,0:T(4,128)}), f32[8,4,1152]{2,1,0:T(4,128)S(1)}, u32[]{:S(2)}, u32[]{:S(2)}) async-start(f32[8,4,1152]{2,1,0:T(4,128)} %get-tuple-element.17), calls=%async_computation | async-start | bytes 294912 | tf_op jit(solution)/shard_map/all_to_all | solution.py:259

commit v7 on v6

--- a/solution.py
+++ b/solution.py
@@ -54,17 +54,23 @@
     return jnp.sum(rows, axis=0, keepdims=True)
 
 
-def put_message(field, columns, far_cols, couple_ref, ranks_ref, sent_ref):
-    (nrhs, panels), rank = field.shape, far_cols.shape[0]
+def put_message(field, columns, cols_ref, couple_ref, ranks_ref, sent_ref, copies=()):
+    (nrhs, panels), rank = field.shape, cols_ref.shape[0]
     strips = sent_ref.shape[0]
+    row = stats_row(columns, rank)
+    for i in range(strips):
+        sent_ref[i, :, :panels] = field
+    for copy in copies[:1]:
+        copy.wait()
     proj = lax.dot_general(
-        field, far_cols, (((1,), (1,)), ((), ())), precision=HIGH, preferred_element_type=F32
+        field, cols_ref[...], (((1,), (1,)), ((), ())), precision=HIGH, preferred_element_type=F32
     )
     wide = jnp.concatenate([proj] * CHUNK, axis=1)
     shape = (CHUNK, CHUNK * rank)
     owner = lax.div(lanes_of(shape), rank)
     inner = lax.rem(lanes_of(shape), rank)
-    row = stats_row(columns, rank)
+    for copy in copies[1:]:
+        copy.wait()
     half = CHUNK // 2
     number = rows_of(shape)
     number = jnp.where(number < half, 2 * number, 2 * (number - half) + 1)
@@ -80,27 +86,23 @@
         blank = jnp.zeros((nrhs - 3, LANES), F32)
         for i in range(half):
             tail = [terms[i : i + 1], terms[half + i : half + i + 1], row, blank]
-            sent_ref[start + i, :, :panels] = field
             sent_ref[start + i, :, panels:] = jnp.concatenate(tail, axis=0)
 
 
-def message_parts(got_ref, panels):
-    terms = jnp.sum(got_ref[:, :, panels:], axis=0)
+def message_parts(got, panels):
+    terms = sum(jnp.sum(ref[:, :, panels:], axis=0) for ref in got)
     terms = jnp.where(lax.axis_index("clus") == 0, terms[0:1], terms[1:2])
-    return terms, got_ref[:, 2, panels:]
-
-
-def window_fields(strips):
-    strip = lax.axis_index("strip")
-    for place in range(3):
-        owner = strip + (place - 1)
+    return terms, jnp.concatenate([ref[:, 2, panels:] for ref in got], axis=0)
+
+
+def window_places(strips):
+    strip, core = lax.axis_index("strip"), lax.axis_index("clus")
+    for step in range(3):
+        owner = strip + (step - 1)
         inside = (owner >= 0) & (owner < strips)
-        for core in range(CORES):
-            yield inside, core * strips + jnp.clip(owner, 0, strips - 1)
-
-
-def own_place(strips):
-    return lax.axis_index("clus") * strips + lax.axis_index("strip")
+        for other in range(CORES):
+            place = CORES * step + (core if other == 0 else 1 - core)
+            yield inside, jnp.clip(owner, 0, strips - 1), other, place
 
 
 def fetch(pairs, sems):
@@ -133,12 +135,12 @@
     loads_hbm, cols_hbm, couple_hbm, ranks_hbm, sent_ref, cols_ref, couple_ref, done_ref, loads_ref, ranks_ref, sems
 ):
     pairs = ((loads_hbm, loads_ref), (cols_hbm, cols_ref), (couple_hbm, couple_ref), (ranks_hbm, ranks_ref))
-    for copy in fetch(pairs, sems):
-        copy.wait()
+    copies = fetch(pairs, sems)
+    copies[0].wait()
     loads = loads_ref[...]
     square = jnp.sum(loads * loads, axis=1, keepdims=True)
-    put_message(loads, [square], cols_ref[...], couple_ref, ranks_ref, sent_ref)
     done_ref[...] = jnp.zeros_like(done_ref)
+    put_message(loads, [square], cols_ref, couple_ref, ranks_ref, sent_ref, copies[1:])
 
 
 def fetch_kernel(done_ref, tiles_hbm, rows_hbm, self_hbm, tiles_ref, rows_ref, self_ref, sems):
@@ -157,19 +159,20 @@
 
 
 def step0_kernel(
-    got_ref, cols_ref, couple_ref, rows_ref, self_ref, tiles_ref, list_hbm, ranks_hbm,
+    own_ref, other_ref, cols_ref, couple_ref, rows_ref, self_ref, tiles_ref, list_hbm, ranks_hbm,
     sent_ref, state_ref, list_ref, ranks_ref, sems, window, *sums,
 ):
     panels, rank = cols_ref.shape[1], cols_ref.shape[0]
-    nrhs, strips = got_ref.shape[1], got_ref.shape[0] // CORES
+    got = (own_ref, other_ref)
+    strips, nrhs = own_ref.shape[:2]
     span = panels // LANES
     copies = fetch(((list_hbm, list_ref), (ranks_hbm, ranks_ref)), sems)
-    terms, stats = message_parts(got_ref, panels)
+    terms, stats = message_parts(got, panels)
     beta = jnp.sqrt(stat_column(total(stats), 0, nrhs, rank))
-    basis = got_ref[own_place(strips), :, :panels] / beta
-    for i, (inside, place) in enumerate(window_fields(strips)):
-        field = jnp.where(inside, got_ref[place, :, :panels], 0.0)
-        put_blocks(field / beta, i * span, window)
+    basis = own_ref[lax.axis_index("strip"), :, :panels] / beta
+    for inside, strip, other, place in window_places(strips):
+        field = jnp.where(inside, got[other][strip, :, :panels], 0.0)
+        put_blocks(field / beta, place * span, window)
     far = far_sum_of(terms, nrhs, rank) / beta
     for copy in copies:
         copy.wait()
@@ -181,37 +184,38 @@
     share = jnp.where(norm > 0, dot / jnp.where(norm > 0, norm, 1.0), 0.0)
     rest = image - share * basis
     rest = jnp.sum(rest * rest, axis=1, keepdims=True)
-    put_message(image, [norm, dot, share, rest], cols_ref[...], couple_ref, ranks_ref, sent_ref)
+    put_message(image, [norm, dot, share, rest], cols_ref, couple_ref, ranks_ref, sent_ref)
 
 
 def step1_kernel(
-    got0_ref, got_ref, state_ref, rows_ref, self_ref, tiles_ref, list_hbm,
+    own0_ref, other0_ref, own_ref, other_ref, state_ref, rows_ref, self_ref, tiles_ref, list_hbm,
     sent_ref, basis_ref, coeff_ref, list_ref, sems, window, *sums,
 ):
     panels, rank = rows_ref.shape[1], rows_ref.shape[0]
-    nrhs, strips = got_ref.shape[1], got_ref.shape[0] // CORES
+    got0, got = (own0_ref, other0_ref), (own_ref, other_ref)
+    strips, nrhs = own_ref.shape[:2]
     span = panels // LANES
     (copy,) = fetch(((list_hbm, list_ref),), sems)
     beta = state_ref[nrhs:, :1]
     far0 = state_ref[:nrhs, :]
-    terms, stats = message_parts(got_ref, panels)
+    terms, stats = message_parts(got, panels)
     summed = total(stats)
     h00 = stat_column(summed, 1, nrhs, rank)
     away = shifted(stats, 2) - shifted(summed, 1)
     rest = total(shifted(stats, 3) + stats * away * away)
     h10 = jnp.sqrt(stat_column(rest, 0, nrhs, rank))
-    mine = own_place(strips)
-    basis0 = got0_ref[mine, :, :panels] / beta
-    basis1 = (got_ref[mine, :, :panels] - h00 * basis0) / h10
-    for i, (inside, place) in enumerate(window_fields(strips)):
-        field = (got_ref[place, :, :panels] - h00 * (got0_ref[place, :, :panels] / beta)) / h10
-        put_blocks(jnp.where(inside, field, 0.0), i * span, window)
+    mine = lax.axis_index("strip")
+    basis0 = own0_ref[mine, :, :panels] / beta
+    basis1 = (own_ref[mine, :, :panels] - h00 * basis0) / h10
+    for inside, strip, other, place in window_places(strips):
+        field = (got[other][strip, :, :panels] - h00 * (got0[other][strip, :, :panels] / beta)) / h10
+        put_blocks(jnp.where(inside, field, 0.0), place * span, window)
     far = (far_sum_of(terms, nrhs, rank) - h00 * far0) / h10
     copy.wait()
     near = near_field(window, tiles_ref, list_ref, sums)
     image = image_of(basis1, far, self_ref, rows_ref, near)
     columns = [jnp.sum(a * image, axis=1, keepdims=True) for a in (basis0, basis1, image)]
-    sent_ref[:, 0, :] = jnp.broadcast_to(stats_row(columns, rank), (strips, LANES))
+    sent_ref[:, 0, :] = jnp.broadcast_to(stats_row(columns, rank), (CORES * strips, LANES))
     basis_ref[...] = jnp.concatenate([basis0, basis1], axis=0)
     coeff_ref[...] = jnp.concatenate([jnp.broadcast_to(v, (nrhs, LANES)) for v in (beta, h00, h10)], axis=0)
 
@@ -256,7 +260,8 @@
 
 
 def exchanged(sent):
-    return lax.all_gather(lax.all_to_all(sent, "strip", 0, 0, tiled=True), "clus", axis=0, tiled=True)
+    got = lax.all_to_all(sent, "strip", 0, 0, tiled=True)
+    return got, lax.ppermute(got, "clus", [(0, 1), (1, 0)])
 
 
 def body(loads, self_term, near_tiles, near_list, far_rows, far_cols, coupling, ranks):
@@ -292,20 +297,21 @@
     got0 = exchanged(sent)
     sent, state = call(
         step0_kernel,
-        (got0, far_cols, couple, far_rows, self_term, near_tiles, near_list, ranks),
+        (*got0, far_cols, couple, far_rows, self_term, near_tiles, near_list, ranks),
         [message, (2 * nrhs, LANES)],
         indices + [pltpu.SemaphoreType.DMA((2,))] + scratch,
-        held=(6, 7),
+        held=(7, 8),
     )
     got1 = exchanged(sent)
     sent, basis, coeff = call(
         step1_kernel,
-        (got0, got1, state, far_rows, self_term, near_tiles, near_list),
-        [(strips, 1, LANES), (2 * nrhs, panels), (3 * nrhs, LANES)],
+        (*got0, *got1, state, far_rows, self_term, near_tiles, near_list),
+        [(CORES * strips, 1, LANES), (2 * nrhs, panels), (3 * nrhs, LANES)],
         indices[:1] + [pltpu.SemaphoreType.DMA((1,))] + scratch,
-        held=(6,),
-    )
-    return call(functools.partial(finish_kernel, rank), (exchanged(sent), basis, coeff), [loads.shape])[0]
+        held=(8,),
+    )
+    got = lax.all_to_all(sent, GROUP, 0, 0, tiled=True)
+    return call(functools.partial(finish_kernel, rank), (got, basis, coeff), [loads.shape])[0]
 
 
 def solution(mesh):

time: 47.6 us -> 44.5 us (0.935)
  blocking collectives: 25.1 us -> 34.2 us
  starting transfers between devices: 7.26 us -> 0.01 us
  waiting for transfers between devices: 5.66 us -> 1.37 us
  Pallas kernels: 9.2 us -> 8.5 us
    all_to_all x2 -> x3, blocking collectives: 19.3 us -> 34.2 us  [the longest x2 25.1 us: exchanged(): got = lax.all_to_all(sent, 'strip', 0, 0, tiled=True)]
    all_to_all x1 -> x0, starting transfers between devices: 7.26 us -> none  [exchanged(): lax.all_to_all(sent, 'strip', 0, 0, tiled=True)]
    all_gather x3 -> x0, blocking collectives: 5.79 us -> none  [exchanged(): lax.all_gather(lax.all_to_all(sent, 'strip', 0, 0, tiled=True), 'clus', a...]
    all_to_all x1 -> x0, waiting for transfers between devices: 5.66 us -> none  [exchanged(): lax.all_to_all(sent, 'strip', 0, 0, tiled=True)]
    ppermute x0 -> x2, waiting for transfers between devices: none -> 1.37 us  [exchanged(): return (got, lax.ppermute(got, 'clus', [(0, 1), (1, 0)]))]
    pallas_call x5, Pallas kernels: 9.2 us -> 8.5 us  [call(): pl.pallas_call(kernel, out_shape=[in_vmem_like(out) if hasattr(out, 'dtyp...]
  transfers between devices with their start and end apart: 1 -> 2, of which waited for: 1 -> 1; matrix products, arithmetic and copies ran while one was open for 0% -> 0% of each run, Pallas kernels for 4% -> 4%
where the time goes in v7:
time: 44.5 us; the launch traced here: 44.1 us
  blocking collectives  34.2 us (77%)
  Pallas kernels  8.5 us (19%)
  waiting for transfers between devices  1.37 us (3%)
    all_to_all x2, blocking collectives, exchanged(): got = lax.all_to_all(sent, 'strip', 0, 0, tiled=True)  25.1 us
    all_to_all x1, blocking collectives, body(): got = lax.all_to_all(sent, GROUP, 0, 0, tiled=True)  9.12 us
    pallas_call x5, Pallas kernels, call(): pl.pallas_call(kernel, out_shape=[in_vmem_like(out) if hasattr(out, 'dtyp...  8.5 us
    ppermute x2, waiting for transfers between devices, exchanged(): return (got, lax.ppermute(got, 'clus', [(0, 1), (1, 0)]))  1.37 us
  transfers between devices with their start and end apart: 2, of which 1 were waited for; matrix products, arithmetic and copies ran while one was open for 0% of the time, Pallas kernels for 4%

profile of v7, /device:TPU:0, one launch (start us, length us, event | category | flops | bytes accessed | tf_op | source)
XLA Modules:
  0.0 44.1 jit_solution(13798236020330467845)
XLA Ops:
  0.0 1.8 %shard_map.82 = (f32[8,4,1152]{2,1,0:T(4,128)S(1)}, f32[32,1024]{1,0:T(8,128)S(1)}, f32[512,32]{1,0:T(8,128)S(1)}, f32[8,128]{1,0:T(8,128)S(1)}) custom-call(f32[4,1024]{1,0:T(4,128)} %loads_hbm.1, f32[32,1024]{1,0:T(8,128)} %cols_hbm.1, f32[512,32]{1,0:T(8,128)} %bitcast.4, s32[1,16]{1,0:T(1,128)} %bitcast.8), custom_call_target="tpu_custom_call" | custom-call | tf_op jit(solution)/shard_map/pallas_call | solution.py:242
  1.8 14.5 %all_to_all.15.own_ref.own0_ref = f32[8,4,1152]{2,1,0:T(4,128)S(1)} all-to-all(f32[8,4,1152]{2,1,0:T(4,128)S(1)} %get-tuple-element.17), channel_id=1, replica_groups=mesh['case'=2,'strip'=8,'clus'=2] {'strip'}, dimensions={0} | all-to-all | bytes 294912 | tf_op jit(solution)/shard_map/all_to_all | solution.py:263
  16.3 0.0 collective-permute-start
  16.3 1.8 %shard_map.83 = (bf16[80,128,128]{2,1,0:T(8,128)(2,1)S(1)}, f32[32,1024]{1,0:T(8,128)S(1)}, f32[1,1024]{1,0:T(1,128)S(1)}) custom-call(f32[8,128]{1,0:T(8,128)S(1)} %get-tuple-element.20.done_ref, bf16[80,128,128]{2,1,0:T(8,128)(2,1)} %tiles_hbm.1, f32[32,1024]{1,0:T(8,128)} %rows_hbm.1, f32[1,1024]{1,0:T(1,128)} %bitcast.5), custom_call_target="tpu_custom_call" | custom-call | tf_op jit(solution)/shard_map/pallas_call | solution.py:242
  18.1 0.0 collective-permute-done.other_ref.other0_ref
  18.1 2.4 %shard_map.84 = (f32[8,4,1152]{2,1,0:T(4,128)S(1)}, f32[8,128]{1,0:T(8,128)S(1)}) custom-call(f32[8,4,1152]{2,1,0:T(4,128)S(1)} %all_to_all.15.own_ref.own0_ref, f32[8,4,1152]{2,1,0:T(4,128)S(1)} %collective-permute-done.other_ref.other0_ref, f32[32,1024]{1,0:T(8,128)S(1)} %get-tuple-element.18.cols_ref, f32[512,32]{1,0:T(8,128)S(1)} %get-tuple-element.19.couple_ref, ...), custom_call_target="tpu_custom_call" | custom-call | tf_op jit(solution)/shard_map/pallas_call | solution.py:242
  20.5 10.6 %all_to_all.16.own_ref = f32[8,4,1152]{2,1,0:T(4,128)S(1)} all-to-all(f32[8,4,1152]{2,1,0:T(4,128)S(1)} %get-tuple-element.24), channel_id=1, replica_groups=mesh['case'=2,'strip'=8,'clus'=2] {'strip'}, dimensions={0} | all-to-all | bytes 294912 | tf_op jit(solution)/shard_map/all_to_all | solution.py:263
  31.0 0.0 collective-permute-start.1
  31.0 1.4 %collective-permute-done.1.other_ref = f32[8,4,1152]{2,1,0:T(4,128)S(1)} collective-permute-done((f32[8,4,1152]{2,1,0:T(4,128)S(1)}, f32[8,4,1152]{2,1,0:T(4,128)S(1)}, u32[]{:S(2)}, u32[]{:S(2)}) %collective-permute-start.1) | collective-permute-done | bytes 147488 | tf_op jit(solution)/shard_map/ppermute | solution.py:264
  32.4 1.8 %shard_map.85 = (f32[16,1,128]{2,1,0:T(1,128)S(1)}, f32[8,1024]{1,0:T(8,128)S(1)}, f32[12,128]{1,0:T(8,128)S(1)}) custom-call(f32[8,4,1152]{2,1,0:T(4,128)S(1)} %all_to_all.15.own_ref.own0_ref, f32[8,4,1152]{2,1,0:T(4,128)S(1)} %collective-permute-done.other_ref.other0_ref, f32[8,4,1152]{2,1,0:T(4,128)S(1)} %all_to_all.16.own_ref, ...), custom_call_target="tpu_custom_call" | custom-call | tf_op jit(solution)/shard_map/pallas_call | solution.py:242
  34.2 9.1 %all_to_all.17.got_ref = f32[16,1,128]{2,1,0:T(1,128)S(1)} all-to-all(f32[16,1,128]{2,1,0:T(1,128)S(1)} %get-tuple-element.26), channel_id=1, replica_groups=mesh['case'=2,'strip'=8,'clus'=2] {'strip','clus'}, dimensions={0} | all-to-all | bytes 16384 | tf_op jit(solution)/shard_map/all_to_all | solution.py:313
  43.3 0.8 %shard_map.86 = f32[4,1024]{1,0:T(4,128)} custom-call(f32[16,1,128]{2,1,0:T(1,128)S(1)} %all_to_all.17.got_ref, f32[8,1024]{1,0:T(8,128)S(1)} %get-tuple-element.27.basis_ref, f32[12,128]{1,0:T(8,128)S(1)} %get-tuple-element.28.coeff_ref), custom_call_target="tpu_custom_call" | custom-call | tf_op jit(solution)/shard_map/pallas_call | solution.py:242
Async XLA Ops:
  16.3 1.8 %collective-permute-start = (f32[8,4,1152]{2,1,0:T(4,128)S(1)}, f32[8,4,1152]{2,1,0:T(4,128)S(1)}, u32[]{:S(2)}, u32[]{:S(2)}) collective-permute-start(f32[8,4,1152]{2,1,0:T(4,128)S(1)} %all_to_all.15.own_ref.own0_ref), channel_id=1, source_target_pairs={{0,1},{1,0},{2,3},{3,2},{4,5},{5,4},{6,7},{7,6},{8,9},{9,8},{10,11... | collective-permute-start | bytes 442376 | tf_op jit(solution)/shard_map/ppermute | solution.py:264
  31.0 1.4 %collective-permute-start.1 = (f32[8,4,1152]{2,1,0:T(4,128)S(1)}, f32[8,4,1152]{2,1,0:T(4,128)S(1)}, u32[]{:S(2)}, u32[]{:S(2)}) collective-permute-start(f32[8,4,1152]{2,1,0:T(4,128)S(1)} %all_to_all.16.own_ref), channel_id=1, source_target_pairs={{0,1},{1,0},{2,3},{3,2},{4,5},{5,4},{6,7},{7,6},{8,9},{9,8},{10,11... | collective-permute-start | bytes 442376 | tf_op jit(solution)/shard_map/ppermute | solution.py:264

commit v8 on v7

v8 whole, which is shorter than its diff:
```python
import functools

import jax
import jax.numpy as jnp
from jax import lax
from jax.experimental import pallas as pl
from jax.experimental.pallas import tpu as pltpu
from jax.sharding import PartitionSpec as P

GROUP = ("strip", "clus")
CORES = 2
LANES = 128
CHUNK = 16
PIECES = 4
F32 = jnp.float32
BF16 = jnp.bfloat16


def lanes_of(shape):
    return lax.broadcasted_iota(jnp.int32, shape, 1)


def rows_of(shape):
    return lax.broadcasted_iota(jnp.int32, shape, 0)


def total(rows):
    return jnp.sum(rows, axis=0, keepdims=True)


def stats_row(columns, rank):
    shape = (columns[0].shape[0], LANES)
    first = lanes_of(shape) - rank * rows_of(shape)
    spread = sum(jnp.where(first == k, column, 0.0) for k, column in enumerate(columns))
    return total(spread)


def stat_column(row, k, nrhs, rank):
    shape = (nrhs, LANES)
    first = lanes_of(shape) - rank * rows_of(shape)
    return jnp.sum(jnp.where(first == k, row, 0.0), axis=1, keepdims=True)


def shifted(value, k):
    return pltpu.roll(value, LANES - k, 1)


def far_sum_of(row, nrhs, rank):
    shape = (nrhs, LANES)
    first = lanes_of(shape) - rank * rows_of(shape)
    own = jnp.where((first >= 0) & (first < rank), row, 0.0)
    return sum((pltpu.roll(own, k * rank, 1) for k in range(1, LANES // rank)), own)


def halves(value):
    high = value.astype(BF16)
    return high, (value - high.astype(F32)).astype(BF16)


def product(left, right_high, right_low, side=0):
    rows = left.shape[0]
    high, low = halves(left)
    dims = (((1,), (side,)), ((), ()))
    both = lax.dot_general(jnp.concatenate([high, low], axis=0), right_high, dims, preferred_element_type=F32)
    return both[:rows] + (both[rows:] + lax.dot_general(high, right_low, dims, preferred_element_type=F32))


def fetch(pairs, sems):
    copies = [pltpu.make_async_copy(a, b, sems.at[i]) for i, (a, b) in enumerate(pairs)]
    for copy in copies:
        copy.start()
    return copies


def put_message(field, columns, cols, couple, masks_ref, sent_ref):
    (nrhs, panels), rank = field.shape, cols[0].shape[0]
    strips = sent_ref.shape[0]
    half = CHUNK // 2
    for i in range(strips):
        sent_ref[i, :, :panels] = field
    proj = product(field, cols[0][...], cols[1][...], 1)
    wide = jnp.concatenate([proj] * CHUNK, axis=1)
    row = stats_row(columns, rank)
    blank = jnp.zeros((nrhs - 3, LANES), F32)
    for start in range(0, strips, half):
        mask = masks_ref[pl.ds(CORES * start, CHUNK), :]
        spread = jnp.concatenate([mask * wide[r : r + 1] for r in range(nrhs)], axis=0)
        here = pl.ds(CORES * start * rank, CHUNK * rank)
        terms = product(spread, couple[0][here, :], couple[1][here, :])
        terms = jnp.concatenate([terms[r * CHUNK : (r + 1) * CHUNK] for r in range(nrhs)], axis=1)
        for i in range(half):
            tail = [terms[i : i + 1], terms[half + i : half + i + 1], row, blank]
            sent_ref[start + i, :, panels:] = jnp.concatenate(tail, axis=0)


def message_parts(got, panels):
    terms = sum(jnp.sum(ref[:, :, panels:], axis=0) for ref in got)
    terms = jnp.where(lax.axis_index("clus") == 0, terms[0:1], terms[1:2])
    return terms, jnp.concatenate([ref[:, 2, panels:] for ref in got], axis=0)


def window_parts(got, panels):
    strips = got[0].shape[0]
    for step in range(3):
        owner = lax.axis_index("strip") + (step - 1)
        inside = (owner >= 0) & (owner < strips)
        owner = jnp.clip(owner, 0, strips - 1)
        yield inside, jnp.concatenate([ref[owner, :, :panels] for ref in got], axis=0)


def put_blocks(part, first, window):
    part = part.astype(BF16).astype(F32)
    for c in range(part.shape[1] // LANES):
        window[first + c] = part[:, c * LANES : (c + 1) * LANES]


def near_field(window, tiles, list_ref, sums, nrhs):
    for held in sums:
        held[...] = jnp.zeros_like(held)
    n = 0
    for tiles_ref in tiles:
        for i in range(tiles_ref.shape[0]):
            held = sums[n % len(sums)]
            source = window[list_ref[1, n]].astype(BF16)
            held[list_ref[0, n]] += jnp.dot(source, tiles_ref[i], preferred_element_type=F32)
            n += 1
    whole = sum((held[...] for held in sums[1:]), sums[0][...])
    rows = whole.shape[0] // CORES
    return jnp.concatenate([whole[b, :nrhs] + whole[rows + b, nrhs:] for b in range(rows)], axis=1)


def start_kernel(
    loads_hbm, cols_hbm, couple_hbm, ranks_hbm, sent_ref, cols_high, cols_low, couple_high, couple_low, masks_ref,
    done_ref, loads_ref, cols_ref, couple_ref, ranks_ref, sems,
):
    rank = cols_ref.shape[0]
    pairs = ((ranks_hbm, ranks_ref), (loads_hbm, loads_ref), (cols_hbm, cols_ref), (couple_hbm, couple_ref))
    copies = fetch(pairs, sems)
    done_ref[...] = jnp.zeros_like(done_ref)
    copies[0].wait()
    shape = (CHUNK, CHUNK * rank)
    owner = lax.div(lanes_of(shape), rank)
    inner = lax.rem(lanes_of(shape), rank)
    half = CHUNK // 2
    number = rows_of(shape)
    number = jnp.where(number < half, CORES * number, CORES * (number - half) + 1)
    for start in range(0, masks_ref.shape[0], CHUNK):
        limit = jnp.zeros((1, CHUNK * rank), jnp.int32)
        for i in range(CHUNK):
            limit = jnp.where(owner[:1] == i, ranks_ref[0, start + i], limit)
        masks_ref[pl.ds(start, CHUNK), :] = jnp.where((owner == number) & (inner < limit), 1.0, 0.0)
    copies[1].wait()
    loads = loads_ref[...]
    square = jnp.sum(loads * loads, axis=1, keepdims=True)
    copies[2].wait()
    cols_high[...], cols_low[...] = halves(cols_ref[...])
    copies[3].wait()
    couple_high[...], couple_low[...] = halves(couple_ref[...])
    put_message(loads, [square], (cols_high, cols_low), (couple_high, couple_low), masks_ref, sent_ref)


def copy_tiles(tiles_hbm, first, tiles_ref, sems):
    every = tiles_ref.shape[0] // PIECES
    pairs = [(pl.ds(first + i * every, every), pl.ds(i * every, every)) for i in range(PIECES)]
    return fetch([(tiles_hbm.at[a], tiles_ref.at[b]) for a, b in pairs], sems)


def fetch0_kernel(done_ref, tiles_hbm, rows_hbm, self_hbm, list_hbm, tiles_ref, rows_high, rows_low, self_ref, list_ref,
                  rows_ref, raw_ref, sems, other_sems):
    del done_ref
    pairs = ((list_hbm, raw_ref), (rows_hbm, rows_ref), (self_hbm, self_ref))
    copies = fetch(pairs, other_sems)
    pieces = copy_tiles(tiles_hbm, 0, tiles_ref, sems)
    copies[0].wait()
    rows = self_ref.shape[1] // tiles_ref.shape[1]
    target, source = raw_ref[0:1, :], raw_ref[1:2, :]
    group, block = lax.div(source, rows), lax.rem(source, rows)
    strip, core = lax.div(group, CORES), lax.rem(group, CORES)
    apart = jnp.where(core == lax.axis_index("clus"), 0, 1)
    list_ref[...] = jnp.concatenate([apart * rows + target, strip * rows + block], axis=0)
    copies[1].wait()
    rows_high[...], rows_low[...] = halves(rows_ref[...])
    copies[2].wait()
    for piece in pieces:
        piece.wait()


def fetch1_kernel(done_ref, tiles_hbm, tiles_ref, sems):
    del done_ref
    for piece in copy_tiles(tiles_hbm, tiles_ref.shape[0], tiles_ref, sems):
        piece.wait()


def image_of(field, far, self_ref, far_rows, near):
    rank = far_rows[0].shape[0]
    return self_ref[...] * field + near + product(far[:, :rank], far_rows[0][...], far_rows[1][...])


def step0_kernel(
    own_ref, other_ref, cols_high, cols_low, couple_high, couple_low, masks_ref, rows_high, rows_low, self_ref,
    tiles0_ref, tiles1_ref, list_vmem, sent_ref, state_ref, list_ref, sems, window, *sums,
):
    rank, panels = rows_high.shape
    nrhs = own_ref.shape[1]
    span = panels // LANES
    (copy,) = fetch(((list_vmem, list_ref),), sems)
    got = (own_ref, other_ref)
    terms, stats = message_parts(got, panels)
    beta = jnp.sqrt(stat_column(total(stats), 0, nrhs, rank))
    scale = 1.0 / beta
    both = jnp.concatenate([scale, scale], axis=0)
    for step, (inside, part) in enumerate(window_parts(got, panels)):
        put_blocks(jnp.where(inside, part * both, 0.0), step * span, window)
    basis = own_ref[lax.axis_index("strip"), :, :panels] * scale
    far = far_sum_of(terms, nrhs, rank) * scale
    copy.wait()
    near = near_field(window, (tiles0_ref, tiles1_ref), list_ref, sums, nrhs)
    image = image_of(basis, far, self_ref, (rows_high, rows_low), near)
    state_ref[...] = jnp.concatenate([far, jnp.broadcast_to(beta, far.shape)], axis=0)
    norm = jnp.sum(basis * basis, axis=1, keepdims=True)
    dot = jnp.sum(basis * image, axis=1, keepdims=True)
    share = jnp.where(norm > 0, dot / jnp.where(norm > 0, norm, 1.0), 0.0)
    rest = image - share * basis
    rest = jnp.sum(rest * rest, axis=1, keepdims=True)
    columns = [norm, dot, share, rest]
    put_message(image, columns, (cols_high, cols_low), (couple_high, couple_low), masks_ref, sent_ref)


def step1_kernel(
    own0_ref, other0_ref, own_ref, other_ref, state_ref, rows_high, rows_low, self_ref, tiles0_ref, tiles1_ref,
    list_vmem, sent_ref, basis_ref, coeff_ref, list_ref, sems, window, *sums,
):
    rank, panels = rows_high.shape
    nrhs = own_ref.shape[1]
    span = panels // LANES
    (copy,) = fetch(((list_vmem, list_ref),), sems)
    got0, got = (own0_ref, other0_ref), (own_ref, other_ref)
    beta = state_ref[nrhs:, :1]
    far0 = state_ref[:nrhs, :]
    terms, stats = message_parts(got, panels)
    summed = total(stats)
    h00 = stat_column(summed, 1, nrhs, rank)
    away = shifted(stats, 2) - shifted(summed, 1)
    rest = total(shifted(stats, 3) + stats * away * away)
    h10 = jnp.sqrt(stat_column(rest, 0, nrhs, rank))
    scale0, scale = 1.0 / beta, 1.0 / h10
    both0, both, both_h00 = (jnp.concatenate([a, a], axis=0) for a in (scale0, scale, h00))
    parts = zip(window_parts(got0, panels), window_parts(got, panels))
    for step, ((inside, part0), (_, part)) in enumerate(parts):
        part = (part - both_h00 * (part0 * both0)) * both
        put_blocks(jnp.where(inside, part, 0.0), step * span, window)
    mine = lax.axis_index("strip")
    basis0 = own0_ref[mine, :, :panels] * scale0
    basis1 = (own_ref[mine, :, :panels] - h00 * basis0) * scale
    far = (far_sum_of(terms, nrhs, rank) - h00 * far0) * scale
    copy.wait()
    near = near_field(window, (tiles0_ref, tiles1_ref), list_ref, sums, nrhs)
    image = image_of(basis1, far, self_ref, (rows_high, rows_low), near)
    columns = [jnp.sum(a * image, axis=1, keepdims=True) for a in (basis0, basis1, image)]
    sent_ref[:, 0, :] = jnp.broadcast_to(stats_row(columns, rank), (sent_ref.shape[0], LANES))
    basis_ref[...] = jnp.concatenate([basis0, basis1], axis=0)
    coeff_ref[...] = jnp.concatenate([jnp.broadcast_to(v, (nrhs, LANES)) for v in (beta, h00, h10)], axis=0)


def finish_kernel(rank, got_ref, basis_ref, coeff_ref, out_ref):
    nrhs = out_ref.shape[0]
    row = total(got_ref[:, 0, :])
    h01, h11, gram11 = (stat_column(row, k, nrhs, rank) for k in range(3))
    beta, h00, h10 = (coeff_ref[k * nrhs : (k + 1) * nrhs, :1] for k in range(3))
    gram00 = h00 * h00 + h10 * h10
    gram01 = h00 * h01 + h10 * h11
    lower00 = jnp.sqrt(gram00)
    lower10 = gram01 / lower00
    lower11 = jnp.sqrt(gram11 - lower10 * lower10)
    middle0 = beta * h00 / lower00
    middle1 = (beta * h01 - lower10 * middle0) / lower11
    y1 = middle1 / lower11
    y0 = (middle0 - lower10 * y1) / lower00
    out_ref[...] = y0 * basis_ref[:nrhs, :] + y1 * basis_ref[nrhs:, :]


def in_vmem_like(array):
    return pltpu.VMEM(array.shape, array.dtype)


def in_vmem(arrays):
    return [pltpu.with_memory_space_constraint(a, pltpu.VMEM) for a in arrays]


def call(kernel, args, outs, scratch=(), held=(), flops=0):
    args = [pltpu.with_memory_space_constraint(a, pltpu.HBM) if i in held else a for i, a in enumerate(args)]
    moved = sum(a.size * a.dtype.itemsize for a in args)
    return pl.pallas_call(
        kernel,
        out_shape=[
            jax.ShapeDtypeStruct(out, F32) if isinstance(out, tuple) else in_vmem_like(out) for out in outs
        ],
        in_specs=[pl.BlockSpec(memory_space=pl.ANY if i in held else pltpu.VMEM) for i in range(len(args))],
        out_specs=[pl.BlockSpec(memory_space=pltpu.VMEM)] * len(outs),
        scratch_shapes=list(scratch),
        compiler_params=pltpu.CompilerParams(vmem_limit_bytes=24 * 2**20),
        cost_estimate=pl.CostEstimate(flops=flops, bytes_accessed=moved, transcendentals=0),
    )(*args)


def exchanged(sent):
    got = lax.all_to_all(sent, "strip", 0, 0, tiled=True)
    return got, lax.ppermute(got, "clus", [(0, 1), (1, 0)])


def body(loads, self_term, near_tiles, near_list, far_rows, far_cols, coupling, ranks):
    nrhs, panels = loads.shape
    rank = far_cols.shape[0]
    blocks, tile = near_tiles.shape[:2]
    rows = panels // tile
    strips = coupling.shape[0] // CORES
    couple = coupling.reshape(CORES * strips * rank, rank)
    near_list = near_list.T
    ranks = ranks.reshape(1, CORES * strips)
    self_term = self_term.reshape(1, panels)
    message = (strips, nrhs, panels + LANES)
    index = pltpu.SMEM(near_list.shape, jnp.int32)
    scratch = [index, pltpu.SemaphoreType.DMA((1,)), pltpu.VMEM((3 * rows, CORES * nrhs, tile), F32)]
    scratch += [pltpu.VMEM((CORES * rows, CORES * nrhs, tile), F32)] * 4

    def twice(array):
        return [jax.ShapeDtypeStruct(array.shape, BF16)] * 2

    sent, *source_side, done = call(
        start_kernel,
        (loads, far_cols, couple, ranks),
        [message, *twice(far_cols), *twice(couple), jax.ShapeDtypeStruct((CORES * strips, CHUNK * rank), F32), (8, LANES)],
        [
            pltpu.VMEM(loads.shape, F32), pltpu.VMEM(far_cols.shape, F32), pltpu.VMEM(couple.shape, F32),
            pltpu.SMEM(ranks.shape, jnp.int32), pltpu.SemaphoreType.DMA((4,)),
        ],
        held=range(4),
    )
    part = jax.ShapeDtypeStruct((blocks // 2, tile, tile), BF16)
    tiles0, *target_side, near_list = call(
        fetch0_kernel,
        (done, near_tiles, far_rows, self_term, near_list),
        [part, *twice(far_rows), self_term, near_list],
        [
            pltpu.VMEM(far_rows.shape, F32), pltpu.VMEM(near_list.shape, jnp.int32),
            pltpu.SemaphoreType.DMA((PIECES,)), pltpu.SemaphoreType.DMA((3,)),
        ],
        held=range(1, 5),
    )
    (tiles1,) = call(
        fetch1_kernel, (done, near_tiles), [part], [pltpu.SemaphoreType.DMA((PIECES,))], held=(1,)
    )
    source_side, target_side = in_vmem(source_side), in_vmem([*target_side, tiles0, tiles1, near_list])
    got0 = exchanged(sent)
    sent, state = call(
        step0_kernel, (*got0, *source_side, *target_side), [message, (CORES * nrhs, LANES)], scratch
    )
    got1 = exchanged(sent)
    sent, basis, coeff = call(
        step1_kernel,
        (*got0, *got1, state, *target_side),
        [(CORES * strips, 1, LANES), (2 * nrhs, panels), (3 * nrhs, LANES)],
        scratch,
    )
    got = lax.all_to_all(sent, GROUP, 0, 0, tiled=True)
    return call(functools.partial(finish_kernel, rank), (got, basis, coeff), [loads.shape])[0]


def solution(mesh):
    every = ("case",) + GROUP
    in_specs = (
        P(None, every),
        P(every),
        P(every, None, None),
        P(every, None),
        P(None, every),
        P(None, every),
        P(None, GROUP, None, None),
        P(None, GROUP),
    )
    return jax.shard_map(body, mesh=mesh, in_specs=in_specs, out_specs=P(None, every), check_vma=False)
```

time: 44.5 us -> 44.5 us (level)
    pallas_call x5 -> x6, Pallas kernels: 8.5 us -> 8.59 us  [call(): pl.pallas_call(kernel, out_shape=[jax.ShapeDtypeStruct(out, F32) if isins...]
  transfers between devices with their start and end apart: 2 -> 2, of which waited for: 1 -> 1; matrix products, arithmetic and copies ran while one was open for 0% -> 0% of each run, Pallas kernels for 4% -> 6%
where the time goes in v8:
time: 44.5 us; the launch traced here: 44.2 us
  blocking collectives  34.2 us (77%)
  Pallas kernels  8.59 us (19%)
  waiting for transfers between devices  1.37 us (3%)
    all_to_all x2, blocking collectives, exchanged(): got = lax.all_to_all(sent, 'strip', 0, 0, tiled=True)  25.1 us
    all_to_all x1, blocking collectives, body(): got = lax.all_to_all(sent, GROUP, 0, 0, tiled=True)  9.12 us
    pallas_call x6, Pallas kernels, call(): pl.pallas_call(kernel, out_shape=[jax.ShapeDtypeStruct(out, F32) if isins...  8.59 us
    ppermute x2, waiting for transfers between devices, exchanged(): return (got, lax.ppermute(got, 'clus', [(0, 1), (1, 0)]))  1.37 us
  transfers between devices with their start and end apart: 2, of which 1 were waited for; matrix products, arithmetic and copies ran while one was open for 0% of the time, Pallas kernels for 6%

profile of v8, /device:TPU:0, one launch (start us, length us, event | category | flops | bytes accessed | tf_op | source)
XLA Modules:
  0.0 44.2 jit_solution(11848623403671159541)
XLA Ops:
  0.0 1.6 %shard_map.82 = (f32[8,4,1152]{2,1,0:T(4,128)S(1)}, bf16[32,1024]{1,0:T(8,128)(2,1)S(1)}, bf16[32,1024]{1,0:T(8,128)(2,1)S(1)}, bf16[512,32]{1,0:T(8,128)(2,1)S(...) custom-call(f32[4,1024]{1,0:T(4,128)} %loads_hbm.1, f32[32,1024]{1,0:T(8,128)} %cols_hbm.1, ...), custom_call_target="tpu_custom_call" | custom-call | bytes 213056 | tf_op jit(solution)/shard_map/pallas_call | solution.py:293
  1.6 14.5 %all_to_all.15.own_ref.own0_ref = f32[8,4,1152]{2,1,0:T(4,128)S(1)} all-to-all(f32[8,4,1152]{2,1,0:T(4,128)S(1)} %get-tuple-element.22), channel_id=1, replica_groups=mesh['case'=2,'strip'=8,'clus'=2] {'strip'}, dimensions={0} | all-to-all | bytes 294912 | tf_op jit(solution)/shard_map/all_to_all | solution.py:307
  16.1 0.0 collective-permute-start
  16.1 1.3 %shard_map.84.tiles1_ref = bf16[40,128,128]{2,1,0:T(8,128)(2,1)S(1)} custom-call(f32[8,128]{1,0:T(8,128)S(1)} %get-tuple-element.28.done_ref, bf16[80,128,128]{2,1,0:T(8,128)(2,1)} %tiles_hbm.3), custom_call_target="tpu_custom_call" | custom-call | bytes 2625536 | tf_op jit(solution)/shard_map/pallas_call | solution.py:293
  17.4 1.4 %shard_map.83 = (bf16[40,128,128]{2,1,0:T(8,128)(2,1)S(1)}, bf16[32,1024]{1,0:T(8,128)(2,1)S(1)}, bf16[32,1024]{1,0:T(8,128)(2,1)S(1)}, f32[1,1024]{1,0:T(1,128)S(1)}, s32[2,80]{1,0:T(2,128)S(1)}) custom-call(f32[8,128]{1,0:T(8,128)S(1)} %get-tuple-element.28.done_ref, bf16[80,128,128]{2,1,0:T(8,128)(2,1)} %tiles_hbm.3, f32[32,1024]{1,0:T(8,128)} %rows_hbm.1, ...), custom_call_target="tpu_custom_call" | custom-call | bytes 2761344 | tf_op jit(solution)/shard_map/pallas_call | solution.py:293
  18.8 0.0 collective-permute-done.other_ref.other0_ref
  18.8 1.9 %shard_map.85 = (f32[8,4,1152]{2,1,0:T(4,128)S(1)}, f32[8,128]{1,0:T(8,128)S(1)}) custom-call(f32[8,4,1152]{2,1,0:T(4,128)S(1)} %all_to_all.15.own_ref.own0_ref, f32[8,4,1152]{2,1,0:T(4,128)S(1)} %collective-permute-done.other_ref.other0_ref, bf16[32,1024]{1,0:T(8,128)(2,1)S(1)} %get-tuple-element.23.cols_high, ...), custom_call_target="tpu_custom_call" | custom-call | bytes 3281536 | tf_op jit(solution)/shard_map/pallas_call | solution.py:293
  20.7 10.6 %all_to_all.16.own_ref = f32[8,4,1152]{2,1,0:T(4,128)S(1)} all-to-all(f32[8,4,1152]{2,1,0:T(4,128)S(1)} %get-tuple-element.34), channel_id=1, replica_groups=mesh['case'=2,'strip'=8,'clus'=2] {'strip'}, dimensions={0} | all-to-all | bytes 294912 | tf_op jit(solution)/shard_map/all_to_all | solution.py:307
  31.3 0.0 collective-permute-start.1
  31.3 1.4 %collective-permute-done.1.other_ref = f32[8,4,1152]{2,1,0:T(4,128)S(1)} collective-permute-done((f32[8,4,1152]{2,1,0:T(4,128)S(1)}, f32[8,4,1152]{2,1,0:T(4,128)S(1)}, u32[]{:S(2)}, u32[]{:S(2)}) %collective-permute-start.1) | collective-permute-done | bytes 147488 | tf_op jit(solution)/shard_map/ppermute | solution.py:308
  32.7 1.6 %shard_map.86 = (f32[16,1,128]{2,1,0:T(1,128)S(1)}, f32[8,1024]{1,0:T(8,128)S(1)}, f32[12,128]{1,0:T(8,128)S(1)}) custom-call(f32[8,4,1152]{2,1,0:T(4,128)S(1)} %all_to_all.15.own_ref.own0_ref, f32[8,4,1152]{2,1,0:T(4,128)S(1)} %collective-permute-done.other_ref.other0_ref, f32[8,4,1152]{2,1,0:T(4,128)S(1)} %all_to_all.16.own_ref, ...), custom_call_target="tpu_custom_call" | custom-call | bytes 3351168 | tf_op jit(solution)/shard_map/pallas_call | solution.py:293
  34.3 9.1 %all_to_all.17.got_ref = f32[16,1,128]{2,1,0:T(1,128)S(1)} all-to-all(f32[16,1,128]{2,1,0:T(1,128)S(1)} %get-tuple-element.36), channel_id=1, replica_groups=mesh['case'=2,'strip'=8,'clus'=2] {'strip','clus'}, dimensions={0} | all-to-all | bytes 16384 | tf_op jit(solution)/shard_map/all_to_all | solution.py:365
  43.4 0.8 %shard_map.87 = f32[4,1024]{1,0:T(4,128)} custom-call(f32[16,1,128]{2,1,0:T(1,128)S(1)} %all_to_all.17.got_ref, f32[8,1024]{1,0:T(8,128)S(1)} %get-tuple-element.37.basis_ref, f32[12,128]{1,0:T(8,128)S(1)} %get-tuple-element.38.coeff_ref), custom_call_target="tpu_custom_call" | custom-call | bytes 47104 | tf_op jit(solution)/shard_map/pallas_call | solution.py:293
Async XLA Ops:
  16.1 2.7 %collective-permute-start = (f32[8,4,1152]{2,1,0:T(4,128)S(1)}, f32[8,4,1152]{2,1,0:T(4,128)S(1)}, u32[]{:S(2)}, u32[]{:S(2)}) collective-permute-start(f32[8,4,1152]{2,1,0:T(4,128)S(1)} %all_to_all.15.own_ref.own0_ref), channel_id=1, source_target_pairs={{0,1},{1,0},{2,3},{3,2},{4,5},{5,4},{6,7},{7,6},{8,9},{9,8},{10,11... | collective-permute-start | bytes 442376 | tf_op jit(solution)/shard_map/ppermute | solution.py:308
  31.3 1.4 %collective-permute-start.1 = (f32[8,4,1152]{2,1,0:T(4,128)S(1)}, f32[8,4,1152]{2,1,0:T(4,128)S(1)}, u32[]{:S(2)}, u32[]{:S(2)}) collective-permute-start(f32[8,4,1152]{2,1,0:T(4,128)S(1)} %all_to_all.16.own_ref), channel_id=1, source_target_pairs={{0,1},{1,0},{2,3},{3,2},{4,5},{5,4},{6,7},{7,6},{8,9},{9,8},{10,11... | collective-permute-start | bytes 442376 | tf_op jit(solution)/shard_map/ppermute | solution.py:308

commit v9 on v8

--- a/solution.py
+++ b/solution.py
@@ -15,6 +15,10 @@
 F32 = jnp.float32
 BF16 = jnp.bfloat16
 
+STEP = 7
+TOP = 32767.0
+ONE = float(2**30)
+
 
 def lanes_of(shape):
     return lax.broadcasted_iota(jnp.int32, shape, 1)
@@ -28,8 +32,8 @@
     return jnp.sum(rows, axis=0, keepdims=True)
 
 
-def stats_row(columns, rank):
-    shape = (columns[0].shape[0], LANES)
+def stats_row(columns, nrhs, rank):
+    shape = (nrhs, LANES)
     first = lanes_of(shape) - rank * rows_of(shape)
     spread = sum(jnp.where(first == k, column, 0.0) for k, column in enumerate(columns))
     return total(spread)
@@ -65,6 +69,27 @@
     return both[:rows] + (both[rows:] + lax.dot_general(high, right_low, dims, preferred_element_type=F32))
 
 
+def coded(value):
+    exponent = jnp.ceil(jnp.log2(jnp.maximum(jnp.abs(value), 1e-30)))
+    return (value * jnp.exp2(-exponent) * ONE).astype(jnp.int32), exponent.astype(jnp.int32)
+
+
+def decoded(mantissa, exponent):
+    return mantissa.astype(F32) * (1.0 / ONE) * jnp.exp2(exponent.astype(F32))
+
+
+def packed(field):
+    top = jnp.max(jnp.abs(field), axis=1, keepdims=True)
+    step = jnp.maximum(top, 1e-30) * (1.0 / TOP)
+    codes = jnp.floor(field * (1.0 / step) + 0.5).astype(jnp.int32)
+    width = field.shape[1] // 2
+    return (codes[:, :width] << 16) | (codes[:, width:] & 0xFFFF), step
+
+
+def unpacked(words):
+    return jnp.concatenate([words >> 16, (words << 16) >> 16], axis=1).astype(F32)
+
+
 def fetch(pairs, sems):
     copies = [pltpu.make_async_copy(a, b, sems.at[i]) for i, (a, b) in enumerate(pairs)]
     for copy in copies:
@@ -73,39 +98,46 @@
 
 
 def put_message(field, columns, cols, couple, masks_ref, sent_ref):
-    (nrhs, panels), rank = field.shape, cols[0].shape[0]
-    strips = sent_ref.shape[0]
-    half = CHUNK // 2
-    for i in range(strips):
-        sent_ref[i, :, :panels] = field
+    nrhs, rank = field.shape[0], cols[0].shape[0]
+    words, step = packed(field)
+    width = words.shape[1]
+    for i in range(sent_ref.shape[0]):
+        sent_ref[i, :, :width] = words
+    columns = columns + [0.0] * (STEP - len(columns)) + [step]
+    stats = coded(stats_row(columns, nrhs, rank))
     proj = product(field, cols[0][...], cols[1][...], 1)
     wide = jnp.concatenate([proj] * CHUNK, axis=1)
-    row = stats_row(columns, rank)
-    blank = jnp.zeros((nrhs - 3, LANES), F32)
-    for start in range(0, strips, half):
-        mask = masks_ref[pl.ds(CORES * start, CHUNK), :]
+    for start in range(0, sent_ref.shape[0], CHUNK):
+        mask = masks_ref[pl.ds(start, CHUNK), :]
         spread = jnp.concatenate([mask * wide[r : r + 1] for r in range(nrhs)], axis=0)
-        here = pl.ds(CORES * start * rank, CHUNK * rank)
+        here = pl.ds(start * rank, CHUNK * rank)
         terms = product(spread, couple[0][here, :], couple[1][here, :])
-        terms = jnp.concatenate([terms[r * CHUNK : (r + 1) * CHUNK] for r in range(nrhs)], axis=1)
-        for i in range(half):
-            tail = [terms[i : i + 1], terms[half + i : half + i + 1], row, blank]
-            sent_ref[start + i, :, panels:] = jnp.concatenate(tail, axis=0)
-
-
-def message_parts(got, panels):
-    terms = sum(jnp.sum(ref[:, :, panels:], axis=0) for ref in got)
-    terms = jnp.where(lax.axis_index("clus") == 0, terms[0:1], terms[1:2])
-    return terms, jnp.concatenate([ref[:, 2, panels:] for ref in got], axis=0)
-
-
-def window_parts(got, panels):
-    strips = got[0].shape[0]
+        terms = coded(jnp.concatenate([terms[r * CHUNK : (r + 1) * CHUNK] for r in range(nrhs)], axis=1))
+        for i in range(CHUNK):
+            tail = [term[i : i + 1] for term in terms] + list(stats)
+            sent_ref[start + i, :, width:] = jnp.concatenate(tail, axis=0)
+
+
+def message_parts(got_ref):
+    width = got_ref.shape[2] - LANES
+    terms, stats = (decoded(got_ref[:, k, width:], got_ref[:, k + 1, width:]) for k in (0, 2))
+    return total(terms), stats
+
+
+def window_parts(got_ref, rank):
+    nrhs, width = got_ref.shape[1], got_ref.shape[2] - LANES
+    strips = got_ref.shape[0] // CORES
+    shape = (CORES * nrhs, LANES)
     for step in range(3):
         owner = lax.axis_index("strip") + (step - 1)
         inside = (owner >= 0) & (owner < strips)
-        owner = jnp.clip(owner, 0, strips - 1)
-        yield inside, jnp.concatenate([ref[owner, :, :panels] for ref in got], axis=0)
+        owner = CORES * jnp.clip(owner, 0, strips - 1)
+        words = jnp.concatenate([got_ref[owner + core, :, :width] for core in range(CORES)], axis=0)
+        tails = [got_ref[owner + core, :, width:] for core in range(CORES)]
+        rows = [decoded(tail[2:3], tail[3:4]) for tail in tails]
+        rows = jnp.where(rows_of(shape) < nrhs, rows[0], rows[1])
+        wanted = lanes_of(shape) == rank * lax.rem(rows_of(shape), nrhs) + STEP
+        yield inside, unpacked(words), jnp.sum(jnp.where(wanted, rows, 0.0), axis=1, keepdims=True)
 
 
 def put_blocks(part, first, window):
@@ -131,7 +163,7 @@
 
 def start_kernel(
     loads_hbm, cols_hbm, couple_hbm, ranks_hbm, sent_ref, cols_high, cols_low, couple_high, couple_low, masks_ref,
-    done_ref, loads_ref, cols_ref, couple_ref, ranks_ref, sems,
+    loads_ref, done_ref, cols_ref, couple_ref, ranks_ref, sems,
 ):
     rank = cols_ref.shape[0]
     pairs = ((ranks_hbm, ranks_ref), (loads_hbm, loads_ref), (cols_hbm, cols_ref), (couple_hbm, couple_ref))
@@ -141,14 +173,11 @@
     shape = (CHUNK, CHUNK * rank)
     owner = lax.div(lanes_of(shape), rank)
     inner = lax.rem(lanes_of(shape), rank)
-    half = CHUNK // 2
-    number = rows_of(shape)
-    number = jnp.where(number < half, CORES * number, CORES * (number - half) + 1)
     for start in range(0, masks_ref.shape[0], CHUNK):
         limit = jnp.zeros((1, CHUNK * rank), jnp.int32)
         for i in range(CHUNK):
             limit = jnp.where(owner[:1] == i, ranks_ref[0, start + i], limit)
-        masks_ref[pl.ds(start, CHUNK), :] = jnp.where((owner == number) & (inner < limit), 1.0, 0.0)
+        masks_ref[pl.ds(start, CHUNK), :] = jnp.where((owner == rows_of(shape)) & (inner < limit), 1.0, 0.0)
     copies[1].wait()
     loads = loads_ref[...]
     square = jnp.sum(loads * loads, axis=1, keepdims=True)
@@ -176,8 +205,7 @@
     target, source = raw_ref[0:1, :], raw_ref[1:2, :]
     group, block = lax.div(source, rows), lax.rem(source, rows)
     strip, core = lax.div(group, CORES), lax.rem(group, CORES)
-    apart = jnp.where(core == lax.axis_index("clus"), 0, 1)
-    list_ref[...] = jnp.concatenate([apart * rows + target, strip * rows + block], axis=0)
+    list_ref[...] = jnp.concatenate([core * rows + target, strip * rows + block], axis=0)
     copies[1].wait()
     rows_high[...], rows_low[...] = halves(rows_ref[...])
     copies[2].wait()
@@ -197,25 +225,27 @@
 
 
 def step0_kernel(
-    own_ref, other_ref, cols_high, cols_low, couple_high, couple_low, masks_ref, rows_high, rows_low, self_ref,
-    tiles0_ref, tiles1_ref, list_vmem, sent_ref, state_ref, list_ref, sems, window, *sums,
+    got_ref, loads_ref, cols_high, cols_low, couple_high, couple_low, masks_ref, rows_high, rows_low, self_ref,
+    tiles0_ref, tiles1_ref, list_vmem, sent_ref, image_ref, window0_ref, state_ref, list_ref, sems, window, *sums,
 ):
-    rank, panels = rows_high.shape
-    nrhs = own_ref.shape[1]
-    span = panels // LANES
+    rank = rows_high.shape[0]
+    nrhs, panels = loads_ref.shape
+    span, rows = panels // LANES, CORES * nrhs
     (copy,) = fetch(((list_vmem, list_ref),), sems)
-    got = (own_ref, other_ref)
-    terms, stats = message_parts(got, panels)
+    terms, stats = message_parts(got_ref)
     beta = jnp.sqrt(stat_column(total(stats), 0, nrhs, rank))
     scale = 1.0 / beta
-    both = jnp.concatenate([scale, scale], axis=0)
-    for step, (inside, part) in enumerate(window_parts(got, panels)):
-        put_blocks(jnp.where(inside, part * both, 0.0), step * span, window)
-    basis = own_ref[lax.axis_index("strip"), :, :panels] * scale
+    both = jnp.concatenate([scale] * CORES, axis=0)
+    for step, (inside, part, unit) in enumerate(window_parts(got_ref, rank)):
+        part = jnp.where(inside, part * (unit * both), 0.0)
+        window0_ref[step * rows : (step + 1) * rows, :] = part
+        put_blocks(part, step * span, window)
+    basis = loads_ref[...] * scale
     far = far_sum_of(terms, nrhs, rank) * scale
     copy.wait()
     near = near_field(window, (tiles0_ref, tiles1_ref), list_ref, sums, nrhs)
     image = image_of(basis, far, self_ref, (rows_high, rows_low), near)
+    image_ref[...] = image
     state_ref[...] = jnp.concatenate([far, jnp.broadcast_to(beta, far.shape)], axis=0)
     norm = jnp.sum(basis * basis, axis=1, keepdims=True)
     dot = jnp.sum(basis * image, axis=1, keepdims=True)
@@ -227,37 +257,34 @@
 
 
 def step1_kernel(
-    own0_ref, other0_ref, own_ref, other_ref, state_ref, rows_high, rows_low, self_ref, tiles0_ref, tiles1_ref,
+    got_ref, loads_ref, image_ref, window0_ref, state_ref, rows_high, rows_low, self_ref, tiles0_ref, tiles1_ref,
     list_vmem, sent_ref, basis_ref, coeff_ref, list_ref, sems, window, *sums,
 ):
-    rank, panels = rows_high.shape
-    nrhs = own_ref.shape[1]
-    span = panels // LANES
+    rank = rows_high.shape[0]
+    nrhs, panels = loads_ref.shape
+    span, rows = panels // LANES, CORES * nrhs
     (copy,) = fetch(((list_vmem, list_ref),), sems)
-    got0, got = (own0_ref, other0_ref), (own_ref, other_ref)
     beta = state_ref[nrhs:, :1]
     far0 = state_ref[:nrhs, :]
-    terms, stats = message_parts(got, panels)
+    terms, stats = message_parts(got_ref)
     summed = total(stats)
     h00 = stat_column(summed, 1, nrhs, rank)
     away = shifted(stats, 2) - shifted(summed, 1)
     rest = total(shifted(stats, 3) + stats * away * away)
     h10 = jnp.sqrt(stat_column(rest, 0, nrhs, rank))
-    scale0, scale = 1.0 / beta, 1.0 / h10
-    both0, both, both_h00 = (jnp.concatenate([a, a], axis=0) for a in (scale0, scale, h00))
-    parts = zip(window_parts(got0, panels), window_parts(got, panels))
-    for step, ((inside, part0), (_, part)) in enumerate(parts):
-        part = (part - both_h00 * (part0 * both0)) * both
+    scale = 1.0 / h10
+    both, both_h00 = (jnp.concatenate([a] * CORES, axis=0) for a in (scale, h00))
+    for step, (inside, part, unit) in enumerate(window_parts(got_ref, rank)):
+        part = (part * unit - both_h00 * window0_ref[step * rows : (step + 1) * rows, :]) * both
         put_blocks(jnp.where(inside, part, 0.0), step * span, window)
-    mine = lax.axis_index("strip")
-    basis0 = own0_ref[mine, :, :panels] * scale0
-    basis1 = (own_ref[mine, :, :panels] - h00 * basis0) * scale
+    basis0 = loads_ref[...] * (1.0 / beta)
+    basis1 = (image_ref[...] - h00 * basis0) * scale
     far = (far_sum_of(terms, nrhs, rank) - h00 * far0) * scale
     copy.wait()
     near = near_field(window, (tiles0_ref, tiles1_ref), list_ref, sums, nrhs)
     image = image_of(basis1, far, self_ref, (rows_high, rows_low), near)
     columns = [jnp.sum(a * image, axis=1, keepdims=True) for a in (basis0, basis1, image)]
-    sent_ref[:, 0, :] = jnp.broadcast_to(stats_row(columns, rank), (sent_ref.shape[0], LANES))
+    sent_ref[:, 0, :] = jnp.broadcast_to(stats_row(columns, nrhs, rank), (sent_ref.shape[0], LANES))
     basis_ref[...] = jnp.concatenate([basis0, basis1], axis=0)
     coeff_ref[...] = jnp.concatenate([jnp.broadcast_to(v, (nrhs, LANES)) for v in (beta, h00, h10)], axis=0)
 
@@ -279,6 +306,10 @@
     out_ref[...] = y0 * basis_ref[:nrhs, :] + y1 * basis_ref[nrhs:, :]
 
 
+class Plain(jax.ShapeDtypeStruct):
+    pass
+
+
 def in_vmem_like(array):
     return pltpu.VMEM(array.shape, array.dtype)
 
@@ -293,7 +324,8 @@
     return pl.pallas_call(
         kernel,
         out_shape=[
-            jax.ShapeDtypeStruct(out, F32) if isinstance(out, tuple) else in_vmem_like(out) for out in outs
+            jax.ShapeDtypeStruct(out, F32) if isinstance(out, tuple) else out if isinstance(out, Plain) else in_vmem_like(out)
+            for out in outs
         ],
         in_specs=[pl.BlockSpec(memory_space=pl.ANY if i in held else pltpu.VMEM) for i in range(len(args))],
         out_specs=[pl.BlockSpec(memory_space=pltpu.VMEM)] * len(outs),
@@ -304,8 +336,7 @@
 
 
 def exchanged(sent):
-    got = lax.all_to_all(sent, "strip", 0, 0, tiled=True)
-    return got, lax.ppermute(got, "clus", [(0, 1), (1, 0)])
+    return lax.all_to_all(sent, GROUP, 0, 0, tiled=True)
 
 
 def body(loads, self_term, near_tiles, near_list, far_rows, far_cols, coupling, ranks):
@@ -318,7 +349,8 @@
     near_list = near_list.T
     ranks = ranks.reshape(1, CORES * strips)
     self_term = self_term.reshape(1, panels)
-    message = (strips, nrhs, panels + LANES)
+    groups = CORES * strips
+    message = Plain((groups, nrhs, panels // 2 + LANES), jnp.int32)
     index = pltpu.SMEM(near_list.shape, jnp.int32)
     scratch = [index, pltpu.SemaphoreType.DMA((1,)), pltpu.VMEM((3 * rows, CORES * nrhs, tile), F32)]
     scratch += [pltpu.VMEM((CORES * rows, CORES * nrhs, tile), F32)] * 4
@@ -326,12 +358,12 @@
     def twice(array):
         return [jax.ShapeDtypeStruct(array.shape, BF16)] * 2
 
-    sent, *source_side, done = call(
+    sent, *source_side, loads, done = call(
         start_kernel,
         (loads, far_cols, couple, ranks),
-        [message, *twice(far_cols), *twice(couple), jax.ShapeDtypeStruct((CORES * strips, CHUNK * rank), F32), (8, LANES)],
+        [message, *twice(far_cols), *twice(couple), jax.ShapeDtypeStruct((groups, CHUNK * rank), F32), loads, (8, LANES)],
         [
-            pltpu.VMEM(loads.shape, F32), pltpu.VMEM(far_cols.shape, F32), pltpu.VMEM(couple.shape, F32),
+            pltpu.VMEM(far_cols.shape, F32), pltpu.VMEM(couple.shape, F32),
             pltpu.SMEM(ranks.shape, jnp.int32), pltpu.SemaphoreType.DMA((4,)),
         ],
         held=range(4),
@@ -350,20 +382,21 @@
     (tiles1,) = call(
         fetch1_kernel, (done, near_tiles), [part], [pltpu.SemaphoreType.DMA((PIECES,))], held=(1,)
     )
-    source_side, target_side = in_vmem(source_side), in_vmem([*target_side, tiles0, tiles1, near_list])
-    got0 = exchanged(sent)
-    sent, state = call(
-        step0_kernel, (*got0, *source_side, *target_side), [message, (CORES * nrhs, LANES)], scratch
-    )
-    got1 = exchanged(sent)
+    source_side, target_side = in_vmem([loads, *source_side]), in_vmem([*target_side, tiles0, tiles1, near_list])
+    loads = source_side[0]
+    sent, image, window0, state = call(
+        step0_kernel,
+        (exchanged(sent), *source_side, *target_side),
+        [message, loads.shape, (3 * CORES * nrhs, panels), (CORES * nrhs, LANES)],
+        scratch,
+    )
     sent, basis, coeff = call(
         step1_kernel,
-        (*got0, *got1, state, *target_side),
-        [(CORES * strips, 1, LANES), (2 * nrhs, panels), (3 * nrhs, LANES)],
+        (exchanged(sent), loads, image, window0, state, *target_side),
+        [(groups, 1, LANES), (2 * nrhs, panels), (3 * nrhs, LANES)],
         scratch,
     )
-    got = lax.all_to_all(sent, GROUP, 0, 0, tiled=True)
-    return call(functools.partial(finish_kernel, rank), (got, basis, coeff), [loads.shape])[0]
+    return call(functools.partial(finish_kernel, rank), (exchanged(sent), basis, coeff), [loads.shape])[0]
 
 
 def solution(mesh):

time: 44.5 us -> 42.7 us (0.960)
  blocking collectives: 34.2 us -> 20 us
  starting transfers between devices: 0.01 us -> 7.37 us
  waiting for transfers between devices: 1.37 us -> 5.73 us
  Pallas kernels: 8.59 us -> 9.19 us
    all_to_all x3 -> x2, blocking collectives: 34.2 us -> 20 us  [exchanged(): return lax.all_to_all(sent, GROUP, 0, 0, tiled=True)]
    all_to_all x0 -> x1, starting transfers between devices: none -> 7.37 us  [exchanged(): return lax.all_to_all(sent, GROUP, 0, 0, tiled=True)]
    all_to_all x0 -> x1, waiting for transfers between devices: none -> 5.73 us  [exchanged(): return lax.all_to_all(sent, GROUP, 0, 0, tiled=True)]
    ppermute x2 -> x0, waiting for transfers between devices: 1.37 us -> none  [exchanged(): return (got, lax.ppermute(got, 'clus', [(0, 1), (1, 0)]))]
    pallas_call x6, Pallas kernels: 8.59 us -> 9.19 us  [call(): pl.pallas_call(kernel, out_shape=[jax.ShapeDtypeStruct(out, F32) if isins...]
  transfers between devices with their start and end apart: 2 -> 1, of which waited for: 1 -> 1; matrix products, arithmetic and copies ran while one was open for 0% -> 0% of each run, Pallas kernels for 6% -> 6%
where the time goes in v9:
time: 42.7 us; the launch traced here: 42.4 us
  blocking collectives  20 us (47%)
  Pallas kernels  9.19 us (22%)
  starting transfers between devices  7.37 us (17%)
  waiting for transfers between devices  5.73 us (13%)
    all_to_all x2, blocking collectives, exchanged(): return lax.all_to_all(sent, GROUP, 0, 0, tiled=True)  20 us
    pallas_call x6, Pallas kernels, call(): pl.pallas_call(kernel, out_shape=[jax.ShapeDtypeStruct(out, F32) if isins...  9.19 us
    all_to_all x1, starting transfers between devices, exchanged(): return lax.all_to_all(sent, GROUP, 0, 0, tiled=True)  7.37 us
    all_to_all x1, waiting for transfers between devices, exchanged(): return lax.all_to_all(sent, GROUP, 0, 0, tiled=True)  5.73 us
  transfers between devices with their start and end apart: 1, of which 1 were waited for; matrix products, arithmetic and copies ran while one was open for 0% of the time, Pallas kernels for 6%

profile of v9, /device:TPU:0, one launch (start us, length us, event | category | flops | bytes accessed | tf_op | source)
XLA Modules:
  0.0 42.4 jit_solution(10959202670470988259)
XLA Ops:
  0.0 2.2 %shard_map.82 = (s32[16,4,640]{2,1,0:T(4,128)}, bf16[32,1024]{1,0:T(8,128)(2,1)S(1)}, bf16[32,1024]{1,0:T(8,128)(2,1)S(1)}, bf16[512,32]{1,0:T(8,128)(2,1)S(1)},...) custom-call(f32[4,1024]{1,0:T(4,128)} %loads_hbm.1, ...), custom_call_target="tpu_custom_call" | custom-call | bytes 213056 | tf_op jit(solution)/shard_map/pallas_call | solution.py:324
  2.3 7.4 %all-to-all-start = ((s32[16,4,640]{2,1,0:T(4,128)}), s32[16,4,640]{2,1,0:T(4,128)S(1)}, u32[]{:S(2)}, u32[]{:S(2)}) async-start(s32[16,4,640]{2,1,0:T(4,128)} %get-tuple-element.25), calls=%async_computation | async-start | bytes 327680 | tf_op jit(solution)/shard_map/all_to_all | solution.py:339
  9.6 1.3 %shard_map.84.tiles1_ref = bf16[40,128,128]{2,1,0:T(8,128)(2,1)S(1)} custom-call(f32[8,128]{1,0:T(8,128)S(1)} %get-tuple-element.32.done_ref, bf16[80,128,128]{2,1,0:T(8,128)(2,1)} %tiles_hbm.3), custom_call_target="tpu_custom_call" | custom-call | bytes 2625536 | tf_op jit(solution)/shard_map/pallas_call | solution.py:324
  11.0 1.4 %shard_map.83 = (bf16[40,128,128]{2,1,0:T(8,128)(2,1)S(1)}, bf16[32,1024]{1,0:T(8,128)(2,1)S(1)}, bf16[32,1024]{1,0:T(8,128)(2,1)S(1)}, f32[1,1024]{1,0:T(1,128)S(1)}, s32[2,80]{1,0:T(2,128)S(1)}) custom-call(f32[8,128]{1,0:T(8,128)S(1)} %get-tuple-element.32.done_ref, bf16[80,128,128]{2,1,0:T(8,128)(2,1)} %tiles_hbm.3, f32[32,1024]{1,0:T(8,128)} %rows_hbm.1, ...), custom_call_target="tpu_custom_call" | custom-call | bytes 2761344 | tf_op jit(solution)/shard_map/pallas_call | solution.py:324
  12.4 5.7 %all-to-all-done.got_ref = s32[16,4,640]{2,1,0:T(4,128)S(1)} async-done(((s32[16,4,640]{2,1,0:T(4,128)}), s32[16,4,640]{2,1,0:T(4,128)S(1)}, u32[]{:S(2)}, u32[]{:S(2)}) %all-to-all-start) | async-done | bytes 163872 | tf_op jit(solution)/shard_map/all_to_all | solution.py:339
  18.1 1.9 %shard_map.85 = (s32[16,4,640]{2,1,0:T(4,128)S(1)}, f32[4,1024]{1,0:T(4,128)S(1)}, f32[24,1024]{1,0:T(8,128)S(1)}, f32[8,128]{1,0:T(8,128)S(1)}) custom-call(s32[16,4,640]{2,1,0:T(4,128)S(1)} %all-to-all-done.got_ref, f32[4,1024]{1,0:T(4,128)S(1)} %get-tuple-element.26.loads_ref, bf16[32,1024]{1,0:T(8,128)(2,1)S(1)} %get-tuple-element.27.cols_high, ...), custom_call_target="tpu_custom_call" | custom-call | bytes 3166848 | tf_op jit(solution)/shard_map/pallas_call | solution.py:324
  20.0 11.1 %all_to_all.15.got_ref = s32[16,4,640]{2,1,0:T(4,128)S(1)} all-to-all(s32[16,4,640]{2,1,0:T(4,128)S(1)} %get-tuple-element.38), channel_id=1, replica_groups=mesh['case'=2,'strip'=8,'clus'=2] {'strip','clus'}, dimensions={0} | all-to-all | bytes 327680 | tf_op jit(solution)/shard_map/all_to_all | solution.py:339
  31.1 1.5 %shard_map.86 = (f32[16,1,128]{2,1,0:T(1,128)S(1)}, f32[8,1024]{1,0:T(8,128)S(1)}, f32[12,128]{1,0:T(8,128)S(1)}) custom-call(s32[16,4,640]{2,1,0:T(4,128)S(1)} %all_to_all.15.got_ref, f32[4,1024]{1,0:T(4,128)S(1)} %get-tuple-element.26.loads_ref, f32[4,1024]{1,0:T(4,128)S(1)} %get-tuple-element.39.image_ref, f32[24,1024]{1,0:T(8,128)S(1)} %get-tuple-element.40.window0_ref, ...), custom_call_target="tpu_custom_call" | custom-call | bytes 3056256 | tf_op jit(solution)/shard_map/pallas_call | solution.py:324
  32.6 9.0 %all_to_all.16.got_ref = f32[16,1,128]{2,1,0:T(1,128)S(1)} all-to-all(f32[16,1,128]{2,1,0:T(1,128)S(1)} %get-tuple-element.42), channel_id=1, replica_groups=mesh['case'=2,'strip'=8,'clus'=2] {'strip','clus'}, dimensions={0} | all-to-all | bytes 16384 | tf_op jit(solution)/shard_map/all_to_all | solution.py:339
  41.6 0.8 %shard_map.87 = f32[4,1024]{1,0:T(4,128)} custom-call(f32[16,1,128]{2,1,0:T(1,128)S(1)} %all_to_all.16.got_ref, f32[8,1024]{1,0:T(8,128)S(1)} %get-tuple-element.43.basis_ref, f32[12,128]{1,0:T(8,128)S(1)} %get-tuple-element.44.coeff_ref), custom_call_target="tpu_custom_call" | custom-call | bytes 47104 | tf_op jit(solution)/shard_map/pallas_call | solution.py:324
Async XLA Ops:
  2.3 15.8 %all-to-all-start = ((s32[16,4,640]{2,1,0:T(4,128)}), s32[16,4,640]{2,1,0:T(4,128)S(1)}, u32[]{:S(2)}, u32[]{:S(2)}) async-start(s32[16,4,640]{2,1,0:T(4,128)} %get-tuple-element.25), calls=%async_computation | async-start | bytes 327680 | tf_op jit(solution)/shard_map/all_to_all | solution.py:339

commit v10 on v9

--- a/solution.py
+++ b/solution.py
@@ -15,7 +15,9 @@
 F32 = jnp.float32
 BF16 = jnp.bfloat16
 
-STEP = 7
+STEP = 8
+COLS_TOP = 0.1875
+COUPLE_TOP = 0.375
 TOP = 32767.0
 ONE = float(2**30)
 
@@ -32,11 +34,22 @@
     return jnp.sum(rows, axis=0, keepdims=True)
 
 
-def stats_row(columns, nrhs, rank):
-    shape = (nrhs, LANES)
+def stats_row(columns, rank, step=None):
+    shape = (columns[0].shape[0], LANES)
     first = lanes_of(shape) - rank * rows_of(shape)
     spread = sum(jnp.where(first == k, column, 0.0) for k, column in enumerate(columns))
+    if step is not None:
+        spread = jnp.where((first >= STEP) & (first < rank), step, spread)
     return total(spread)
+
+
+def steps_of(stats, rank):
+    inner = lax.rem(lanes_of(stats.shape), rank)
+    return jnp.where(inner < STEP, shifted(stats, STEP), stats)
+
+
+def term_unit(panels, rank):
+    return panels * rank * COLS_TOP * COUPLE_TOP * TOP / ONE
 
 
 def stat_column(row, k, nrhs, rank):
@@ -99,28 +112,31 @@
 
 def put_message(field, columns, cols, couple, masks_ref, sent_ref):
     nrhs, rank = field.shape[0], cols[0].shape[0]
+    unit = term_unit(field.shape[1], rank)
+    proj = product(field, cols[0][...], cols[1][...], 1)
+    wide = jnp.concatenate([proj] * CHUNK, axis=1)
     words, step = packed(field)
     width = words.shape[1]
+    row = stats_row(columns, rank, step)
+    finer = 1.0 / (steps_of(row, rank) * unit)
     for i in range(sent_ref.shape[0]):
         sent_ref[i, :, :width] = words
-    columns = columns + [0.0] * (STEP - len(columns)) + [step]
-    stats = coded(stats_row(columns, nrhs, rank))
-    proj = product(field, cols[0][...], cols[1][...], 1)
-    wide = jnp.concatenate([proj] * CHUNK, axis=1)
+    stats = [jnp.broadcast_to(a, (CHUNK, LANES)) for a in coded(row)]
     for start in range(0, sent_ref.shape[0], CHUNK):
         mask = masks_ref[pl.ds(start, CHUNK), :]
         spread = jnp.concatenate([mask * wide[r : r + 1] for r in range(nrhs)], axis=0)
         here = pl.ds(start * rank, CHUNK * rank)
         terms = product(spread, couple[0][here, :], couple[1][here, :])
-        terms = coded(jnp.concatenate([terms[r * CHUNK : (r + 1) * CHUNK] for r in range(nrhs)], axis=1))
-        for i in range(CHUNK):
-            tail = [term[i : i + 1] for term in terms] + list(stats)
-            sent_ref[start + i, :, width:] = jnp.concatenate(tail, axis=0)
-
-
-def message_parts(got_ref):
+        terms = jnp.concatenate([terms[r * CHUNK : (r + 1) * CHUNK] for r in range(nrhs)], axis=1)
+        here = pl.ds(start, CHUNK)
+        for k, value in enumerate([(terms * finer).astype(jnp.int32)] + stats + [stats[0]] * (nrhs - 3)):
+            sent_ref[here, k, width:] = value
+
+
+def message_parts(got_ref, rank):
     width = got_ref.shape[2] - LANES
-    terms, stats = (decoded(got_ref[:, k, width:], got_ref[:, k + 1, width:]) for k in (0, 2))
+    stats = decoded(got_ref[:, 1, width:], got_ref[:, 2, width:])
+    terms = got_ref[:, 0, width:].astype(F32) * (steps_of(stats, rank) * term_unit(2 * width, rank))
     return total(terms), stats
 
 
@@ -134,7 +150,7 @@
         owner = CORES * jnp.clip(owner, 0, strips - 1)
         words = jnp.concatenate([got_ref[owner + core, :, :width] for core in range(CORES)], axis=0)
         tails = [got_ref[owner + core, :, width:] for core in range(CORES)]
-        rows = [decoded(tail[2:3], tail[3:4]) for tail in tails]
+        rows = [decoded(tail[1:2], tail[2:3]) for tail in tails]
         rows = jnp.where(rows_of(shape) < nrhs, rows[0], rows[1])
         wanted = lanes_of(shape) == rank * lax.rem(rows_of(shape), nrhs) + STEP
         yield inside, unpacked(words), jnp.sum(jnp.where(wanted, rows, 0.0), axis=1, keepdims=True)
@@ -151,11 +167,20 @@
         held[...] = jnp.zeros_like(held)
     n = 0
     for tiles_ref in tiles:
-        for i in range(tiles_ref.shape[0]):
-            held = sums[n % len(sums)]
-            source = window[list_ref[1, n]].astype(BF16)
-            held[list_ref[0, n]] += jnp.dot(source, tiles_ref[i], preferred_element_type=F32)
-            n += 1
+        for first in range(0, tiles_ref.shape[0], 4):
+            sources = [window[list_ref[1, n + i]] for i in range(4)]
+            blank = jnp.zeros_like(sources[0])
+            upper = [sources[0], blank, sources[2], blank]
+            lower = [blank, sources[1], blank, sources[3]]
+            left = jnp.concatenate([jnp.concatenate(a, axis=0).astype(BF16) for a in (upper, lower)], axis=1)
+            four = [tiles_ref[first + i] for i in range(4)]
+            right = [jnp.concatenate([four[i], four[i + 2]], axis=1) for i in range(2)]
+            both = jnp.dot(left, jnp.concatenate(right, axis=0), preferred_element_type=F32)
+            for i, held in enumerate(sums):
+                side = i // 2 * LANES
+                rows = i * window.shape[1]
+                held[list_ref[0, n + i]] += both[rows : rows + window.shape[1], side : side + LANES]
+            n += 4
     whole = sum((held[...] for held in sums[1:]), sums[0][...])
     rows = whole.shape[0] // CORES
     return jnp.concatenate([whole[b, :nrhs] + whole[rows + b, nrhs:] for b in range(rows)], axis=1)
@@ -166,10 +191,17 @@
     loads_ref, done_ref, cols_ref, couple_ref, ranks_ref, sems,
 ):
     rank = cols_ref.shape[0]
-    pairs = ((ranks_hbm, ranks_ref), (loads_hbm, loads_ref), (cols_hbm, cols_ref), (couple_hbm, couple_ref))
+    pairs = ((loads_hbm, loads_ref), (cols_hbm, cols_ref), (couple_hbm, couple_ref), (ranks_hbm, ranks_ref))
     copies = fetch(pairs, sems)
     done_ref[...] = jnp.zeros_like(done_ref)
     copies[0].wait()
+    loads = loads_ref[...]
+    square = jnp.sum(loads * loads, axis=1, keepdims=True)
+    copies[1].wait()
+    cols_high[...], cols_low[...] = halves(cols_ref[...])
+    copies[2].wait()
+    couple_high[...], couple_low[...] = halves(couple_ref[...])
+    copies[3].wait()
     shape = (CHUNK, CHUNK * rank)
     owner = lax.div(lanes_of(shape), rank)
     inner = lax.rem(lanes_of(shape), rank)
@@ -178,13 +210,6 @@
         for i in range(CHUNK):
             limit = jnp.where(owner[:1] == i, ranks_ref[0, start + i], limit)
         masks_ref[pl.ds(start, CHUNK), :] = jnp.where((owner == rows_of(shape)) & (inner < limit), 1.0, 0.0)
-    copies[1].wait()
-    loads = loads_ref[...]
-    square = jnp.sum(loads * loads, axis=1, keepdims=True)
-    copies[2].wait()
-    cols_high[...], cols_low[...] = halves(cols_ref[...])
-    copies[3].wait()
-    couple_high[...], couple_low[...] = halves(couple_ref[...])
     put_message(loads, [square], (cols_high, cols_low), (couple_high, couple_low), masks_ref, sent_ref)
 
 
@@ -232,7 +257,7 @@
     nrhs, panels = loads_ref.shape
     span, rows = panels // LANES, CORES * nrhs
     (copy,) = fetch(((list_vmem, list_ref),), sems)
-    terms, stats = message_parts(got_ref)
+    terms, stats = message_parts(got_ref, rank)
     beta = jnp.sqrt(stat_column(total(stats), 0, nrhs, rank))
     scale = 1.0 / beta
     both = jnp.concatenate([scale] * CORES, axis=0)
@@ -266,7 +291,7 @@
     (copy,) = fetch(((list_vmem, list_ref),), sems)
     beta = state_ref[nrhs:, :1]
     far0 = state_ref[:nrhs, :]
-    terms, stats = message_parts(got_ref)
+    terms, stats = message_parts(got_ref, rank)
     summed = total(stats)
     h00 = stat_column(summed, 1, nrhs, rank)
     away = shifted(stats, 2) - shifted(summed, 1)
@@ -284,7 +309,7 @@
     near = near_field(window, (tiles0_ref, tiles1_ref), list_ref, sums, nrhs)
     image = image_of(basis1, far, self_ref, (rows_high, rows_low), near)
     columns = [jnp.sum(a * image, axis=1, keepdims=True) for a in (basis0, basis1, image)]
-    sent_ref[:, 0, :] = jnp.broadcast_to(stats_row(columns, nrhs, rank), (sent_ref.shape[0], LANES))
+    sent_ref[:, 0, :] = jnp.broadcast_to(stats_row(columns, rank), (sent_ref.shape[0], LANES))
     basis_ref[...] = jnp.concatenate([basis0, basis1], axis=0)
     coeff_ref[...] = jnp.concatenate([jnp.broadcast_to(v, (nrhs, LANES)) for v in (beta, h00, h10)], axis=0)
 

time: 42.7 us -> 42.3 us (level)
  Pallas kernels: 9.19 us -> 8.75 us
    pallas_call x6, Pallas kernels: 9.19 us -> 8.75 us  [call(): pl.pallas_call(kernel, out_shape=[jax.ShapeDtypeStruct(out, F32) if isins...]
where the time goes in v10:
time: 42.3 us; the launch traced here: 41.9 us
  blocking collectives  20 us (47%)
  Pallas kernels  8.75 us (21%)
  starting transfers between devices  7.37 us (17%)
  waiting for transfers between devices  5.73 us (14%)
    all_to_all x2, blocking collectives, exchanged(): return lax.all_to_all(sent, GROUP, 0, 0, tiled=True)  20 us
    pallas_call x6, Pallas kernels, call(): pl.pallas_call(kernel, out_shape=[jax.ShapeDtypeStruct(out, F32) if isins...  8.75 us
    all_to_all x1, starting transfers between devices, exchanged(): return lax.all_to_all(sent, GROUP, 0, 0, tiled=True)  7.37 us
    all_to_all x1, waiting for transfers between devices, exchanged(): return lax.all_to_all(sent, GROUP, 0, 0, tiled=True)  5.73 us
  transfers between devices with their start and end apart: 1, of which 1 were waited for; matrix products, arithmetic and copies ran while one was open for 0% of the time, Pallas kernels for 6%

profile of v10, /device:TPU:0, one launch (start us, length us, event | category | flops | bytes accessed | tf_op | source)
XLA Modules:
  0.0 41.9 jit_solution(4106573943392583571)
XLA Ops:
  0.0 2.3 %shard_map.82 = (s32[16,4,640]{2,1,0:T(4,128)}, bf16[32,1024]{1,0:T(8,128)(2,1)S(1)}, bf16[32,1024]{1,0:T(8,128)(2,1)S(1)}, bf16[512,32]{1,0:T(8,128)(2,1)S(1)},...) custom-call(f32[4,1024]{1,0:T(4,128)} %loads_hbm.1, ...), custom_call_target="tpu_custom_call" | custom-call | bytes 213056 | tf_op jit(solution)/shard_map/pallas_call | solution.py:349
  2.3 7.4 %all-to-all-start = ((s32[16,4,640]{2,1,0:T(4,128)}), s32[16,4,640]{2,1,0:T(4,128)S(1)}, u32[]{:S(2)}, u32[]{:S(2)}) async-start(s32[16,4,640]{2,1,0:T(4,128)} %get-tuple-element.25), calls=%async_computation | async-start | bytes 327680 | tf_op jit(solution)/shard_map/all_to_all | solution.py:364
  9.7 1.3 %shard_map.84.tiles1_ref = bf16[40,128,128]{2,1,0:T(8,128)(2,1)S(1)} custom-call(f32[8,128]{1,0:T(8,128)S(1)} %get-tuple-element.32.done_ref, bf16[80,128,128]{2,1,0:T(8,128)(2,1)} %tiles_hbm.3), custom_call_target="tpu_custom_call" | custom-call | bytes 2625536 | tf_op jit(solution)/shard_map/pallas_call | solution.py:349
  11.0 1.4 %shard_map.83 = (bf16[40,128,128]{2,1,0:T(8,128)(2,1)S(1)}, bf16[32,1024]{1,0:T(8,128)(2,1)S(1)}, bf16[32,1024]{1,0:T(8,128)(2,1)S(1)}, f32[1,1024]{1,0:T(1,128)S(1)}, s32[2,80]{1,0:T(2,128)S(1)}) custom-call(f32[8,128]{1,0:T(8,128)S(1)} %get-tuple-element.32.done_ref, bf16[80,128,128]{2,1,0:T(8,128)(2,1)} %tiles_hbm.3, f32[32,1024]{1,0:T(8,128)} %rows_hbm.1, ...), custom_call_target="tpu_custom_call" | custom-call | bytes 2761344 | tf_op jit(solution)/shard_map/pallas_call | solution.py:349
  12.4 5.7 %all-to-all-done.got_ref = s32[16,4,640]{2,1,0:T(4,128)S(1)} async-done(((s32[16,4,640]{2,1,0:T(4,128)}), s32[16,4,640]{2,1,0:T(4,128)S(1)}, u32[]{:S(2)}, u32[]{:S(2)}) %all-to-all-start) | async-done | bytes 163872 | tf_op jit(solution)/shard_map/all_to_all | solution.py:364
  18.1 1.7 %shard_map.85 = (s32[16,4,640]{2,1,0:T(4,128)S(1)}, f32[4,1024]{1,0:T(4,128)S(1)}, f32[24,1024]{1,0:T(8,128)S(1)}, f32[8,128]{1,0:T(8,128)S(1)}) custom-call(s32[16,4,640]{2,1,0:T(4,128)S(1)} %all-to-all-done.got_ref, f32[4,1024]{1,0:T(4,128)S(1)} %get-tuple-element.26.loads_ref, bf16[32,1024]{1,0:T(8,128)(2,1)S(1)} %get-tuple-element.27.cols_high, ...), custom_call_target="tpu_custom_call" | custom-call | bytes 3166848 | tf_op jit(solution)/shard_map/pallas_call | solution.py:349
  19.8 11.1 %all_to_all.15.got_ref = s32[16,4,640]{2,1,0:T(4,128)S(1)} all-to-all(s32[16,4,640]{2,1,0:T(4,128)S(1)} %get-tuple-element.38), channel_id=1, replica_groups=mesh['case'=2,'strip'=8,'clus'=2] {'strip','clus'}, dimensions={0} | all-to-all | bytes 327680 | tf_op jit(solution)/shard_map/all_to_all | solution.py:364
  30.9 1.3 %shard_map.86 = (f32[16,1,128]{2,1,0:T(1,128)S(1)}, f32[8,1024]{1,0:T(8,128)S(1)}, f32[12,128]{1,0:T(8,128)S(1)}) custom-call(s32[16,4,640]{2,1,0:T(4,128)S(1)} %all_to_all.15.got_ref, f32[4,1024]{1,0:T(4,128)S(1)} %get-tuple-element.26.loads_ref, f32[4,1024]{1,0:T(4,128)S(1)} %get-tuple-element.39.image_ref, f32[24,1024]{1,0:T(8,128)S(1)} %get-tuple-element.40.window0_ref, ...), custom_call_target="tpu_custom_call" | custom-call | bytes 3056256 | tf_op jit(solution)/shard_map/pallas_call | solution.py:349
  32.1 9.0 %all_to_all.16.got_ref = f32[16,1,128]{2,1,0:T(1,128)S(1)} all-to-all(f32[16,1,128]{2,1,0:T(1,128)S(1)} %get-tuple-element.42), channel_id=1, replica_groups=mesh['case'=2,'strip'=8,'clus'=2] {'strip','clus'}, dimensions={0} | all-to-all | bytes 16384 | tf_op jit(solution)/shard_map/all_to_all | solution.py:364
  41.1 0.8 %shard_map.87 = f32[4,1024]{1,0:T(4,128)} custom-call(f32[16,1,128]{2,1,0:T(1,128)S(1)} %all_to_all.16.got_ref, f32[8,1024]{1,0:T(8,128)S(1)} %get-tuple-element.43.basis_ref, f32[12,128]{1,0:T(8,128)S(1)} %get-tuple-element.44.coeff_ref), custom_call_target="tpu_custom_call" | custom-call | bytes 47104 | tf_op jit(solution)/shard_map/pallas_call | solution.py:349
Async XLA Ops:
  2.3 15.8 %all-to-all-start = ((s32[16,4,640]{2,1,0:T(4,128)}), s32[16,4,640]{2,1,0:T(4,128)S(1)}, u32[]{:S(2)}, u32[]{:S(2)}) async-start(s32[16,4,640]{2,1,0:T(4,128)} %get-tuple-element.25), calls=%async_computation | async-start | bytes 327680 | tf_op jit(solution)/shard_map/all_to_all | solution.py:364

commit v11 on v10

--- a/solution.py
+++ b/solution.py
@@ -375,7 +375,7 @@
     ranks = ranks.reshape(1, CORES * strips)
     self_term = self_term.reshape(1, panels)
     groups = CORES * strips
-    message = Plain((groups, nrhs, panels // 2 + LANES), jnp.int32)
+    message = jax.ShapeDtypeStruct((groups, nrhs, panels // 2 + LANES), jnp.int32)
     index = pltpu.SMEM(near_list.shape, jnp.int32)
     scratch = [index, pltpu.SemaphoreType.DMA((1,)), pltpu.VMEM((3 * rows, CORES * nrhs, tile), F32)]
     scratch += [pltpu.VMEM((CORES * rows, CORES * nrhs, tile), F32)] * 4

time: 42.3 us -> 42.3 us (level)
  no operation moved by 1% of the time
where the time goes in v11:
time: 42.3 us; the launch traced here: 41.9 us
  blocking collectives  20 us (47%)
  Pallas kernels  8.75 us (21%)
  starting transfers between devices  7.37 us (17%)
  waiting for transfers between devices  5.73 us (14%)
    all_to_all x2, blocking collectives, exchanged(): return lax.all_to_all(sent, GROUP, 0, 0, tiled=True)  20 us
    pallas_call x6, Pallas kernels, call(): pl.pallas_call(kernel, out_shape=[jax.ShapeDtypeStruct(out, F32) if isins...  8.75 us
    all_to_all x1, starting transfers between devices, exchanged(): return lax.all_to_all(sent, GROUP, 0, 0, tiled=True)  7.37 us
    all_to_all x1, waiting for transfers between devices, exchanged(): return lax.all_to_all(sent, GROUP, 0, 0, tiled=True)  5.73 us
  transfers between devices with their start and end apart: 1, of which 1 were waited for; matrix products, arithmetic and copies ran while one was open for 0% of the time, Pallas kernels for 6%

profile of v11, /device:TPU:0, one launch (start us, length us, event | category | flops | bytes accessed | tf_op | source)
XLA Modules:
  0.0 41.9 jit_solution(4106573943392583571)
XLA Ops:
  0.0 2.3 %shard_map.82 = (s32[16,4,640]{2,1,0:T(4,128)}, bf16[32,1024]{1,0:T(8,128)(2,1)S(1)}, bf16[32,1024]{1,0:T(8,128)(2,1)S(1)}, bf16[512,32]{1,0:T(8,128)(2,1)S(1)},...) custom-call(f32[4,1024]{1,0:T(4,128)} %loads_hbm.1, ...), custom_call_target="tpu_custom_call" | custom-call | bytes 213056 | tf_op jit(solution)/shard_map/pallas_call | solution.py:349
  2.3 7.4 %all-to-all-start = ((s32[16,4,640]{2,1,0:T(4,128)}), s32[16,4,640]{2,1,0:T(4,128)S(1)}, u32[]{:S(2)}, u32[]{:S(2)}) async-start(s32[16,4,640]{2,1,0:T(4,128)} %get-tuple-element.25), calls=%async_computation | async-start | bytes 327680 | tf_op jit(solution)/shard_map/all_to_all | solution.py:364
  9.7 1.3 %shard_map.84.tiles1_ref = bf16[40,128,128]{2,1,0:T(8,128)(2,1)S(1)} custom-call(f32[8,128]{1,0:T(8,128)S(1)} %get-tuple-element.32.done_ref, bf16[80,128,128]{2,1,0:T(8,128)(2,1)} %tiles_hbm.3), custom_call_target="tpu_custom_call" | custom-call | bytes 2625536 | tf_op jit(solution)/shard_map/pallas_call | solution.py:349
  11.0 1.4 %shard_map.83 = (bf16[40,128,128]{2,1,0:T(8,128)(2,1)S(1)}, bf16[32,1024]{1,0:T(8,128)(2,1)S(1)}, bf16[32,1024]{1,0:T(8,128)(2,1)S(1)}, f32[1,1024]{1,0:T(1,128)S(1)}, s32[2,80]{1,0:T(2,128)S(1)}) custom-call(f32[8,128]{1,0:T(8,128)S(1)} %get-tuple-element.32.done_ref, bf16[80,128,128]{2,1,0:T(8,128)(2,1)} %tiles_hbm.3, f32[32,1024]{1,0:T(8,128)} %rows_hbm.1, ...), custom_call_target="tpu_custom_call" | custom-call | bytes 2761344 | tf_op jit(solution)/shard_map/pallas_call | solution.py:349
  12.4 5.7 %all-to-all-done.got_ref = s32[16,4,640]{2,1,0:T(4,128)S(1)} async-done(((s32[16,4,640]{2,1,0:T(4,128)}), s32[16,4,640]{2,1,0:T(4,128)S(1)}, u32[]{:S(2)}, u32[]{:S(2)}) %all-to-all-start) | async-done | bytes 163872 | tf_op jit(solution)/shard_map/all_to_all | solution.py:364
  18.1 1.7 %shard_map.85 = (s32[16,4,640]{2,1,0:T(4,128)S(1)}, f32[4,1024]{1,0:T(4,128)S(1)}, f32[24,1024]{1,0:T(8,128)S(1)}, f32[8,128]{1,0:T(8,128)S(1)}) custom-call(s32[16,4,640]{2,1,0:T(4,128)S(1)} %all-to-all-done.got_ref, f32[4,1024]{1,0:T(4,128)S(1)} %get-tuple-element.26.loads_ref, bf16[32,1024]{1,0:T(8,128)(2,1)S(1)} %get-tuple-element.27.cols_high, ...), custom_call_target="tpu_custom_call" | custom-call | bytes 3166848 | tf_op jit(solution)/shard_map/pallas_call | solution.py:349
  19.8 11.1 %all_to_all.15.got_ref = s32[16,4,640]{2,1,0:T(4,128)S(1)} all-to-all(s32[16,4,640]{2,1,0:T(4,128)S(1)} %get-tuple-element.38), channel_id=1, replica_groups=mesh['case'=2,'strip'=8,'clus'=2] {'strip','clus'}, dimensions={0} | all-to-all | bytes 327680 | tf_op jit(solution)/shard_map/all_to_all | solution.py:364
  30.9 1.3 %shard_map.86 = (f32[16,1,128]{2,1,0:T(1,128)S(1)}, f32[8,1024]{1,0:T(8,128)S(1)}, f32[12,128]{1,0:T(8,128)S(1)}) custom-call(s32[16,4,640]{2,1,0:T(4,128)S(1)} %all_to_all.15.got_ref, f32[4,1024]{1,0:T(4,128)S(1)} %get-tuple-element.26.loads_ref, f32[4,1024]{1,0:T(4,128)S(1)} %get-tuple-element.39.image_ref, f32[24,1024]{1,0:T(8,128)S(1)} %get-tuple-element.40.window0_ref, ...), custom_call_target="tpu_custom_call" | custom-call | bytes 3056256 | tf_op jit(solution)/shard_map/pallas_call | solution.py:349
  32.2 9.0 %all_to_all.16.got_ref = f32[16,1,128]{2,1,0:T(1,128)S(1)} all-to-all(f32[16,1,128]{2,1,0:T(1,128)S(1)} %get-tuple-element.42), channel_id=1, replica_groups=mesh['case'=2,'strip'=8,'clus'=2] {'strip','clus'}, dimensions={0} | all-to-all | bytes 16384 | tf_op jit(solution)/shard_map/all_to_all | solution.py:364
  41.1 0.8 %shard_map.87 = f32[4,1024]{1,0:T(4,128)} custom-call(f32[16,1,128]{2,1,0:T(1,128)S(1)} %all_to_all.16.got_ref, f32[8,1024]{1,0:T(8,128)S(1)} %get-tuple-element.43.basis_ref, f32[12,128]{1,0:T(8,128)S(1)} %get-tuple-element.44.coeff_ref), custom_call_target="tpu_custom_call" | custom-call | bytes 47104 | tf_op jit(solution)/shard_map/pallas_call | solution.py:349
Async XLA Ops:
  2.3 15.8 %all-to-all-start = ((s32[16,4,640]{2,1,0:T(4,128)}), s32[16,4,640]{2,1,0:T(4,128)S(1)}, u32[]{:S(2)}, u32[]{:S(2)}) async-start(s32[16,4,640]{2,1,0:T(4,128)} %get-tuple-element.25), calls=%async_computation | async-start | bytes 327680 | tf_op jit(solution)/shard_map/all_to_all | solution.py:364

commit v12 on v10

--- a/solution.py
+++ b/solution.py
@@ -110,17 +110,18 @@
     return copies
 
 
-def put_message(field, columns, cols, couple, masks_ref, sent_ref):
+def put_message(field, columns, cols, couple, masks_ref, sent_ref, field_is_put=lambda: None):
     nrhs, rank = field.shape[0], cols[0].shape[0]
     unit = term_unit(field.shape[1], rank)
+    words, step = packed(field)
+    width = words.shape[1]
+    for i in range(sent_ref.shape[0]):
+        sent_ref[i, :, :width] = words
+    field_is_put()
     proj = product(field, cols[0][...], cols[1][...], 1)
     wide = jnp.concatenate([proj] * CHUNK, axis=1)
-    words, step = packed(field)
-    width = words.shape[1]
     row = stats_row(columns, rank, step)
     finer = 1.0 / (steps_of(row, rank) * unit)
-    for i in range(sent_ref.shape[0]):
-        sent_ref[i, :, :width] = words
     stats = [jnp.broadcast_to(a, (CHUNK, LANES)) for a in coded(row)]
     for start in range(0, sent_ref.shape[0], CHUNK):
         mask = masks_ref[pl.ds(start, CHUNK), :]
@@ -187,30 +188,44 @@
 
 
 def start_kernel(
-    loads_hbm, cols_hbm, couple_hbm, ranks_hbm, sent_ref, cols_high, cols_low, couple_high, couple_low, masks_ref,
-    loads_ref, done_ref, cols_ref, couple_ref, ranks_ref, sems,
+    loads_hbm, cols_hbm, couple_hbm, ranks_hbm, sent_any, cols_high, cols_low, couple_high, couple_low, masks_ref,
+    loads_ref, done_ref, cols_ref, couple_ref, ranks_ref, sent_ref, sems, sent_sems,
 ):
-    rank = cols_ref.shape[0]
+    rank, panels = cols_ref.shape
     pairs = ((loads_hbm, loads_ref), (cols_hbm, cols_ref), (couple_hbm, couple_ref), (ranks_hbm, ranks_ref))
     copies = fetch(pairs, sems)
     done_ref[...] = jnp.zeros_like(done_ref)
     copies[0].wait()
     loads = loads_ref[...]
     square = jnp.sum(loads * loads, axis=1, keepdims=True)
-    copies[1].wait()
-    cols_high[...], cols_low[...] = halves(cols_ref[...])
-    copies[2].wait()
-    couple_high[...], couple_low[...] = halves(couple_ref[...])
-    copies[3].wait()
-    shape = (CHUNK, CHUNK * rank)
-    owner = lax.div(lanes_of(shape), rank)
-    inner = lax.rem(lanes_of(shape), rank)
-    for start in range(0, masks_ref.shape[0], CHUNK):
-        limit = jnp.zeros((1, CHUNK * rank), jnp.int32)
-        for i in range(CHUNK):
-            limit = jnp.where(owner[:1] == i, ranks_ref[0, start + i], limit)
-        masks_ref[pl.ds(start, CHUNK), :] = jnp.where((owner == rows_of(shape)) & (inner < limit), 1.0, 0.0)
-    put_message(loads, [square], (cols_high, cols_low), (couple_high, couple_low), masks_ref, sent_ref)
+    width = panels // 2
+    sides = [pl.ds(0, width), pl.ds(width, LANES)]
+    out = [
+        pltpu.make_async_copy(sent_ref.at[:, :, side], sent_any.at[:, :, side], sent_sems.at[i])
+        for i, side in enumerate(sides)
+    ]
+
+    def field_is_put():
+        out[0].start()
+        copies[1].wait()
+        cols_high[...], cols_low[...] = halves(cols_ref[...])
+        copies[2].wait()
+        couple_high[...], couple_low[...] = halves(couple_ref[...])
+        copies[3].wait()
+        shape = (CHUNK, CHUNK * rank)
+        owner = lax.div(lanes_of(shape), rank)
+        inner = lax.rem(lanes_of(shape), rank)
+        for start in range(0, masks_ref.shape[0], CHUNK):
+            limit = jnp.zeros((1, CHUNK * rank), jnp.int32)
+            for i in range(CHUNK):
+                limit = jnp.where(owner[:1] == i, ranks_ref[0, start + i], limit)
+            masks_ref[pl.ds(start, CHUNK), :] = jnp.where((owner == rows_of(shape)) & (inner < limit), 1.0, 0.0)
+
+    cols, couple = (cols_high, cols_low), (couple_high, couple_low)
+    put_message(loads, [square], cols, couple, masks_ref, sent_ref, field_is_put)
+    out[1].start()
+    for copy in out:
+        copy.wait()
 
 
 def copy_tiles(tiles_hbm, first, tiles_ref, sems):
@@ -343,7 +358,7 @@
     return [pltpu.with_memory_space_constraint(a, pltpu.VMEM) for a in arrays]
 
 
-def call(kernel, args, outs, scratch=(), held=(), flops=0):
+def call(kernel, args, outs, scratch=(), held=(), placed=()):
     args = [pltpu.with_memory_space_constraint(a, pltpu.HBM) if i in held else a for i, a in enumerate(args)]
     moved = sum(a.size * a.dtype.itemsize for a in args)
     return pl.pallas_call(
@@ -353,10 +368,10 @@
             for out in outs
         ],
         in_specs=[pl.BlockSpec(memory_space=pl.ANY if i in held else pltpu.VMEM) for i in range(len(args))],
-        out_specs=[pl.BlockSpec(memory_space=pltpu.VMEM)] * len(outs),
+        out_specs=[pl.BlockSpec(memory_space=pl.ANY if i in placed else pltpu.VMEM) for i in range(len(outs))],
         scratch_shapes=list(scratch),
         compiler_params=pltpu.CompilerParams(vmem_limit_bytes=24 * 2**20),
-        cost_estimate=pl.CostEstimate(flops=flops, bytes_accessed=moved, transcendentals=0),
+        cost_estimate=pl.CostEstimate(flops=0, bytes_accessed=moved, transcendentals=0),
     )(*args)
 
 
@@ -388,10 +403,11 @@
         (loads, far_cols, couple, ranks),
         [message, *twice(far_cols), *twice(couple), jax.ShapeDtypeStruct((groups, CHUNK * rank), F32), loads, (8, LANES)],
         [
-            pltpu.VMEM(far_cols.shape, F32), pltpu.VMEM(couple.shape, F32),
-            pltpu.SMEM(ranks.shape, jnp.int32), pltpu.SemaphoreType.DMA((4,)),
+            pltpu.VMEM(far_cols.shape, F32), pltpu.VMEM(couple.shape, F32), pltpu.SMEM(ranks.shape, jnp.int32),
+            pltpu.VMEM(message.shape, jnp.int32), pltpu.SemaphoreType.DMA((4,)), pltpu.SemaphoreType.DMA((2,)),
         ],
         held=range(4),
+        placed=(0,),
     )
     part = jax.ShapeDtypeStruct((blocks // 2, tile, tile), BF16)
     tiles0, *target_side, near_list = call(

time: 42.3 us -> 42.3 us (level)
  no operation moved by 1% of the time
where the time goes in v12:
time: 42.3 us; the launch traced here: 41.9 us
  blocking collectives  20 us (47%)
  Pallas kernels  8.74 us (21%)
  starting transfers between devices  7.37 us (17%)
  waiting for transfers between devices  5.73 us (14%)
    all_to_all x2, blocking collectives, exchanged(): return lax.all_to_all(sent, GROUP, 0, 0, tiled=True)  20 us
    pallas_call x6, Pallas kernels, call(): pl.pallas_call(kernel, out_shape=[jax.ShapeDtypeStruct(out, F32) if isins...  8.74 us
    all_to_all x1, starting transfers between devices, exchanged(): return lax.all_to_all(sent, GROUP, 0, 0, tiled=True)  7.37 us
    all_to_all x1, waiting for transfers between devices, exchanged(): return lax.all_to_all(sent, GROUP, 0, 0, tiled=True)  5.73 us
  transfers between devices with their start and end apart: 1, of which 1 were waited for; matrix products, arithmetic and copies ran while one was open for 0% of the time, Pallas kernels for 6%

profile of v12, /device:TPU:0, one launch (start us, length us, event | category | flops | bytes accessed | tf_op | source)
XLA Modules:
  0.0 41.9 jit_solution(10441994673026557396)
XLA Ops:
  0.0 2.3 %shard_map.82 = (s32[16,4,640]{2,1,0:T(4,128)}, bf16[32,1024]{1,0:T(8,128)(2,1)S(1)}, bf16[32,1024]{1,0:T(8,128)(2,1)S(1)}, bf16[512,32]{1,0:T(8,128)(2,1)S(1)},...) custom-call(f32[4,1024]{1,0:T(4,128)} %loads_hbm.1, ...), custom_call_target="tpu_custom_call" | custom-call | bytes 213056 | tf_op jit(solution)/shard_map/pallas_call | solution.py:364
  2.3 7.4 %all-to-all-start = ((s32[16,4,640]{2,1,0:T(4,128)}), s32[16,4,640]{2,1,0:T(4,128)S(1)}, u32[]{:S(2)}, u32[]{:S(2)}) async-start(s32[16,4,640]{2,1,0:T(4,128)} %get-tuple-element.25), calls=%async_computation | async-start | bytes 327680 | tf_op jit(solution)/shard_map/all_to_all | solution.py:379
  9.7 1.3 %shard_map.84.tiles1_ref = bf16[40,128,128]{2,1,0:T(8,128)(2,1)S(1)} custom-call(f32[8,128]{1,0:T(8,128)S(1)} %get-tuple-element.32.done_ref, bf16[80,128,128]{2,1,0:T(8,128)(2,1)} %tiles_hbm.3), custom_call_target="tpu_custom_call" | custom-call | bytes 2625536 | tf_op jit(solution)/shard_map/pallas_call | solution.py:364
  11.0 1.4 %shard_map.83 = (bf16[40,128,128]{2,1,0:T(8,128)(2,1)S(1)}, bf16[32,1024]{1,0:T(8,128)(2,1)S(1)}, bf16[32,1024]{1,0:T(8,128)(2,1)S(1)}, f32[1,1024]{1,0:T(1,128)S(1)}, s32[2,80]{1,0:T(2,128)S(1)}) custom-call(f32[8,128]{1,0:T(8,128)S(1)} %get-tuple-element.32.done_ref, bf16[80,128,128]{2,1,0:T(8,128)(2,1)} %tiles_hbm.3, f32[32,1024]{1,0:T(8,128)} %rows_hbm.1, ...), custom_call_target="tpu_custom_call" | custom-call | bytes 2761344 | tf_op jit(solution)/shard_map/pallas_call | solution.py:364
  12.4 5.7 %all-to-all-done.got_ref = s32[16,4,640]{2,1,0:T(4,128)S(1)} async-done(((s32[16,4,640]{2,1,0:T(4,128)}), s32[16,4,640]{2,1,0:T(4,128)S(1)}, u32[]{:S(2)}, u32[]{:S(2)}) %all-to-all-start) | async-done | bytes 163872 | tf_op jit(solution)/shard_map/all_to_all | solution.py:379
  18.1 1.7 %shard_map.85 = (s32[16,4,640]{2,1,0:T(4,128)S(1)}, f32[4,1024]{1,0:T(4,128)S(1)}, f32[24,1024]{1,0:T(8,128)S(1)}, f32[8,128]{1,0:T(8,128)S(1)}) custom-call(s32[16,4,640]{2,1,0:T(4,128)S(1)} %all-to-all-done.got_ref, f32[4,1024]{1,0:T(4,128)S(1)} %get-tuple-element.26.loads_ref, bf16[32,1024]{1,0:T(8,128)(2,1)S(1)} %get-tuple-element.27.cols_high, ...), custom_call_target="tpu_custom_call" | custom-call | bytes 3166848 | tf_op jit(solution)/shard_map/pallas_call | solution.py:364
  19.8 11.1 %all_to_all.15.got_ref = s32[16,4,640]{2,1,0:T(4,128)S(1)} all-to-all(s32[16,4,640]{2,1,0:T(4,128)S(1)} %get-tuple-element.38), channel_id=1, replica_groups=mesh['case'=2,'strip'=8,'clus'=2] {'strip','clus'}, dimensions={0} | all-to-all | bytes 327680 | tf_op jit(solution)/shard_map/all_to_all | solution.py:379
  30.9 1.3 %shard_map.86 = (f32[16,1,128]{2,1,0:T(1,128)S(1)}, f32[8,1024]{1,0:T(8,128)S(1)}, f32[12,128]{1,0:T(8,128)S(1)}) custom-call(s32[16,4,640]{2,1,0:T(4,128)S(1)} %all_to_all.15.got_ref, f32[4,1024]{1,0:T(4,128)S(1)} %get-tuple-element.26.loads_ref, f32[4,1024]{1,0:T(4,128)S(1)} %get-tuple-element.39.image_ref, f32[24,1024]{1,0:T(8,128)S(1)} %get-tuple-element.40.window0_ref, ...), custom_call_target="tpu_custom_call" | custom-call | bytes 3056256 | tf_op jit(solution)/shard_map/pallas_call | solution.py:364
  32.1 9.0 %all_to_all.16.got_ref = f32[16,1,128]{2,1,0:T(1,128)S(1)} all-to-all(f32[16,1,128]{2,1,0:T(1,128)S(1)} %get-tuple-element.42), channel_id=1, replica_groups=mesh['case'=2,'strip'=8,'clus'=2] {'strip','clus'}, dimensions={0} | all-to-all | bytes 16384 | tf_op jit(solution)/shard_map/all_to_all | solution.py:379
  41.1 0.8 %shard_map.87 = f32[4,1024]{1,0:T(4,128)} custom-call(f32[16,1,128]{2,1,0:T(1,128)S(1)} %all_to_all.16.got_ref, f32[8,1024]{1,0:T(8,128)S(1)} %get-tuple-element.43.basis_ref, f32[12,128]{1,0:T(8,128)S(1)} %get-tuple-element.44.coeff_ref), custom_call_target="tpu_custom_call" | custom-call | bytes 47104 | tf_op jit(solution)/shard_map/pallas_call | solution.py:364
Async XLA Ops:
  2.3 15.8 %all-to-all-start = ((s32[16,4,640]{2,1,0:T(4,128)}), s32[16,4,640]{2,1,0:T(4,128)S(1)}, u32[]{:S(2)}, u32[]{:S(2)}) async-start(s32[16,4,640]{2,1,0:T(4,128)} %get-tuple-element.25), calls=%async_computation | async-start | bytes 327680 | tf_op jit(solution)/shard_map/all_to_all | solution.py:379

commit v13 on v10

--- a/solution.py
+++ b/solution.py
@@ -11,7 +11,7 @@
 CORES = 2
 LANES = 128
 CHUNK = 16
-PIECES = 4
+PIECES = 10
 F32 = jnp.float32
 BF16 = jnp.bfloat16
 
@@ -187,13 +187,18 @@
 
 
 def start_kernel(
-    loads_hbm, cols_hbm, couple_hbm, ranks_hbm, sent_ref, cols_high, cols_low, couple_high, couple_low, masks_ref,
-    loads_ref, done_ref, cols_ref, couple_ref, ranks_ref, sems,
+    loads_hbm, cols_hbm, couple_hbm, ranks_hbm, list_hbm, rows_hbm, self_hbm, tiles_hbm, sent_ref, cols_high, cols_low, couple_high,
+    couple_low, masks_ref, rows_high, rows_low, list_ref, loads_ref, self_ref, tiles_ref, cols_ref, couple_ref, ranks_ref, raw_ref,
+    rows_ref, sems,
 ):
-    rank = cols_ref.shape[0]
-    pairs = ((loads_hbm, loads_ref), (cols_hbm, cols_ref), (couple_hbm, couple_ref), (ranks_hbm, ranks_ref))
-    copies = fetch(pairs, sems)
-    done_ref[...] = jnp.zeros_like(done_ref)
+    rank, panels = cols_ref.shape
+    pairs = (
+        (loads_hbm, loads_ref), (cols_hbm, cols_ref), (couple_hbm, couple_ref), (ranks_hbm, ranks_ref),
+        (list_hbm, raw_ref), (rows_hbm, rows_ref), (self_hbm, self_ref),
+    )
+    every = tiles_ref.shape[0] // PIECES
+    pieces = [pl.ds(i * every, every) for i in range(PIECES)]
+    copies = fetch(pairs + tuple((tiles_hbm.at[p], tiles_ref.at[p]) for p in pieces), sems)
     copies[0].wait()
     loads = loads_ref[...]
     square = jnp.sum(loads * loads, axis=1, keepdims=True)
@@ -210,38 +215,17 @@
         for i in range(CHUNK):
             limit = jnp.where(owner[:1] == i, ranks_ref[0, start + i], limit)
         masks_ref[pl.ds(start, CHUNK), :] = jnp.where((owner == rows_of(shape)) & (inner < limit), 1.0, 0.0)
+    copies[4].wait()
+    count = panels // LANES
+    target, source = raw_ref[0:1, :], raw_ref[1:2, :]
+    group, block = lax.div(source, count), lax.rem(source, count)
+    strip, core = lax.div(group, CORES), lax.rem(group, CORES)
+    list_ref[...] = jnp.concatenate([core * count + target, strip * count + block], axis=0)
+    copies[5].wait()
+    rows_high[...], rows_low[...] = halves(rows_ref[...])
     put_message(loads, [square], (cols_high, cols_low), (couple_high, couple_low), masks_ref, sent_ref)
-
-
-def copy_tiles(tiles_hbm, first, tiles_ref, sems):
-    every = tiles_ref.shape[0] // PIECES
-    pairs = [(pl.ds(first + i * every, every), pl.ds(i * every, every)) for i in range(PIECES)]
-    return fetch([(tiles_hbm.at[a], tiles_ref.at[b]) for a, b in pairs], sems)
-
-
-def fetch0_kernel(done_ref, tiles_hbm, rows_hbm, self_hbm, list_hbm, tiles_ref, rows_high, rows_low, self_ref, list_ref,
-                  rows_ref, raw_ref, sems, other_sems):
-    del done_ref
-    pairs = ((list_hbm, raw_ref), (rows_hbm, rows_ref), (self_hbm, self_ref))
-    copies = fetch(pairs, other_sems)
-    pieces = copy_tiles(tiles_hbm, 0, tiles_ref, sems)
-    copies[0].wait()
-    rows = self_ref.shape[1] // tiles_ref.shape[1]
-    target, source = raw_ref[0:1, :], raw_ref[1:2, :]
-    group, block = lax.div(source, rows), lax.rem(source, rows)
-    strip, core = lax.div(group, CORES), lax.rem(group, CORES)
-    list_ref[...] = jnp.concatenate([core * rows + target, strip * rows + block], axis=0)
-    copies[1].wait()
-    rows_high[...], rows_low[...] = halves(rows_ref[...])
-    copies[2].wait()
-    for piece in pieces:
-        piece.wait()
-
-
-def fetch1_kernel(done_ref, tiles_hbm, tiles_ref, sems):
-    del done_ref
-    for piece in copy_tiles(tiles_hbm, tiles_ref.shape[0], tiles_ref, sems):
-        piece.wait()
+    for copy in copies[6:]:
+        copy.wait()
 
 
 def image_of(field, far, self_ref, far_rows, near):
@@ -251,7 +235,7 @@
 
 def step0_kernel(
     got_ref, loads_ref, cols_high, cols_low, couple_high, couple_low, masks_ref, rows_high, rows_low, self_ref,
-    tiles0_ref, tiles1_ref, list_vmem, sent_ref, image_ref, window0_ref, state_ref, list_ref, sems, window, *sums,
+    tiles_ref, list_vmem, sent_ref, image_ref, window0_ref, state_ref, list_ref, sems, window, *sums,
 ):
     rank = rows_high.shape[0]
     nrhs, panels = loads_ref.shape
@@ -268,7 +252,7 @@
     basis = loads_ref[...] * scale
     far = far_sum_of(terms, nrhs, rank) * scale
     copy.wait()
-    near = near_field(window, (tiles0_ref, tiles1_ref), list_ref, sums, nrhs)
+    near = near_field(window, (tiles_ref,), list_ref, sums, nrhs)
     image = image_of(basis, far, self_ref, (rows_high, rows_low), near)
     image_ref[...] = image
     state_ref[...] = jnp.concatenate([far, jnp.broadcast_to(beta, far.shape)], axis=0)
@@ -282,7 +266,7 @@
 
 
 def step1_kernel(
-    got_ref, loads_ref, image_ref, window0_ref, state_ref, rows_high, rows_low, self_ref, tiles0_ref, tiles1_ref,
+    got_ref, loads_ref, image_ref, window0_ref, state_ref, rows_high, rows_low, self_ref, tiles_ref,
     list_vmem, sent_ref, basis_ref, coeff_ref, list_ref, sems, window, *sums,
 ):
     rank = rows_high.shape[0]
@@ -306,7 +290,7 @@
     basis1 = (image_ref[...] - h00 * basis0) * scale
     far = (far_sum_of(terms, nrhs, rank) - h00 * far0) * scale
     copy.wait()
-    near = near_field(window, (tiles0_ref, tiles1_ref), list_ref, sums, nrhs)
+    near = near_field(window, (tiles_ref,), list_ref, sums, nrhs)
     image = image_of(basis1, far, self_ref, (rows_high, rows_low), near)
     columns = [jnp.sum(a * image, axis=1, keepdims=True) for a in (basis0, basis1, image)]
     sent_ref[:, 0, :] = jnp.broadcast_to(stats_row(columns, rank), (sent_ref.shape[0], LANES))
@@ -343,7 +327,7 @@
     return [pltpu.with_memory_space_constraint(a, pltpu.VMEM) for a in arrays]
 
 
-def call(kernel, args, outs, scratch=(), held=(), flops=0):
+def call(kernel, args, outs, scratch=(), held=()):
     args = [pltpu.with_memory_space_constraint(a, pltpu.HBM) if i in held else a for i, a in enumerate(args)]
     moved = sum(a.size * a.dtype.itemsize for a in args)
     return pl.pallas_call(
@@ -356,7 +340,7 @@
         out_specs=[pl.BlockSpec(memory_space=pltpu.VMEM)] * len(outs),
         scratch_shapes=list(scratch),
         compiler_params=pltpu.CompilerParams(vmem_limit_bytes=24 * 2**20),
-        cost_estimate=pl.CostEstimate(flops=flops, bytes_accessed=moved, transcendentals=0),
+        cost_estimate=pl.CostEstimate(flops=0, bytes_accessed=moved, transcendentals=0),
     )(*args)
 
 
@@ -383,32 +367,21 @@
     def twice(array):
         return [jax.ShapeDtypeStruct(array.shape, BF16)] * 2
 
-    sent, *source_side, loads, done = call(
+    sent, *held, near_list, loads, self_term, near_tiles = call(
         start_kernel,
-        (loads, far_cols, couple, ranks),
-        [message, *twice(far_cols), *twice(couple), jax.ShapeDtypeStruct((groups, CHUNK * rank), F32), loads, (8, LANES)],
+        (loads, far_cols, couple, ranks, near_list, far_rows, self_term, near_tiles),
         [
-            pltpu.VMEM(far_cols.shape, F32), pltpu.VMEM(couple.shape, F32),
-            pltpu.SMEM(ranks.shape, jnp.int32), pltpu.SemaphoreType.DMA((4,)),
+            message, *twice(far_cols), *twice(couple), jax.ShapeDtypeStruct((groups, CHUNK * rank), F32),
+            *twice(far_rows), near_list, loads, self_term, near_tiles,
         ],
-        held=range(4),
+        [
+            pltpu.VMEM(far_cols.shape, F32), pltpu.VMEM(couple.shape, F32), pltpu.SMEM(ranks.shape, jnp.int32),
+            pltpu.VMEM(near_list.shape, jnp.int32), pltpu.VMEM(far_rows.shape, F32), pltpu.SemaphoreType.DMA((7 + PIECES,)),
+        ],
+        held=range(8),
     )
-    part = jax.ShapeDtypeStruct((blocks // 2, tile, tile), BF16)
-    tiles0, *target_side, near_list = call(
-        fetch0_kernel,
-        (done, near_tiles, far_rows, self_term, near_list),
-        [part, *twice(far_rows), self_term, near_list],
-        [
-            pltpu.VMEM(far_rows.shape, F32), pltpu.VMEM(near_list.shape, jnp.int32),
-            pltpu.SemaphoreType.DMA((PIECES,)), pltpu.SemaphoreType.DMA((3,)),
-        ],
-        held=range(1, 5),
-    )
-    (tiles1,) = call(
-        fetch1_kernel, (done, near_tiles), [part], [pltpu.SemaphoreType.DMA((PIECES,))], held=(1,)
-    )
-    source_side, target_side = in_vmem([loads, *source_side]), in_vmem([*target_side, tiles0, tiles1, near_list])
-    loads = source_side[0]
+    loads, *held, self_term, near_tiles, near_list = in_vmem([loads, *held, self_term, near_tiles, near_list])
+    source_side, target_side = [loads, *held[:5]], [*held[5:], self_term, near_tiles, near_list]
     sent, image, window0, state = call(
         step0_kernel,
         (exchanged(sent), *source_side, *target_side),
@@ -421,7 +394,8 @@
         [(groups, 1, LANES), (2 * nrhs, panels), (3 * nrhs, LANES)],
         scratch,
     )
-    return call(functools.partial(finish_kernel, rank), (exchanged(sent), basis, coeff), [loads.shape])[0]
+    got = lax.all_to_all(sent, GROUP[::-1], 0, 0, tiled=True)
+    return call(functools.partial(finish_kernel, rank), (got, basis, coeff), [loads.shape])[0]
 
 
 def solution(mesh):

time: 42.3 us -> 41.7 us (0.986)
  blocking collectives: 20 us -> 35.6 us
  starting transfers between devices: 7.37 us -> 0 us
  waiting for transfers between devices: 5.73 us -> 0 us
  Pallas kernels: 8.75 us -> 5.83 us
    all_to_all x0 -> x1, blocking collectives: none -> 8.91 us  [body(): got = lax.all_to_all(sent, GROUP[::-1], 0, 0, tiled=True)]
    all_to_all x1 -> x0, starting transfers between devices: 7.37 us -> none  [exchanged(): return lax.all_to_all(sent, GROUP, 0, 0, tiled=True)]
    all_to_all x2, blocking collectives: 20 us -> 26.7 us  [exchanged(): return lax.all_to_all(sent, GROUP, 0, 0, tiled=True)]
    all_to_all x1 -> x0, waiting for transfers between devices: 5.73 us -> none  [exchanged(): return lax.all_to_all(sent, GROUP, 0, 0, tiled=True)]
    pallas_call x6 -> x4, Pallas kernels: 8.75 us -> 5.83 us  [call(): pl.pallas_call(kernel, out_shape=[jax.ShapeDtypeStruct(out, F32) if isins...]
  transfers between devices with their start and end apart: 1 -> 0, of which waited for: 1 -> 0; matrix products, arithmetic and copies ran while one was open for 0% -> 0% of each run, Pallas kernels for 6% -> 0%
where the time goes in v13:
time: 41.7 us; the launch traced here: 41.4 us
  blocking collectives  35.6 us (85%)
  Pallas kernels  5.83 us (14%)
    all_to_all x2, blocking collectives, exchanged(): return lax.all_to_all(sent, GROUP, 0, 0, tiled=True)  26.7 us
    all_to_all x1, blocking collectives, body(): got = lax.all_to_all(sent, GROUP[::-1], 0, 0, tiled=True)  8.91 us
    pallas_call x4, Pallas kernels, call(): pl.pallas_call(kernel, out_shape=[jax.ShapeDtypeStruct(out, F32) if isins...  5.83 us

profile of v13, /device:TPU:0, one launch (start us, length us, event | category | flops | bytes accessed | tf_op | source)
XLA Modules:
  0.0 41.4 jit_solution(597185426840219478)
XLA Ops:
  0.0 2.1 %shard_map.82 = (s32[16,4,640]{2,1,0:T(4,128)S(1)}, bf16[32,1024]{1,0:T(8,128)(2,1)S(1)}, bf16[32,1024]{1,0:T(8,128)(2,1)S(1)}, bf16[512,32]{1,0:T(8,128)(2,1)S(...) custom-call(f32[4,1024]{1,0:T(4,128)} %loads_hbm.1, ...), custom_call_target="tpu_custom_call" | custom-call | bytes 2970304 | tf_op jit(solution)/shard_map/pallas_call | solution.py:333
  2.1 15.6 %all_to_all.15.got_ref = s32[16,4,640]{2,1,0:T(4,128)S(1)} all-to-all(s32[16,4,640]{2,1,0:T(4,128)S(1)} %get-tuple-element.24), channel_id=1, replica_groups=mesh['case'=2,'strip'=8,'clus'=2] {'strip','clus'}, dimensions={0} | all-to-all | bytes 327680 | tf_op jit(solution)/shard_map/all_to_all | solution.py:348
  17.7 1.7 %shard_map.83 = (s32[16,4,640]{2,1,0:T(4,128)S(1)}, f32[4,1024]{1,0:T(4,128)S(1)}, f32[24,1024]{1,0:T(8,128)S(1)}, f32[8,128]{1,0:T(8,128)S(1)}) custom-call(s32[16,4,640]{2,1,0:T(4,128)S(1)} %all_to_all.15.got_ref, f32[4,1024]{1,0:T(4,128)S(1)} %get-tuple-element.25.loads_ref, bf16[32,1024]{1,0:T(8,128)(2,1)S(1)} %get-tuple-element.26.cols_high, ...), custom_call_target="tpu_custom_call" | custom-call | bytes 3166848 | tf_op jit(solution)/shard_map/pallas_call | solution.py:333
  19.4 11.1 %all_to_all.16.got_ref = s32[16,4,640]{2,1,0:T(4,128)S(1)} all-to-all(s32[16,4,640]{2,1,0:T(4,128)S(1)} %get-tuple-element.36), channel_id=1, replica_groups=mesh['case'=2,'strip'=8,'clus'=2] {'strip','clus'}, dimensions={0} | all-to-all | bytes 327680 | tf_op jit(solution)/shard_map/all_to_all | solution.py:348
  30.4 1.3 %shard_map.84 = (f32[16,1,128]{2,1,0:T(1,128)S(1)}, f32[8,1024]{1,0:T(8,128)S(1)}, f32[12,128]{1,0:T(8,128)S(1)}) custom-call(s32[16,4,640]{2,1,0:T(4,128)S(1)} %all_to_all.16.got_ref, f32[4,1024]{1,0:T(4,128)S(1)} %get-tuple-element.25.loads_ref, f32[4,1024]{1,0:T(4,128)S(1)} %get-tuple-element.37.image_ref, f32[24,1024]{1,0:T(8,128)S(1)} %get-tuple-element.38.window0_ref, ...), custom_call_target="tpu_custom_call" | custom-call | bytes 3056256 | tf_op jit(solution)/shard_map/pallas_call | solution.py:333
  31.7 8.9 %all_to_all.17.got_ref = f32[16,1,128]{2,1,0:T(1,128)S(1)} all-to-all(f32[16,1,128]{2,1,0:T(1,128)S(1)} %get-tuple-element.40), channel_id=1, replica_groups=mesh['case'=2,'strip'=8,'clus'=2] {'clus','strip'}, dimensions={0} | all-to-all | bytes 16384 | tf_op jit(solution)/shard_map/all_to_all | solution.py:397
  40.6 0.8 %shard_map.85 = f32[4,1024]{1,0:T(4,128)} custom-call(f32[16,1,128]{2,1,0:T(1,128)S(1)} %all_to_all.17.got_ref, f32[8,1024]{1,0:T(8,128)S(1)} %get-tuple-element.41.basis_ref, f32[12,128]{1,0:T(8,128)S(1)} %get-tuple-element.42.coeff_ref), custom_call_target="tpu_custom_call" | custom-call | bytes 47104 | tf_op jit(solution)/shard_map/pallas_call | solution.py:333

commit v14 on v13

--- a/solution.py
+++ b/solution.py
@@ -11,7 +11,7 @@
 CORES = 2
 LANES = 128
 CHUNK = 16
-PIECES = 10
+PIECE = 4
 F32 = jnp.float32
 BF16 = jnp.bfloat16
 
@@ -162,12 +162,14 @@
         window[first + c] = part[:, c * LANES : (c + 1) * LANES]
 
 
-def near_field(window, tiles, list_ref, sums, nrhs):
+def near_field(window, tiles, list_ref, sums, nrhs, copies=()):
     for held in sums:
         held[...] = jnp.zeros_like(held)
     n = 0
     for tiles_ref in tiles:
         for first in range(0, tiles_ref.shape[0], 4):
+            if copies and tiles_ref is tiles[1]:
+                copies[first // PIECE].wait()
             sources = [window[list_ref[1, n + i]] for i in range(4)]
             blank = jnp.zeros_like(sources[0])
             upper = [sources[0], blank, sources[2], blank]
@@ -186,6 +188,11 @@
     return jnp.concatenate([whole[b, :nrhs] + whole[rows + b, nrhs:] for b in range(rows)], axis=1)
 
 
+def tile_pieces(tiles_hbm, first, tiles_ref):
+    starts = range(0, tiles_ref.shape[0], PIECE)
+    return tuple((tiles_hbm.at[pl.ds(first + i, PIECE)], tiles_ref.at[pl.ds(i, PIECE)]) for i in starts)
+
+
 def start_kernel(
     loads_hbm, cols_hbm, couple_hbm, ranks_hbm, list_hbm, rows_hbm, self_hbm, tiles_hbm, sent_ref, cols_high, cols_low, couple_high,
     couple_low, masks_ref, rows_high, rows_low, list_ref, loads_ref, self_ref, tiles_ref, cols_ref, couple_ref, ranks_ref, raw_ref,
@@ -196,9 +203,7 @@
         (loads_hbm, loads_ref), (cols_hbm, cols_ref), (couple_hbm, couple_ref), (ranks_hbm, ranks_ref),
         (list_hbm, raw_ref), (rows_hbm, rows_ref), (self_hbm, self_ref),
     )
-    every = tiles_ref.shape[0] // PIECES
-    pieces = [pl.ds(i * every, every) for i in range(PIECES)]
-    copies = fetch(pairs + tuple((tiles_hbm.at[p], tiles_ref.at[p]) for p in pieces), sems)
+    copies = fetch(pairs + tile_pieces(tiles_hbm, 0, tiles_ref), sems)
     copies[0].wait()
     loads = loads_ref[...]
     square = jnp.sum(loads * loads, axis=1, keepdims=True)
@@ -235,12 +240,14 @@
 
 def step0_kernel(
     got_ref, loads_ref, cols_high, cols_low, couple_high, couple_low, masks_ref, rows_high, rows_low, self_ref,
-    tiles_ref, list_vmem, sent_ref, image_ref, window0_ref, state_ref, list_ref, sems, window, *sums,
+    tiles0_ref, list_vmem, tiles_hbm, sent_ref, image_ref, window0_ref, state_ref, tiles1_ref, list_ref, sems, tile_sems,
+    window, *sums,
 ):
     rank = rows_high.shape[0]
     nrhs, panels = loads_ref.shape
     span, rows = panels // LANES, CORES * nrhs
     (copy,) = fetch(((list_vmem, list_ref),), sems)
+    copies = fetch(tile_pieces(tiles_hbm, tiles0_ref.shape[0], tiles1_ref), tile_sems)
     terms, stats = message_parts(got_ref, rank)
     beta = jnp.sqrt(stat_column(total(stats), 0, nrhs, rank))
     scale = 1.0 / beta
@@ -252,7 +259,7 @@
     basis = loads_ref[...] * scale
     far = far_sum_of(terms, nrhs, rank) * scale
     copy.wait()
-    near = near_field(window, (tiles_ref,), list_ref, sums, nrhs)
+    near = near_field(window, (tiles0_ref, tiles1_ref), list_ref, sums, nrhs, copies)
     image = image_of(basis, far, self_ref, (rows_high, rows_low), near)
     image_ref[...] = image
     state_ref[...] = jnp.concatenate([far, jnp.broadcast_to(beta, far.shape)], axis=0)
@@ -266,8 +273,8 @@
 
 
 def step1_kernel(
-    got_ref, loads_ref, image_ref, window0_ref, state_ref, rows_high, rows_low, self_ref, tiles_ref,
-    list_vmem, sent_ref, basis_ref, coeff_ref, list_ref, sems, window, *sums,
+    got_ref, loads_ref, image_ref, window0_ref, state_ref, rows_high, rows_low, self_ref, tiles0_ref,
+    list_vmem, tiles1_ref, sent_ref, basis_ref, coeff_ref, list_ref, sems, window, *sums,
 ):
     rank = rows_high.shape[0]
     nrhs, panels = loads_ref.shape
@@ -290,7 +297,7 @@
     basis1 = (image_ref[...] - h00 * basis0) * scale
     far = (far_sum_of(terms, nrhs, rank) - h00 * far0) * scale
     copy.wait()
-    near = near_field(window, (tiles_ref,), list_ref, sums, nrhs)
+    near = near_field(window, (tiles0_ref, tiles1_ref), list_ref, sums, nrhs)
     image = image_of(basis1, far, self_ref, (rows_high, rows_low), near)
     columns = [jnp.sum(a * image, axis=1, keepdims=True) for a in (basis0, basis1, image)]
     sent_ref[:, 0, :] = jnp.broadcast_to(stats_row(columns, rank), (sent_ref.shape[0], LANES))
@@ -361,41 +368,44 @@
     groups = CORES * strips
     message = Plain((groups, nrhs, panels // 2 + LANES), jnp.int32)
     index = pltpu.SMEM(near_list.shape, jnp.int32)
-    scratch = [index, pltpu.SemaphoreType.DMA((1,)), pltpu.VMEM((3 * rows, CORES * nrhs, tile), F32)]
+    index = [index, pltpu.SemaphoreType.DMA((1,))]
+    scratch = [pltpu.VMEM((3 * rows, CORES * nrhs, tile), F32)]
+    early = PIECE * (blocks * 3 // (5 * PIECE))
+    tiles0, tiles1 = (jax.ShapeDtypeStruct((count, tile, tile), BF16) for count in (early, blocks - early))
     scratch += [pltpu.VMEM((CORES * rows, CORES * nrhs, tile), F32)] * 4
 
     def twice(array):
         return [jax.ShapeDtypeStruct(array.shape, BF16)] * 2
 
-    sent, *held, near_list, loads, self_term, near_tiles = call(
+    sent, *held, near_list, loads, self_term, tiles0 = call(
         start_kernel,
         (loads, far_cols, couple, ranks, near_list, far_rows, self_term, near_tiles),
         [
             message, *twice(far_cols), *twice(couple), jax.ShapeDtypeStruct((groups, CHUNK * rank), F32),
-            *twice(far_rows), near_list, loads, self_term, near_tiles,
+            *twice(far_rows), near_list, loads, self_term, tiles0,
         ],
         [
             pltpu.VMEM(far_cols.shape, F32), pltpu.VMEM(couple.shape, F32), pltpu.SMEM(ranks.shape, jnp.int32),
-            pltpu.VMEM(near_list.shape, jnp.int32), pltpu.VMEM(far_rows.shape, F32), pltpu.SemaphoreType.DMA((7 + PIECES,)),
+            pltpu.VMEM(near_list.shape, jnp.int32), pltpu.VMEM(far_rows.shape, F32), pltpu.SemaphoreType.DMA((7 + early // PIECE,)),
         ],
         held=range(8),
     )
-    loads, *held, self_term, near_tiles, near_list = in_vmem([loads, *held, self_term, near_tiles, near_list])
-    source_side, target_side = [loads, *held[:5]], [*held[5:], self_term, near_tiles, near_list]
-    sent, image, window0, state = call(
+    loads, *held, self_term, tiles0, near_list = in_vmem([loads, *held, self_term, tiles0, near_list])
+    source_side, target_side = [loads, *held[:5]], [*held[5:], self_term, tiles0, near_list]
+    sent, image, window0, state, tiles1 = call(
         step0_kernel,
-        (exchanged(sent), *source_side, *target_side),
-        [message, loads.shape, (3 * CORES * nrhs, panels), (CORES * nrhs, LANES)],
-        scratch,
+        (exchanged(sent), *source_side, *target_side, near_tiles),
+        [message, loads.shape, (3 * CORES * nrhs, panels), (CORES * nrhs, LANES), tiles1],
+        index + [pltpu.SemaphoreType.DMA((tiles1.shape[0] // PIECE,))] + scratch,
+        held=(1 + len(source_side) + len(target_side),),
     )
     sent, basis, coeff = call(
         step1_kernel,
-        (exchanged(sent), loads, image, window0, state, *target_side),
+        (exchanged(sent), loads, image, window0, state, *target_side, *in_vmem([tiles1])),
         [(groups, 1, LANES), (2 * nrhs, panels), (3 * nrhs, LANES)],
-        scratch,
+        index + scratch,
     )
-    got = lax.all_to_all(sent, GROUP[::-1], 0, 0, tiled=True)
-    return call(functools.partial(finish_kernel, rank), (got, basis, coeff), [loads.shape])[0]
+    return call(functools.partial(finish_kernel, rank), (exchanged(sent), basis, coeff), [loads.shape])[0]
 
 
 def solution(mesh):

time: 41.7 us -> 42.8 us (1.026)
  Pallas kernels: 5.83 us -> 6.83 us
    all_to_all x2 -> x3, blocking collectives: 26.7 us -> 35.6 us  [exchanged(): return lax.all_to_all(sent, GROUP, 0, 0, tiled=True)]
    all_to_all x1 -> x0, blocking collectives: 8.91 us -> none  [body(): got = lax.all_to_all(sent, GROUP[::-1], 0, 0, tiled=True)]
    pallas_call x4, Pallas kernels: 5.83 us -> 6.83 us  [call(): pl.pallas_call(kernel, out_shape=[jax.ShapeDtypeStruct(out, F32) if isins...]
where the time goes in v14:
time: 42.8 us; the launch traced here: 42.5 us
  blocking collectives  35.6 us (83%)
  Pallas kernels  6.83 us (16%)
    all_to_all x3, blocking collectives, exchanged(): return lax.all_to_all(sent, GROUP, 0, 0, tiled=True)  35.6 us
    pallas_call x4, Pallas kernels, call(): pl.pallas_call(kernel, out_shape=[jax.ShapeDtypeStruct(out, F32) if isins...  6.83 us

profile of v14, /device:TPU:0, one launch (start us, length us, event | category | flops | bytes accessed | tf_op | source)
XLA Modules:
  0.0 42.5 jit_solution(14307777685841611610)
XLA Ops:
  0.0 1.8 %shard_map.82 = (s32[16,4,640]{2,1,0:T(4,128)S(1)}, bf16[32,1024]{1,0:T(8,128)(2,1)S(1)}, bf16[32,1024]{1,0:T(8,128)(2,1)S(1)}, bf16[512,32]{1,0:T(8,128)(2,1)S(...) custom-call(f32[4,1024]{1,0:T(4,128)} %loads_hbm.1, ...), custom_call_target="tpu_custom_call" | custom-call | bytes 2970304 | tf_op jit(solution)/shard_map/pallas_call | solution.py:340
  1.8 15.6 %all_to_all.15.got_ref = s32[16,4,640]{2,1,0:T(4,128)S(1)} all-to-all(s32[16,4,640]{2,1,0:T(4,128)S(1)} %get-tuple-element.25), channel_id=1, replica_groups=mesh['case'=2,'strip'=8,'clus'=2] {'strip','clus'}, dimensions={0} | all-to-all | bytes 327680 | tf_op jit(solution)/shard_map/all_to_all | solution.py:355
  17.5 2.9 %shard_map.83 = (s32[16,4,640]{2,1,0:T(4,128)S(1)}, f32[4,1024]{1,0:T(4,128)S(1)}, f32[24,1024]{1,0:T(8,128)S(1)}, f32[8,128]{1,0:T(8,128)S(1)}, bf16[32,128,128]{2,1,0:T(8,128)(2,1)S(1)}) custom-call(s32[16,4,640]{2,1,0:T(4,128)S(1)} %all_to_all.15.got_ref, f32[4,1024]{1,0:T(4,128)S(1)} %get-tuple-element.26.loads_ref, ...), custom_call_target="tpu_custom_call" | custom-call | bytes 4739712 | tf_op jit(solution)/shard_map/pallas_call | solution.py:340
  20.4 11.1 %all_to_all.16.got_ref = s32[16,4,640]{2,1,0:T(4,128)S(1)} all-to-all(s32[16,4,640]{2,1,0:T(4,128)S(1)} %get-tuple-element.37), channel_id=1, replica_groups=mesh['case'=2,'strip'=8,'clus'=2] {'strip','clus'}, dimensions={0} | all-to-all | bytes 327680 | tf_op jit(solution)/shard_map/all_to_all | solution.py:355
  31.4 1.3 %shard_map.84 = (f32[16,1,128]{2,1,0:T(1,128)S(1)}, f32[8,1024]{1,0:T(8,128)S(1)}, f32[12,128]{1,0:T(8,128)S(1)}) custom-call(s32[16,4,640]{2,1,0:T(4,128)S(1)} %all_to_all.16.got_ref, f32[4,1024]{1,0:T(4,128)S(1)} %get-tuple-element.26.loads_ref, f32[4,1024]{1,0:T(4,128)S(1)} %get-tuple-element.38.image_ref, f32[24,1024]{1,0:T(8,128)S(1)} %get-tuple-element.39.window0_ref, ...), custom_call_target="tpu_custom_call" | custom-call | bytes 3056256 | tf_op jit(solution)/shard_map/pallas_call | solution.py:340
  32.7 9.0 %all_to_all.17.got_ref = f32[16,1,128]{2,1,0:T(1,128)S(1)} all-to-all(f32[16,1,128]{2,1,0:T(1,128)S(1)} %get-tuple-element.42), channel_id=1, replica_groups=mesh['case'=2,'strip'=8,'clus'=2] {'strip','clus'}, dimensions={0} | all-to-all | bytes 16384 | tf_op jit(solution)/shard_map/all_to_all | solution.py:355
  41.7 0.8 %shard_map.85 = f32[4,1024]{1,0:T(4,128)} custom-call(f32[16,1,128]{2,1,0:T(1,128)S(1)} %all_to_all.17.got_ref, f32[8,1024]{1,0:T(8,128)S(1)} %get-tuple-element.43.basis_ref, f32[12,128]{1,0:T(8,128)S(1)} %get-tuple-element.44.coeff_ref), custom_call_target="tpu_custom_call" | custom-call | bytes 47104 | tf_op jit(solution)/shard_map/pallas_call | solution.py:340

commit v15 on v13

--- a/solution.py
+++ b/solution.py
@@ -167,20 +167,15 @@
         held[...] = jnp.zeros_like(held)
     n = 0
     for tiles_ref in tiles:
-        for first in range(0, tiles_ref.shape[0], 4):
-            sources = [window[list_ref[1, n + i]] for i in range(4)]
-            blank = jnp.zeros_like(sources[0])
-            upper = [sources[0], blank, sources[2], blank]
-            lower = [blank, sources[1], blank, sources[3]]
-            left = jnp.concatenate([jnp.concatenate(a, axis=0).astype(BF16) for a in (upper, lower)], axis=1)
-            four = [tiles_ref[first + i] for i in range(4)]
-            right = [jnp.concatenate([four[i], four[i + 2]], axis=1) for i in range(2)]
-            both = jnp.dot(left, jnp.concatenate(right, axis=0), preferred_element_type=F32)
-            for i, held in enumerate(sums):
-                side = i // 2 * LANES
-                rows = i * window.shape[1]
-                held[list_ref[0, n + i]] += both[rows : rows + window.shape[1], side : side + LANES]
-            n += 4
+        for first in range(0, tiles_ref.shape[0], 2):
+            left = jnp.concatenate([window[list_ref[1, n + i]] for i in range(2)], axis=0).astype(BF16)
+            right = jnp.concatenate([tiles_ref[first + i] for i in range(2)], axis=1)
+            both = jnp.dot(left, right, preferred_element_type=F32)
+            rows = window.shape[1]
+            for i in range(2):
+                held = sums[(n + i) % len(sums)]
+                held[list_ref[0, n + i]] += both[i * rows : (i + 1) * rows, i * LANES : (i + 1) * LANES]
+            n += 2
     whole = sum((held[...] for held in sums[1:]), sums[0][...])
     rows = whole.shape[0] // CORES
     return jnp.concatenate([whole[b, :nrhs] + whole[rows + b, nrhs:] for b in range(rows)], axis=1)
@@ -293,7 +288,7 @@
     near = near_field(window, (tiles_ref,), list_ref, sums, nrhs)
     image = image_of(basis1, far, self_ref, (rows_high, rows_low), near)
     columns = [jnp.sum(a * image, axis=1, keepdims=True) for a in (basis0, basis1, image)]
-    sent_ref[:, 0, :] = jnp.broadcast_to(stats_row(columns, rank), (sent_ref.shape[0], LANES))
+    sent_ref[...] = jnp.broadcast_to(stats_row(columns, rank)[None], sent_ref.shape)
     basis_ref[...] = jnp.concatenate([basis0, basis1], axis=0)
     coeff_ref[...] = jnp.concatenate([jnp.broadcast_to(v, (nrhs, LANES)) for v in (beta, h00, h10)], axis=0)
 
@@ -391,11 +386,10 @@
     sent, basis, coeff = call(
         step1_kernel,
         (exchanged(sent), loads, image, window0, state, *target_side),
-        [(groups, 1, LANES), (2 * nrhs, panels), (3 * nrhs, LANES)],
+        [(groups, 8, LANES), (2 * nrhs, panels), (3 * nrhs, LANES)],
         scratch,
     )
-    got = lax.all_to_all(sent, GROUP[::-1], 0, 0, tiled=True)
-    return call(functools.partial(finish_kernel, rank), (got, basis, coeff), [loads.shape])[0]
+    return call(functools.partial(finish_kernel, rank), (exchanged(sent), basis, coeff), [loads.shape])[0]
 
 
 def solution(mesh):

time: 41.7 us -> 42.1 us (level)
  blocking collectives: 35.6 us -> 36.1 us
    all_to_all x2 -> x3, blocking collectives: 26.7 us -> 36.1 us  [exchanged(): return lax.all_to_all(sent, GROUP, 0, 0, tiled=True)]
    all_to_all x1 -> x0, blocking collectives: 8.91 us -> none  [body(): got = lax.all_to_all(sent, GROUP[::-1], 0, 0, tiled=True)]
where the time goes in v15:
time: 42.1 us; the launch traced here: 41.8 us
  blocking collectives  36.1 us (86%)
  Pallas kernels  5.63 us (13%)
    all_to_all x3, blocking collectives, exchanged(): return lax.all_to_all(sent, GROUP, 0, 0, tiled=True)  36.1 us
    pallas_call x4, Pallas kernels, call(): pl.pallas_call(kernel, out_shape=[jax.ShapeDtypeStruct(out, F32) if isins...  5.63 us

profile of v15, /device:TPU:0, one launch (start us, length us, event | category | flops | bytes accessed | tf_op | source)
XLA Modules:
  0.0 41.8 jit_solution(3264887628745024864)
XLA Ops:
  0.0 2.1 %shard_map.82 = (s32[16,4,640]{2,1,0:T(4,128)S(1)}, bf16[32,1024]{1,0:T(8,128)(2,1)S(1)}, bf16[32,1024]{1,0:T(8,128)(2,1)S(1)}, bf16[512,32]{1,0:T(8,128)(2,1)S(...) custom-call(f32[4,1024]{1,0:T(4,128)} %loads_hbm.1, ...), custom_call_target="tpu_custom_call" | custom-call | bytes 2970304 | tf_op jit(solution)/shard_map/pallas_call | solution.py:328
  2.1 15.6 %all_to_all.15.got_ref = s32[16,4,640]{2,1,0:T(4,128)S(1)} all-to-all(s32[16,4,640]{2,1,0:T(4,128)S(1)} %get-tuple-element.24), channel_id=1, replica_groups=mesh['case'=2,'strip'=8,'clus'=2] {'strip','clus'}, dimensions={0} | all-to-all | bytes 327680 | tf_op jit(solution)/shard_map/all_to_all | solution.py:343
  17.7 1.6 %shard_map.83 = (s32[16,4,640]{2,1,0:T(4,128)S(1)}, f32[4,1024]{1,0:T(4,128)S(1)}, f32[24,1024]{1,0:T(8,128)S(1)}, f32[8,128]{1,0:T(8,128)S(1)}) custom-call(s32[16,4,640]{2,1,0:T(4,128)S(1)} %all_to_all.15.got_ref, f32[4,1024]{1,0:T(4,128)S(1)} %get-tuple-element.25.loads_ref, bf16[32,1024]{1,0:T(8,128)(2,1)S(1)} %get-tuple-element.26.cols_high, ...), custom_call_target="tpu_custom_call" | custom-call | bytes 3166848 | tf_op jit(solution)/shard_map/pallas_call | solution.py:328
  19.3 11.1 %all_to_all.16.got_ref = s32[16,4,640]{2,1,0:T(4,128)S(1)} all-to-all(s32[16,4,640]{2,1,0:T(4,128)S(1)} %get-tuple-element.36), channel_id=1, replica_groups=mesh['case'=2,'strip'=8,'clus'=2] {'strip','clus'}, dimensions={0} | all-to-all | bytes 327680 | tf_op jit(solution)/shard_map/all_to_all | solution.py:343
  30.3 1.2 %shard_map.84 = (f32[16,8,128]{2,1,0:T(8,128)S(1)}, f32[8,1024]{1,0:T(8,128)S(1)}, f32[12,128]{1,0:T(8,128)S(1)}) custom-call(s32[16,4,640]{2,1,0:T(4,128)S(1)} %all_to_all.16.got_ref, f32[4,1024]{1,0:T(4,128)S(1)} %get-tuple-element.25.loads_ref, f32[4,1024]{1,0:T(4,128)S(1)} %get-tuple-element.37.image_ref, f32[24,1024]{1,0:T(8,128)S(1)} %get-tuple-element.38.window0_ref, ...), custom_call_target="tpu_custom_call" | custom-call | bytes 3056256 | tf_op jit(solution)/shard_map/pallas_call | solution.py:328
  31.5 9.5 %all_to_all.17.got_ref = f32[16,8,128]{2,1,0:T(8,128)S(1)} all-to-all(f32[16,8,128]{2,1,0:T(8,128)S(1)} %get-tuple-element.40), channel_id=1, replica_groups=mesh['case'=2,'strip'=8,'clus'=2] {'strip','clus'}, dimensions={0} | all-to-all | bytes 131072 | tf_op jit(solution)/shard_map/all_to_all | solution.py:343
  41.0 0.8 %shard_map.85 = f32[4,1024]{1,0:T(4,128)} custom-call(f32[16,8,128]{2,1,0:T(8,128)S(1)} %all_to_all.17.got_ref, f32[8,1024]{1,0:T(8,128)S(1)} %get-tuple-element.41.basis_ref, f32[12,128]{1,0:T(8,128)S(1)} %get-tuple-element.42.coeff_ref), custom_call_target="tpu_custom_call" | custom-call | bytes 104448 | tf_op jit(solution)/shard_map/pallas_call | solution.py:328

commit v16 on v15

--- a/solution.py
+++ b/solution.py
@@ -288,7 +288,7 @@
     near = near_field(window, (tiles_ref,), list_ref, sums, nrhs)
     image = image_of(basis1, far, self_ref, (rows_high, rows_low), near)
     columns = [jnp.sum(a * image, axis=1, keepdims=True) for a in (basis0, basis1, image)]
-    sent_ref[...] = jnp.broadcast_to(stats_row(columns, rank)[None], sent_ref.shape)
+    sent_ref[:, 0, :] = jnp.broadcast_to(stats_row(columns, rank), (sent_ref.shape[0], LANES))
     basis_ref[...] = jnp.concatenate([basis0, basis1], axis=0)
     coeff_ref[...] = jnp.concatenate([jnp.broadcast_to(v, (nrhs, LANES)) for v in (beta, h00, h10)], axis=0)
 
@@ -386,7 +386,7 @@
     sent, basis, coeff = call(
         step1_kernel,
         (exchanged(sent), loads, image, window0, state, *target_side),
-        [(groups, 8, LANES), (2 * nrhs, panels), (3 * nrhs, LANES)],
+        [(groups, 1, LANES), (2 * nrhs, panels), (3 * nrhs, LANES)],
         scratch,
     )
     return call(functools.partial(finish_kernel, rank), (exchanged(sent), basis, coeff), [loads.shape])[0]

time: 42.1 us -> 41.6 us (0.988)
  blocking collectives: 36.1 us -> 35.6 us
    all_to_all x3, blocking collectives: 36.1 us -> 35.6 us  [exchanged(): return lax.all_to_all(sent, GROUP, 0, 0, tiled=True)]
where the time goes in v16:
time: 41.6 us; the launch traced here: 41.3 us
  blocking collectives  35.6 us (86%)
  Pallas kernels  5.62 us (14%)
    all_to_all x3, blocking collectives, exchanged(): return lax.all_to_all(sent, GROUP, 0, 0, tiled=True)  35.6 us
    pallas_call x4, Pallas kernels, call(): pl.pallas_call(kernel, out_shape=[jax.ShapeDtypeStruct(out, F32) if isins...  5.62 us

profile of v16, /device:TPU:0, one launch (start us, length us, event | category | flops | bytes accessed | tf_op | source)
XLA Modules:
  0.0 41.3 jit_solution(5761631373526477544)
XLA Ops:
  0.0 2.1 %shard_map.82 = (s32[16,4,640]{2,1,0:T(4,128)S(1)}, bf16[32,1024]{1,0:T(8,128)(2,1)S(1)}, bf16[32,1024]{1,0:T(8,128)(2,1)S(1)}, bf16[512,32]{1,0:T(8,128)(2,1)S(...) custom-call(f32[4,1024]{1,0:T(4,128)} %loads_hbm.1, ...), custom_call_target="tpu_custom_call" | custom-call | bytes 2970304 | tf_op jit(solution)/shard_map/pallas_call | solution.py:328
  2.1 15.6 %all_to_all.15.got_ref = s32[16,4,640]{2,1,0:T(4,128)S(1)} all-to-all(s32[16,4,640]{2,1,0:T(4,128)S(1)} %get-tuple-element.24), channel_id=1, replica_groups=mesh['case'=2,'strip'=8,'clus'=2] {'strip','clus'}, dimensions={0} | all-to-all | bytes 327680 | tf_op jit(solution)/shard_map/all_to_all | solution.py:343
  17.7 1.6 %shard_map.83 = (s32[16,4,640]{2,1,0:T(4,128)S(1)}, f32[4,1024]{1,0:T(4,128)S(1)}, f32[24,1024]{1,0:T(8,128)S(1)}, f32[8,128]{1,0:T(8,128)S(1)}) custom-call(s32[16,4,640]{2,1,0:T(4,128)S(1)} %all_to_all.15.got_ref, f32[4,1024]{1,0:T(4,128)S(1)} %get-tuple-element.25.loads_ref, bf16[32,1024]{1,0:T(8,128)(2,1)S(1)} %get-tuple-element.26.cols_high, ...), custom_call_target="tpu_custom_call" | custom-call | bytes 3166848 | tf_op jit(solution)/shard_map/pallas_call | solution.py:328
  19.3 11.1 %all_to_all.16.got_ref = s32[16,4,640]{2,1,0:T(4,128)S(1)} all-to-all(s32[16,4,640]{2,1,0:T(4,128)S(1)} %get-tuple-element.36), channel_id=1, replica_groups=mesh['case'=2,'strip'=8,'clus'=2] {'strip','clus'}, dimensions={0} | all-to-all | bytes 327680 | tf_op jit(solution)/shard_map/all_to_all | solution.py:343
  30.3 1.2 %shard_map.84 = (f32[16,1,128]{2,1,0:T(1,128)S(1)}, f32[8,1024]{1,0:T(8,128)S(1)}, f32[12,128]{1,0:T(8,128)S(1)}) custom-call(s32[16,4,640]{2,1,0:T(4,128)S(1)} %all_to_all.16.got_ref, f32[4,1024]{1,0:T(4,128)S(1)} %get-tuple-element.25.loads_ref, f32[4,1024]{1,0:T(4,128)S(1)} %get-tuple-element.37.image_ref, f32[24,1024]{1,0:T(8,128)S(1)} %get-tuple-element.38.window0_ref, ...), custom_call_target="tpu_custom_call" | custom-call | bytes 3056256 | tf_op jit(solution)/shard_map/pallas_call | solution.py:328
  31.5 9.0 %all_to_all.17.got_ref = f32[16,1,128]{2,1,0:T(1,128)S(1)} all-to-all(f32[16,1,128]{2,1,0:T(1,128)S(1)} %get-tuple-element.40), channel_id=1, replica_groups=mesh['case'=2,'strip'=8,'clus'=2] {'strip','clus'}, dimensions={0} | all-to-all | bytes 16384 | tf_op jit(solution)/shard_map/all_to_all | solution.py:343
  40.5 0.8 %shard_map.85 = f32[4,1024]{1,0:T(4,128)} custom-call(f32[16,1,128]{2,1,0:T(1,128)S(1)} %all_to_all.17.got_ref, f32[8,1024]{1,0:T(8,128)S(1)} %get-tuple-element.41.basis_ref, f32[12,128]{1,0:T(8,128)S(1)} %get-tuple-element.42.coeff_ref), custom_call_target="tpu_custom_call" | custom-call | bytes 47104 | tf_op jit(solution)/shard_map/pallas_call | solution.py:328

commit v17 on v16

--- a/solution.py
+++ b/solution.py
@@ -11,7 +11,7 @@
 CORES = 2
 LANES = 128
 CHUNK = 16
-PIECES = 10
+PIECES = 5
 F32 = jnp.float32
 BF16 = jnp.bfloat16
 
@@ -194,14 +194,12 @@
     every = tiles_ref.shape[0] // PIECES
     pieces = [pl.ds(i * every, every) for i in range(PIECES)]
     copies = fetch(pairs + tuple((tiles_hbm.at[p], tiles_ref.at[p]) for p in pieces), sems)
-    copies[0].wait()
+    for copy in copies[: len(pairs)]:
+        copy.wait()
     loads = loads_ref[...]
     square = jnp.sum(loads * loads, axis=1, keepdims=True)
-    copies[1].wait()
     cols_high[...], cols_low[...] = halves(cols_ref[...])
-    copies[2].wait()
     couple_high[...], couple_low[...] = halves(couple_ref[...])
-    copies[3].wait()
     shape = (CHUNK, CHUNK * rank)
     owner = lax.div(lanes_of(shape), rank)
     inner = lax.rem(lanes_of(shape), rank)
@@ -210,22 +208,19 @@
         for i in range(CHUNK):
             limit = jnp.where(owner[:1] == i, ranks_ref[0, start + i], limit)
         masks_ref[pl.ds(start, CHUNK), :] = jnp.where((owner == rows_of(shape)) & (inner < limit), 1.0, 0.0)
-    copies[4].wait()
+    put_message(loads, [square], (cols_high, cols_low), (couple_high, couple_low), masks_ref, sent_ref)
     count = panels // LANES
     target, source = raw_ref[0:1, :], raw_ref[1:2, :]
     group, block = lax.div(source, count), lax.rem(source, count)
     strip, core = lax.div(group, CORES), lax.rem(group, CORES)
     list_ref[...] = jnp.concatenate([core * count + target, strip * count + block], axis=0)
-    copies[5].wait()
     rows_high[...], rows_low[...] = halves(rows_ref[...])
-    put_message(loads, [square], (cols_high, cols_low), (couple_high, couple_low), masks_ref, sent_ref)
-    for copy in copies[6:]:
+    for copy in copies[len(pairs) :]:
         copy.wait()
 
 
-def image_of(field, far, self_ref, far_rows, near):
-    rank = far_rows[0].shape[0]
-    return self_ref[...] * field + near + product(far[:, :rank], far_rows[0][...], far_rows[1][...])
+def far_field(far, far_rows):
+    return product(far[:, : far_rows[0].shape[0]], far_rows[0][...], far_rows[1][...])
 
 
 def step0_kernel(
@@ -246,12 +241,12 @@
         put_blocks(part, step * span, window)
     basis = loads_ref[...] * scale
     far = far_sum_of(terms, nrhs, rank) * scale
+    image = self_ref[...] * basis + far_field(far, (rows_high, rows_low))
+    norm = jnp.sum(basis * basis, axis=1, keepdims=True)
     copy.wait()
-    near = near_field(window, (tiles_ref,), list_ref, sums, nrhs)
-    image = image_of(basis, far, self_ref, (rows_high, rows_low), near)
+    image = image + near_field(window, (tiles_ref,), list_ref, sums, nrhs)
     image_ref[...] = image
     state_ref[...] = jnp.concatenate([far, jnp.broadcast_to(beta, far.shape)], axis=0)
-    norm = jnp.sum(basis * basis, axis=1, keepdims=True)
     dot = jnp.sum(basis * image, axis=1, keepdims=True)
     share = jnp.where(norm > 0, dot / jnp.where(norm > 0, norm, 1.0), 0.0)
     rest = image - share * basis
@@ -284,9 +279,9 @@
     basis0 = loads_ref[...] * (1.0 / beta)
     basis1 = (image_ref[...] - h00 * basis0) * scale
     far = (far_sum_of(terms, nrhs, rank) - h00 * far0) * scale
+    image = self_ref[...] * basis1 + far_field(far, (rows_high, rows_low))
     copy.wait()
-    near = near_field(window, (tiles_ref,), list_ref, sums, nrhs)
-    image = image_of(basis1, far, self_ref, (rows_high, rows_low), near)
+    image = image + near_field(window, (tiles_ref,), list_ref, sums, nrhs)
     columns = [jnp.sum(a * image, axis=1, keepdims=True) for a in (basis0, basis1, image)]
     sent_ref[:, 0, :] = jnp.broadcast_to(stats_row(columns, rank), (sent_ref.shape[0], LANES))
     basis_ref[...] = jnp.concatenate([basis0, basis1], axis=0)

time: 41.6 us -> 41.8 us (level)
  no operation moved by 1% of the time
where the time goes in v17:
time: 41.8 us; the launch traced here: 41.4 us
  blocking collectives  35.6 us (85%)
  Pallas kernels  5.77 us (14%)
    all_to_all x3, blocking collectives, exchanged(): return lax.all_to_all(sent, GROUP, 0, 0, tiled=True)  35.6 us
    pallas_call x4, Pallas kernels, call(): pl.pallas_call(kernel, out_shape=[jax.ShapeDtypeStruct(out, F32) if isins...  5.77 us

profile of v17, /device:TPU:0, one launch (start us, length us, event | category | flops | bytes accessed | tf_op | source)
XLA Modules:
  0.0 41.4 jit_solution(457063265323988800)
XLA Ops:
  0.0 2.0 %shard_map.82 = (s32[16,4,640]{2,1,0:T(4,128)S(1)}, bf16[32,1024]{1,0:T(8,128)(2,1)S(1)}, bf16[32,1024]{1,0:T(8,128)(2,1)S(1)}, bf16[512,32]{1,0:T(8,128)(2,1)S(...) custom-call(f32[4,1024]{1,0:T(4,128)} %loads_hbm.1, ...), custom_call_target="tpu_custom_call" | custom-call | bytes 2970304 | tf_op jit(solution)/shard_map/pallas_call | solution.py:323
  2.0 15.6 %all_to_all.15.got_ref = s32[16,4,640]{2,1,0:T(4,128)S(1)} all-to-all(s32[16,4,640]{2,1,0:T(4,128)S(1)} %get-tuple-element.24), channel_id=1, replica_groups=mesh['case'=2,'strip'=8,'clus'=2] {'strip','clus'}, dimensions={0} | all-to-all | bytes 327680 | tf_op jit(solution)/shard_map/all_to_all | solution.py:338
  17.7 1.6 %shard_map.83 = (s32[16,4,640]{2,1,0:T(4,128)S(1)}, f32[4,1024]{1,0:T(4,128)S(1)}, f32[24,1024]{1,0:T(8,128)S(1)}, f32[8,128]{1,0:T(8,128)S(1)}) custom-call(s32[16,4,640]{2,1,0:T(4,128)S(1)} %all_to_all.15.got_ref, f32[4,1024]{1,0:T(4,128)S(1)} %get-tuple-element.25.loads_ref, bf16[32,1024]{1,0:T(8,128)(2,1)S(1)} %get-tuple-element.26.cols_high, ...), custom_call_target="tpu_custom_call" | custom-call | bytes 3166848 | tf_op jit(solution)/shard_map/pallas_call | solution.py:323
  19.2 11.1 %all_to_all.16.got_ref = s32[16,4,640]{2,1,0:T(4,128)S(1)} all-to-all(s32[16,4,640]{2,1,0:T(4,128)S(1)} %get-tuple-element.36), channel_id=1, replica_groups=mesh['case'=2,'strip'=8,'clus'=2] {'strip','clus'}, dimensions={0} | all-to-all | bytes 327680 | tf_op jit(solution)/shard_map/all_to_all | solution.py:338
  30.3 1.4 %shard_map.84 = (f32[16,1,128]{2,1,0:T(1,128)S(1)}, f32[8,1024]{1,0:T(8,128)S(1)}, f32[12,128]{1,0:T(8,128)S(1)}) custom-call(s32[16,4,640]{2,1,0:T(4,128)S(1)} %all_to_all.16.got_ref, f32[4,1024]{1,0:T(4,128)S(1)} %get-tuple-element.25.loads_ref, f32[4,1024]{1,0:T(4,128)S(1)} %get-tuple-element.37.image_ref, f32[24,1024]{1,0:T(8,128)S(1)} %get-tuple-element.38.window0_ref, ...), custom_call_target="tpu_custom_call" | custom-call | bytes 3056256 | tf_op jit(solution)/shard_map/pallas_call | solution.py:323
  31.7 9.0 %all_to_all.17.got_ref = f32[16,1,128]{2,1,0:T(1,128)S(1)} all-to-all(f32[16,1,128]{2,1,0:T(1,128)S(1)} %get-tuple-element.40), channel_id=1, replica_groups=mesh['case'=2,'strip'=8,'clus'=2] {'strip','clus'}, dimensions={0} | all-to-all | bytes 16384 | tf_op jit(solution)/shard_map/all_to_all | solution.py:338
  40.6 0.8 %shard_map.85 = f32[4,1024]{1,0:T(4,128)} custom-call(f32[16,1,128]{2,1,0:T(1,128)S(1)} %all_to_all.17.got_ref, f32[8,1024]{1,0:T(8,128)S(1)} %get-tuple-element.41.basis_ref, f32[12,128]{1,0:T(8,128)S(1)} %get-tuple-element.42.coeff_ref), custom_call_target="tpu_custom_call" | custom-call | bytes 47104 | tf_op jit(solution)/shard_map/pallas_call | solution.py:323

commit v18 on v16

--- a/solution.py
+++ b/solution.py
@@ -239,6 +239,7 @@
     terms, stats = message_parts(got_ref, rank)
     beta = jnp.sqrt(stat_column(total(stats), 0, nrhs, rank))
     scale = 1.0 / beta
+    copy.wait()
     both = jnp.concatenate([scale] * CORES, axis=0)
     for step, (inside, part, unit) in enumerate(window_parts(got_ref, rank)):
         part = jnp.where(inside, part * (unit * both), 0.0)
@@ -246,7 +247,6 @@
         put_blocks(part, step * span, window)
     basis = loads_ref[...] * scale
     far = far_sum_of(terms, nrhs, rank) * scale
-    copy.wait()
     near = near_field(window, (tiles_ref,), list_ref, sums, nrhs)
     image = image_of(basis, far, self_ref, (rows_high, rows_low), near)
     image_ref[...] = image
@@ -277,6 +277,7 @@
     rest = total(shifted(stats, 3) + stats * away * away)
     h10 = jnp.sqrt(stat_column(rest, 0, nrhs, rank))
     scale = 1.0 / h10
+    copy.wait()
     both, both_h00 = (jnp.concatenate([a] * CORES, axis=0) for a in (scale, h00))
     for step, (inside, part, unit) in enumerate(window_parts(got_ref, rank)):
         part = (part * unit - both_h00 * window0_ref[step * rows : (step + 1) * rows, :]) * both
@@ -284,7 +285,6 @@
     basis0 = loads_ref[...] * (1.0 / beta)
     basis1 = (image_ref[...] - h00 * basis0) * scale
     far = (far_sum_of(terms, nrhs, rank) - h00 * far0) * scale
-    copy.wait()
     near = near_field(window, (tiles_ref,), list_ref, sums, nrhs)
     image = image_of(basis1, far, self_ref, (rows_high, rows_low), near)
     columns = [jnp.sum(a * image, axis=1, keepdims=True) for a in (basis0, basis1, image)]

time: 41.6 us -> 41.9 us (level)
  no operation moved by 1% of the time
where the time goes in v18:
time: 41.9 us; the launch traced here: 41.6 us
  blocking collectives  35.6 us (85%)
  Pallas kernels  5.9 us (14%)
    all_to_all x3, blocking collectives, exchanged(): return lax.all_to_all(sent, GROUP, 0, 0, tiled=True)  35.6 us
    pallas_call x4, Pallas kernels, call(): pl.pallas_call(kernel, out_shape=[jax.ShapeDtypeStruct(out, F32) if isins...  5.9 us

profile of v18, /device:TPU:0, one launch (start us, length us, event | category | flops | bytes accessed | tf_op | source)
XLA Modules:
  0.0 41.6 jit_solution(11648543799989759716)
XLA Ops:
  0.0 2.1 %shard_map.82 = (s32[16,4,640]{2,1,0:T(4,128)S(1)}, bf16[32,1024]{1,0:T(8,128)(2,1)S(1)}, bf16[32,1024]{1,0:T(8,128)(2,1)S(1)}, bf16[512,32]{1,0:T(8,128)(2,1)S(...) custom-call(f32[4,1024]{1,0:T(4,128)} %loads_hbm.1, ...), custom_call_target="tpu_custom_call" | custom-call | bytes 2970304 | tf_op jit(solution)/shard_map/pallas_call | solution.py:328
  2.1 15.6 %all_to_all.15.got_ref = s32[16,4,640]{2,1,0:T(4,128)S(1)} all-to-all(s32[16,4,640]{2,1,0:T(4,128)S(1)} %get-tuple-element.24), channel_id=1, replica_groups=mesh['case'=2,'strip'=8,'clus'=2] {'strip','clus'}, dimensions={0} | all-to-all | bytes 327680 | tf_op jit(solution)/shard_map/all_to_all | solution.py:343
  17.7 1.7 %shard_map.83 = (s32[16,4,640]{2,1,0:T(4,128)S(1)}, f32[4,1024]{1,0:T(4,128)S(1)}, f32[24,1024]{1,0:T(8,128)S(1)}, f32[8,128]{1,0:T(8,128)S(1)}) custom-call(s32[16,4,640]{2,1,0:T(4,128)S(1)} %all_to_all.15.got_ref, f32[4,1024]{1,0:T(4,128)S(1)} %get-tuple-element.25.loads_ref, bf16[32,1024]{1,0:T(8,128)(2,1)S(1)} %get-tuple-element.26.cols_high, ...), custom_call_target="tpu_custom_call" | custom-call | bytes 3166848 | tf_op jit(solution)/shard_map/pallas_call | solution.py:328
  19.4 11.1 %all_to_all.16.got_ref = s32[16,4,640]{2,1,0:T(4,128)S(1)} all-to-all(s32[16,4,640]{2,1,0:T(4,128)S(1)} %get-tuple-element.36), channel_id=1, replica_groups=mesh['case'=2,'strip'=8,'clus'=2] {'strip','clus'}, dimensions={0} | all-to-all | bytes 327680 | tf_op jit(solution)/shard_map/all_to_all | solution.py:343
  30.5 1.3 %shard_map.84 = (f32[16,1,128]{2,1,0:T(1,128)S(1)}, f32[8,1024]{1,0:T(8,128)S(1)}, f32[12,128]{1,0:T(8,128)S(1)}) custom-call(s32[16,4,640]{2,1,0:T(4,128)S(1)} %all_to_all.16.got_ref, f32[4,1024]{1,0:T(4,128)S(1)} %get-tuple-element.25.loads_ref, f32[4,1024]{1,0:T(4,128)S(1)} %get-tuple-element.37.image_ref, f32[24,1024]{1,0:T(8,128)S(1)} %get-tuple-element.38.window0_ref, ...), custom_call_target="tpu_custom_call" | custom-call | bytes 3056256 | tf_op jit(solution)/shard_map/pallas_call | solution.py:328
  31.8 9.0 %all_to_all.17.got_ref = f32[16,1,128]{2,1,0:T(1,128)S(1)} all-to-all(f32[16,1,128]{2,1,0:T(1,128)S(1)} %get-tuple-element.40), channel_id=1, replica_groups=mesh['case'=2,'strip'=8,'clus'=2] {'strip','clus'}, dimensions={0} | all-to-all | bytes 16384 | tf_op jit(solution)/shard_map/all_to_all | solution.py:343
  40.8 0.8 %shard_map.85 = f32[4,1024]{1,0:T(4,128)} custom-call(f32[16,1,128]{2,1,0:T(1,128)S(1)} %all_to_all.17.got_ref, f32[8,1024]{1,0:T(8,128)S(1)} %get-tuple-element.41.basis_ref, f32[12,128]{1,0:T(8,128)S(1)} %get-tuple-element.42.coeff_ref), custom_call_target="tpu_custom_call" | custom-call | bytes 47104 | tf_op jit(solution)/shard_map/pallas_call | solution.py:328

commit v19 on v16

--- a/solution.py
+++ b/solution.py
@@ -163,8 +163,6 @@
 
 
 def near_field(window, tiles, list_ref, sums, nrhs):
-    for held in sums:
-        held[...] = jnp.zeros_like(held)
     n = 0
     for tiles_ref in tiles:
         for first in range(0, tiles_ref.shape[0], 2):
@@ -236,6 +234,8 @@
     nrhs, panels = loads_ref.shape
     span, rows = panels // LANES, CORES * nrhs
     (copy,) = fetch(((list_vmem, list_ref),), sems)
+    for held in sums:
+        held[...] = jnp.zeros_like(held)
     terms, stats = message_parts(got_ref, rank)
     beta = jnp.sqrt(stat_column(total(stats), 0, nrhs, rank))
     scale = 1.0 / beta
@@ -246,12 +246,12 @@
         put_blocks(part, step * span, window)
     basis = loads_ref[...] * scale
     far = far_sum_of(terms, nrhs, rank) * scale
+    norm = jnp.sum(basis * basis, axis=1, keepdims=True)
     copy.wait()
     near = near_field(window, (tiles_ref,), list_ref, sums, nrhs)
     image = image_of(basis, far, self_ref, (rows_high, rows_low), near)
     image_ref[...] = image
     state_ref[...] = jnp.concatenate([far, jnp.broadcast_to(beta, far.shape)], axis=0)
-    norm = jnp.sum(basis * basis, axis=1, keepdims=True)
     dot = jnp.sum(basis * image, axis=1, keepdims=True)
     share = jnp.where(norm > 0, dot / jnp.where(norm > 0, norm, 1.0), 0.0)
     rest = image - share * basis
@@ -270,6 +270,8 @@
     (copy,) = fetch(((list_vmem, list_ref),), sems)
     beta = state_ref[nrhs:, :1]
     far0 = state_ref[:nrhs, :]
+    for held in sums:
+        held[...] = jnp.zeros_like(held)
     terms, stats = message_parts(got_ref, rank)
     summed = total(stats)
     h00 = stat_column(summed, 1, nrhs, rank)

time: 41.6 us -> 41.6 us (level)
  no operation moved by 1% of the time
where the time goes in v19:
time: 41.6 us; the launch traced here: 41.3 us
  blocking collectives  35.6 us (86%)
  Pallas kernels  5.63 us (14%)
    all_to_all x3, blocking collectives, exchanged(): return lax.all_to_all(sent, GROUP, 0, 0, tiled=True)  35.6 us
    pallas_call x4, Pallas kernels, call(): pl.pallas_call(kernel, out_shape=[jax.ShapeDtypeStruct(out, F32) if isins...  5.63 us

profile of v19, /device:TPU:0, one launch (start us, length us, event | category | flops | bytes accessed | tf_op | source)
XLA Modules:
  0.0 41.3 jit_solution(12607207569216222714)
XLA Ops:
  0.0 2.1 %shard_map.82 = (s32[16,4,640]{2,1,0:T(4,128)S(1)}, bf16[32,1024]{1,0:T(8,128)(2,1)S(1)}, bf16[32,1024]{1,0:T(8,128)(2,1)S(1)}, bf16[512,32]{1,0:T(8,128)(2,1)S(...) custom-call(f32[4,1024]{1,0:T(4,128)} %loads_hbm.1, ...), custom_call_target="tpu_custom_call" | custom-call | bytes 2970304 | tf_op jit(solution)/shard_map/pallas_call | solution.py:330
  2.1 15.6 %all_to_all.15.got_ref = s32[16,4,640]{2,1,0:T(4,128)S(1)} all-to-all(s32[16,4,640]{2,1,0:T(4,128)S(1)} %get-tuple-element.24), channel_id=1, replica_groups=mesh['case'=2,'strip'=8,'clus'=2] {'strip','clus'}, dimensions={0} | all-to-all | bytes 327680 | tf_op jit(solution)/shard_map/all_to_all | solution.py:345
  17.7 1.6 %shard_map.83 = (s32[16,4,640]{2,1,0:T(4,128)S(1)}, f32[4,1024]{1,0:T(4,128)S(1)}, f32[24,1024]{1,0:T(8,128)S(1)}, f32[8,128]{1,0:T(8,128)S(1)}) custom-call(s32[16,4,640]{2,1,0:T(4,128)S(1)} %all_to_all.15.got_ref, f32[4,1024]{1,0:T(4,128)S(1)} %get-tuple-element.25.loads_ref, bf16[32,1024]{1,0:T(8,128)(2,1)S(1)} %get-tuple-element.26.cols_high, ...), custom_call_target="tpu_custom_call" | custom-call | bytes 3166848 | tf_op jit(solution)/shard_map/pallas_call | solution.py:330
  19.3 11.1 %all_to_all.16.got_ref = s32[16,4,640]{2,1,0:T(4,128)S(1)} all-to-all(s32[16,4,640]{2,1,0:T(4,128)S(1)} %get-tuple-element.36), channel_id=1, replica_groups=mesh['case'=2,'strip'=8,'clus'=2] {'strip','clus'}, dimensions={0} | all-to-all | bytes 327680 | tf_op jit(solution)/shard_map/all_to_all | solution.py:345
  30.3 1.2 %shard_map.84 = (f32[16,1,128]{2,1,0:T(1,128)S(1)}, f32[8,1024]{1,0:T(8,128)S(1)}, f32[12,128]{1,0:T(8,128)S(1)}) custom-call(s32[16,4,640]{2,1,0:T(4,128)S(1)} %all_to_all.16.got_ref, f32[4,1024]{1,0:T(4,128)S(1)} %get-tuple-element.25.loads_ref, f32[4,1024]{1,0:T(4,128)S(1)} %get-tuple-element.37.image_ref, f32[24,1024]{1,0:T(8,128)S(1)} %get-tuple-element.38.window0_ref, ...), custom_call_target="tpu_custom_call" | custom-call | bytes 3056256 | tf_op jit(solution)/shard_map/pallas_call | solution.py:330
  31.5 9.0 %all_to_all.17.got_ref = f32[16,1,128]{2,1,0:T(1,128)S(1)} all-to-all(f32[16,1,128]{2,1,0:T(1,128)S(1)} %get-tuple-element.40), channel_id=1, replica_groups=mesh['case'=2,'strip'=8,'clus'=2] {'strip','clus'}, dimensions={0} | all-to-all | bytes 16384 | tf_op jit(solution)/shard_map/all_to_all | solution.py:345
  40.5 0.8 %shard_map.85 = f32[4,1024]{1,0:T(4,128)} custom-call(f32[16,1,128]{2,1,0:T(1,128)S(1)} %all_to_all.17.got_ref, f32[8,1024]{1,0:T(8,128)S(1)} %get-tuple-element.41.basis_ref, f32[12,128]{1,0:T(8,128)S(1)} %get-tuple-element.42.coeff_ref), custom_call_target="tpu_custom_call" | custom-call | bytes 47104 | tf_op jit(solution)/shard_map/pallas_call | solution.py:330

commit v20 on v19

--- a/solution.py
+++ b/solution.py
@@ -121,36 +121,39 @@
     finer = 1.0 / (steps_of(row, rank) * unit)
     for i in range(sent_ref.shape[0]):
         sent_ref[i, :, :width] = words
-    stats = [jnp.broadcast_to(a, (CHUNK, LANES)) for a in coded(row)]
-    for start in range(0, sent_ref.shape[0], CHUNK):
-        mask = masks_ref[pl.ds(start, CHUNK), :]
+    half = CHUNK // CORES
+    stats = [jnp.broadcast_to(a, (half, LANES)) for a in coded(row)]
+    for start in range(0, sent_ref.shape[0], half):
+        mask = masks_ref[pl.ds(CORES * start, CHUNK), :]
         spread = jnp.concatenate([mask * wide[r : r + 1] for r in range(nrhs)], axis=0)
-        here = pl.ds(start * rank, CHUNK * rank)
+        here = pl.ds(CORES * start * rank, CHUNK * rank)
         terms = product(spread, couple[0][here, :], couple[1][here, :])
         terms = jnp.concatenate([terms[r * CHUNK : (r + 1) * CHUNK] for r in range(nrhs)], axis=1)
-        here = pl.ds(start, CHUNK)
-        for k, value in enumerate([(terms * finer).astype(jnp.int32)] + stats + [stats[0]] * (nrhs - 3)):
+        terms = (terms * finer).astype(jnp.int32)
+        here = pl.ds(start, half)
+        for k, value in enumerate([terms[:half], terms[half:]] + stats):
             sent_ref[here, k, width:] = value
 
 
-def message_parts(got_ref, rank):
-    width = got_ref.shape[2] - LANES
-    stats = decoded(got_ref[:, 1, width:], got_ref[:, 2, width:])
-    terms = got_ref[:, 0, width:].astype(F32) * (steps_of(stats, rank) * term_unit(2 * width, rank))
-    return total(terms), stats
-
-
-def window_parts(got_ref, rank):
-    nrhs, width = got_ref.shape[1], got_ref.shape[2] - LANES
-    strips = got_ref.shape[0] // CORES
+def message_parts(got, rank):
+    width = got[0].shape[2] - LANES
+    first, second, mantissa, exponent = (jnp.concatenate([ref[:, k, width:] for ref in got], axis=0) for k in range(4))
+    stats = decoded(mantissa, exponent)
+    terms = jnp.where(lax.axis_index("clus") == 0, first, second).astype(F32)
+    return total(terms * (steps_of(stats, rank) * term_unit(2 * width, rank))), stats
+
+
+def window_parts(got, rank):
+    strips, nrhs, width = got[0].shape
+    width -= LANES
     shape = (CORES * nrhs, LANES)
     for step in range(3):
         owner = lax.axis_index("strip") + (step - 1)
         inside = (owner >= 0) & (owner < strips)
-        owner = CORES * jnp.clip(owner, 0, strips - 1)
-        words = jnp.concatenate([got_ref[owner + core, :, :width] for core in range(CORES)], axis=0)
-        tails = [got_ref[owner + core, :, width:] for core in range(CORES)]
-        rows = [decoded(tail[1:2], tail[2:3]) for tail in tails]
+        owner = jnp.clip(owner, 0, strips - 1)
+        words = jnp.concatenate([ref[owner, :, :width] for ref in got], axis=0)
+        tails = [ref[owner, :, width:] for ref in got]
+        rows = [decoded(tail[2:3], tail[3:4]) for tail in tails]
         rows = jnp.where(rows_of(shape) < nrhs, rows[0], rows[1])
         wanted = lanes_of(shape) == rank * lax.rem(rows_of(shape), nrhs) + STEP
         yield inside, unpacked(words), jnp.sum(jnp.where(wanted, rows, 0.0), axis=1, keepdims=True)
@@ -203,17 +206,20 @@
     shape = (CHUNK, CHUNK * rank)
     owner = lax.div(lanes_of(shape), rank)
     inner = lax.rem(lanes_of(shape), rank)
+    half = CHUNK // CORES
+    number = CORES * lax.rem(rows_of(shape), half) + lax.div(rows_of(shape), half)
     for start in range(0, masks_ref.shape[0], CHUNK):
         limit = jnp.zeros((1, CHUNK * rank), jnp.int32)
         for i in range(CHUNK):
             limit = jnp.where(owner[:1] == i, ranks_ref[0, start + i], limit)
-        masks_ref[pl.ds(start, CHUNK), :] = jnp.where((owner == rows_of(shape)) & (inner < limit), 1.0, 0.0)
+        masks_ref[pl.ds(start, CHUNK), :] = jnp.where((owner == number) & (inner < limit), 1.0, 0.0)
     copies[4].wait()
     count = panels // LANES
     target, source = raw_ref[0:1, :], raw_ref[1:2, :]
     group, block = lax.div(source, count), lax.rem(source, count)
     strip, core = lax.div(group, CORES), lax.rem(group, CORES)
-    list_ref[...] = jnp.concatenate([core * count + target, strip * count + block], axis=0)
+    apart = jnp.where(core == lax.axis_index("clus"), 0, 1)
+    list_ref[...] = jnp.concatenate([apart * count + target, strip * count + block], axis=0)
     copies[5].wait()
     rows_high[...], rows_low[...] = halves(rows_ref[...])
     put_message(loads, [square], (cols_high, cols_low), (couple_high, couple_low), masks_ref, sent_ref)
@@ -227,7 +233,7 @@
 
 
 def step0_kernel(
-    got_ref, loads_ref, cols_high, cols_low, couple_high, couple_low, masks_ref, rows_high, rows_low, self_ref,
+    own_ref, other_ref, loads_ref, cols_high, cols_low, couple_high, couple_low, masks_ref, rows_high, rows_low, self_ref,
     tiles_ref, list_vmem, sent_ref, image_ref, window0_ref, state_ref, list_ref, sems, window, *sums,
 ):
     rank = rows_high.shape[0]
@@ -236,11 +242,12 @@
     (copy,) = fetch(((list_vmem, list_ref),), sems)
     for held in sums:
         held[...] = jnp.zeros_like(held)
-    terms, stats = message_parts(got_ref, rank)
+    got = (own_ref, other_ref)
+    terms, stats = message_parts(got, rank)
     beta = jnp.sqrt(stat_column(total(stats), 0, nrhs, rank))
     scale = 1.0 / beta
     both = jnp.concatenate([scale] * CORES, axis=0)
-    for step, (inside, part, unit) in enumerate(window_parts(got_ref, rank)):
+    for step, (inside, part, unit) in enumerate(window_parts(got, rank)):
         part = jnp.where(inside, part * (unit * both), 0.0)
         window0_ref[step * rows : (step + 1) * rows, :] = part
         put_blocks(part, step * span, window)
@@ -261,7 +268,7 @@
 
 
 def step1_kernel(
-    got_ref, loads_ref, image_ref, window0_ref, state_ref, rows_high, rows_low, self_ref, tiles_ref,
+    own_ref, other_ref, loads_ref, image_ref, window0_ref, state_ref, rows_high, rows_low, self_ref, tiles_ref,
     list_vmem, sent_ref, basis_ref, coeff_ref, list_ref, sems, window, *sums,
 ):
     rank = rows_high.shape[0]
@@ -272,7 +279,8 @@
     far0 = state_ref[:nrhs, :]
     for held in sums:
         held[...] = jnp.zeros_like(held)
-    terms, stats = message_parts(got_ref, rank)
+    got = (own_ref, other_ref)
+    terms, stats = message_parts(got, rank)
     summed = total(stats)
     h00 = stat_column(summed, 1, nrhs, rank)
     away = shifted(stats, 2) - shifted(summed, 1)
@@ -280,7 +288,7 @@
     h10 = jnp.sqrt(stat_column(rest, 0, nrhs, rank))
     scale = 1.0 / h10
     both, both_h00 = (jnp.concatenate([a] * CORES, axis=0) for a in (scale, h00))
-    for step, (inside, part, unit) in enumerate(window_parts(got_ref, rank)):
+    for step, (inside, part, unit) in enumerate(window_parts(got, rank)):
         part = (part * unit - both_h00 * window0_ref[step * rows : (step + 1) * rows, :]) * both
         put_blocks(jnp.where(inside, part, 0.0), step * span, window)
     basis0 = loads_ref[...] * (1.0 / beta)
@@ -342,7 +350,8 @@
 
 
 def exchanged(sent):
-    return lax.all_to_all(sent, GROUP, 0, 0, tiled=True)
+    got = lax.all_to_all(sent, "strip", 0, 0, tiled=True)
+    return got, lax.ppermute(got, "clus", [(0, 1), (1, 0)])
 
 
 def body(loads, self_term, near_tiles, near_list, far_rows, far_cols, coupling, ranks):
@@ -356,7 +365,7 @@
     ranks = ranks.reshape(1, CORES * strips)
     self_term = self_term.reshape(1, panels)
     groups = CORES * strips
-    message = Plain((groups, nrhs, panels // 2 + LANES), jnp.int32)
+    message = Plain((strips, nrhs, panels // 2 + LANES), jnp.int32)
     index = pltpu.SMEM(near_list.shape, jnp.int32)
     scratch = [index, pltpu.SemaphoreType.DMA((1,)), pltpu.VMEM((3 * rows, CORES * nrhs, tile), F32)]
     scratch += [pltpu.VMEM((CORES * rows, CORES * nrhs, tile), F32)] * 4
@@ -381,17 +390,18 @@
     source_side, target_side = [loads, *held[:5]], [*held[5:], self_term, near_tiles, near_list]
     sent, image, window0, state = call(
         step0_kernel,
-        (exchanged(sent), *source_side, *target_side),
+        (*exchanged(sent), *source_side, *target_side),
         [message, loads.shape, (3 * CORES * nrhs, panels), (CORES * nrhs, LANES)],
         scratch,
     )
     sent, basis, coeff = call(
         step1_kernel,
-        (exchanged(sent), loads, image, window0, state, *target_side),
+        (*exchanged(sent), loads, image, window0, state, *target_side),
         [(groups, 1, LANES), (2 * nrhs, panels), (3 * nrhs, LANES)],
         scratch,
     )
-    return call(functools.partial(finish_kernel, rank), (exchanged(sent), basis, coeff), [loads.shape])[0]
+    got = lax.all_to_all(sent, GROUP, 0, 0, tiled=True)
+    return call(functools.partial(finish_kernel, rank), (got, basis, coeff), [loads.shape])[0]
 
 
 def solution(mesh):

time: 41.6 us -> 40.9 us (0.983)
  blocking collectives: 35.6 us -> 32.4 us
  waiting for transfers between devices: 0 us -> 2.55 us
    all_to_all x3, blocking collectives: 35.6 us -> 32.4 us  [the longest x2 23.5 us: exchanged(): got = lax.all_to_all(sent, 'strip', 0, 0, tiled=True)]
    ppermute x0 -> x2, waiting for transfers between devices: none -> 2.55 us  [exchanged(): return (got, lax.ppermute(got, 'clus', [(0, 1), (1, 0)]))]
  transfers between devices with their start and end apart: 0 -> 2, of which waited for: 0 -> 2; matrix products, arithmetic and copies ran while one was open for 0% -> 0% of each run, Pallas kernels for 0% -> 0%
where the time goes in v20:
time: 40.9 us; the launch traced here: 40.6 us
  blocking collectives  32.4 us (79%)
  Pallas kernels  5.6 us (14%)
  waiting for transfers between devices  2.55 us (6%)
    all_to_all x2, blocking collectives, exchanged(): got = lax.all_to_all(sent, 'strip', 0, 0, tiled=True)  23.5 us
    all_to_all x1, blocking collectives, body(): got = lax.all_to_all(sent, GROUP, 0, 0, tiled=True)  8.98 us
    pallas_call x4, Pallas kernels, call(): pl.pallas_call(kernel, out_shape=[jax.ShapeDtypeStruct(out, F32) if isins...  5.6 us
    ppermute x2, waiting for transfers between devices, exchanged(): return (got, lax.ppermute(got, 'clus', [(0, 1), (1, 0)]))  2.55 us
  transfers between devices with their start and end apart: 2, of which 2 were waited for; matrix products, arithmetic and copies ran while one was open for 0% of the time, Pallas kernels for 0%

profile of v20, /device:TPU:0, one launch (start us, length us, event | category | flops | bytes accessed | tf_op | source)
XLA Modules:
  0.0 40.6 jit_solution(4727990505283025316)
XLA Ops:
  0.0 2.1 %shard_map.82 = (s32[8,4,640]{2,1,0:T(4,128)S(1)}, bf16[32,1024]{1,0:T(8,128)(2,1)S(1)}, bf16[32,1024]{1,0:T(8,128)(2,1)S(1)}, bf16[512,32]{1,0:T(8,128)(2,1)S(1...) custom-call(f32[4,1024]{1,0:T(4,128)} %loads_hbm.1, ...), custom_call_target="tpu_custom_call" | custom-call | bytes 2970304 | tf_op jit(solution)/shard_map/pallas_call | solution.py:338
  2.1 14.1 %all_to_all.15.own_ref = s32[8,4,640]{2,1,0:T(4,128)S(1)} all-to-all(s32[8,4,640]{2,1,0:T(4,128)S(1)} %get-tuple-element.24), channel_id=1, replica_groups=mesh['case'=2,'strip'=8,'clus'=2] {'strip'}, dimensions={0} | all-to-all | bytes 163840 | tf_op jit(solution)/shard_map/all_to_all | solution.py:353
  16.1 0.0 collective-permute-start
  16.1 1.3 %collective-permute-done.other_ref = s32[8,4,640]{2,1,0:T(4,128)S(1)} collective-permute-done((s32[8,4,640]{2,1,0:T(4,128)S(1)}, s32[8,4,640]{2,1,0:T(4,128)S(1)}, u32[]{:S(2)}, u32[]{:S(2)}) %collective-permute-start) | collective-permute-done | bytes 81952 | tf_op jit(solution)/shard_map/ppermute | solution.py:354
  17.4 1.6 %shard_map.83 = (s32[8,4,640]{2,1,0:T(4,128)S(1)}, f32[4,1024]{1,0:T(4,128)S(1)}, f32[24,1024]{1,0:T(8,128)S(1)}, f32[8,128]{1,0:T(8,128)S(1)}) custom-call(s32[8,4,640]{2,1,0:T(4,128)S(1)} %all_to_all.15.own_ref, s32[8,4,640]{2,1,0:T(4,128)S(1)} %collective-permute-done.other_ref, f32[4,1024]{1,0:T(4,128)S(1)} %get-tuple-element.25.loads_ref, ...), custom_call_target="tpu_custom_call" | custom-call | bytes 3166848 | tf_op jit(solution)/shard_map/pallas_call | solution.py:338
  19.0 9.4 %all_to_all.16.own_ref = s32[8,4,640]{2,1,0:T(4,128)S(1)} all-to-all(s32[8,4,640]{2,1,0:T(4,128)S(1)} %get-tuple-element.36), channel_id=1, replica_groups=mesh['case'=2,'strip'=8,'clus'=2] {'strip'}, dimensions={0} | all-to-all | bytes 163840 | tf_op jit(solution)/shard_map/all_to_all | solution.py:353
  28.4 0.0 collective-permute-start.1
  28.4 1.3 %collective-permute-done.1.other_ref = s32[8,4,640]{2,1,0:T(4,128)S(1)} collective-permute-done((s32[8,4,640]{2,1,0:T(4,128)S(1)}, s32[8,4,640]{2,1,0:T(4,128)S(1)}, u32[]{:S(2)}, u32[]{:S(2)}) %collective-permute-start.1) | collective-permute-done | bytes 81952 | tf_op jit(solution)/shard_map/ppermute | solution.py:354
  29.7 1.2 %shard_map.84 = (f32[16,1,128]{2,1,0:T(1,128)S(1)}, f32[8,1024]{1,0:T(8,128)S(1)}, f32[12,128]{1,0:T(8,128)S(1)}) custom-call(s32[8,4,640]{2,1,0:T(4,128)S(1)} %all_to_all.16.own_ref, s32[8,4,640]{2,1,0:T(4,128)S(1)} %collective-permute-done.1.other_ref, f32[4,1024]{1,0:T(4,128)S(1)} %get-tuple-element.25.loads_ref, ...), custom_call_target="tpu_custom_call" | custom-call | bytes 3056256 | tf_op jit(solution)/shard_map/pallas_call | solution.py:338
  30.8 9.0 %all_to_all.17.got_ref = f32[16,1,128]{2,1,0:T(1,128)S(1)} all-to-all(f32[16,1,128]{2,1,0:T(1,128)S(1)} %get-tuple-element.40), channel_id=1, replica_groups=mesh['case'=2,'strip'=8,'clus'=2] {'strip','clus'}, dimensions={0} | all-to-all | bytes 16384 | tf_op jit(solution)/shard_map/all_to_all | solution.py:403
  39.8 0.8 %shard_map.85 = f32[4,1024]{1,0:T(4,128)} custom-call(f32[16,1,128]{2,1,0:T(1,128)S(1)} %all_to_all.17.got_ref, f32[8,1024]{1,0:T(8,128)S(1)} %get-tuple-element.41.basis_ref, f32[12,128]{1,0:T(8,128)S(1)} %get-tuple-element.42.coeff_ref), custom_call_target="tpu_custom_call" | custom-call | bytes 47104 | tf_op jit(solution)/shard_map/pallas_call | solution.py:338
Async XLA Ops:
  16.1 1.3 %collective-permute-start = (s32[8,4,640]{2,1,0:T(4,128)S(1)}, s32[8,4,640]{2,1,0:T(4,128)S(1)}, u32[]{:S(2)}, u32[]{:S(2)}) collective-permute-start(s32[8,4,640]{2,1,0:T(4,128)S(1)} %all_to_all.15.own_ref), channel_id=1, source_target_pairs={{0,1},{1,0},{2,3},{3,2},{4,5},{5,4},{6,7},{7,6},{8,9},{9,8},{10,11... | collective-permute-start | bytes 245768 | tf_op jit(solution)/shard_map/ppermute | solution.py:354
  28.4 1.3 %collective-permute-start.1 = (s32[8,4,640]{2,1,0:T(4,128)S(1)}, s32[8,4,640]{2,1,0:T(4,128)S(1)}, u32[]{:S(2)}, u32[]{:S(2)}) collective-permute-start(s32[8,4,640]{2,1,0:T(4,128)S(1)} %all_to_all.16.own_ref), channel_id=1, source_target_pairs={{0,1},{1,0},{2,3},{3,2},{4,5},{5,4},{6,7},{7,6},{8,9},{9,8},{10,11... | collective-permute-start | bytes 245768 | tf_op jit(solution)/shard_map/ppermute | solution.py:354

commit v21 on v20

--- a/solution.py
+++ b/solution.py
@@ -11,7 +11,7 @@
 CORES = 2
 LANES = 128
 CHUNK = 16
-PIECES = 10
+PIECE = 8
 F32 = jnp.float32
 BF16 = jnp.bfloat16
 
@@ -182,6 +182,17 @@
     return jnp.concatenate([whole[b, :nrhs] + whole[rows + b, nrhs:] for b in range(rows)], axis=1)
 
 
+def tile_pieces(tiles_hbm, first, tiles_ref):
+    starts = range(0, tiles_ref.shape[0], PIECE)
+    return tuple((tiles_hbm.at[pl.ds(first + i, PIECE)], tiles_ref.at[pl.ds(i, PIECE)]) for i in starts)
+
+
+def fetch_kernel(list_ref, tiles_hbm, tiles_ref, sems):
+    del list_ref
+    for copy in fetch(tile_pieces(tiles_hbm, tiles_hbm.shape[0] - tiles_ref.shape[0], tiles_ref), sems):
+        copy.wait()
+
+
 def start_kernel(
     loads_hbm, cols_hbm, couple_hbm, ranks_hbm, list_hbm, rows_hbm, self_hbm, tiles_hbm, sent_ref, cols_high, cols_low, couple_high,
     couple_low, masks_ref, rows_high, rows_low, list_ref, loads_ref, self_ref, tiles_ref, cols_ref, couple_ref, ranks_ref, raw_ref,
@@ -192,9 +203,7 @@
         (loads_hbm, loads_ref), (cols_hbm, cols_ref), (couple_hbm, couple_ref), (ranks_hbm, ranks_ref),
         (list_hbm, raw_ref), (rows_hbm, rows_ref), (self_hbm, self_ref),
     )
-    every = tiles_ref.shape[0] // PIECES
-    pieces = [pl.ds(i * every, every) for i in range(PIECES)]
-    copies = fetch(pairs + tuple((tiles_hbm.at[p], tiles_ref.at[p]) for p in pieces), sems)
+    copies = fetch(pairs + tile_pieces(tiles_hbm, 0, tiles_ref), sems)
     copies[0].wait()
     loads = loads_ref[...]
     square = jnp.sum(loads * loads, axis=1, keepdims=True)
@@ -234,7 +243,7 @@
 
 def step0_kernel(
     own_ref, other_ref, loads_ref, cols_high, cols_low, couple_high, couple_low, masks_ref, rows_high, rows_low, self_ref,
-    tiles_ref, list_vmem, sent_ref, image_ref, window0_ref, state_ref, list_ref, sems, window, *sums,
+    tiles0_ref, tiles1_ref, list_vmem, sent_ref, image_ref, window0_ref, state_ref, list_ref, sems, window, *sums,
 ):
     rank = rows_high.shape[0]
     nrhs, panels = loads_ref.shape
@@ -255,7 +264,7 @@
     far = far_sum_of(terms, nrhs, rank) * scale
     norm = jnp.sum(basis * basis, axis=1, keepdims=True)
     copy.wait()
-    near = near_field(window, (tiles_ref,), list_ref, sums, nrhs)
+    near = near_field(window, (tiles0_ref, tiles1_ref), list_ref, sums, nrhs)
     image = image_of(basis, far, self_ref, (rows_high, rows_low), near)
     image_ref[...] = image
     state_ref[...] = jnp.concatenate([far, jnp.broadcast_to(beta, far.shape)], axis=0)
@@ -268,7 +277,7 @@
 
 
 def step1_kernel(
-    own_ref, other_ref, loads_ref, image_ref, window0_ref, state_ref, rows_high, rows_low, self_ref, tiles_ref,
+    own_ref, other_ref, loads_ref, image_ref, window0_ref, state_ref, rows_high, rows_low, self_ref, tiles0_ref, tiles1_ref,
     list_vmem, sent_ref, basis_ref, coeff_ref, list_ref, sems, window, *sums,
 ):
     rank = rows_high.shape[0]
@@ -295,7 +304,7 @@
     basis1 = (image_ref[...] - h00 * basis0) * scale
     far = (far_sum_of(terms, nrhs, rank) - h00 * far0) * scale
     copy.wait()
-    near = near_field(window, (tiles_ref,), list_ref, sums, nrhs)
+    near = near_field(window, (tiles0_ref, tiles1_ref), list_ref, sums, nrhs)
     image = image_of(basis1, far, self_ref, (rows_high, rows_low), near)
     columns = [jnp.sum(a * image, axis=1, keepdims=True) for a in (basis0, basis1, image)]
     sent_ref[:, 0, :] = jnp.broadcast_to(stats_row(columns, rank), (sent_ref.shape[0], LANES))
@@ -368,26 +377,33 @@
     message = Plain((strips, nrhs, panels // 2 + LANES), jnp.int32)
     index = pltpu.SMEM(near_list.shape, jnp.int32)
     scratch = [index, pltpu.SemaphoreType.DMA((1,)), pltpu.VMEM((3 * rows, CORES * nrhs, tile), F32)]
+    late = PIECE * (blocks * 3 // (10 * PIECE))
+    tiles0, tiles1 = (jax.ShapeDtypeStruct((count, tile, tile), BF16) for count in (blocks - late, late))
     scratch += [pltpu.VMEM((CORES * rows, CORES * nrhs, tile), F32)] * 4
 
     def twice(array):
         return [jax.ShapeDtypeStruct(array.shape, BF16)] * 2
 
-    sent, *held, near_list, loads, self_term, near_tiles = call(
+    sent, *held, near_list, loads, self_term, tiles0 = call(
         start_kernel,
         (loads, far_cols, couple, ranks, near_list, far_rows, self_term, near_tiles),
         [
             message, *twice(far_cols), *twice(couple), jax.ShapeDtypeStruct((groups, CHUNK * rank), F32),
-            *twice(far_rows), near_list, loads, self_term, near_tiles,
+            *twice(far_rows), near_list, loads, self_term, tiles0,
         ],
         [
             pltpu.VMEM(far_cols.shape, F32), pltpu.VMEM(couple.shape, F32), pltpu.SMEM(ranks.shape, jnp.int32),
-            pltpu.VMEM(near_list.shape, jnp.int32), pltpu.VMEM(far_rows.shape, F32), pltpu.SemaphoreType.DMA((7 + PIECES,)),
+            pltpu.VMEM(near_list.shape, jnp.int32), pltpu.VMEM(far_rows.shape, F32), pltpu.SemaphoreType.DMA((7 + tiles0.shape[0] // PIECE,)),
         ],
         held=range(8),
     )
-    loads, *held, self_term, near_tiles, near_list = in_vmem([loads, *held, self_term, near_tiles, near_list])
-    source_side, target_side = [loads, *held[:5]], [*held[5:], self_term, near_tiles, near_list]
+    (tiles1,) = call(
+        fetch_kernel, (near_list, near_tiles), [tiles1], [pltpu.SemaphoreType.DMA((late // PIECE,))], held=(1,)
+    )
+    loads, *held, self_term, tiles0, tiles1, near_list = in_vmem(
+        [loads, *held, self_term, tiles0, tiles1, near_list]
+    )
+    source_side, target_side = [loads, *held[:5]], [*held[5:], self_term, tiles0, tiles1, near_list]
     sent, image, window0, state = call(
         step0_kernel,
         (*exchanged(sent), *source_side, *target_side),

time: 40.9 us -> 40.8 us (level)
  waiting for transfers between devices: 2.55 us -> 1.41 us
  Pallas kernels: 5.6 us -> 6.51 us
    ppermute x2, waiting for transfers between devices: 2.55 us -> 1.41 us  [exchanged(): return (got, lax.ppermute(got, 'clus', [(0, 1), (1, 0)]))]
    pallas_call x4 -> x5, Pallas kernels: 5.6 us -> 6.51 us  [call(): pl.pallas_call(kernel, out_shape=[jax.ShapeDtypeStruct(out, F32) if isins...]
  transfers between devices with their start and end apart: 2 -> 2, of which waited for: 2 -> 2; matrix products, arithmetic and copies ran while one was open for 0% -> 0% of each run, Pallas kernels for 0% -> 3%
where the time goes in v21:
time: 40.8 us; the launch traced here: 40.5 us
  blocking collectives  32.5 us (80%)
  Pallas kernels  6.51 us (16%)
  waiting for transfers between devices  1.41 us (3%)
    all_to_all x2, blocking collectives, exchanged(): got = lax.all_to_all(sent, 'strip', 0, 0, tiled=True)  23.5 us
    all_to_all x1, blocking collectives, body(): got = lax.all_to_all(sent, GROUP, 0, 0, tiled=True)  8.98 us
    pallas_call x5, Pallas kernels, call(): pl.pallas_call(kernel, out_shape=[jax.ShapeDtypeStruct(out, F32) if isins...  6.51 us
    ppermute x2, waiting for transfers between devices, exchanged(): return (got, lax.ppermute(got, 'clus', [(0, 1), (1, 0)]))  1.41 us
  transfers between devices with their start and end apart: 2, of which 2 were waited for; matrix products, arithmetic and copies ran while one was open for 0% of the time, Pallas kernels for 3%

profile of v21, /device:TPU:0, one launch (start us, length us, event | category | flops | bytes accessed | tf_op | source)
XLA Modules:
  0.0 40.5 jit_solution(3630936019473881279)
XLA Ops:
  0.0 1.8 %shard_map.82 = (s32[8,4,640]{2,1,0:T(4,128)S(1)}, bf16[32,1024]{1,0:T(8,128)(2,1)S(1)}, bf16[32,1024]{1,0:T(8,128)(2,1)S(1)}, bf16[512,32]{1,0:T(8,128)(2,1)S(1...) custom-call(f32[4,1024]{1,0:T(4,128)} %loads_hbm.1, ...), custom_call_target="tpu_custom_call" | custom-call | bytes 2970304 | tf_op jit(solution)/shard_map/pallas_call | solution.py:347
  1.8 14.1 %all_to_all.15.own_ref = s32[8,4,640]{2,1,0:T(4,128)S(1)} all-to-all(s32[8,4,640]{2,1,0:T(4,128)S(1)} %get-tuple-element.24), channel_id=1, replica_groups=mesh['case'=2,'strip'=8,'clus'=2] {'strip'}, dimensions={0} | all-to-all | bytes 163840 | tf_op jit(solution)/shard_map/all_to_all | solution.py:362
  15.9 0.0 collective-permute-start
  15.9 1.1 %shard_map.83.tiles1_ref = bf16[24,128,128]{2,1,0:T(8,128)(2,1)S(1)} custom-call(s32[2,80]{1,0:T(2,128)S(1)} %get-tuple-element.35.list_ref.list_vmem, bf16[80,128,128]{2,1,0:T(8,128)(2,1)} %tiles_hbm.3), custom_call_target="tpu_custom_call" | custom-call | bytes 2622080 | tf_op jit(solution)/shard_map/pallas_call | solution.py:347
  17.0 0.1 collective-permute-done.other_ref
  17.2 1.6 %shard_map.84 = (s32[8,4,640]{2,1,0:T(4,128)S(1)}, f32[4,1024]{1,0:T(4,128)S(1)}, f32[24,1024]{1,0:T(8,128)S(1)}, f32[8,128]{1,0:T(8,128)S(1)}) custom-call(s32[8,4,640]{2,1,0:T(4,128)S(1)} %all_to_all.15.own_ref, s32[8,4,640]{2,1,0:T(4,128)S(1)} %collective-permute-done.other_ref, f32[4,1024]{1,0:T(4,128)S(1)} %get-tuple-element.25.loads_ref, ...), custom_call_target="tpu_custom_call" | custom-call | bytes 3166848 | tf_op jit(solution)/shard_map/pallas_call | solution.py:347
  18.7 9.5 %all_to_all.16.own_ref = s32[8,4,640]{2,1,0:T(4,128)S(1)} all-to-all(s32[8,4,640]{2,1,0:T(4,128)S(1)} %get-tuple-element.36), channel_id=1, replica_groups=mesh['case'=2,'strip'=8,'clus'=2] {'strip'}, dimensions={0} | all-to-all | bytes 163840 | tf_op jit(solution)/shard_map/all_to_all | solution.py:362
  28.2 0.0 collective-permute-start.1
  28.2 1.3 %collective-permute-done.1.other_ref = s32[8,4,640]{2,1,0:T(4,128)S(1)} collective-permute-done((s32[8,4,640]{2,1,0:T(4,128)S(1)}, s32[8,4,640]{2,1,0:T(4,128)S(1)}, u32[]{:S(2)}, u32[]{:S(2)}) %collective-permute-start.1) | collective-permute-done | bytes 81952 | tf_op jit(solution)/shard_map/ppermute | solution.py:363
  29.5 1.2 %shard_map.85 = (f32[16,1,128]{2,1,0:T(1,128)S(1)}, f32[8,1024]{1,0:T(8,128)S(1)}, f32[12,128]{1,0:T(8,128)S(1)}) custom-call(s32[8,4,640]{2,1,0:T(4,128)S(1)} %all_to_all.16.own_ref, s32[8,4,640]{2,1,0:T(4,128)S(1)} %collective-permute-done.1.other_ref, f32[4,1024]{1,0:T(4,128)S(1)} %get-tuple-element.25.loads_ref, ...), custom_call_target="tpu_custom_call" | custom-call | bytes 3056256 | tf_op jit(solution)/shard_map/pallas_call | solution.py:347
  30.7 9.0 %all_to_all.17.got_ref = f32[16,1,128]{2,1,0:T(1,128)S(1)} all-to-all(f32[16,1,128]{2,1,0:T(1,128)S(1)} %get-tuple-element.40), channel_id=1, replica_groups=mesh['case'=2,'strip'=8,'clus'=2] {'strip','clus'}, dimensions={0} | all-to-all | bytes 16384 | tf_op jit(solution)/shard_map/all_to_all | solution.py:419
  39.7 0.8 %shard_map.86 = f32[4,1024]{1,0:T(4,128)} custom-call(f32[16,1,128]{2,1,0:T(1,128)S(1)} %all_to_all.17.got_ref, f32[8,1024]{1,0:T(8,128)S(1)} %get-tuple-element.41.basis_ref, f32[12,128]{1,0:T(8,128)S(1)} %get-tuple-element.42.coeff_ref), custom_call_target="tpu_custom_call" | custom-call | bytes 47104 | tf_op jit(solution)/shard_map/pallas_call | solution.py:347
Async XLA Ops:
  15.9 1.3 %collective-permute-start = (s32[8,4,640]{2,1,0:T(4,128)S(1)}, s32[8,4,640]{2,1,0:T(4,128)S(1)}, u32[]{:S(2)}, u32[]{:S(2)}) collective-permute-start(s32[8,4,640]{2,1,0:T(4,128)S(1)} %all_to_all.15.own_ref), channel_id=1, source_target_pairs={{0,1},{1,0},{2,3},{3,2},{4,5},{5,4},{6,7},{7,6},{8,9},{9,8},{10,11... | collective-permute-start | bytes 245768 | tf_op jit(solution)/shard_map/ppermute | solution.py:363
  28.2 1.3 %collective-permute-start.1 = (s32[8,4,640]{2,1,0:T(4,128)S(1)}, s32[8,4,640]{2,1,0:T(4,128)S(1)}, u32[]{:S(2)}, u32[]{:S(2)}) collective-permute-start(s32[8,4,640]{2,1,0:T(4,128)S(1)} %all_to_all.16.own_ref), channel_id=1, source_target_pairs={{0,1},{1,0},{2,3},{3,2},{4,5},{5,4},{6,7},{7,6},{8,9},{9,8},{10,11... | collective-permute-start | bytes 245768 | tf_op jit(solution)/shard_map/ppermute | solution.py:363

commit v22 on v21

--- a/solution.py
+++ b/solution.py
@@ -377,9 +377,9 @@
     message = Plain((strips, nrhs, panels // 2 + LANES), jnp.int32)
     index = pltpu.SMEM(near_list.shape, jnp.int32)
     scratch = [index, pltpu.SemaphoreType.DMA((1,)), pltpu.VMEM((3 * rows, CORES * nrhs, tile), F32)]
-    late = PIECE * (blocks * 3 // (10 * PIECE))
+    late = PIECE * (blocks * 2 // (5 * PIECE))
     tiles0, tiles1 = (jax.ShapeDtypeStruct((count, tile, tile), BF16) for count in (blocks - late, late))
-    scratch += [pltpu.VMEM((CORES * rows, CORES * nrhs, tile), F32)] * 4
+    scratch += [pltpu.VMEM((CORES * rows, CORES * nrhs, tile), F32)] * 2
 
     def twice(array):
         return [jax.ShapeDtypeStruct(array.shape, BF16)] * 2

time: 40.8 us -> 40.9 us (level)
  transfers between devices with their start and end apart: 2 -> 2, of which waited for: 2 -> 1; matrix products, arithmetic and copies ran while one was open for 0% -> 0% of each run, Pallas kernels for 3% -> 3%
where the time goes in v22:
time: 40.9 us; the launch traced here: 40.5 us
  blocking collectives  32.6 us (80%)
  Pallas kernels  6.57 us (16%)
  waiting for transfers between devices  1.32 us (3%)
    all_to_all x2, blocking collectives, exchanged(): got = lax.all_to_all(sent, 'strip', 0, 0, tiled=True)  23.6 us
    all_to_all x1, blocking collectives, body(): got = lax.all_to_all(sent, GROUP, 0, 0, tiled=True)  8.98 us
    pallas_call x5, Pallas kernels, call(): pl.pallas_call(kernel, out_shape=[jax.ShapeDtypeStruct(out, F32) if isins...  6.57 us
    ppermute x2, waiting for transfers between devices, exchanged(): return (got, lax.ppermute(got, 'clus', [(0, 1), (1, 0)]))  1.32 us
  transfers between devices with their start and end apart: 2, of which 1 were waited for; matrix products, arithmetic and copies ran while one was open for 0% of the time, Pallas kernels for 3%

profile of v22, /device:TPU:0, one launch (start us, length us, event | category | flops | bytes accessed | tf_op | source)
XLA Modules:
  0.0 40.5 jit_solution(7034097859961649887)
XLA Ops:
  0.0 1.8 %shard_map.82 = (s32[8,4,640]{2,1,0:T(4,128)S(1)}, bf16[32,1024]{1,0:T(8,128)(2,1)S(1)}, bf16[32,1024]{1,0:T(8,128)(2,1)S(1)}, bf16[512,32]{1,0:T(8,128)(2,1)S(1...) custom-call(f32[4,1024]{1,0:T(4,128)} %loads_hbm.1, ...), custom_call_target="tpu_custom_call" | custom-call | bytes 2970304 | tf_op jit(solution)/shard_map/pallas_call | solution.py:347
  1.8 14.1 %all_to_all.15.own_ref = s32[8,4,640]{2,1,0:T(4,128)S(1)} all-to-all(s32[8,4,640]{2,1,0:T(4,128)S(1)} %get-tuple-element.24), channel_id=1, replica_groups=mesh['case'=2,'strip'=8,'clus'=2] {'strip'}, dimensions={0} | all-to-all | bytes 163840 | tf_op jit(solution)/shard_map/all_to_all | solution.py:362
  15.8 0.0 collective-permute-start
  15.8 1.2 %shard_map.83.tiles1_ref = bf16[32,128,128]{2,1,0:T(8,128)(2,1)S(1)} custom-call(s32[2,80]{1,0:T(2,128)S(1)} %get-tuple-element.35.list_ref.list_vmem, bf16[80,128,128]{2,1,0:T(8,128)(2,1)} %tiles_hbm.3), custom_call_target="tpu_custom_call" | custom-call | bytes 2622080 | tf_op jit(solution)/shard_map/pallas_call | solution.py:347
  17.1 0.0 collective-permute-done.other_ref
  17.1 1.6 %shard_map.84 = (s32[8,4,640]{2,1,0:T(4,128)S(1)}, f32[4,1024]{1,0:T(4,128)S(1)}, f32[24,1024]{1,0:T(8,128)S(1)}, f32[8,128]{1,0:T(8,128)S(1)}) custom-call(s32[8,4,640]{2,1,0:T(4,128)S(1)} %all_to_all.15.own_ref, s32[8,4,640]{2,1,0:T(4,128)S(1)} %collective-permute-done.other_ref, f32[4,1024]{1,0:T(4,128)S(1)} %get-tuple-element.25.loads_ref, ...), custom_call_target="tpu_custom_call" | custom-call | bytes 3166848 | tf_op jit(solution)/shard_map/pallas_call | solution.py:347
  18.7 9.6 %all_to_all.16.own_ref = s32[8,4,640]{2,1,0:T(4,128)S(1)} all-to-all(s32[8,4,640]{2,1,0:T(4,128)S(1)} %get-tuple-element.36), channel_id=1, replica_groups=mesh['case'=2,'strip'=8,'clus'=2] {'strip'}, dimensions={0} | all-to-all | bytes 163840 | tf_op jit(solution)/shard_map/all_to_all | solution.py:362
  28.3 0.0 collective-permute-start.1
  28.3 1.3 %collective-permute-done.1.other_ref = s32[8,4,640]{2,1,0:T(4,128)S(1)} collective-permute-done((s32[8,4,640]{2,1,0:T(4,128)S(1)}, s32[8,4,640]{2,1,0:T(4,128)S(1)}, u32[]{:S(2)}, u32[]{:S(2)}) %collective-permute-start.1) | collective-permute-done | bytes 81952 | tf_op jit(solution)/shard_map/ppermute | solution.py:363
  29.5 1.2 %shard_map.85 = (f32[16,1,128]{2,1,0:T(1,128)S(1)}, f32[8,1024]{1,0:T(8,128)S(1)}, f32[12,128]{1,0:T(8,128)S(1)}) custom-call(s32[8,4,640]{2,1,0:T(4,128)S(1)} %all_to_all.16.own_ref, s32[8,4,640]{2,1,0:T(4,128)S(1)} %collective-permute-done.1.other_ref, f32[4,1024]{1,0:T(4,128)S(1)} %get-tuple-element.25.loads_ref, ...), custom_call_target="tpu_custom_call" | custom-call | bytes 3056256 | tf_op jit(solution)/shard_map/pallas_call | solution.py:347
  30.8 9.0 %all_to_all.17.got_ref = f32[16,1,128]{2,1,0:T(1,128)S(1)} all-to-all(f32[16,1,128]{2,1,0:T(1,128)S(1)} %get-tuple-element.40), channel_id=1, replica_groups=mesh['case'=2,'strip'=8,'clus'=2] {'strip','clus'}, dimensions={0} | all-to-all | bytes 16384 | tf_op jit(solution)/shard_map/all_to_all | solution.py:419
  39.7 0.8 %shard_map.86 = f32[4,1024]{1,0:T(4,128)} custom-call(f32[16,1,128]{2,1,0:T(1,128)S(1)} %all_to_all.17.got_ref, f32[8,1024]{1,0:T(8,128)S(1)} %get-tuple-element.41.basis_ref, f32[12,128]{1,0:T(8,128)S(1)} %get-tuple-element.42.coeff_ref), custom_call_target="tpu_custom_call" | custom-call | bytes 47104 | tf_op jit(solution)/shard_map/pallas_call | solution.py:347
Async XLA Ops:
  15.8 1.3 %collective-permute-start = (s32[8,4,640]{2,1,0:T(4,128)S(1)}, s32[8,4,640]{2,1,0:T(4,128)S(1)}, u32[]{:S(2)}, u32[]{:S(2)}) collective-permute-start(s32[8,4,640]{2,1,0:T(4,128)S(1)} %all_to_all.15.own_ref), channel_id=1, source_target_pairs={{0,1},{1,0},{2,3},{3,2},{4,5},{5,4},{6,7},{7,6},{8,9},{9,8},{10,11... | collective-permute-start | bytes 245768 | tf_op jit(solution)/shard_map/ppermute | solution.py:363
  28.3 1.3 %collective-permute-start.1 = (s32[8,4,640]{2,1,0:T(4,128)S(1)}, s32[8,4,640]{2,1,0:T(4,128)S(1)}, u32[]{:S(2)}, u32[]{:S(2)}) collective-permute-start(s32[8,4,640]{2,1,0:T(4,128)S(1)} %all_to_all.16.own_ref), channel_id=1, source_target_pairs={{0,1},{1,0},{2,3},{3,2},{4,5},{5,4},{6,7},{7,6},{8,9},{9,8},{10,11... | collective-permute-start | bytes 245768 | tf_op jit(solution)/shard_map/ppermute | solution.py:363

commit v23 on v21

--- a/solution.py
+++ b/solution.py
@@ -187,21 +187,33 @@
     return tuple((tiles_hbm.at[pl.ds(first + i, PIECE)], tiles_ref.at[pl.ds(i, PIECE)]) for i in starts)
 
 
-def fetch_kernel(list_ref, tiles_hbm, tiles_ref, sems):
-    del list_ref
-    for copy in fetch(tile_pieces(tiles_hbm, tiles_hbm.shape[0] - tiles_ref.shape[0], tiles_ref), sems):
+def fetch_kernel(
+    loads_ref, list_hbm, rows_hbm, tiles_hbm, list_ref, rows_high, rows_low, tiles_ref, raw_ref, rows_ref, sems
+):
+    panels = loads_ref.shape[1]
+    first = tiles_hbm.shape[0] - tiles_ref.shape[0]
+    copies = fetch(((list_hbm, raw_ref), (rows_hbm, rows_ref)) + tile_pieces(tiles_hbm, first, tiles_ref), sems)
+    copies[0].wait()
+    count = panels // LANES
+    target, source = raw_ref[0:1, :], raw_ref[1:2, :]
+    group, block = lax.div(source, count), lax.rem(source, count)
+    strip, core = lax.div(group, CORES), lax.rem(group, CORES)
+    apart = jnp.where(core == lax.axis_index("clus"), 0, 1)
+    list_ref[...] = jnp.concatenate([apart * count + target, strip * count + block], axis=0)
+    copies[1].wait()
+    rows_high[...], rows_low[...] = halves(rows_ref[...])
+    for copy in copies[2:]:
         copy.wait()
 
 
 def start_kernel(
-    loads_hbm, cols_hbm, couple_hbm, ranks_hbm, list_hbm, rows_hbm, self_hbm, tiles_hbm, sent_ref, cols_high, cols_low, couple_high,
-    couple_low, masks_ref, rows_high, rows_low, list_ref, loads_ref, self_ref, tiles_ref, cols_ref, couple_ref, ranks_ref, raw_ref,
-    rows_ref, sems,
+    loads_hbm, cols_hbm, couple_hbm, ranks_hbm, self_hbm, tiles_hbm, sent_ref, cols_high, cols_low, couple_high,
+    couple_low, masks_ref, loads_ref, self_ref, tiles_ref, cols_ref, couple_ref, ranks_ref, sems,
 ):
     rank, panels = cols_ref.shape
     pairs = (
         (loads_hbm, loads_ref), (cols_hbm, cols_ref), (couple_hbm, couple_ref), (ranks_hbm, ranks_ref),
-        (list_hbm, raw_ref), (rows_hbm, rows_ref), (self_hbm, self_ref),
+        (self_hbm, self_ref),
     )
     copies = fetch(pairs + tile_pieces(tiles_hbm, 0, tiles_ref), sems)
     copies[0].wait()
@@ -222,17 +234,8 @@
         for i in range(CHUNK):
             limit = jnp.where(owner[:1] == i, ranks_ref[0, start + i], limit)
         masks_ref[pl.ds(start, CHUNK), :] = jnp.where((owner == number) & (inner < limit), 1.0, 0.0)
-    copies[4].wait()
-    count = panels // LANES
-    target, source = raw_ref[0:1, :], raw_ref[1:2, :]
-    group, block = lax.div(source, count), lax.rem(source, count)
-    strip, core = lax.div(group, CORES), lax.rem(group, CORES)
-    apart = jnp.where(core == lax.axis_index("clus"), 0, 1)
-    list_ref[...] = jnp.concatenate([apart * count + target, strip * count + block], axis=0)
-    copies[5].wait()
-    rows_high[...], rows_low[...] = halves(rows_ref[...])
     put_message(loads, [square], (cols_high, cols_low), (couple_high, couple_low), masks_ref, sent_ref)
-    for copy in copies[6:]:
+    for copy in copies[4:]:
         copy.wait()
 
 
@@ -384,26 +387,33 @@
     def twice(array):
         return [jax.ShapeDtypeStruct(array.shape, BF16)] * 2
 
-    sent, *held, near_list, loads, self_term, tiles0 = call(
+    sent, *held, loads, self_term, tiles0 = call(
         start_kernel,
-        (loads, far_cols, couple, ranks, near_list, far_rows, self_term, near_tiles),
+        (loads, far_cols, couple, ranks, self_term, near_tiles),
         [
             message, *twice(far_cols), *twice(couple), jax.ShapeDtypeStruct((groups, CHUNK * rank), F32),
-            *twice(far_rows), near_list, loads, self_term, tiles0,
+            loads, self_term, tiles0,
         ],
         [
             pltpu.VMEM(far_cols.shape, F32), pltpu.VMEM(couple.shape, F32), pltpu.SMEM(ranks.shape, jnp.int32),
-            pltpu.VMEM(near_list.shape, jnp.int32), pltpu.VMEM(far_rows.shape, F32), pltpu.SemaphoreType.DMA((7 + tiles0.shape[0] // PIECE,)),
+            pltpu.SemaphoreType.DMA((5 + tiles0.shape[0] // PIECE,)),
         ],
-        held=range(8),
-    )
-    (tiles1,) = call(
-        fetch_kernel, (near_list, near_tiles), [tiles1], [pltpu.SemaphoreType.DMA((late // PIECE,))], held=(1,)
-    )
-    loads, *held, self_term, tiles0, tiles1, near_list = in_vmem(
-        [loads, *held, self_term, tiles0, tiles1, near_list]
-    )
-    source_side, target_side = [loads, *held[:5]], [*held[5:], self_term, tiles0, tiles1, near_list]
+        held=range(6),
+    )
+    loads, *held, self_term, tiles0 = in_vmem([loads, *held, self_term, tiles0])
+    near_list, *far_rows, tiles1 = in_vmem(
+        call(
+            fetch_kernel,
+            (loads, near_list, far_rows, near_tiles),
+            [near_list, *twice(far_rows), tiles1],
+            [
+                pltpu.VMEM(near_list.shape, jnp.int32), pltpu.VMEM(far_rows.shape, F32),
+                pltpu.SemaphoreType.DMA((2 + late // PIECE,)),
+            ],
+            held=range(1, 4),
+        )
+    )
+    source_side, target_side = [loads, *held], [*far_rows, self_term, tiles0, tiles1, near_list]
     sent, image, window0, state = call(
         step0_kernel,
         (*exchanged(sent), *source_side, *target_side),

time: 40.8 us -> 40.8 us (level)
  transfers between devices with their start and end apart: 2 -> 2, of which waited for: 2 -> 1; matrix products, arithmetic and copies ran while one was open for 0% -> 0% of each run, Pallas kernels for 3% -> 3%
where the time goes in v23:
time: 40.8 us; the launch traced here: 40.5 us
  blocking collectives  32.6 us (80%)
  Pallas kernels  6.52 us (16%)
  waiting for transfers between devices  1.31 us (3%)
    all_to_all x2, blocking collectives, exchanged(): got = lax.all_to_all(sent, 'strip', 0, 0, tiled=True)  23.6 us
    all_to_all x1, blocking collectives, body(): got = lax.all_to_all(sent, GROUP, 0, 0, tiled=True)  8.98 us
    pallas_call x5, Pallas kernels, call(): pl.pallas_call(kernel, out_shape=[jax.ShapeDtypeStruct(out, F32) if isins...  6.52 us
    ppermute x2, waiting for transfers between devices, exchanged(): return (got, lax.ppermute(got, 'clus', [(0, 1), (1, 0)]))  1.31 us
  transfers between devices with their start and end apart: 2, of which 1 were waited for; matrix products, arithmetic and copies ran while one was open for 0% of the time, Pallas kernels for 3%

profile of v23, /device:TPU:0, one launch (start us, length us, event | category | flops | bytes accessed | tf_op | source)
XLA Modules:
  0.0 40.5 jit_solution(17551790271961399686)
XLA Ops:
  0.0 1.7 %shard_map.82 = (s32[8,4,640]{2,1,0:T(4,128)S(1)}, bf16[32,1024]{1,0:T(8,128)(2,1)S(1)}, bf16[32,1024]{1,0:T(8,128)(2,1)S(1)}, bf16[512,32]{1,0:T(8,128)(2,1)S(1...) custom-call(f32[4,1024]{1,0:T(4,128)} %loads_hbm.1, ...), custom_call_target="tpu_custom_call" | custom-call | bytes 2838592 | tf_op jit(solution)/shard_map/pallas_call | solution.py:350
  1.7 14.1 %all_to_all.15.own_ref = s32[8,4,640]{2,1,0:T(4,128)S(1)} all-to-all(s32[8,4,640]{2,1,0:T(4,128)S(1)} %get-tuple-element.25), channel_id=1, replica_groups=mesh['case'=2,'strip'=8,'clus'=2] {'strip'}, dimensions={0} | all-to-all | bytes 163840 | tf_op jit(solution)/shard_map/all_to_all | solution.py:365
  15.8 0.0 collective-permute-start
  15.8 1.2 %shard_map.83 = (s32[2,80]{1,0:T(2,128)S(1)}, bf16[32,1024]{1,0:T(8,128)(2,1)S(1)}, bf16[32,1024]{1,0:T(8,128)(2,1)S(1)}, bf16[24,128,128]{2,1,0:T(8,128)(2,1)S(1)}) custom-call(f32[4,1024]{1,0:T(4,128)S(1)} %get-tuple-element.26.loads_ref, s32[2,80]{1,0:T(2,128)} %bitcast.6, f32[32,1024]{1,0:T(8,128)} %rows_hbm.1, bf16[80,128,128]{2,1,0:T(8,128)(2,1)} %tiles_hbm.3), custom_call_target="tpu_custom_call" | custom-call | bytes 2769536 | tf_op jit(solution)/shard_map/pallas_call | solution.py:350
  17.0 0.0 collective-permute-done.other_ref
  17.1 1.6 %shard_map.84 = (s32[8,4,640]{2,1,0:T(4,128)S(1)}, f32[4,1024]{1,0:T(4,128)S(1)}, f32[24,1024]{1,0:T(8,128)S(1)}, f32[8,128]{1,0:T(8,128)S(1)}) custom-call(s32[8,4,640]{2,1,0:T(4,128)S(1)} %all_to_all.15.own_ref, s32[8,4,640]{2,1,0:T(4,128)S(1)} %collective-permute-done.other_ref, f32[4,1024]{1,0:T(4,128)S(1)} %get-tuple-element.26.loads_ref, ...), custom_call_target="tpu_custom_call" | custom-call | bytes 3166848 | tf_op jit(solution)/shard_map/pallas_call | solution.py:350
  18.6 9.6 %all_to_all.16.own_ref = s32[8,4,640]{2,1,0:T(4,128)S(1)} all-to-all(s32[8,4,640]{2,1,0:T(4,128)S(1)} %get-tuple-element.38), channel_id=1, replica_groups=mesh['case'=2,'strip'=8,'clus'=2] {'strip'}, dimensions={0} | all-to-all | bytes 163840 | tf_op jit(solution)/shard_map/all_to_all | solution.py:365
  28.2 0.0 collective-permute-start.1
  28.2 1.3 %collective-permute-done.1.other_ref = s32[8,4,640]{2,1,0:T(4,128)S(1)} collective-permute-done((s32[8,4,640]{2,1,0:T(4,128)S(1)}, s32[8,4,640]{2,1,0:T(4,128)S(1)}, u32[]{:S(2)}, u32[]{:S(2)}) %collective-permute-start.1) | collective-permute-done | bytes 81952 | tf_op jit(solution)/shard_map/ppermute | solution.py:366
  29.5 1.2 %shard_map.85 = (f32[16,1,128]{2,1,0:T(1,128)S(1)}, f32[8,1024]{1,0:T(8,128)S(1)}, f32[12,128]{1,0:T(8,128)S(1)}) custom-call(s32[8,4,640]{2,1,0:T(4,128)S(1)} %all_to_all.16.own_ref, s32[8,4,640]{2,1,0:T(4,128)S(1)} %collective-permute-done.1.other_ref, f32[4,1024]{1,0:T(4,128)S(1)} %get-tuple-element.26.loads_ref, ...), custom_call_target="tpu_custom_call" | custom-call | bytes 3056256 | tf_op jit(solution)/shard_map/pallas_call | solution.py:350
  30.7 9.0 %all_to_all.17.got_ref = f32[16,1,128]{2,1,0:T(1,128)S(1)} all-to-all(f32[16,1,128]{2,1,0:T(1,128)S(1)} %get-tuple-element.42), channel_id=1, replica_groups=mesh['case'=2,'strip'=8,'clus'=2] {'strip','clus'}, dimensions={0} | all-to-all | bytes 16384 | tf_op jit(solution)/shard_map/all_to_all | solution.py:429
  39.7 0.8 %shard_map.86 = f32[4,1024]{1,0:T(4,128)} custom-call(f32[16,1,128]{2,1,0:T(1,128)S(1)} %all_to_all.17.got_ref, f32[8,1024]{1,0:T(8,128)S(1)} %get-tuple-element.43.basis_ref, f32[12,128]{1,0:T(8,128)S(1)} %get-tuple-element.44.coeff_ref), custom_call_target="tpu_custom_call" | custom-call | bytes 47104 | tf_op jit(solution)/shard_map/pallas_call | solution.py:350
Async XLA Ops:
  15.8 1.3 %collective-permute-start = (s32[8,4,640]{2,1,0:T(4,128)S(1)}, s32[8,4,640]{2,1,0:T(4,128)S(1)}, u32[]{:S(2)}, u32[]{:S(2)}) collective-permute-start(s32[8,4,640]{2,1,0:T(4,128)S(1)} %all_to_all.15.own_ref), channel_id=1, source_target_pairs={{0,1},{1,0},{2,3},{3,2},{4,5},{5,4},{6,7},{7,6},{8,9},{9,8},{10,11... | collective-permute-start | bytes 245768 | tf_op jit(solution)/shard_map/ppermute | solution.py:366
  28.2 1.3 %collective-permute-start.1 = (s32[8,4,640]{2,1,0:T(4,128)S(1)}, s32[8,4,640]{2,1,0:T(4,128)S(1)}, u32[]{:S(2)}, u32[]{:S(2)}) collective-permute-start(s32[8,4,640]{2,1,0:T(4,128)S(1)} %all_to_all.16.own_ref), channel_id=1, source_target_pairs={{0,1},{1,0},{2,3},{3,2},{4,5},{5,4},{6,7},{7,6},{8,9},{9,8},{10,11... | collective-permute-start | bytes 245768 | tf_op jit(solution)/shard_map/ppermute | solution.py:366

commit v24 on v23

--- a/solution.py
+++ b/solution.py
@@ -219,10 +219,6 @@
     copies[0].wait()
     loads = loads_ref[...]
     square = jnp.sum(loads * loads, axis=1, keepdims=True)
-    copies[1].wait()
-    cols_high[...], cols_low[...] = halves(cols_ref[...])
-    copies[2].wait()
-    couple_high[...], couple_low[...] = halves(couple_ref[...])
     copies[3].wait()
     shape = (CHUNK, CHUNK * rank)
     owner = lax.div(lanes_of(shape), rank)
@@ -234,6 +230,10 @@
         for i in range(CHUNK):
             limit = jnp.where(owner[:1] == i, ranks_ref[0, start + i], limit)
         masks_ref[pl.ds(start, CHUNK), :] = jnp.where((owner == number) & (inner < limit), 1.0, 0.0)
+    copies[1].wait()
+    cols_high[...], cols_low[...] = halves(cols_ref[...])
+    copies[2].wait()
+    couple_high[...], couple_low[...] = halves(couple_ref[...])
     put_message(loads, [square], (cols_high, cols_low), (couple_high, couple_low), masks_ref, sent_ref)
     for copy in copies[4:]:
         copy.wait()

time: 40.8 us -> 40.8 us (level)
  no operation moved by 1% of the time
where the time goes in v24:
time: 40.8 us; the launch traced here: 40.5 us
  blocking collectives  32.6 us (80%)
  Pallas kernels  6.52 us (16%)
  waiting for transfers between devices  1.31 us (3%)
    all_to_all x2, blocking collectives, exchanged(): got = lax.all_to_all(sent, 'strip', 0, 0, tiled=True)  23.6 us
    all_to_all x1, blocking collectives, body(): got = lax.all_to_all(sent, GROUP, 0, 0, tiled=True)  8.98 us
    pallas_call x5, Pallas kernels, call(): pl.pallas_call(kernel, out_shape=[jax.ShapeDtypeStruct(out, F32) if isins...  6.52 us
    ppermute x2, waiting for transfers between devices, exchanged(): return (got, lax.ppermute(got, 'clus', [(0, 1), (1, 0)]))  1.31 us
  transfers between devices with their start and end apart: 2, of which 1 were waited for; matrix products, arithmetic and copies ran while one was open for 0% of the time, Pallas kernels for 3%

profile of v24, /device:TPU:0, one launch (start us, length us, event | category | flops | bytes accessed | tf_op | source)
XLA Modules:
  0.0 40.5 jit_solution(4523179725099709863)
XLA Ops:
  0.0 1.7 %shard_map.82 = (s32[8,4,640]{2,1,0:T(4,128)S(1)}, bf16[32,1024]{1,0:T(8,128)(2,1)S(1)}, bf16[32,1024]{1,0:T(8,128)(2,1)S(1)}, bf16[512,32]{1,0:T(8,128)(2,1)S(1...) custom-call(f32[4,1024]{1,0:T(4,128)} %loads_hbm.1, ...), custom_call_target="tpu_custom_call" | custom-call | bytes 2838592 | tf_op jit(solution)/shard_map/pallas_call | solution.py:350
  1.7 14.1 %all_to_all.15.own_ref = s32[8,4,640]{2,1,0:T(4,128)S(1)} all-to-all(s32[8,4,640]{2,1,0:T(4,128)S(1)} %get-tuple-element.25), channel_id=1, replica_groups=mesh['case'=2,'strip'=8,'clus'=2] {'strip'}, dimensions={0} | all-to-all | bytes 163840 | tf_op jit(solution)/shard_map/all_to_all | solution.py:365
  15.8 0.0 collective-permute-start
  15.8 1.2 %shard_map.83 = (s32[2,80]{1,0:T(2,128)S(1)}, bf16[32,1024]{1,0:T(8,128)(2,1)S(1)}, bf16[32,1024]{1,0:T(8,128)(2,1)S(1)}, bf16[24,128,128]{2,1,0:T(8,128)(2,1)S(1)}) custom-call(f32[4,1024]{1,0:T(4,128)S(1)} %get-tuple-element.26.loads_ref, s32[2,80]{1,0:T(2,128)} %bitcast.6, f32[32,1024]{1,0:T(8,128)} %rows_hbm.1, bf16[80,128,128]{2,1,0:T(8,128)(2,1)} %tiles_hbm.3), custom_call_target="tpu_custom_call" | custom-call | bytes 2769536 | tf_op jit(solution)/shard_map/pallas_call | solution.py:350
  17.0 0.0 collective-permute-done.other_ref
  17.1 1.6 %shard_map.84 = (s32[8,4,640]{2,1,0:T(4,128)S(1)}, f32[4,1024]{1,0:T(4,128)S(1)}, f32[24,1024]{1,0:T(8,128)S(1)}, f32[8,128]{1,0:T(8,128)S(1)}) custom-call(s32[8,4,640]{2,1,0:T(4,128)S(1)} %all_to_all.15.own_ref, s32[8,4,640]{2,1,0:T(4,128)S(1)} %collective-permute-done.other_ref, f32[4,1024]{1,0:T(4,128)S(1)} %get-tuple-element.26.loads_ref, ...), custom_call_target="tpu_custom_call" | custom-call | bytes 3166848 | tf_op jit(solution)/shard_map/pallas_call | solution.py:350
  18.6 9.6 %all_to_all.16.own_ref = s32[8,4,640]{2,1,0:T(4,128)S(1)} all-to-all(s32[8,4,640]{2,1,0:T(4,128)S(1)} %get-tuple-element.38), channel_id=1, replica_groups=mesh['case'=2,'strip'=8,'clus'=2] {'strip'}, dimensions={0} | all-to-all | bytes 163840 | tf_op jit(solution)/shard_map/all_to_all | solution.py:365
  28.2 0.0 collective-permute-start.1
  28.2 1.3 %collective-permute-done.1.other_ref = s32[8,4,640]{2,1,0:T(4,128)S(1)} collective-permute-done((s32[8,4,640]{2,1,0:T(4,128)S(1)}, s32[8,4,640]{2,1,0:T(4,128)S(1)}, u32[]{:S(2)}, u32[]{:S(2)}) %collective-permute-start.1) | collective-permute-done | bytes 81952 | tf_op jit(solution)/shard_map/ppermute | solution.py:366
  29.5 1.2 %shard_map.85 = (f32[16,1,128]{2,1,0:T(1,128)S(1)}, f32[8,1024]{1,0:T(8,128)S(1)}, f32[12,128]{1,0:T(8,128)S(1)}) custom-call(s32[8,4,640]{2,1,0:T(4,128)S(1)} %all_to_all.16.own_ref, s32[8,4,640]{2,1,0:T(4,128)S(1)} %collective-permute-done.1.other_ref, f32[4,1024]{1,0:T(4,128)S(1)} %get-tuple-element.26.loads_ref, ...), custom_call_target="tpu_custom_call" | custom-call | bytes 3056256 | tf_op jit(solution)/shard_map/pallas_call | solution.py:350
  30.7 9.0 %all_to_all.17.got_ref = f32[16,1,128]{2,1,0:T(1,128)S(1)} all-to-all(f32[16,1,128]{2,1,0:T(1,128)S(1)} %get-tuple-element.42), channel_id=1, replica_groups=mesh['case'=2,'strip'=8,'clus'=2] {'strip','clus'}, dimensions={0} | all-to-all | bytes 16384 | tf_op jit(solution)/shard_map/all_to_all | solution.py:429
  39.7 0.8 %shard_map.86 = f32[4,1024]{1,0:T(4,128)} custom-call(f32[16,1,128]{2,1,0:T(1,128)S(1)} %all_to_all.17.got_ref, f32[8,1024]{1,0:T(8,128)S(1)} %get-tuple-element.43.basis_ref, f32[12,128]{1,0:T(8,128)S(1)} %get-tuple-element.44.coeff_ref), custom_call_target="tpu_custom_call" | custom-call | bytes 47104 | tf_op jit(solution)/shard_map/pallas_call | solution.py:350
Async XLA Ops:
  15.8 1.3 %collective-permute-start = (s32[8,4,640]{2,1,0:T(4,128)S(1)}, s32[8,4,640]{2,1,0:T(4,128)S(1)}, u32[]{:S(2)}, u32[]{:S(2)}) collective-permute-start(s32[8,4,640]{2,1,0:T(4,128)S(1)} %all_to_all.15.own_ref), channel_id=1, source_target_pairs={{0,1},{1,0},{2,3},{3,2},{4,5},{5,4},{6,7},{7,6},{8,9},{9,8},{10,11... | collective-permute-start | bytes 245768 | tf_op jit(solution)/shard_map/ppermute | solution.py:366
  28.2 1.3 %collective-permute-start.1 = (s32[8,4,640]{2,1,0:T(4,128)S(1)}, s32[8,4,640]{2,1,0:T(4,128)S(1)}, u32[]{:S(2)}, u32[]{:S(2)}) collective-permute-start(s32[8,4,640]{2,1,0:T(4,128)S(1)} %all_to_all.16.own_ref), channel_id=1, source_target_pairs={{0,1},{1,0},{2,3},{3,2},{4,5},{5,4},{6,7},{7,6},{8,9},{9,8},{10,11... | collective-permute-start | bytes 245768 | tf_op jit(solution)/shard_map/ppermute | solution.py:366

commit v25 on v24

--- a/solution.py
+++ b/solution.py
@@ -380,7 +380,7 @@
     message = Plain((strips, nrhs, panels // 2 + LANES), jnp.int32)
     index = pltpu.SMEM(near_list.shape, jnp.int32)
     scratch = [index, pltpu.SemaphoreType.DMA((1,)), pltpu.VMEM((3 * rows, CORES * nrhs, tile), F32)]
-    late = PIECE * (blocks * 3 // (10 * PIECE))
+    late = PIECE * (blocks // (5 * PIECE))
     tiles0, tiles1 = (jax.ShapeDtypeStruct((count, tile, tile), BF16) for count in (blocks - late, late))
     scratch += [pltpu.VMEM((CORES * rows, CORES * nrhs, tile), F32)] * 4
 

time: 40.8 us -> 40.8 us (level)
  transfers between devices with their start and end apart: 2 -> 2, of which waited for: 1 -> 2; matrix products, arithmetic and copies ran while one was open for 0% -> 0% of each run, Pallas kernels for 3% -> 3%
where the time goes in v25:
time: 40.8 us; the launch traced here: 40.5 us
  blocking collectives  32.6 us (80%)
  Pallas kernels  6.51 us (16%)
  waiting for transfers between devices  1.4 us (3%)
    all_to_all x2, blocking collectives, exchanged(): got = lax.all_to_all(sent, 'strip', 0, 0, tiled=True)  23.6 us
    all_to_all x1, blocking collectives, body(): got = lax.all_to_all(sent, GROUP, 0, 0, tiled=True)  8.98 us
    pallas_call x5, Pallas kernels, call(): pl.pallas_call(kernel, out_shape=[jax.ShapeDtypeStruct(out, F32) if isins...  6.51 us
    ppermute x2, waiting for transfers between devices, exchanged(): return (got, lax.ppermute(got, 'clus', [(0, 1), (1, 0)]))  1.4 us
  transfers between devices with their start and end apart: 2, of which 2 were waited for; matrix products, arithmetic and copies ran while one was open for 0% of the time, Pallas kernels for 3%

profile of v25, /device:TPU:0, one launch (start us, length us, event | category | flops | bytes accessed | tf_op | source)
XLA Modules:
  0.0 40.5 jit_solution(2537361671568332357)
XLA Ops:
  0.0 1.8 %shard_map.82 = (s32[8,4,640]{2,1,0:T(4,128)S(1)}, bf16[32,1024]{1,0:T(8,128)(2,1)S(1)}, bf16[32,1024]{1,0:T(8,128)(2,1)S(1)}, bf16[512,32]{1,0:T(8,128)(2,1)S(1...) custom-call(f32[4,1024]{1,0:T(4,128)} %loads_hbm.1, ...), custom_call_target="tpu_custom_call" | custom-call | bytes 2838592 | tf_op jit(solution)/shard_map/pallas_call | solution.py:350
  1.8 14.1 %all_to_all.15.own_ref = s32[8,4,640]{2,1,0:T(4,128)S(1)} all-to-all(s32[8,4,640]{2,1,0:T(4,128)S(1)} %get-tuple-element.25), channel_id=1, replica_groups=mesh['case'=2,'strip'=8,'clus'=2] {'strip'}, dimensions={0} | all-to-all | bytes 163840 | tf_op jit(solution)/shard_map/all_to_all | solution.py:365
  15.9 0.0 collective-permute-start
  15.9 1.1 %shard_map.83 = (s32[2,80]{1,0:T(2,128)S(1)}, bf16[32,1024]{1,0:T(8,128)(2,1)S(1)}, bf16[32,1024]{1,0:T(8,128)(2,1)S(1)}, bf16[16,128,128]{2,1,0:T(8,128)(2,1)S(1)}) custom-call(f32[4,1024]{1,0:T(4,128)S(1)} %get-tuple-element.26.loads_ref, s32[2,80]{1,0:T(2,128)} %bitcast.6, f32[32,1024]{1,0:T(8,128)} %rows_hbm.1, bf16[80,128,128]{2,1,0:T(8,128)(2,1)} %tiles_hbm.3), custom_call_target="tpu_custom_call" | custom-call | bytes 2769536 | tf_op jit(solution)/shard_map/pallas_call | solution.py:350
  17.0 0.1 collective-permute-done.other_ref
  17.1 1.6 %shard_map.84 = (s32[8,4,640]{2,1,0:T(4,128)S(1)}, f32[4,1024]{1,0:T(4,128)S(1)}, f32[24,1024]{1,0:T(8,128)S(1)}, f32[8,128]{1,0:T(8,128)S(1)}) custom-call(s32[8,4,640]{2,1,0:T(4,128)S(1)} %all_to_all.15.own_ref, s32[8,4,640]{2,1,0:T(4,128)S(1)} %collective-permute-done.other_ref, f32[4,1024]{1,0:T(4,128)S(1)} %get-tuple-element.26.loads_ref, ...), custom_call_target="tpu_custom_call" | custom-call | bytes 3166848 | tf_op jit(solution)/shard_map/pallas_call | solution.py:350
  18.7 9.5 %all_to_all.16.own_ref = s32[8,4,640]{2,1,0:T(4,128)S(1)} all-to-all(s32[8,4,640]{2,1,0:T(4,128)S(1)} %get-tuple-element.38), channel_id=1, replica_groups=mesh['case'=2,'strip'=8,'clus'=2] {'strip'}, dimensions={0} | all-to-all | bytes 163840 | tf_op jit(solution)/shard_map/all_to_all | solution.py:365
  28.2 0.0 collective-permute-start.1
  28.2 1.3 %collective-permute-done.1.other_ref = s32[8,4,640]{2,1,0:T(4,128)S(1)} collective-permute-done((s32[8,4,640]{2,1,0:T(4,128)S(1)}, s32[8,4,640]{2,1,0:T(4,128)S(1)}, u32[]{:S(2)}, u32[]{:S(2)}) %collective-permute-start.1) | collective-permute-done | bytes 81952 | tf_op jit(solution)/shard_map/ppermute | solution.py:366
  29.5 1.2 %shard_map.85 = (f32[16,1,128]{2,1,0:T(1,128)S(1)}, f32[8,1024]{1,0:T(8,128)S(1)}, f32[12,128]{1,0:T(8,128)S(1)}) custom-call(s32[8,4,640]{2,1,0:T(4,128)S(1)} %all_to_all.16.own_ref, s32[8,4,640]{2,1,0:T(4,128)S(1)} %collective-permute-done.1.other_ref, f32[4,1024]{1,0:T(4,128)S(1)} %get-tuple-element.26.loads_ref, ...), custom_call_target="tpu_custom_call" | custom-call | bytes 3056256 | tf_op jit(solution)/shard_map/pallas_call | solution.py:350
  30.7 9.0 %all_to_all.17.got_ref = f32[16,1,128]{2,1,0:T(1,128)S(1)} all-to-all(f32[16,1,128]{2,1,0:T(1,128)S(1)} %get-tuple-element.42), channel_id=1, replica_groups=mesh['case'=2,'strip'=8,'clus'=2] {'strip','clus'}, dimensions={0} | all-to-all | bytes 16384 | tf_op jit(solution)/shard_map/all_to_all | solution.py:429
  39.7 0.8 %shard_map.86 = f32[4,1024]{1,0:T(4,128)} custom-call(f32[16,1,128]{2,1,0:T(1,128)S(1)} %all_to_all.17.got_ref, f32[8,1024]{1,0:T(8,128)S(1)} %get-tuple-element.43.basis_ref, f32[12,128]{1,0:T(8,128)S(1)} %get-tuple-element.44.coeff_ref), custom_call_target="tpu_custom_call" | custom-call | bytes 47104 | tf_op jit(solution)/shard_map/pallas_call | solution.py:350
Async XLA Ops:
  15.9 1.3 %collective-permute-start = (s32[8,4,640]{2,1,0:T(4,128)S(1)}, s32[8,4,640]{2,1,0:T(4,128)S(1)}, u32[]{:S(2)}, u32[]{:S(2)}) collective-permute-start(s32[8,4,640]{2,1,0:T(4,128)S(1)} %all_to_all.15.own_ref), channel_id=1, source_target_pairs={{0,1},{1,0},{2,3},{3,2},{4,5},{5,4},{6,7},{7,6},{8,9},{9,8},{10,11... | collective-permute-start | bytes 245768 | tf_op jit(solution)/shard_map/ppermute | solution.py:366
  28.2 1.3 %collective-permute-start.1 = (s32[8,4,640]{2,1,0:T(4,128)S(1)}, s32[8,4,640]{2,1,0:T(4,128)S(1)}, u32[]{:S(2)}, u32[]{:S(2)}) collective-permute-start(s32[8,4,640]{2,1,0:T(4,128)S(1)} %all_to_all.16.own_ref), channel_id=1, source_target_pairs={{0,1},{1,0},{2,3},{3,2},{4,5},{5,4},{6,7},{7,6},{8,9},{9,8},{10,11... | collective-permute-start | bytes 245768 | tf_op jit(solution)/shard_map/ppermute | solution.py:366
